TPU v7x, 32 devices: a whole 2x2x4 slice. The times are simulated.
32 devices in a mesh: dp: 4 (over z), seq: 8 (over y, x, core).
Axes of the slice: x: 2, y: 2, z: 4, core: 2. Of those that a mesh axis runs over, the one named last changes fastest.
Arguments:
- features: bfloat16 [4, 8, 128, 2560], P('dp', None, 'seq'), may hold values from -6 to 6
- frozen_query_weight: bfloat16 [4, 8, 128, 1024], P('dp', None, 'seq'), may hold values from -100 to 100
- source_keys: bfloat16 [4, 8, 128, 1024], P('dp', None, 'seq'), may hold values from -6 to 6
- source_values: bfloat16 [4, 8, 128, 1024], P('dp', None, 'seq'), may hold values from -6 to 6
- output_gradient: bfloat16 [4, 8, 128, 1024], P('dp', None, 'seq'), may hold values from -6 to 6
- adapter_down_weight: bfloat16 [2560, 64], replicated, may hold values from -0.125 to 0.125
- adapter_up_weight: bfloat16 [64, 1024], replicated, may hold values from -0.75 to 0.75
- source_block_plan: int32 [4, 8], replicated, may hold values from 0 to 31, as said below
- segments: int32 [4, 1024], P('dp'), may hold values from 0 to 1, never falling along the last dimension, each value on 1 to 640 neighbouring positions
Outputs:
- down_grad: float32 [2560, 64], P('seq')
- up_grad: float32 [64, 1024], P(None, 'seq')
- log_norm: float32 [4, 8, 1024], P('dp', 'seq')
Inputs may be any that keep to these rules, and one draw needn't show every extreme that they name: `source_block_plan`: each entry names a source block as group * 8 + block; every source block is named exactly once; from one group to another group at most 2 blocks go, and some pairs of groups carry exactly 2. Within a group the segment numbers never fall and all 2 segments occur; a segment spans at most 640 positions.
All inputs are finite; a program needn't handle non-finite values.
Results may differ from a plain program's by a relative error of at most 0.0087.
Values may be sent and summed in bfloat16 or wider, within the bound.
No kernel may reach another device: no remote copies, remote signals or barrier semaphores. Data moves between devices by JAX's collectives and lax.ppermute only.
A program may use at most 64 MiB of HBM per device.

v0:
```python
import math

import jax
import jax.numpy as jnp
from jax import lax
from jax.sharding import PartitionSpec as P

CAP = 2
CLIPS = 2


def attend_head(query, key_rows, value_rows, cotangent, segment, clip_count, reach_rows):
    length = query.shape[0]
    width = query.shape[1]
    piece_count = 8
    piece_rows = reach_rows // piece_count
    scaling = 1.0 / math.sqrt(width)
    query_padded = jnp.pad(query, ((0, reach_rows), (0, 0)))
    grad_padded = jnp.pad(cotangent, ((0, reach_rows), (0, 0)))
    keys_padded = jnp.pad(key_rows, ((0, reach_rows), (0, 0)))
    values_padded = jnp.pad(value_rows, ((0, reach_rows), (0, 0)))
    segment_padded = jnp.pad(segment, (0, reach_rows), constant_values=-1)
    clip_ids = jnp.arange(clip_count, dtype=jnp.int32)
    starts = jnp.sum((segment[None, :] < clip_ids[:, None]).astype(jnp.int32), axis=1)

    def piece_pass(piece_index):
        clip_slice = piece_index // piece_count
        start = lax.dynamic_index_in_dim(starts, clip_slice, 0, keepdims=False)
        query_start = start + piece_index % piece_count * piece_rows
        query_tile = lax.dynamic_slice_in_dim(query_padded, query_start, piece_rows, 0)
        grad_tile = lax.dynamic_slice_in_dim(grad_padded, query_start, piece_rows, 0)
        seg_tile = lax.dynamic_slice_in_dim(segment_padded, query_start, piece_rows, 0)
        key_tile = lax.dynamic_slice_in_dim(keys_padded, start, reach_rows, 0)
        value_tile = lax.dynamic_slice_in_dim(values_padded, start, reach_rows, 0)
        seg_cols = lax.dynamic_slice_in_dim(segment_padded, start, reach_rows, 0)
        in_clip = seg_tile == clip_slice
        allowed = in_clip[:, None] & (seg_cols == clip_slice)[None, :]
        scores = (
            lax.dot_general(
                query_tile, key_tile, (((1,), (1,)), ((), ())), preferred_element_type=jnp.float32
            )
            * scaling
        )
        scores = jnp.where(allowed, scores, -1e30)
        maximum = jnp.max(scores, axis=1, keepdims=True)
        exponent = jnp.where(allowed, jnp.exp(scores - maximum), 0.0)
        totals = jnp.where(in_clip[:, None], jnp.sum(exponent, axis=1, keepdims=True), 1.0)
        log_norm = jnp.where(in_clip, maximum[:, 0] + jnp.log(totals[:, 0]), 0.0)
        probs = exponent / totals
        weights = probs.astype(jnp.bfloat16)
        attended = jnp.dot(weights, value_tile, preferred_element_type=jnp.float32)
        delta = jnp.sum(grad_tile.astype(jnp.float32) * attended, axis=1, keepdims=True)
        dprob = lax.dot_general(
            grad_tile, value_tile, (((1,), (1,)), ((), ())), preferred_element_type=jnp.float32
        )
        dscore = (probs * (dprob - delta)).astype(jnp.bfloat16)
        query_gradient = (
            jnp.dot(dscore, key_tile, preferred_element_type=jnp.float32) * scaling
        ).astype(jnp.bfloat16)
        query_gradient = jnp.where(in_clip[:, None], query_gradient, jnp.zeros((), jnp.bfloat16))
        return (query_gradient, log_norm, query_start)

    total_pieces = piece_count * (clip_count - 1)
    dquery_pieces, log_pieces, piece_starts = lax.map(
        piece_pass, jnp.arange(total_pieces, dtype=jnp.int32)
    )

    def place(index, carry):
        grad_total, log_total = carry
        where_at = lax.dynamic_index_in_dim(piece_starts, index, 0, keepdims=False)
        grad_piece = lax.dynamic_index_in_dim(dquery_pieces, index, 0, keepdims=False)
        log_piece = lax.dynamic_index_in_dim(log_pieces, index, 0, keepdims=False)
        grad_old = lax.dynamic_slice_in_dim(grad_total, where_at, piece_rows, 0)
        log_old = lax.dynamic_slice_in_dim(log_total, where_at, piece_rows, 0)
        grad_total = lax.dynamic_update_slice_in_dim(grad_total, grad_old + grad_piece, where_at, 0)
        log_total = lax.dynamic_update_slice_in_dim(log_total, log_old + log_piece, where_at, 0)
        return (grad_total, log_total)

    grad_init = jnp.zeros((length + reach_rows, width), jnp.bfloat16)
    log_init = jnp.zeros((length + reach_rows,), jnp.float32)
    grad_total, log_total = lax.fori_loop(0, total_pieces, place, (grad_init, log_init))
    return (grad_total[:length], log_total[:length])


def routing_tables(source_block_plan, group_index, cap_slots):
    group_count, block_count = source_block_plan.shape
    source_group = source_block_plan // block_count
    source_local = source_block_plan % block_count
    dest_groups = jnp.arange(group_count, dtype=jnp.int32)[:, None]
    outgoing = (source_group == group_index) & (dest_groups != group_index)
    out_rank = jnp.cumsum(outgoing.astype(jnp.int32), axis=1) - 1
    slot_ids = jnp.arange(cap_slots, dtype=jnp.int32)
    chosen = outgoing[:, :, None] & (out_rank[:, :, None] == slot_ids[None, None, :])
    send_index = jnp.sum(jnp.where(chosen, source_local[:, :, None], 0), axis=1)
    send_valid = jnp.any(chosen, axis=1)
    own_group = lax.dynamic_index_in_dim(source_group, group_index, 0, keepdims=False)
    own_local = lax.dynamic_index_in_dim(source_local, group_index, 0, keepdims=False)
    incoming = own_group != group_index
    positions = jnp.arange(block_count, dtype=jnp.int32)
    earlier = (own_group[None, :] == own_group[:, None]) & (positions[None, :] < positions[:, None])
    in_rank = jnp.sum(earlier.astype(jnp.int32), axis=1)
    return (send_index, send_valid, incoming, own_group, in_rank, own_local)


def pack_blocks(local, send_index, send_valid):
    picked = jnp.take(local, send_index, axis=0)
    return jnp.where(send_valid[:, :, None, None], picked, jnp.zeros((), local.dtype))


def unpack_blocks(received, local, tables, cap_slots):
    incoming, own_group, in_rank, own_local = tables
    flat = received.reshape((-1,) + received.shape[2:])
    slot_index = jnp.where(incoming, own_group * cap_slots + in_rank, 0)
    remote = jnp.take(flat, slot_index, axis=0)
    staying = jnp.take(local, own_local, axis=0)
    return jnp.where(incoming[:, None, None], remote, staying)


def per_device(
    features,
    frozen_query_weight,
    source_keys,
    source_values,
    output_gradient,
    adapter_down_weight,
    adapter_up_weight,
    source_block_plan,
    segments,
):
    group_count = lax.axis_size("dp")
    group_index = lax.axis_index("dp")
    block_count = features.shape[1]
    feat_local = features[0]
    base_local = frozen_query_weight[0]
    keys_local = source_keys[0]
    values_local = source_values[0]
    send_index, send_valid, incoming, own_group, in_rank, own_local = routing_tables(
        source_block_plan, group_index, CAP
    )
    tables = (incoming, own_group, in_rank, own_local)
    contract_final_axis = (((2,), (0,)), ((), ()))
    shuffled = (
        lax.all_to_all(
            pack_blocks(feat_local, send_index, send_valid),
            "dp",
            split_axis=0,
            concat_axis=0,
            tiled=True,
        ),
        lax.all_to_all(
            pack_blocks(base_local, send_index, send_valid),
            "dp",
            split_axis=0,
            concat_axis=0,
            tiled=True,
        ),
        lax.all_to_all(
            pack_blocks(keys_local, send_index, send_valid),
            "dp",
            split_axis=0,
            concat_axis=0,
            tiled=True,
        ),
        lax.all_to_all(
            pack_blocks(values_local, send_index, send_valid),
            "dp",
            split_axis=0,
            concat_axis=0,
            tiled=True,
        ),
    )
    feature_dest = unpack_blocks(shuffled[0], feat_local, tables, CAP)
    base_query_dest = unpack_blocks(shuffled[1], base_local, tables, CAP)
    keys_dest = unpack_blocks(shuffled[2], keys_local, tables, CAP)
    values_dest = unpack_blocks(shuffled[3], values_local, tables, CAP)
    adapter_params = lax.dot_general(
        feature_dest, adapter_down_weight, contract_final_axis, preferred_element_type=jnp.float32
    ).astype(jnp.bfloat16)
    query_rows = (
        base_query_dest.astype(jnp.float32)
        + lax.dot_general(
            adapter_params,
            adapter_up_weight,
            contract_final_axis,
            preferred_element_type=jnp.float32,
        )
    ).astype(jnp.bfloat16)
    head_query, head_keys, head_values, head_grads = (
        lax.all_to_all(query_rows, "seq", split_axis=2, concat_axis=1, tiled=True),
        lax.all_to_all(keys_dest, "seq", split_axis=2, concat_axis=1, tiled=True),
        lax.all_to_all(values_dest, "seq", split_axis=2, concat_axis=1, tiled=True),
        lax.all_to_all(output_gradient[0], "seq", split_axis=2, concat_axis=1, tiled=True),
    )
    length = head_query.shape[0] * head_query.shape[1]
    reach_rows = length // 2 + length // 8
    head_width = head_query.shape[2]
    segment = segments[0]
    head_query = head_query.reshape(length, head_width)
    head_keys = head_keys.reshape(length, head_width)
    head_values = head_values.reshape(length, head_width)
    head_grads = head_grads.reshape(length, head_width)
    dquery_head, log_head = attend_head(
        head_query, head_keys, head_values, head_grads, segment, CLIPS, reach_rows
    )
    norm_pieces = [log_head]
    log_norm = jnp.stack(norm_pieces, axis=0)
    query_gradient = lax.all_to_all(
        dquery_head.reshape(block_count, length // block_count, head_width),
        "seq",
        split_axis=1,
        concat_axis=2,
        tiled=True,
    )
    adapter_gradient = lax.dot_general(
        query_gradient,
        adapter_up_weight,
        (((2,), (1,)), ((), ())),
        preferred_element_type=jnp.float32,
    ).astype(jnp.bfloat16)
    contract_tokens = (((0, 1), (0, 1)), ((), ()))
    down_part = lax.dot_general(
        feature_dest, adapter_gradient, contract_tokens, preferred_element_type=jnp.float32
    )
    up_part = lax.dot_general(
        adapter_params, query_gradient, contract_tokens, preferred_element_type=jnp.float32
    )
    down_share, up_share = (
        lax.psum_scatter(down_part, "seq", scatter_dimension=0, tiled=True),
        lax.psum_scatter(up_part, "seq", scatter_dimension=1, tiled=True),
    )
    down_total, up_total = lax.psum((down_share, up_share), "dp")
    grad_norm = 4.0 / math.sqrt(group_count * length)
    return (down_total * grad_norm, up_total * grad_norm, log_norm[None])


def solution(mesh):
    in_specs = (
        P("dp", None, "seq", None),
        P("dp", None, "seq", None),
        P("dp", None, "seq", None),
        P("dp", None, "seq", None),
        P("dp", None, "seq", None),
        P(),
        P(),
        P(),
        P("dp", None),
    )
    out_specs = (P("seq", None), P(None, "seq"), P("dp", "seq", None))
    return jax.shard_map(
        per_device, mesh=mesh, in_specs=in_specs, out_specs=out_specs, check_vma=False
    )
```

profile of v0, /device:TPU:0, one launch (start us, length us, event | category | flops | bytes accessed | tf_op | source)
XLA Modules:
  0.0 380.8 jit_solution(11136346795563694115)
XLA Ops:
  9.6 1.5 gather_fusion.3
  11.1 1.5 gather_fusion.6
  12.7 1.5 gather_fusion.9
  15.1 15.1 %all_to_all.98 = bf16[4,2,16,1024]{3,2,1,0:T(8,128)(2,1)} all-to-all(bf16[4,2,16,1024]{3,2,1,0:T(8,128)(2,1)S(1)} %get-tuple-element.314), channel_id=1, replica_groups=mesh['dp'=4,'seq'=8] {'dp'}, dimensions={0} | all-to-all | bytes 524288 | tf_op jit(solution)/shard_map/all_to_all | solution.py:150
  30.2 3.4 all-to-all-start.3
  34.4 7.1 %all-to-all-done.3 = bf16[4,2,16,1024]{3,2,1,0:T(8,128)(2,1)S(1)} async-done(((bf16[4,2,16,1024]{3,2,1,0:T(8,128)(2,1)}), bf16[4,2,16,1024]{3,2,1,0:T(8,128)(2,1)S(1)}, u32[]{:S(2)}, u32[]{:S(2)}) %all-to-all-start.3) | async-done | bytes 262176 | tf_op jit(solution)/shard_map/all_to_all | solution.py:157
  42.2 3.4 all-to-all-start.6
  46.9 5.5 %all-to-all-done.6 = bf16[4,2,16,1024]{3,2,1,0:T(8,128)(2,1)S(1)} async-done(((bf16[4,2,16,1024]{3,2,1,0:T(8,128)(2,1)}), bf16[4,2,16,1024]{3,2,1,0:T(8,128)(2,1)S(1)}, u32[]{:S(2)}, u32[]{:S(2)}) %all-to-all-start.6) | async-done | bytes 262176 | tf_op jit(solution)/shard_map/all_to_all | solution.py:164
  52.4 3.5 all-to-all-start
  61.2 2.5 copy.62
  63.6 1.7 bitcast_bitcast_fusion
  65.4 2.8 reshape.257
  68.2 2.2 gather_fusion.4
  70.4 1.5 gather_fusion.7
  71.9 1.5 gather_fusion.10
  73.4 2.0 select_select_fusion.2
  75.5 2.5 copy.60
  78.0 2.8 reshape.255
  80.8 2.5 copy.66
  83.3 2.8 reshape.259
  86.1 3.9 %all-to-all-start.5 = ((bf16[8,2,8192]{2,1,0:T(2,128)(2,1)}), bf16[8,2,8192]{2,1,0:T(2,128)(2,1)S(1)}, u32[]{:S(2)}, u32[]{:S(2)}) async-start(bf16[8,2,8192]{2,1,0:T(2,128)(2,1)} %reshape.257), calls=%async_computation.5 | async-start | bytes 524288 | tf_op jit(solution)/shard_map/all_to_all | solution.py:192
  90.8 6.1 %all-to-all-done.5 = bf16[8,2,8192]{2,1,0:T(2,128)(2,1)S(1)} async-done(((bf16[8,2,8192]{2,1,0:T(2,128)(2,1)}), bf16[8,2,8192]{2,1,0:T(2,128)(2,1)S(1)}, u32[]{:S(2)}, u32[]{:S(2)}) %all-to-all-start.5) | async-done | bytes 262176 | tf_op jit(solution)/shard_map/all_to_all | solution.py:192
  96.9 3.4 all-to-all-start.4
  101.6 5.6 %all-to-all-done.4 = bf16[8,2,8192]{2,1,0:T(2,128)(2,1)S(1)} async-done(((bf16[8,2,8192]{2,1,0:T(2,128)(2,1)}), bf16[8,2,8192]{2,1,0:T(2,128)(2,1)S(1)}, u32[]{:S(2)}, u32[]{:S(2)}) %all-to-all-start.4) | async-done | bytes 262176 | tf_op jit(solution)/shard_map/all_to_all | solution.py:190
  107.2 3.4 all-to-all-start.7
  110.6 1.9 fusion.31
  112.6 2.5 copy.56
  115.1 2.8 reshape.253
  117.9 4.1 %all-to-all-start.2 = ((bf16[8,2,8192]{2,1,0:T(2,128)(2,1)}), bf16[8,2,8192]{2,1,0:T(2,128)(2,1)}, u32[]{:S(2)}, u32[]{:S(2)}) async-start(bf16[8,2,8192]{2,1,0:T(2,128)(2,1)} %reshape.253), calls=%async_computation.2 | async-start | bytes 524288 | tf_op jit(solution)/shard_map/all_to_all | solution.py:189
  133.2 2.4 reshape.254
  137.1 81.9 %while.33 = (s32[]{:T(128)}, bf16[8,80,128]{2,1,0:T(8,128)(2,1)}, f32[8,80]{1,0:T(8,128)S(1)}, s32[8]{0:T(128)S(1)}, s32[8]{0:T(128)S(1)}, /*index=5*/s32[2]{0:T...) while((s32[]{:T(128)}, bf16[8,80,128]{2,1,0:T(8,128)(2,1)}, ...), condition=%wide.region_9.13_spmd.clone, body=%wide.region_5.12_spmd.sunk.clone | while | flops 53515072 | bytes 1573350 | solution.py:64
  145.4 1.9 fusion.77
  155.6 1.9 fusion.77
  165.8 1.9 fusion.77
  176.1 1.9 fusion.77
  186.3 1.9 fusion.77
  196.6 1.9 fusion.77
  206.8 1.9 fusion.77
  217.0 1.9 fusion.77
  219.2 29.8 %while.34 = (s32[]{:T(128)}, bf16[1664,128]{1,0:T(8,128)(2,1)S(1)}, f32[1664]{0:T(1024)S(1)}, s32[8]{0:T(128)S(1)}, bf16[8,80,128]{2,1,0:T(8,128)(2,1)}, /*index=5*/f32[8,80]{1,0:T(8,128)S(1)}) while((s32[]{:T(128)}, bf16[1664,128]{1,0:T(8,128)(2,1)S(1)}, f32[1664]{0:T(1024)S(1)}, s32[8]{0:T(128)S(1)}, ...), condition=%wide.region_11.15_spmd.clone, body=%wide.region_10.14_spmd.sunk.clone | while | flops 41045 | bytes 104071 | solution.py:81
  249.2 10.7 %all_to_all.99 = bf16[8,128,128]{2,0,1:T(8,128)(2,1)S(1)} all-to-all(bf16[8,128,128]{2,0,1:T(8,128)(2,1)S(1)} %copy.68), channel_id=1, replica_groups=mesh['dp'=4,'seq'=8] {'seq'}, dimensions={1} | all-to-all | bytes 524288 | tf_op jit(solution)/shard_map/all_to_all | solution.py:207
  261.2 1.7 convolution_bitcast_fusion
  263.6 30.9 %reduce-scatter.5.cloned.1.call-done = f32[64,128]{1,0:T(8,128)} async-done(((f32[64,1024]{1,0:T(8,128)}), f32[64,128]{1,0:T(8,128)}) %reduce-scatter.5.cloned.1.call-update) | async-done | bytes 32784 | tf_op jit(solution)/shard_map/reduce_scatter | solution.py:229
  294.5 19.6 %psum.15 = f32[64,128]{1,0:T(8,128)S(1)} all-reduce(f32[64,128]{1,0:T(8,128)} %reduce-scatter.5.cloned.1.call-done), channel_id=1, replica_groups=mesh['dp'=4,'seq'=8] {'dp'}, use_global_device_ids=true, to_apply=%region_15.19 | all-reduce | flops 8192 | bytes 65536 | tf_op jit(solution)/shard_map/psum | solution.py:231
  314.1 21.3 %reduce-scatter.7.cloned.1.call-done = f32[320,64]{1,0:T(8,128)} async-done(((f32[2560,64]{1,0:T(8,128)}), f32[320,64]{1,0:T(8,128)}) %reduce-scatter.7.cloned.1.call-update) | async-done | bytes 81936
  335.4 1.7 copy.73
  337.7 35.0 %all-reduce.7.cloned.1.call-done = f32[320,64]{0,1:T(8,128)} async-done(((f32[320,64]{0,1:T(8,128)}), f32[320,64]{0,1:T(8,128)}) %all-reduce.7.cloned.1.call-update) | async-done | bytes 81936 | tf_op jit(solution)/shard_map/psum | solution.py:231
  372.7 1.5 broadcast_multiply_fusion
  (214 shorter events, 70.1 us)
Async XLA Ops:
  7.2 26.7 %copy-start = (bf16[1,8,16,2560]{3,2,1,0:T(8,128)(2,1)S(1)}, bf16[1,8,16,2560]{3,2,1,0:T(8,128)(2,1)}, u32[]{:S(2)}) copy-start(bf16[1,8,16,2560]{3,2,1,0:T(8,128)(2,1)} %param.19) | copy-start | bytes 1966084
  30.2 11.3 %all-to-all-start.3 = ((bf16[4,2,16,1024]{3,2,1,0:T(8,128)(2,1)}), bf16[4,2,16,1024]{3,2,1,0:T(8,128)(2,1)S(1)}, u32[]{:S(2)}, u32[]{:S(2)}) async-start(bf16[4,2,16,1024]{3,2,1,0:T(8,128)(2,1)} %get-tuple-element.313), calls=%async_computation.3 | async-start | bytes 524288 | tf_op jit(solution)/shard_map/all_to_all | solution.py:157
  41.6 0.7 copy-start.7
  42.2 10.2 %all-to-all-start.6 = ((bf16[4,2,16,1024]{3,2,1,0:T(8,128)(2,1)}), bf16[4,2,16,1024]{3,2,1,0:T(8,128)(2,1)S(1)}, u32[]{:S(2)}, u32[]{:S(2)}) async-start(bf16[4,2,16,1024]{3,2,1,0:T(8,128)(2,1)} %get-tuple-element.312), calls=%async_computation.6 | async-start | bytes 524288 | tf_op jit(solution)/shard_map/all_to_all | solution.py:164
  45.7 11.7 %copy-start.4 = (bf16[1,8,16,1024]{3,2,1,0:T(8,128)(2,1)S(1)}, bf16[1,8,16,1024]{3,2,1,0:T(8,128)(2,1)}, u32[]{:S(2)}) copy-start(bf16[1,8,16,1024]{3,2,1,0:T(8,128)(2,1)} %param.20) | copy-start | bytes 786436
  45.7 13.0 %copy-start.5 = (bf16[1,8,16,1024]{3,2,1,0:T(8,128)(2,1)S(1)}, bf16[1,8,16,1024]{3,2,1,0:T(8,128)(2,1)}, u32[]{:S(2)}) copy-start(bf16[1,8,16,1024]{3,2,1,0:T(8,128)(2,1)} %param.21) | copy-start | bytes 786436
  46.7 13.2 %copy-start.6 = (bf16[1,8,16,1024]{3,2,1,0:T(8,128)(2,1)S(1)}, bf16[1,8,16,1024]{3,2,1,0:T(8,128)(2,1)}, u32[]{:S(2)}) copy-start(bf16[1,8,16,1024]{3,2,1,0:T(8,128)(2,1)} %param.22) | copy-start | bytes 786436
  46.9 14.3 %copy-start.9 = (bf16[1,8,16,1024]{3,2,1,0:T(8,128)(2,1)S(1)}, bf16[1,8,16,1024]{3,2,1,0:T(8,128)(2,1)}, u32[]{:S(2)}) copy-start(bf16[1,8,16,1024]{3,2,1,0:T(8,128)(2,1)} %param.23) | copy-start | bytes 786436
  52.4 8.8 %copy-start.8 = (bf16[4,2,16,1024]{3,2,1,0:T(8,128)(2,1)}, bf16[4,2,16,1024]{3,2,1,0:T(8,128)(2,1)S(1)}, u32[]{:S(2)}) copy-start(bf16[4,2,16,1024]{3,2,1,0:T(8,128)(2,1)S(1)} %all-to-all-done.6) | copy-start | bytes 786436
  52.4 33.7 %all-to-all-start = ((bf16[4,2,16,2560]{3,2,1,0:T(8,128)(2,1)}), bf16[4,2,16,2560]{3,2,1,0:T(8,128)(2,1)S(1)}, u32[]{:S(2)}, u32[]{:S(2)}) async-start(bf16[4,2,16,2560]{3,2,1,0:T(8,128)(2,1)} %select_select_fusion.1), calls=%async_computation | async-start | bytes 1310720 | tf_op jit(solution)/shard_map/all_to_all | solution.py:143
  86.1 4.5 %copy-start.3 = (bf16[8,16,2560]{2,1,0:T(8,128)(2,1)S(1)}, bf16[8,16,2560]{2,1,0:T(8,128)(2,1)}, u32[]{:S(2)}) copy-start(bf16[8,16,2560]{2,1,0:T(8,128)(2,1)} %gather_fusion.2) | copy-start | bytes 1966084
  86.1 10.8 %all-to-all-start.5 = ((bf16[8,2,8192]{2,1,0:T(2,128)(2,1)}), bf16[8,2,8192]{2,1,0:T(2,128)(2,1)S(1)}, u32[]{:S(2)}, u32[]{:S(2)}) async-start(bf16[8,2,8192]{2,1,0:T(2,128)(2,1)} %reshape.257), calls=%async_computation.5 | async-start | bytes 524288 | tf_op jit(solution)/shard_map/all_to_all | solution.py:192
  90.6 20.1 %copy-start.14 = (bf16[64,1024]{1,0:T(8,128)(2,1)S(1)}, bf16[64,1024]{1,0:T(8,128)(2,1)}, u32[]{:S(2)}) copy-start(bf16[64,1024]{1,0:T(8,128)(2,1)} %param.25) | copy-start | bytes 393220
  90.8 19.8 %copy-start.1 = (bf16[8,16,2560]{2,1,0:T(8,128)(2,1)}, bf16[8,16,2560]{2,1,0:T(8,128)(2,1)S(1)}, u32[]{:S(2)}) copy-start(bf16[8,16,2560]{2,1,0:T(8,128)(2,1)S(1)} %select_select_fusion) | copy-start | bytes 1966084
  96.9 10.3 %all-to-all-start.4 = ((bf16[8,2,8192]{2,1,0:T(2,128)(2,1)}), bf16[8,2,8192]{2,1,0:T(2,128)(2,1)S(1)}, u32[]{:S(2)}, u32[]{:S(2)}) async-start(bf16[8,2,8192]{2,1,0:T(2,128)(2,1)} %reshape.255), calls=%async_computation.4 | async-start | bytes 524288 | tf_op jit(solution)/shard_map/all_to_all | solution.py:190
  101.6 9.0 %copy-start.10 = (bf16[8,16,64]{2,1,0:T(8,128)(2,1)}, bf16[8,16,64]{2,1,0:T(8,128)(2,1)S(1)}, u32[]{:S(2)}) copy-start(bf16[8,16,64]{2,1,0:T(8,128)(2,1)S(1)} %convolution_convert_fusion) | copy-start | bytes 49156
  107.2 10.7 %all-to-all-start.7 = ((bf16[8,2,8192]{2,1,0:T(2,128)(2,1)}), bf16[8,2,8192]{2,1,0:T(2,128)(2,1)S(1)}, u32[]{:S(2)}, u32[]{:S(2)}) async-start(bf16[8,2,8192]{2,1,0:T(2,128)(2,1)} %reshape.259), calls=%async_computation.7 | async-start | bytes 524288 | tf_op jit(solution)/shard_map/all_to_all | solution.py:191
  112.6 9.7 %copy-start.12 = (s32[1,1024]{1,0:T(1,128)S(1)}, s32[1,1024]{1,0:T(1,128)}, u32[]{:S(2)}) copy-start(s32[1,1024]{1,0:T(1,128)} %param.27) | copy-start | bytes 12292
  117.9 15.3 %all-to-all-start.2 = ((bf16[8,2,8192]{2,1,0:T(2,128)(2,1)}), bf16[8,2,8192]{2,1,0:T(2,128)(2,1)}, u32[]{:S(2)}, u32[]{:S(2)}) async-start(bf16[8,2,8192]{2,1,0:T(2,128)(2,1)} %reshape.253), calls=%async_computation.2 | async-start | bytes 524288 | tf_op jit(solution)/shard_map/all_to_all | solution.py:189
  122.0 172.4 %reduce-scatter.5.cloned.1.call-start = ((), (), s32[]{:S(2)}) async-start(), calls=%async_computation.12 | async-start | bytes 294912 | tf_op jit(solution)/shard_map/reduce_scatter | solution.py:229
  135.6 1.5 copy-start.13
  135.6 1.5 copy-start.16
  219.1 41.2 %copy-start.11 = (bf16[8,16,64]{2,1,0:T(8,128)(2,1)S(1)}, bf16[8,16,64]{2,1,0:T(8,128)(2,1)}, u32[]{:S(2)}) copy-start(bf16[8,16,64]{2,1,0:T(8,128)(2,1)} %copy-done.10) | copy-start | bytes 49156
  219.1 42.1 %copy-start.2 = (bf16[8,16,2560]{2,1,0:T(8,128)(2,1)S(1)}, bf16[8,16,2560]{2,1,0:T(8,128)(2,1)}, u32[]{:S(2)}) copy-start(bf16[8,16,2560]{2,1,0:T(8,128)(2,1)} %copy-done.1) | copy-start | bytes 1966084
  219.1 42.1 %copy-start.15 = (bf16[64,1024]{1,0:T(8,128)(2,1)S(1)}, bf16[64,1024]{1,0:T(8,128)(2,1)}, u32[]{:S(2)}) copy-start(bf16[64,1024]{1,0:T(8,128)(2,1)} %param.25) | copy-start | bytes 393220
  261.1 74.2 %reduce-scatter.7.cloned.1.call-start = ((), (), s32[]{:S(2)}) async-start(), calls=%async_computation.13 | async-start | bytes 1474560
  263.0 109.7 %all-reduce.7.cloned.1.call-start = ((), (), s32[]{:S(2)}) async-start(), calls=%async_computation.11 | async-start | bytes 196608 | tf_op jit(solution)/shard_map/psum | solution.py:231
Sparse Core Ops, SparseCore 0:
  261.3 33.1 reduce-scatter.4
  298.0 37.2 reduce-scatter.6
  338.4 34.2 all-reduce.6
where the time goes:
time: 384 us; the launch traced here: 381 us
  waiting for transfers between devices  112 us (29%)
  local copies, waits for them, and re-layouts  74.7 us (19%)
  loops' own time  55.3 us (14%)
  blocking collectives  45.4 us (12%)
  matrix products  33.7 us (9%)
  starting transfers between devices  25.4 us (7%)
  other arithmetic  20.6 us (5%)
  between operations  14.2 us (4%)
    another operation x1, loops' own time, attend_head(): lax.map(piece_pass, jnp.arange(total_pieces, dtype=jnp.int32))  39.7 us
    psum x1, waiting for transfers between devices, per_device(): down_total, up_total = lax.psum((down_share, up_share), 'dp')  35 us
    reduce_scatter x1, waiting for transfers between devices, per_device(): lax.psum_scatter(up_part, 'seq', scatter_dimension=1, tiled=True)  30.9 us
    unnamed x45, local copies, waits for them, and re-layouts  24.6 us
    unnamed x4, waiting for transfers between devices  21.4 us
    psum x1, blocking collectives, per_device(): down_total, up_total = lax.psum((down_share, up_share), 'dp')  19.6 us
    another operation x1, loops' own time, attend_head(): lax.fori_loop(0, total_pieces, place, (grad_init, log_init))  15.7 us
    dot_general x8, matrix products, piece_pass(): jnp.dot(dscore, key_tile, preferred_element_type=jnp.float32) * scaling  15.1 us
  transfers between devices with their start and end apart: 10, of which 7 were waited for; matrix products, arithmetic and copies ran while one was open for 15% of the time, Pallas kernels for 0%

commit v1 on v0

--- a/solution.py
+++ b/solution.py
@@ -1,12 +1,584 @@
+import functools
 import math
 
 import jax
 import jax.numpy as jnp
 from jax import lax
+from jax.experimental import pallas as pl
+from jax.experimental.pallas import tpu as pltpu
 from jax.sharding import PartitionSpec as P
 
 CAP = 2
 CLIPS = 2
+LANES = 128
+HALF = 64
+CORES = 2
+LOG2E = math.log2(math.e)
+VMEM = pl.BlockSpec(memory_space=pltpu.VMEM)
+SMEM = pl.BlockSpec(memory_space=pltpu.SMEM)
+ANY = pl.BlockSpec(memory_space=pl.ANY)
+NT = (((1,), (1,)), ((), ()))
+
+
+def low_lanes(rows):
+    return lax.broadcasted_iota(jnp.int32, (rows, LANES), 1) < HALF
+
+
+def swap_halves(tile):
+    return pltpu.roll(tile, HALF, 1)
+
+
+def lane_tile(index):
+    return pl.ds(pl.multiple_of(index * LANES, LANES), LANES)
+
+
+def row_tile(index, rows):
+    return pl.ds(pl.multiple_of(index * rows, rows), rows)
+
+
+def quotient(value, size):
+    return lax.shift_right_logical(value, size.bit_length() - 1)
+
+
+def remainder(value, size):
+    return value & (size - 1)
+
+
+def each_hit(plan, me, groups, blocks, live, put):
+    def over_dest(dest, _):
+        def over_position(position, slot):
+            source = plan[dest, position]
+            hit = quotient(source, blocks) == me
+
+            @pl.when(hit)
+            def _():
+                put(dest, slot, remainder(source, blocks))
+
+            return slot + hit.astype(jnp.int32)
+
+        lax.fori_loop(0, live, over_position, jnp.int32(0))
+        return 0
+
+    lax.fori_loop(0, groups, over_dest, 0)
+
+
+def each_block(plan, me, blocks, live, take):
+    def over_position(position, _):
+        group = quotient(plan[me, position], blocks)
+        slot = jnp.int32(0)
+        for other in range(live):
+            same = (quotient(plan[me, other], blocks) == group) & (other < position)
+            slot = slot + same.astype(jnp.int32)
+        take(position, group, slot)
+        return 0
+
+    lax.fori_loop(0, live, over_position, 0)
+
+
+def each_half(slot, store):
+    @pl.when(remainder(slot, 2) == 0)
+    def _():
+        store(slice(0, HALF))
+
+    @pl.when(remainder(slot, 2) == 1)
+    def _():
+        store(slice(HALF, LANES))
+
+
+def split(slot, pair):
+    pair = pair.astype(jnp.float32)
+    return jnp.where(remainder(slot, 2) == 0, pair, swap_halves(pair))
+
+
+def pack_far_kernel(dims, plan_hbm, feat_hbm, base_hbm, keys_hbm, vals_hbm, down_hbm, up_hbm, *rest):
+    groups, blocks, heads, rows, live = dims
+    far_hbm, qbuf, abuf = rest[:3]
+    plan, feat, base, keys, vals, down, up, far_out, sems, out_sems = rest[3:]
+    me = lax.axis_index("dp")
+    copies = [
+        pltpu.make_async_copy(source, target, sems.at[index])
+        for index, (source, target) in enumerate(
+            (
+                (plan_hbm, plan),
+                (keys_hbm, keys),
+                (vals_hbm, vals),
+                (feat_hbm, feat),
+                (down_hbm, down),
+                (base_hbm, base),
+                (up_hbm, up),
+            )
+        )
+    ]
+    for copy in copies:
+        copy.start()
+
+    def put_blocks(sources, first):
+        def put(dest, slot, local):
+            @pl.when(slot < CAP)
+            def _():
+                for head in range(heads):
+                    columns = slice(head * LANES, (head + 1) * LANES)
+                    for index, source in enumerate(sources):
+                        far_out[head * groups + dest, (first + index) * CAP + slot] = source[
+                            local, :, columns
+                        ]
+
+        each_hit(plan, me, groups, blocks, live, put)
+
+    def send(first, count, index):
+        tiles = pl.ds(first, count)
+        copy = pltpu.make_async_copy(far_out.at[:, tiles], far_hbm.at[:, tiles], out_sems.at[index])
+        copy.start()
+        return copy
+
+    for copy in copies[:3]:
+        copy.wait()
+    put_blocks((keys, vals), 0)
+    early = send(0, 2 * CAP, 0)
+    for copy in copies[3:]:
+        copy.wait()
+    rank = up.shape[0]
+    twice = jnp.concatenate([down[...], down[...]], axis=0)
+    adapter = lax.dot_general(feat[...], twice, NT, preferred_element_type=jnp.float32).astype(
+        jnp.bfloat16
+    )
+    abuf[...] = adapter.reshape(abuf.shape)
+    lift = jnp.dot(adapter[:, :rank], up[...], preferred_element_type=jnp.float32)
+    qbuf[...] = (base[...].astype(jnp.float32) + lift.reshape(base.shape)).astype(jnp.bfloat16)
+
+    def put_adapter(dest, slot, local):
+        def store(lanes):
+            for head in range(heads):
+                far_out[head * groups + dest, CAP * 3, :, lanes] = abuf[local, :, lanes]
+
+        @pl.when(slot < CAP)
+        def _():
+            each_half(slot, store)
+
+    each_hit(plan, me, groups, blocks, live, put_adapter)
+    put_blocks((qbuf,), 2)
+    late = send(2 * CAP, CAP + 1, 1)
+    early.wait()
+    late.wait()
+
+
+def pack_own_kernel(dims, plan, keys, vals, grad, queries, adapter, *own_outs):
+    groups, blocks, heads, rows, live = dims
+    extras = live - CAP
+    me = lax.axis_index("dp")
+    seq = lax.axis_index("seq")
+    sources = (keys, vals, queries)
+
+    def put(dest, slot, local):
+        @pl.when(slot >= CAP)
+        def _():
+            extra = slot - CAP
+            where = extras * 3 + live + quotient(extra, 2)
+            for turn in range(heads):
+                columns = lane_tile(seq ^ turn)
+                for index, source in enumerate(sources):
+                    own_outs[turn][index * extras + extra] = source[local, :, columns]
+
+            def store(lanes):
+                for turn in range(heads):
+                    own_outs[turn][where, :, lanes] = adapter[local, :, lanes]
+
+            each_half(slot, store)
+
+    each_hit(plan, me, groups, blocks, live, put)
+    for turn in range(heads):
+        columns = lane_tile(seq ^ turn)
+        for position in range(live):
+            own_outs[turn][extras * 3 + position] = grad[position, :, columns]
+
+
+def attend_kernel(dims, plan, seg, up, far_in, *rest):
+    groups, blocks, heads, rows, live = dims
+    own_ins = rest[:heads]
+    part_out = rest[heads]
+    own_parts = rest[heads + 1 : heads + 1 + heads // CORES]
+    up_out, log_out, qs, ks, vs, gs, ads, dqs, parts = rest[heads + 1 + heads // CORES :]
+    extras = live - CAP
+    me = lax.axis_index("dp")
+    seq = lax.axis_index("seq")
+    rank = up.shape[0]
+    length = seg.shape[1]
+    reach = live * LANES
+    scaling = 1.0 / math.sqrt(LANES)
+
+    ads[...] = jnp.zeros_like(ads)
+
+    def take(position, group, slot):
+        far = (group != me) | (slot < CAP)
+
+        @pl.when(far)
+        def _():
+            for part in range(heads):
+                index = part * groups + group
+                where = row_tile(position * heads + part, rows)
+                ks[where, :] = far_in[index, slot]
+                vs[where, :] = far_in[index, CAP + slot]
+                qs[where, :] = far_in[index, 2 * CAP + slot]
+
+            def store(lanes):
+                for part in range(heads):
+                    where = row_tile(position * heads + part, rows)
+                    ads[where, lanes] = far_in[part * groups + group, CAP * 3, :, lanes]
+
+            each_half(slot, store)
+
+        @pl.when(jnp.logical_not(far))
+        def _():
+            extra = slot - CAP
+            pair = extras * 3 + live + quotient(extra, 2)
+            for turn in range(heads):
+                where = row_tile(position * heads + (seq ^ turn), rows)
+                ks[where, :] = own_ins[turn][extra]
+                vs[where, :] = own_ins[turn][extras + extra]
+                qs[where, :] = own_ins[turn][2 * extras + extra]
+
+            def store(lanes):
+                for turn in range(heads):
+                    where = row_tile(position * heads + (seq ^ turn), rows)
+                    ads[where, lanes] = own_ins[turn][pair, :, lanes]
+
+            each_half(slot, store)
+
+    each_block(plan, me, blocks, live, take)
+    for turn in range(heads):
+        for position in range(live):
+            gs[row_tile(position * heads + (seq ^ turn), rows), :] = own_ins[turn][
+                extras * 3 + position
+            ]
+
+    count = jnp.sum((seg[...] < CLIPS - 1).astype(jnp.float32), axis=1, keepdims=True).astype(
+        jnp.int32
+    )
+    key_rows = ks[...]
+    value_rows = vs[...]
+    key_columns = key_rows.T
+    key_index = lax.broadcasted_iota(jnp.int32, (reach, 1), 0)
+    always = length - reach
+    up_head = up[:, lane_tile(seq)]
+    up_twice = jnp.concatenate([up_head, up_head], axis=0)
+    for start in range(0, reach, 2 * LANES):
+        count_here = min(2 * LANES, reach - start)
+        span = slice(start, start + count_here)
+        scores = lax.dot_general(key_rows, qs[span, :], NT, preferred_element_type=jnp.float32)
+        scores = jnp.concatenate(
+            [
+                scores[:always],
+                jnp.where(key_index[always:] < count, scores[always:], -1e30),
+            ],
+            axis=0,
+        )
+        dprob = lax.dot_general(value_rows, gs[span, :], NT, preferred_element_type=jnp.float32)
+        maximum = jnp.max(scores, axis=0, keepdims=True)
+        exponent = jnp.exp2((scores - maximum) * (scaling * LOG2E))
+        total = jnp.sum(exponent, axis=0, keepdims=True)
+        delta = jnp.sum(exponent * dprob, axis=0, keepdims=True) / total
+        dscore = (exponent * (dprob - delta)).astype(jnp.bfloat16)
+        dquery = jnp.dot(key_columns, dscore, preferred_element_type=jnp.float32)
+        query_index = lax.broadcasted_iota(jnp.int32, (1, count_here), 1) + start
+        in_clip = query_index < count
+        dquery = jnp.where(in_clip, dquery * (scaling / total), 0.0).astype(jnp.bfloat16)
+        dqs[:, span] = dquery
+        log_out[0, :, span] = jnp.where(in_clip, maximum * scaling + jnp.log(total), 0.0)
+    log_out[0, :, reach:] = jnp.zeros((1, length - reach), jnp.float32)
+    dquery_all = dqs[...]
+    parts[...] = lax.dot_general(
+        dquery_all, up_twice, (((0,), (1,)), ((), ())), preferred_element_type=jnp.float32
+    ).astype(jnp.bfloat16)
+
+    def put(position, group, slot):
+        far = (group != me) | (slot < CAP)
+
+        @pl.when(far)
+        def _():
+            def store(lanes):
+                for part in range(heads):
+                    where = row_tile(position * heads + part, rows)
+                    part_out[part * groups + group, :, lanes] = parts[where, lanes]
+
+            each_half(slot, store)
+
+        @pl.when(jnp.logical_not(far))
+        def _():
+            pair = quotient(slot - CAP, 2)
+
+            def store(lanes):
+                for turn in range(heads):
+                    where = row_tile(position * heads + (seq ^ turn), rows)
+                    own_parts[turn // CORES][turn % CORES, pair, :, lanes] = parts[where, lanes]
+
+            each_half(slot, store)
+
+    each_block(plan, me, blocks, live, put)
+    up_part = jnp.dot(dquery_all, ads[...], preferred_element_type=jnp.float32)
+    up_out[...] = (up_part + swap_halves(up_part)).T[:rank].astype(jnp.bfloat16)
+
+
+def chip_sum_kernel(*refs):
+    parts, outs = refs[:-CORES], refs[-CORES:]
+    for core in range(CORES):
+        total = parts[0][core].astype(jnp.float32)
+        for part in parts[1:]:
+            total = total + part[core].astype(jnp.float32)
+        outs[core][...] = total.astype(jnp.bfloat16)
+
+
+def product_kernel(dims, plan, parts, feat, own_mine, own_other, out, sums, grads):
+    groups, blocks, heads, rows, live = dims
+    me = lax.axis_index("dp")
+    for group in range(groups):
+        total = parts[group].astype(jnp.float32)
+        for head in range(1, heads):
+            total = total + parts[head * groups + group].astype(jnp.float32)
+        sums[group] = total
+    for pair in range(own_mine.shape[0]):
+        sums[groups + pair] = own_mine[pair].astype(jnp.float32) + own_other[pair].astype(
+            jnp.float32
+        )
+    grads[...] = jnp.zeros_like(grads)
+
+    def put(dest, slot, local):
+        index = jnp.where(slot < CAP, dest, groups - 1 + quotient(slot, 2))
+        grads[local] = split(slot, sums[index]).astype(jnp.bfloat16)
+
+    each_hit(plan, me, groups, blocks, live, put)
+    low = low_lanes(HALF // 2)
+    columns = grads[...].reshape(blocks * rows, LANES).astype(jnp.float32).T[:HALF]
+    columns = columns.astype(jnp.bfloat16)
+    for pair in range(heads // 2):
+        tiles = jnp.dot(
+            columns,
+            feat[:, pair * 5 * LANES : (pair + 1) * 5 * LANES],
+            preferred_element_type=jnp.float32,
+        )
+        shared = tiles[:, 2 * LANES : 3 * LANES]
+        upper, lower = shared[: HALF // 2], shared[HALF // 2 :]
+        for part in range(2):
+            ahead = tiles[:, part * 3 * LANES : (part * 3 + 2) * LANES].astype(jnp.bfloat16)
+            out[pair * 2 + part, :HALF] = ahead[:, :LANES]
+            out[pair * 2 + part, HALF : 2 * HALF] = ahead[:, LANES:]
+            if part == 0:
+                rest = jnp.where(low, upper, swap_halves(lower))
+            else:
+                rest = jnp.where(low, swap_halves(upper), lower)
+            out[pair * 2 + part, 2 * HALF :] = rest.astype(jnp.bfloat16)
+
+
+def join_kernel(parts, up_part, out):
+    total = parts[0].astype(jnp.float32)
+    for head in range(1, parts.shape[0]):
+        total = total + parts[head].astype(jnp.float32)
+    out[: total.shape[0]] = total.astype(jnp.bfloat16)
+    out[total.shape[0] :] = up_part[...]
+
+
+def total_kernel(grad_norm, *rest):
+    groups = len(rest) - 3
+    down_out, up_out, held = rest[groups:]
+    me = lax.axis_index("dp")
+    seq = lax.axis_index("seq")
+    for turn in range(groups):
+        held[me ^ turn] = rest[turn][...].astype(jnp.float32)
+    total = held[0]
+    for group in range(1, groups):
+        total = total + held[group]
+    total = total * grad_norm
+    first, second = total[:HALF], total[HALF : 2 * HALF]
+    shared = total[2 * HALF : 2 * HALF + HALF // 2]
+    up_out[...] = total[2 * HALF + HALF // 2 :]
+    swapped = swap_halves(shared)
+    low_half = jnp.concatenate([shared, swapped], axis=0)
+    high_half = jnp.concatenate([swapped, shared], axis=0)
+    even = jnp.concatenate([first, second, low_half], axis=1)
+    odd = pltpu.roll(jnp.concatenate([first, second, high_half], axis=1), HALF, 1)
+    down = jnp.where(remainder(seq, 2) == 0, even, odd)
+    down_out[...] = down[:, : down_out.shape[1]]
+
+
+def call(kernel, outs, specs, scratch, flops, moved, *args, vmem_mib=32, out_specs=None):
+    shapes = [jax.ShapeDtypeStruct(shape, dtype) for shape, dtype in outs]
+    return pl.pallas_call(
+        kernel,
+        out_shape=shapes,
+        in_specs=specs,
+        out_specs=out_specs or [VMEM] * len(shapes),
+        scratch_shapes=scratch,
+        compiler_params=pltpu.CompilerParams(vmem_limit_bytes=vmem_mib << 20),
+        cost_estimate=pl.CostEstimate(flops=flops, bytes_accessed=moved, transcendentals=0),
+    )(*args)
+
+
+def exchange(value, axis, turn):
+    peers = lax.axis_size(axis)
+    return lax.ppermute(value, axis, [(peer, peer ^ turn) for peer in range(peers)])
+
+
+def per_device_tiles(
+    features,
+    frozen_query_weight,
+    source_keys,
+    source_values,
+    output_gradient,
+    adapter_down_weight,
+    adapter_up_weight,
+    source_block_plan,
+    segments,
+):
+    groups = lax.axis_size("dp")
+    heads = lax.axis_size("seq")
+    _, blocks, rows, width = features.shape
+    length = segments.shape[1]
+    live = (length // 2 + length // 8) // LANES
+    reach = live * LANES
+    rank = adapter_up_weight.shape[0]
+    extras = live - CAP
+    pairs = (extras + 1) // 2
+    dims = (groups, blocks, heads, rows, live)
+    bf16 = jnp.bfloat16
+    f32 = jnp.float32
+    peers = groups * heads
+    everyone = ("seq", "dp")
+    flat = features[0].reshape(blocks * rows, width)
+    far_shape = (peers, CAP * 3 + 1, rows, LANES)
+    own_shape = (extras * 3 + live + pairs, rows, LANES)
+    rows_shape = (blocks, rows, heads * LANES)
+
+    far_send, queries, adapter = call(
+        functools.partial(pack_far_kernel, dims),
+        [(far_shape, bf16), (rows_shape, bf16), ((blocks, rows, LANES), bf16)],
+        [ANY] * 7,
+        [
+            pltpu.SMEM((groups, blocks), jnp.int32),
+            pltpu.VMEM((blocks * rows, width), bf16),
+            pltpu.VMEM(rows_shape, bf16),
+            pltpu.VMEM(rows_shape, bf16),
+            pltpu.VMEM(rows_shape, bf16),
+            pltpu.VMEM((rank, width), bf16),
+            pltpu.VMEM((rank, heads * LANES), bf16),
+            pltpu.VMEM(far_shape, bf16),
+            pltpu.SemaphoreType.DMA((7,)),
+            pltpu.SemaphoreType.DMA((2,)),
+        ],
+        60_000_000,
+        4_000_000,
+        source_block_plan,
+        flat,
+        frozen_query_weight[0],
+        source_keys[0],
+        source_values[0],
+        adapter_down_weight.T,
+        adapter_up_weight,
+        vmem_mib=60,
+        out_specs=[ANY, VMEM, VMEM],
+    )
+    own_send = call(
+        functools.partial(pack_own_kernel, dims),
+        [(own_shape, bf16)] * heads,
+        [SMEM] + [VMEM] * 5,
+        [],
+        0,
+        1_600_000,
+        source_block_plan,
+        source_keys[0],
+        source_values[0],
+        output_gradient[0],
+        queries,
+        adapter,
+    )
+    own = [own_send[0]] + [exchange(own_send[turn], "seq", turn) for turn in range(1, heads)]
+    far = lax.all_to_all(far_send, everyone, 0, 0, tiled=True)
+    attended = call(
+        functools.partial(attend_kernel, dims),
+        [((peers, rows, LANES), bf16)]
+        + [((CORES, pairs, rows, LANES), bf16)] * (heads // CORES)
+        + [((rank, LANES), bf16), ((1, 1, length), f32)],
+        [SMEM] + [VMEM] * (3 + heads),
+        [pltpu.VMEM((reach, LANES), bf16)] * 5
+        + [pltpu.VMEM((LANES, reach), bf16), pltpu.VMEM((reach, LANES), bf16)],
+        600_000_000,
+        3_000_000,
+        source_block_plan,
+        segments,
+        adapter_up_weight,
+        far,
+        *own,
+    )
+    own_parts = [
+        exchange(attended[1 + chip], "seq", chip * CORES) for chip in range(heads // CORES - 1, 0, -1)
+    ]
+    own_mine, own_other = call(
+        chip_sum_kernel,
+        [((pairs, rows, LANES), bf16)] * CORES,
+        [VMEM] * (heads // CORES),
+        [],
+        0,
+        100_000,
+        *own_parts,
+        attended[1],
+    )
+    own_other = exchange(own_other, "seq", 1)
+    part = lax.all_to_all(attended[0], everyone, 0, 0, tiled=True)
+    up_part, log_norm = attended[1 + heads // CORES :]
+    (shares,) = call(
+        functools.partial(product_kernel, dims),
+        [((heads, HALF * 5 // 2, LANES), bf16)],
+        [SMEM] + [VMEM] * 4,
+        [
+            pltpu.VMEM((groups + pairs, rows, LANES), f32),
+            pltpu.VMEM((blocks, rows, LANES), bf16),
+        ],
+        40_000_000,
+        2_000_000,
+        source_block_plan,
+        part,
+        flat,
+        own_mine,
+        own_other,
+    )
+    shares = lax.all_to_all(shares, "seq", 0, 0, tiled=True)
+    (joined,) = call(
+        join_kernel,
+        [((HALF * 5 // 2 + rank, LANES), bf16)],
+        [VMEM] * 2,
+        [],
+        0,
+        600_000,
+        shares,
+        up_part,
+    )
+    sums = [joined] + [exchange(joined, "dp", turn) for turn in range(1, groups)]
+    down, up = call(
+        functools.partial(total_kernel, 4.0 / math.sqrt(groups * length)),
+        [((rank, width // heads), f32), ((rank, LANES), f32)],
+        [VMEM] * groups,
+        [pltpu.VMEM((groups,) + joined.shape, f32)],
+        0,
+        400_000,
+        *sums,
+    )
+    return (down.T, up, log_norm)
+
+
+def power_of_two(size):
+    return size > 1 and size & (size - 1) == 0
+
+
+def fits_tiles(mesh, features, adapter_up_weight):
+    groups, heads = mesh.shape["dp"], mesh.shape["seq"]
+    rows = features.shape[2] // heads
+    return (
+        rows % 16 == 0
+        and features.shape[2] == LANES
+        and features.shape[3] * 2 == heads * 5 * LANES
+        and power_of_two(heads)
+        and power_of_two(groups)
+        and power_of_two(features.shape[1])
+        and adapter_up_weight.shape == (HALF, heads * LANES)
+    )
 
 
 def attend_head(query, key_rows, value_rows, cotangent, segment, clip_count, reach_rows):
@@ -246,6 +818,15 @@
         P("dp", None),
     )
     out_specs = (P("seq", None), P(None, "seq"), P("dp", "seq", None))
-    return jax.shard_map(
-        per_device, mesh=mesh, in_specs=in_specs, out_specs=out_specs, check_vma=False
-    )
+
+    def whole(features, *rest):
+        fits = fits_tiles(mesh, features, rest[5])
+        return jax.shard_map(
+            per_device_tiles if fits else per_device,
+            mesh=mesh,
+            in_specs=in_specs,
+            out_specs=out_specs,
+            check_vma=False,
+        )(features, *rest)
+
+    return whole

time: 384 us -> 72.5 us (0.19)
  waiting for transfers between devices: 112 us -> 22.7 us
  local copies, waits for them, and re-layouts: 74.7 us -> 0.67 us
  loops' own time: 55.3 us -> 0 us
  blocking collectives: 45.4 us -> 10.1 us
  matrix products: 33.7 us -> 0 us
  other arithmetic: 20.6 us -> 0 us
  between operations: 14.2 us -> 0.78 us
  Pallas kernels: 0 us -> 11.4 us
    another operation x2 -> x0, loops' own time: 55.3 us -> none  [the longest x1 39.7 us: attend_head(): lax.map(piece_pass, jnp.arange(total_pieces, dtype=jnp.int32))]
    psum x1 -> x0, waiting for transfers between devices: 35 us -> none  [per_device(): down_total, up_total = lax.psum((down_share, up_share), 'dp')]
    dot_general x28 -> x0, matrix products: 33.7 us -> none  [the longest x8 15.1 us: piece_pass(): jnp.dot(dscore, key_tile, preferred_element_type=jnp.float32) * scaling]
    reduce_scatter x1 -> x0, waiting for transfers between devices: 30.9 us -> none  [per_device(): lax.psum_scatter(up_part, 'seq', scatter_dimension=1, tiled=True)]
    unnamed x45 -> x18, local copies, waits for them, and re-layouts: 24.6 us -> 0.67 us
    unnamed x4 -> x0, waiting for transfers between devices: 21.4 us -> none
    psum x1 -> x0, blocking collectives: 19.6 us -> none  [per_device(): down_total, up_total = lax.psum((down_share, up_share), 'dp')]
    all_to_all x7 -> x2, waiting for transfers between devices: 24.3 us -> 6.18 us  [the longest x1 6.06 us: per_device_tiles(): far = lax.all_to_all(far_send, everyone, 0, 0, tiled=True)]
  transfers between devices with their start and end apart: 10 -> 16, of which waited for: 7 -> 13; matrix products, arithmetic and copies ran while one was open for 15% -> 0% of each run, Pallas kernels for 0% -> 2%
where the time goes in v1:
time: 72.5 us; the launch traced here: 72.2 us
  starting transfers between devices  26.6 us (37%)
  waiting for transfers between devices  22.7 us (31%)
  Pallas kernels  11.4 us (16%)
  blocking collectives  10.1 us (14%)
  between operations  0.78 us (1%)
    ppermute x14, waiting for transfers between devices, exchange(): lax.ppermute(value, axis, [(peer, peer ^ turn) for peer in range(peers)])  16.5 us
    ppermute x14, starting transfers between devices, exchange(): lax.ppermute(value, axis, [(peer, peer ^ turn) for peer in range(peers)])  14.8 us
    pallas_call x7, Pallas kernels, call(): pl.pallas_call(kernel, out_shape=shapes, in_specs=specs, out_specs=out_sp...  11.4 us
    all_to_all x1, blocking collectives, per_device_tiles(): shares = lax.all_to_all(shares, 'seq', 0, 0, tiled=True)  10.1 us
    all_to_all x1, starting transfers between devices, per_device_tiles(): far = lax.all_to_all(far_send, everyone, 0, 0, tiled=True)  7.31 us
    all_to_all x1, waiting for transfers between devices, per_device_tiles(): far = lax.all_to_all(far_send, everyone, 0, 0, tiled=True)  6.06 us
    all_to_all x1, starting transfers between devices, per_device_tiles(): part = lax.all_to_all(attended[0], everyone, 0, 0, tiled=True)  4.41 us
  transfers between devices with their start and end apart: 16, of which 13 were waited for; matrix products, arithmetic and copies ran while one was open for 0% of the time, Pallas kernels for 2%

profile of v1, /device:TPU:0, one launch (start us, length us, event | category | flops | bytes accessed | tf_op | source)
XLA Modules:
  0.0 72.2 jit_solution(16674113884648414467)
XLA Ops:
  0.6 4.4 %shard_map.112 = (bf16[32,7,16,128]{3,2,1,0:T(8,128)(2,1)}, bf16[8,16,1024]{2,1,0:T(8,128)(2,1)}, bf16[8,16,128]{2,1,0:T(8,128)(2,1)}) custom-call(s32[4,8]{1,0:T(4,128)} %plan.5, bf16[128,2560]{1,0:T(8,128)(2,1)} %bitcast.7, bf16[8,16,1024]{2,1,0:T(8,128)(2,1)} %bitcast.15, bf16[8,16,1024]{2,1,0:T(8,128)(2,1)} %bitcast.9, bf16[8,16,1024]{2,1,0:T(8,128)(2,1)} %bitcast.11, ...), custom_call_target="tpu_custom_call" | custom-call | flops 60000000 | bytes 4000000 | tf_op jit(solution)/shard_map/pallas_call | solution.py:404
  5.0 0.0 copy-start.1
  5.0 0.0 copy-start.2
  5.0 0.0 copy-start.3
  5.1 0.0 copy-start.4
  5.1 0.0 copy-start.6
  5.1 7.3 %all-to-all-start = ((bf16[32,7,16,128]{3,2,1,0:T(8,128)(2,1)}), bf16[32,7,16,128]{3,2,1,0:T(8,128)(2,1)S(1)}, u32[]{:S(2)}, u32[]{:S(2)}) async-start(bf16[32,7,16,128]{3,2,1,0:T(8,128)(2,1)} %get-tuple-element.25), calls=%async_computation | async-start | bytes 1835008 | tf_op jit(solution)/shard_map/all_to_all | solution.py:493
  12.4 0.0 copy-start.7
  12.4 0.0 copy-done.1
  12.4 0.0 copy-done.2
  12.4 0.0 copy-done.3
  12.4 0.6 copy-done.7
  13.1 1.1 %shard_map.113 = (bf16[16,16,128]{2,1,0:T(8,128)(2,1)S(1)}, bf16[16,16,128]{2,1,0:T(8,128)(2,1)S(1)}, bf16[16,16,128]{2,1,0:T(8,128)(2,1)S(1)}, bf16[16,16,128]{...) custom-call(s32[4,8]{1,0:T(4,128)S(1)} %copy-done.7, ...), custom_call_target="tpu_custom_call" | custom-call | bytes 1600000 | tf_op jit(solution)/shard_map/pallas_call | solution.py:404
  14.2 0.3 collective-permute-start
  14.5 1.7 %collective-permute-start.1 = (bf16[16,16,128]{2,1,0:T(8,128)(2,1)S(1)}, bf16[16,16,128]{2,1,0:T(8,128)(2,1)S(1)}, u32[]{:S(2)}, u32[]{:S(2)}) collective-permute-start(bf16[16,16,128]{2,1,0:T(8,128)(2,1)S(1)} %get-tuple-element.30), channel_id=1, source_target_pairs={{0,2},{1,3},{2,0},{3,1},{4,6},{5,7},{6,4},{7,5},{8,10},{9,11},{10,... | collective-permute-start | bytes 196616 | tf_op jit(solution)/shard_map/ppermute | solution.py:417
  16.2 0.0 collective-permute-start.2
  16.2 1.7 %collective-permute-start.3 = (bf16[16,16,128]{2,1,0:T(8,128)(2,1)S(1)}, bf16[16,16,128]{2,1,0:T(8,128)(2,1)S(1)}, u32[]{:S(2)}, u32[]{:S(2)}) collective-permute-start(bf16[16,16,128]{2,1,0:T(8,128)(2,1)S(1)} %get-tuple-element.32), channel_id=1, source_target_pairs={{0,4},{1,5},{2,6},{3,7},{4,0},{5,1},{6,2},{7,3},{8,12},{9,13},{10,... | collective-permute-start | bytes 196616 | tf_op jit(solution)/shard_map/ppermute | solution.py:417
  17.9 0.1 collective-permute-start.4
  18.0 0.0 collective-permute-done.rest_1_
  18.0 2.6 %collective-permute-start.5 = (bf16[16,16,128]{2,1,0:T(8,128)(2,1)S(1)}, bf16[16,16,128]{2,1,0:T(8,128)(2,1)S(1)}, u32[]{:S(2)}, u32[]{:S(2)}) collective-permute-start(bf16[16,16,128]{2,1,0:T(8,128)(2,1)S(1)} %get-tuple-element.34), channel_id=1, source_target_pairs={{0,6},{1,7},{2,4},{3,5},{4,2},{5,3},{6,0},{7,1},{8,14},{9,15},{10,... | collective-permute-start | bytes 196616 | tf_op jit(solution)/shard_map/ppermute | solution.py:417
  20.6 1.8 %collective-permute-done.1.rest_2_ = bf16[16,16,128]{2,1,0:T(8,128)(2,1)S(1)} collective-permute-done((bf16[16,16,128]{2,1,0:T(8,128)(2,1)S(1)}, bf16[16,16,128]{2,1,0:T(8,128)(2,1)S(1)}, u32[]{:S(2)}, u32[]{:S(2)}) %collective-permute-start.1) | collective-permute-done | bytes 65568 | tf_op jit(solution)/shard_map/ppermute | solution.py:417
  22.4 0.4 collective-permute-start.6
  22.8 1.3 %collective-permute-done.2.rest_3_ = bf16[16,16,128]{2,1,0:T(8,128)(2,1)S(1)} collective-permute-done((bf16[16,16,128]{2,1,0:T(8,128)(2,1)S(1)}, bf16[16,16,128]{2,1,0:T(8,128)(2,1)S(1)}, u32[]{:S(2)}, u32[]{:S(2)}) %collective-permute-start.2) | collective-permute-done | bytes 65568 | tf_op jit(solution)/shard_map/ppermute | solution.py:417
  24.1 0.0 collective-permute-done.3.rest_4_
  24.1 2.3 %collective-permute-done.4.rest_5_ = bf16[16,16,128]{2,1,0:T(8,128)(2,1)S(1)} collective-permute-done((bf16[16,16,128]{2,1,0:T(8,128)(2,1)S(1)}, bf16[16,16,128]{2,1,0:T(8,128)(2,1)S(1)}, u32[]{:S(2)}, u32[]{:S(2)}) %collective-permute-start.4) | collective-permute-done | bytes 65568 | tf_op jit(solution)/shard_map/ppermute | solution.py:417
  26.4 1.5 %collective-permute-done.5.rest_6_ = bf16[16,16,128]{2,1,0:T(8,128)(2,1)S(1)} collective-permute-done((bf16[16,16,128]{2,1,0:T(8,128)(2,1)S(1)}, bf16[16,16,128]{2,1,0:T(8,128)(2,1)S(1)}, u32[]{:S(2)}, u32[]{:S(2)}) %collective-permute-start.5) | collective-permute-done | bytes 65568 | tf_op jit(solution)/shard_map/ppermute | solution.py:417
  28.0 0.7 collective-permute-done.6.rest_7_
  28.7 6.1 %all-to-all-done.far_in = bf16[32,7,16,128]{3,2,1,0:T(8,128)(2,1)S(1)} async-done(((bf16[32,7,16,128]{3,2,1,0:T(8,128)(2,1)}), bf16[32,7,16,128]{3,2,1,0:T(8,128)(2,1)S(1)}, u32[]{:S(2)}, u32[]{:S(2)}) %all-to-all-start) | async-done | bytes 917536 | tf_op jit(solution)/shard_map/all_to_all | solution.py:493
  34.7 3.6 %shard_map.114 = (bf16[32,16,128]{2,1,0:T(8,128)(2,1)}, bf16[2,2,16,128]{3,2,1,0:T(8,128)(2,1)S(1)}, bf16[2,2,16,128]{3,2,1,0:T(8,128)(2,1)S(1)}, bf16[2,2,16,12...) custom-call(s32[4,8]{1,0:T(4,128)S(1)} %copy-done.7, ...), custom_call_target="tpu_custom_call" | custom-call | flops 600000000 | bytes 3000000 | tf_op jit(solution)/shard_map/pallas_call | solution.py:404
  38.4 4.4 %all-to-all-start.1 = ((bf16[32,16,128]{2,1,0:T(8,128)(2,1)}), bf16[32,16,128]{2,1,0:T(8,128)(2,1)S(1)}, u32[]{:S(2)}, u32[]{:S(2)}) async-start(bf16[32,16,128]{2,1,0:T(8,128)(2,1)} %get-tuple-element.36), calls=%async_computation.1 | async-start | bytes 262144 | tf_op jit(solution)/shard_map/all_to_all | solution.py:524
  42.8 2.7 %collective-permute-start.7 = (bf16[2,2,16,128]{3,2,1,0:T(8,128)(2,1)S(1)}, bf16[2,2,16,128]{3,2,1,0:T(8,128)(2,1)S(1)}, u32[]{:S(2)}, u32[]{:S(2)}) collective-permute-start(bf16[2,2,16,128]{3,2,1,0:T(8,128)(2,1)S(1)} %get-tuple-element.37), channel_id=1, source_target_pairs={{0,6},{1,7},{2,4},{3,5},{4,2},{5,3},{6,0},{7,1},{8,14},{9,15},{10,... | collective-permute-start | bytes 49160 | tf_op jit(solution)/shard_map/ppermute | solution.py:417
  45.5 0.6 collective-permute-start.8
  46.1 0.3 collective-permute-start.9
  46.3 1.1 %collective-permute-done.7.refs_0_ = bf16[2,2,16,128]{3,2,1,0:T(8,128)(2,1)S(1)} collective-permute-done((bf16[2,2,16,128]{3,2,1,0:T(8,128)(2,1)S(1)}, bf16[2,2,16,128]{3,2,1,0:T(8,128)(2,1)S(1)}, u32[]{:S(2)}, u32[]{:S(2)}) %collective-permute-start.7) | collective-permute-done | bytes 16416 | tf_op jit(solution)/shard_map/ppermute | solution.py:417
  47.5 1.8 %collective-permute-done.8.refs_1_ = bf16[2,2,16,128]{3,2,1,0:T(8,128)(2,1)S(1)} collective-permute-done((bf16[2,2,16,128]{3,2,1,0:T(8,128)(2,1)S(1)}, bf16[2,2,16,128]{3,2,1,0:T(8,128)(2,1)S(1)}, u32[]{:S(2)}, u32[]{:S(2)}) %collective-permute-start.8) | collective-permute-done | bytes 16416 | tf_op jit(solution)/shard_map/ppermute | solution.py:417
  49.3 0.5 collective-permute-done.9.refs_2_
  49.8 0.1 collective-permute-start.10
  49.9 1.2 %collective-permute-done.10.own_other = bf16[2,16,128]{2,1,0:T(8,128)(2,1)S(1)} collective-permute-done((bf16[2,16,128]{2,1,0:T(8,128)(2,1)S(1)}, bf16[2,16,128]{2,1,0:T(8,128)(2,1)S(1)}, u32[]{:S(2)}, u32[]{:S(2)}) %collective-permute-start.10) | collective-permute-done | bytes 8224 | tf_op jit(solution)/shard_map/ppermute | solution.py:417
  51.1 0.1 all-to-all-done.1.parts
  51.2 1.4 %shard_map.116 = bf16[8,160,128]{2,1,0:T(8,128)(2,1)S(1)} custom-call(s32[4,8]{1,0:T(4,128)S(1)} %copy-done.7, bf16[32,16,128]{2,1,0:T(8,128)(2,1)S(1)} %all-to-all-done.1.parts, bf16[128,2560]{1,0:T(8,128)(2,1)S(1)} %bitcast.8, bf16[2,16,128]{2,1,0:T(8,128)(2,1)S(1)} %get-tuple-element.41.own_mine, bf16[2,16,128]{2,1,0:T(8,128)(2,1)S(1)} %collective-permute-done.10.own_other), custom_call_target="tpu_custom_call" | custom-call | flops 40000000 | bytes 2000000 | tf_op jit(solution)/shard_map/pallas_call | solution.py:404
  52.6 10.1 %all_to_all.15.parts = bf16[8,160,128]{2,1,0:T(8,128)(2,1)S(1)} all-to-all(bf16[8,160,128]{2,1,0:T(8,128)(2,1)S(1)} %shard_map.116), channel_id=1, replica_groups=mesh['dp'=4,'seq'=8] {'seq'}, dimensions={0} | all-to-all | bytes 655360 | tf_op jit(solution)/shard_map/all_to_all | solution.py:542
  62.7 3.5 %collective-permute-start.13 = (bf16[224,128]{1,0:T(8,128)(2,1)S(1)}, bf16[224,128]{1,0:T(8,128)(2,1)S(1)}, u32[]{:S(2)}, u32[]{:S(2)}) collective-permute-start(bf16[224,128]{1,0:T(8,128)(2,1)S(1)} %shard_map.117.rest_0_), channel_id=1, source_target_pairs={{0,24},{8,16},{16,8},{24,0},{1,25},{9,17},{17,9},{25,1},{2,26},{10... | collective-permute-start | bytes 172040 | tf_op jit(solution)/shard_map/ppermute | solution.py:417
  66.2 0.0 collective-permute-start.12
  66.2 1.0 %collective-permute-start.11 = (bf16[224,128]{1,0:T(8,128)(2,1)S(1)}, bf16[224,128]{1,0:T(8,128)(2,1)S(1)}, u32[]{:S(2)}, u32[]{:S(2)}) collective-permute-start(bf16[224,128]{1,0:T(8,128)(2,1)S(1)} %shard_map.117.rest_0_), channel_id=1, source_target_pairs={{0,8},{8,0},{16,24},{24,16},{1,9},{9,1},{17,25},{25,17},{2,10},{10... | collective-permute-start | bytes 172040 | tf_op jit(solution)/shard_map/ppermute | solution.py:417
  67.2 2.3 %collective-permute-done.13.rest_3_ = bf16[224,128]{1,0:T(8,128)(2,1)S(1)} collective-permute-done((bf16[224,128]{1,0:T(8,128)(2,1)S(1)}, bf16[224,128]{1,0:T(8,128)(2,1)S(1)}, u32[]{:S(2)}, u32[]{:S(2)}) %collective-permute-start.13) | collective-permute-done | bytes 57376 | tf_op jit(solution)/shard_map/ppermute | solution.py:417
  69.4 1.9 %collective-permute-done.12.rest_2_ = bf16[224,128]{1,0:T(8,128)(2,1)S(1)} collective-permute-done((bf16[224,128]{1,0:T(8,128)(2,1)S(1)}, bf16[224,128]{1,0:T(8,128)(2,1)S(1)}, u32[]{:S(2)}, u32[]{:S(2)}) %collective-permute-start.12) | collective-permute-done | bytes 57376 | tf_op jit(solution)/shard_map/ppermute | solution.py:417
  71.3 0.0 collective-permute-done.11.rest_1_
  71.4 0.8 %shard_map.118 = (f32[64,320]{1,0:T(8,128)}, f32[64,128]{1,0:T(8,128)}) custom-call(bf16[224,128]{1,0:T(8,128)(2,1)S(1)} %shard_map.117.rest_0_, bf16[224,128]{1,0:T(8,128)(2,1)S(1)} %collective-permute-done.11.rest_1_, bf16[224,128]{1,0:T(8,128)(2,1)S(1)} %collective-permute-done.12.rest_2_, bf16[224,128]{1,0:T(8,128)(2,1)S(1)} %collective-permute-done.13.rest_3_), custom_call_target="tpu_custom_call" | custom-call | bytes 400000 | tf_op jit(solution)/shard_map/pallas_call | solution.py:404
  (10 shorter events, 0.1 us)
Async XLA Ops:
  5.0 7.4 %copy-start.1 = (bf16[1,8,16,1024]{3,2,1,0:T(8,128)(2,1)S(1)}, bf16[1,8,16,1024]{3,2,1,0:T(8,128)(2,1)}, u32[]{:S(2)}) copy-start(bf16[1,8,16,1024]{3,2,1,0:T(8,128)(2,1)} %param.11) | copy-start | bytes 786436
  5.0 7.4 %copy-start.2 = (bf16[1,8,16,1024]{3,2,1,0:T(8,128)(2,1)S(1)}, bf16[1,8,16,1024]{3,2,1,0:T(8,128)(2,1)}, u32[]{:S(2)}) copy-start(bf16[1,8,16,1024]{3,2,1,0:T(8,128)(2,1)} %param.12) | copy-start | bytes 786436
  5.0 7.4 %copy-start.3 = (bf16[1,8,16,1024]{3,2,1,0:T(8,128)(2,1)S(1)}, bf16[1,8,16,1024]{3,2,1,0:T(8,128)(2,1)}, u32[]{:S(2)}) copy-start(bf16[1,8,16,1024]{3,2,1,0:T(8,128)(2,1)} %param.13) | copy-start | bytes 786436
  5.1 7.4 %copy-start.4 = (bf16[8,16,1024]{2,1,0:T(8,128)(2,1)S(1)}, bf16[8,16,1024]{2,1,0:T(8,128)(2,1)}, u32[]{:S(2)}) copy-start(bf16[8,16,1024]{2,1,0:T(8,128)(2,1)} %get-tuple-element.26.queries) | copy-start | bytes 786436
  5.1 7.4 %copy-start.6 = (bf16[8,16,128]{2,1,0:T(8,128)(2,1)S(1)}, bf16[8,16,128]{2,1,0:T(8,128)(2,1)}, u32[]{:S(2)}) copy-start(bf16[8,16,128]{2,1,0:T(8,128)(2,1)} %get-tuple-element.27.adapter) | copy-start | bytes 98308
  5.1 29.6 %all-to-all-start = ((bf16[32,7,16,128]{3,2,1,0:T(8,128)(2,1)}), bf16[32,7,16,128]{3,2,1,0:T(8,128)(2,1)S(1)}, u32[]{:S(2)}, u32[]{:S(2)}) async-start(bf16[32,7,16,128]{3,2,1,0:T(8,128)(2,1)} %get-tuple-element.25), calls=%async_computation | async-start | bytes 1835008 | tf_op jit(solution)/shard_map/all_to_all | solution.py:493
  12.4 0.7 copy-start.7
  13.1 21.7 %copy-start.5 = (bf16[64,1024]{1,0:T(8,128)(2,1)S(1)}, bf16[64,1024]{1,0:T(8,128)(2,1)}, u32[]{:S(2)}) copy-start(bf16[64,1024]{1,0:T(8,128)(2,1)} %up.1) | copy-start | bytes 393220
  14.2 3.8 %collective-permute-start = (bf16[16,16,128]{2,1,0:T(8,128)(2,1)S(1)}, bf16[16,16,128]{2,1,0:T(8,128)(2,1)S(1)}, u32[]{:S(2)}, u32[]{:S(2)}) collective-permute-start(bf16[16,16,128]{2,1,0:T(8,128)(2,1)S(1)} %get-tuple-element.29), channel_id=1, source_target_pairs={{0,1},{1,0},{2,3},{3,2},{4,5},{5,4},{6,7},{7,6},{8,9},{9,8},{10,11... | collective-permute-start | bytes 196616 | tf_op jit(solution)/shard_map/ppermute | solution.py:417
  14.5 7.9 %collective-permute-start.1 = (bf16[16,16,128]{2,1,0:T(8,128)(2,1)S(1)}, bf16[16,16,128]{2,1,0:T(8,128)(2,1)S(1)}, u32[]{:S(2)}, u32[]{:S(2)}) collective-permute-start(bf16[16,16,128]{2,1,0:T(8,128)(2,1)S(1)} %get-tuple-element.30), channel_id=1, source_target_pairs={{0,2},{1,3},{2,0},{3,1},{4,6},{5,7},{6,4},{7,5},{8,10},{9,11},{10,... | collective-permute-start | bytes 196616 | tf_op jit(solution)/shard_map/ppermute | solution.py:417
  16.2 7.9 %collective-permute-start.2 = (bf16[16,16,128]{2,1,0:T(8,128)(2,1)S(1)}, bf16[16,16,128]{2,1,0:T(8,128)(2,1)S(1)}, u32[]{:S(2)}, u32[]{:S(2)}) collective-permute-start(bf16[16,16,128]{2,1,0:T(8,128)(2,1)S(1)} %get-tuple-element.31), channel_id=1, source_target_pairs={{0,3},{1,2},{2,1},{3,0},{4,7},{5,6},{6,5},{7,4},{8,11},{9,10},{10,... | collective-permute-start | bytes 196616 | tf_op jit(solution)/shard_map/ppermute | solution.py:417
  16.2 18.5 %copy-start.8 = (s32[1,1024]{1,0:T(1,128)S(1)}, s32[1,1024]{1,0:T(1,128)}, u32[]{:S(2)}) copy-start(s32[1,1024]{1,0:T(1,128)} %seg.1) | copy-start | bytes 12292
  16.2 7.9 %collective-permute-start.3 = (bf16[16,16,128]{2,1,0:T(8,128)(2,1)S(1)}, bf16[16,16,128]{2,1,0:T(8,128)(2,1)S(1)}, u32[]{:S(2)}, u32[]{:S(2)}) collective-permute-start(bf16[16,16,128]{2,1,0:T(8,128)(2,1)S(1)} %get-tuple-element.32), channel_id=1, source_target_pairs={{0,4},{1,5},{2,6},{3,7},{4,0},{5,1},{6,2},{7,3},{8,12},{9,13},{10,... | collective-permute-start | bytes 196616 | tf_op jit(solution)/shard_map/ppermute | solution.py:417
  17.9 8.5 %collective-permute-start.4 = (bf16[16,16,128]{2,1,0:T(8,128)(2,1)S(1)}, bf16[16,16,128]{2,1,0:T(8,128)(2,1)S(1)}, u32[]{:S(2)}, u32[]{:S(2)}) collective-permute-start(bf16[16,16,128]{2,1,0:T(8,128)(2,1)S(1)} %get-tuple-element.33), channel_id=1, source_target_pairs={{0,5},{1,4},{2,7},{3,6},{4,1},{5,0},{6,3},{7,2},{8,13},{9,12},{10,... | collective-permute-start | bytes 196616 | tf_op jit(solution)/shard_map/ppermute | solution.py:417
  18.0 10.0 %collective-permute-start.5 = (bf16[16,16,128]{2,1,0:T(8,128)(2,1)S(1)}, bf16[16,16,128]{2,1,0:T(8,128)(2,1)S(1)}, u32[]{:S(2)}, u32[]{:S(2)}) collective-permute-start(bf16[16,16,128]{2,1,0:T(8,128)(2,1)S(1)} %get-tuple-element.34), channel_id=1, source_target_pairs={{0,6},{1,7},{2,4},{3,5},{4,2},{5,3},{6,0},{7,1},{8,14},{9,15},{10,... | collective-permute-start | bytes 196616 | tf_op jit(solution)/shard_map/ppermute | solution.py:417
  22.4 6.2 %collective-permute-start.6 = (bf16[16,16,128]{2,1,0:T(8,128)(2,1)S(1)}, bf16[16,16,128]{2,1,0:T(8,128)(2,1)S(1)}, u32[]{:S(2)}, u32[]{:S(2)}) collective-permute-start(bf16[16,16,128]{2,1,0:T(8,128)(2,1)S(1)} %get-tuple-element.35), channel_id=1, source_target_pairs={{0,7},{1,6},{2,5},{3,4},{4,3},{5,2},{6,1},{7,0},{8,15},{9,14},{10,... | collective-permute-start | bytes 196616 | tf_op jit(solution)/shard_map/ppermute | solution.py:417
  34.7 16.5 %copy-start = (bf16[1,8,16,2560]{3,2,1,0:T(8,128)(2,1)S(1)}, bf16[1,8,16,2560]{3,2,1,0:T(8,128)(2,1)}, u32[]{:S(2)}) copy-start(bf16[1,8,16,2560]{3,2,1,0:T(8,128)(2,1)} %param.9) | copy-start | bytes 1966084
  38.4 12.8 %all-to-all-start.1 = ((bf16[32,16,128]{2,1,0:T(8,128)(2,1)}), bf16[32,16,128]{2,1,0:T(8,128)(2,1)S(1)}, u32[]{:S(2)}, u32[]{:S(2)}) async-start(bf16[32,16,128]{2,1,0:T(8,128)(2,1)} %get-tuple-element.36), calls=%async_computation.1 | async-start | bytes 262144 | tf_op jit(solution)/shard_map/all_to_all | solution.py:524
  42.8 4.7 %collective-permute-start.7 = (bf16[2,2,16,128]{3,2,1,0:T(8,128)(2,1)S(1)}, bf16[2,2,16,128]{3,2,1,0:T(8,128)(2,1)S(1)}, u32[]{:S(2)}, u32[]{:S(2)}) collective-permute-start(bf16[2,2,16,128]{3,2,1,0:T(8,128)(2,1)S(1)} %get-tuple-element.37), channel_id=1, source_target_pairs={{0,6},{1,7},{2,4},{3,5},{4,2},{5,3},{6,0},{7,1},{8,14},{9,15},{10,... | collective-permute-start | bytes 49160 | tf_op jit(solution)/shard_map/ppermute | solution.py:417
  45.5 3.8 %collective-permute-start.8 = (bf16[2,2,16,128]{3,2,1,0:T(8,128)(2,1)S(1)}, bf16[2,2,16,128]{3,2,1,0:T(8,128)(2,1)S(1)}, u32[]{:S(2)}, u32[]{:S(2)}) collective-permute-start(bf16[2,2,16,128]{3,2,1,0:T(8,128)(2,1)S(1)} %get-tuple-element.38), channel_id=1, source_target_pairs={{0,4},{1,5},{2,6},{3,7},{4,0},{5,1},{6,2},{7,3},{8,12},{9,13},{10,... | collective-permute-start | bytes 49160 | tf_op jit(solution)/shard_map/ppermute | solution.py:417
  46.1 3.7 %collective-permute-start.9 = (bf16[2,2,16,128]{3,2,1,0:T(8,128)(2,1)S(1)}, bf16[2,2,16,128]{3,2,1,0:T(8,128)(2,1)S(1)}, u32[]{:S(2)}, u32[]{:S(2)}) collective-permute-start(bf16[2,2,16,128]{3,2,1,0:T(8,128)(2,1)S(1)} %get-tuple-element.39), channel_id=1, source_target_pairs={{0,2},{1,3},{2,0},{3,1},{4,6},{5,7},{6,4},{7,5},{8,10},{9,11},{10,... | collective-permute-start | bytes 49160 | tf_op jit(solution)/shard_map/ppermute | solution.py:417
  49.8 1.2 %collective-permute-start.10 = (bf16[2,16,128]{2,1,0:T(8,128)(2,1)S(1)}, bf16[2,16,128]{2,1,0:T(8,128)(2,1)S(1)}, u32[]{:S(2)}, u32[]{:S(2)}) collective-permute-start(bf16[2,16,128]{2,1,0:T(8,128)(2,1)S(1)} %get-tuple-element.42), channel_id=1, source_target_pairs={{0,1},{1,0},{2,3},{3,2},{4,5},{5,4},{6,7},{7,6},{8,9},{9,8},{10,11... | collective-permute-start | bytes 24584 | tf_op jit(solution)/shard_map/ppermute | solution.py:417
  62.7 6.7 %collective-permute-start.13 = (bf16[224,128]{1,0:T(8,128)(2,1)S(1)}, bf16[224,128]{1,0:T(8,128)(2,1)S(1)}, u32[]{:S(2)}, u32[]{:S(2)}) collective-permute-start(bf16[224,128]{1,0:T(8,128)(2,1)S(1)} %shard_map.117.rest_0_), channel_id=1, source_target_pairs={{0,24},{8,16},{16,8},{24,0},{1,25},{9,17},{17,9},{25,1},{2,26},{10... | collective-permute-start | bytes 172040 | tf_op jit(solution)/shard_map/ppermute | solution.py:417
  66.2 5.2 %collective-permute-start.12 = (bf16[224,128]{1,0:T(8,128)(2,1)S(1)}, bf16[224,128]{1,0:T(8,128)(2,1)S(1)}, u32[]{:S(2)}, u32[]{:S(2)}) collective-permute-start(bf16[224,128]{1,0:T(8,128)(2,1)S(1)} %shard_map.117.rest_0_), channel_id=1, source_target_pairs={{0,16},{8,24},{16,0},{24,8},{1,17},{9,25},{17,1},{25,9},{2,18},{10... | collective-permute-start | bytes 172040 | tf_op jit(solution)/shard_map/ppermute | solution.py:417
  66.2 5.2 %collective-permute-start.11 = (bf16[224,128]{1,0:T(8,128)(2,1)S(1)}, bf16[224,128]{1,0:T(8,128)(2,1)S(1)}, u32[]{:S(2)}, u32[]{:S(2)}) collective-permute-start(bf16[224,128]{1,0:T(8,128)(2,1)S(1)} %shard_map.117.rest_0_), channel_id=1, source_target_pairs={{0,8},{8,0},{16,24},{24,16},{1,9},{9,1},{17,25},{25,17},{2,10},{10... | collective-permute-start | bytes 172040 | tf_op jit(solution)/shard_map/ppermute | solution.py:417

commit v2 on v1

--- a/solution.py
+++ b/solution.py
@@ -13,6 +13,7 @@
 LANES = 128
 HALF = 64
 CORES = 2
+QUERIES = 640
 LOG2E = math.log2(math.e)
 VMEM = pl.BlockSpec(memory_space=pltpu.VMEM)
 SMEM = pl.BlockSpec(memory_space=pltpu.SMEM)
@@ -137,13 +138,10 @@
     early = send(0, 2 * CAP, 0)
     for copy in copies[3:]:
         copy.wait()
-    rank = up.shape[0]
-    twice = jnp.concatenate([down[...], down[...]], axis=0)
-    adapter = lax.dot_general(feat[...], twice, NT, preferred_element_type=jnp.float32).astype(
-        jnp.bfloat16
-    )
-    abuf[...] = adapter.reshape(abuf.shape)
-    lift = jnp.dot(adapter[:, :rank], up[...], preferred_element_type=jnp.float32)
+    narrow = lax.dot_general(feat[...], down[...], NT, preferred_element_type=jnp.float32)
+    adapter = narrow.astype(jnp.bfloat16)
+    lift = jnp.dot(adapter, up[...], preferred_element_type=jnp.float32)
+    abuf[...] = jnp.concatenate([narrow, narrow], axis=1).astype(jnp.bfloat16).reshape(abuf.shape)
     qbuf[...] = (base[...].astype(jnp.float32) + lift.reshape(base.shape)).astype(jnp.bfloat16)
 
     def put_adapter(dest, slot, local):
@@ -261,8 +259,8 @@
     always = length - reach
     up_head = up[:, lane_tile(seq)]
     up_twice = jnp.concatenate([up_head, up_head], axis=0)
-    for start in range(0, reach, 2 * LANES):
-        count_here = min(2 * LANES, reach - start)
+    for start in range(0, reach, QUERIES):
+        count_here = min(QUERIES, reach - start)
         span = slice(start, start + count_here)
         scores = lax.dot_general(key_rows, qs[span, :], NT, preferred_element_type=jnp.float32)
         scores = jnp.concatenate(

time: 72.5 us -> 72 us (level)
  no operation moved by 1% of the time
where the time goes in v2:
time: 72 us; the launch traced here: 71.7 us
  starting transfers between devices  26.5 us (37%)
  waiting for transfers between devices  22.6 us (31%)
  Pallas kernels  11.1 us (15%)
  blocking collectives  10.1 us (14%)
  between operations  0.78 us (1%)
    ppermute x14, waiting for transfers between devices, exchange(): lax.ppermute(value, axis, [(peer, peer ^ turn) for peer in range(peers)])  16.4 us
    ppermute x14, starting transfers between devices, exchange(): lax.ppermute(value, axis, [(peer, peer ^ turn) for peer in range(peers)])  14.8 us
    pallas_call x7, Pallas kernels, call(): pl.pallas_call(kernel, out_shape=shapes, in_specs=specs, out_specs=out_sp...  11.1 us
    all_to_all x1, blocking collectives, per_device_tiles(): shares = lax.all_to_all(shares, 'seq', 0, 0, tiled=True)  10.1 us
    all_to_all x1, starting transfers between devices, per_device_tiles(): far = lax.all_to_all(far_send, everyone, 0, 0, tiled=True)  7.27 us
    all_to_all x1, waiting for transfers between devices, per_device_tiles(): far = lax.all_to_all(far_send, everyone, 0, 0, tiled=True)  6.06 us
    all_to_all x1, starting transfers between devices, per_device_tiles(): part = lax.all_to_all(attended[0], everyone, 0, 0, tiled=True)  4.41 us
  transfers between devices with their start and end apart: 16, of which 13 were waited for; matrix products, arithmetic and copies ran while one was open for 0% of the time, Pallas kernels for 2%

profile of v2, /device:TPU:0, one launch (start us, length us, event | category | flops | bytes accessed | tf_op | source)
XLA Modules:
  0.0 71.7 jit_solution(2186249041108025526)
XLA Ops:
  0.6 4.4 %shard_map.112 = (bf16[32,7,16,128]{3,2,1,0:T(8,128)(2,1)}, bf16[8,16,1024]{2,1,0:T(8,128)(2,1)}, bf16[8,16,128]{2,1,0:T(8,128)(2,1)}) custom-call(s32[4,8]{1,0:T(4,128)} %plan.5, bf16[128,2560]{1,0:T(8,128)(2,1)} %bitcast.7, bf16[8,16,1024]{2,1,0:T(8,128)(2,1)} %bitcast.15, bf16[8,16,1024]{2,1,0:T(8,128)(2,1)} %bitcast.9, bf16[8,16,1024]{2,1,0:T(8,128)(2,1)} %bitcast.11, ...), custom_call_target="tpu_custom_call" | custom-call | flops 60000000 | bytes 4000000 | tf_op jit(solution)/shard_map/pallas_call | solution.py:402
  5.0 0.0 copy-start.1
  5.0 0.0 copy-start.2
  5.0 0.0 copy-start.3
  5.0 0.0 copy-start.4
  5.1 0.0 copy-start.6
  5.1 7.3 %all-to-all-start = ((bf16[32,7,16,128]{3,2,1,0:T(8,128)(2,1)}), bf16[32,7,16,128]{3,2,1,0:T(8,128)(2,1)S(1)}, u32[]{:S(2)}, u32[]{:S(2)}) async-start(bf16[32,7,16,128]{3,2,1,0:T(8,128)(2,1)} %get-tuple-element.25), calls=%async_computation | async-start | bytes 1835008 | tf_op jit(solution)/shard_map/all_to_all | solution.py:491
  12.4 0.0 copy-start.7
  12.4 0.0 copy-done.1
  12.4 0.0 copy-done.2
  12.4 0.0 copy-done.3
  12.4 0.6 copy-done.7
  13.0 1.1 %shard_map.113 = (bf16[16,16,128]{2,1,0:T(8,128)(2,1)S(1)}, bf16[16,16,128]{2,1,0:T(8,128)(2,1)S(1)}, bf16[16,16,128]{2,1,0:T(8,128)(2,1)S(1)}, bf16[16,16,128]{...) custom-call(s32[4,8]{1,0:T(4,128)S(1)} %copy-done.7, ...), custom_call_target="tpu_custom_call" | custom-call | bytes 1600000 | tf_op jit(solution)/shard_map/pallas_call | solution.py:402
  14.2 0.3 collective-permute-start
  14.5 1.7 %collective-permute-start.1 = (bf16[16,16,128]{2,1,0:T(8,128)(2,1)S(1)}, bf16[16,16,128]{2,1,0:T(8,128)(2,1)S(1)}, u32[]{:S(2)}, u32[]{:S(2)}) collective-permute-start(bf16[16,16,128]{2,1,0:T(8,128)(2,1)S(1)} %get-tuple-element.30), channel_id=1, source_target_pairs={{0,2},{1,3},{2,0},{3,1},{4,6},{5,7},{6,4},{7,5},{8,10},{9,11},{10,... | collective-permute-start | bytes 196616 | tf_op jit(solution)/shard_map/ppermute | solution.py:415
  16.2 0.0 collective-permute-start.2
  16.2 1.7 %collective-permute-start.3 = (bf16[16,16,128]{2,1,0:T(8,128)(2,1)S(1)}, bf16[16,16,128]{2,1,0:T(8,128)(2,1)S(1)}, u32[]{:S(2)}, u32[]{:S(2)}) collective-permute-start(bf16[16,16,128]{2,1,0:T(8,128)(2,1)S(1)} %get-tuple-element.32), channel_id=1, source_target_pairs={{0,4},{1,5},{2,6},{3,7},{4,0},{5,1},{6,2},{7,3},{8,12},{9,13},{10,... | collective-permute-start | bytes 196616 | tf_op jit(solution)/shard_map/ppermute | solution.py:415
  17.9 0.1 collective-permute-start.4
  18.0 0.0 collective-permute-done.rest_1_
  18.0 2.6 %collective-permute-start.5 = (bf16[16,16,128]{2,1,0:T(8,128)(2,1)S(1)}, bf16[16,16,128]{2,1,0:T(8,128)(2,1)S(1)}, u32[]{:S(2)}, u32[]{:S(2)}) collective-permute-start(bf16[16,16,128]{2,1,0:T(8,128)(2,1)S(1)} %get-tuple-element.34), channel_id=1, source_target_pairs={{0,6},{1,7},{2,4},{3,5},{4,2},{5,3},{6,0},{7,1},{8,14},{9,15},{10,... | collective-permute-start | bytes 196616 | tf_op jit(solution)/shard_map/ppermute | solution.py:415
  20.6 1.8 %collective-permute-done.1.rest_2_ = bf16[16,16,128]{2,1,0:T(8,128)(2,1)S(1)} collective-permute-done((bf16[16,16,128]{2,1,0:T(8,128)(2,1)S(1)}, bf16[16,16,128]{2,1,0:T(8,128)(2,1)S(1)}, u32[]{:S(2)}, u32[]{:S(2)}) %collective-permute-start.1) | collective-permute-done | bytes 65568 | tf_op jit(solution)/shard_map/ppermute | solution.py:415
  22.4 0.4 collective-permute-start.6
  22.8 1.3 %collective-permute-done.2.rest_3_ = bf16[16,16,128]{2,1,0:T(8,128)(2,1)S(1)} collective-permute-done((bf16[16,16,128]{2,1,0:T(8,128)(2,1)S(1)}, bf16[16,16,128]{2,1,0:T(8,128)(2,1)S(1)}, u32[]{:S(2)}, u32[]{:S(2)}) %collective-permute-start.2) | collective-permute-done | bytes 65568 | tf_op jit(solution)/shard_map/ppermute | solution.py:415
  24.1 0.0 collective-permute-done.3.rest_4_
  24.1 2.3 %collective-permute-done.4.rest_5_ = bf16[16,16,128]{2,1,0:T(8,128)(2,1)S(1)} collective-permute-done((bf16[16,16,128]{2,1,0:T(8,128)(2,1)S(1)}, bf16[16,16,128]{2,1,0:T(8,128)(2,1)S(1)}, u32[]{:S(2)}, u32[]{:S(2)}) %collective-permute-start.4) | collective-permute-done | bytes 65568 | tf_op jit(solution)/shard_map/ppermute | solution.py:415
  26.4 1.5 %collective-permute-done.5.rest_6_ = bf16[16,16,128]{2,1,0:T(8,128)(2,1)S(1)} collective-permute-done((bf16[16,16,128]{2,1,0:T(8,128)(2,1)S(1)}, bf16[16,16,128]{2,1,0:T(8,128)(2,1)S(1)}, u32[]{:S(2)}, u32[]{:S(2)}) %collective-permute-start.5) | collective-permute-done | bytes 65568 | tf_op jit(solution)/shard_map/ppermute | solution.py:415
  28.0 0.7 collective-permute-done.6.rest_7_
  28.6 6.1 %all-to-all-done.far_in = bf16[32,7,16,128]{3,2,1,0:T(8,128)(2,1)S(1)} async-done(((bf16[32,7,16,128]{3,2,1,0:T(8,128)(2,1)}), bf16[32,7,16,128]{3,2,1,0:T(8,128)(2,1)S(1)}, u32[]{:S(2)}, u32[]{:S(2)}) %all-to-all-start) | async-done | bytes 917536 | tf_op jit(solution)/shard_map/all_to_all | solution.py:491
  34.7 3.3 %shard_map.114 = (bf16[32,16,128]{2,1,0:T(8,128)(2,1)}, bf16[2,2,16,128]{3,2,1,0:T(8,128)(2,1)S(1)}, bf16[2,2,16,128]{3,2,1,0:T(8,128)(2,1)S(1)}, bf16[2,2,16,12...) custom-call(s32[4,8]{1,0:T(4,128)S(1)} %copy-done.7, ...), custom_call_target="tpu_custom_call" | custom-call | flops 600000000 | bytes 3000000 | tf_op jit(solution)/shard_map/pallas_call | solution.py:402
  38.0 4.4 %all-to-all-start.1 = ((bf16[32,16,128]{2,1,0:T(8,128)(2,1)}), bf16[32,16,128]{2,1,0:T(8,128)(2,1)S(1)}, u32[]{:S(2)}, u32[]{:S(2)}) async-start(bf16[32,16,128]{2,1,0:T(8,128)(2,1)} %get-tuple-element.36), calls=%async_computation.1 | async-start | bytes 262144 | tf_op jit(solution)/shard_map/all_to_all | solution.py:522
  42.4 2.7 %collective-permute-start.7 = (bf16[2,2,16,128]{3,2,1,0:T(8,128)(2,1)S(1)}, bf16[2,2,16,128]{3,2,1,0:T(8,128)(2,1)S(1)}, u32[]{:S(2)}, u32[]{:S(2)}) collective-permute-start(bf16[2,2,16,128]{3,2,1,0:T(8,128)(2,1)S(1)} %get-tuple-element.37), channel_id=1, source_target_pairs={{0,6},{1,7},{2,4},{3,5},{4,2},{5,3},{6,0},{7,1},{8,14},{9,15},{10,... | collective-permute-start | bytes 49160 | tf_op jit(solution)/shard_map/ppermute | solution.py:415
  45.1 0.6 collective-permute-start.8
  45.7 0.3 collective-permute-start.9
  45.9 1.1 %collective-permute-done.7.refs_0_ = bf16[2,2,16,128]{3,2,1,0:T(8,128)(2,1)S(1)} collective-permute-done((bf16[2,2,16,128]{3,2,1,0:T(8,128)(2,1)S(1)}, bf16[2,2,16,128]{3,2,1,0:T(8,128)(2,1)S(1)}, u32[]{:S(2)}, u32[]{:S(2)}) %collective-permute-start.7) | collective-permute-done | bytes 16416 | tf_op jit(solution)/shard_map/ppermute | solution.py:415
  47.1 1.8 %collective-permute-done.8.refs_1_ = bf16[2,2,16,128]{3,2,1,0:T(8,128)(2,1)S(1)} collective-permute-done((bf16[2,2,16,128]{3,2,1,0:T(8,128)(2,1)S(1)}, bf16[2,2,16,128]{3,2,1,0:T(8,128)(2,1)S(1)}, u32[]{:S(2)}, u32[]{:S(2)}) %collective-permute-start.8) | collective-permute-done | bytes 16416 | tf_op jit(solution)/shard_map/ppermute | solution.py:415
  48.9 0.5 collective-permute-done.9.refs_2_
  49.4 0.1 collective-permute-start.10
  49.5 1.2 %collective-permute-done.10.own_other = bf16[2,16,128]{2,1,0:T(8,128)(2,1)S(1)} collective-permute-done((bf16[2,16,128]{2,1,0:T(8,128)(2,1)S(1)}, bf16[2,16,128]{2,1,0:T(8,128)(2,1)S(1)}, u32[]{:S(2)}, u32[]{:S(2)}) %collective-permute-start.10) | collective-permute-done | bytes 8224 | tf_op jit(solution)/shard_map/ppermute | solution.py:415
  50.7 0.1 all-to-all-done.1.parts
  50.8 1.4 %shard_map.116 = bf16[8,160,128]{2,1,0:T(8,128)(2,1)S(1)} custom-call(s32[4,8]{1,0:T(4,128)S(1)} %copy-done.7, bf16[32,16,128]{2,1,0:T(8,128)(2,1)S(1)} %all-to-all-done.1.parts, bf16[128,2560]{1,0:T(8,128)(2,1)S(1)} %bitcast.8, bf16[2,16,128]{2,1,0:T(8,128)(2,1)S(1)} %get-tuple-element.41.own_mine, bf16[2,16,128]{2,1,0:T(8,128)(2,1)S(1)} %collective-permute-done.10.own_other), custom_call_target="tpu_custom_call" | custom-call | flops 40000000 | bytes 2000000 | tf_op jit(solution)/shard_map/pallas_call | solution.py:402
  52.2 10.1 %all_to_all.15.parts = bf16[8,160,128]{2,1,0:T(8,128)(2,1)S(1)} all-to-all(bf16[8,160,128]{2,1,0:T(8,128)(2,1)S(1)} %shard_map.116), channel_id=1, replica_groups=mesh['dp'=4,'seq'=8] {'seq'}, dimensions={0} | all-to-all | bytes 655360 | tf_op jit(solution)/shard_map/all_to_all | solution.py:540
  62.3 3.4 %collective-permute-start.13 = (bf16[224,128]{1,0:T(8,128)(2,1)S(1)}, bf16[224,128]{1,0:T(8,128)(2,1)S(1)}, u32[]{:S(2)}, u32[]{:S(2)}) collective-permute-start(bf16[224,128]{1,0:T(8,128)(2,1)S(1)} %shard_map.117.rest_0_), channel_id=1, source_target_pairs={{0,24},{8,16},{16,8},{24,0},{1,25},{9,17},{17,9},{25,1},{2,26},{10... | collective-permute-start | bytes 172040 | tf_op jit(solution)/shard_map/ppermute | solution.py:415
  65.7 0.0 collective-permute-start.12
  65.7 1.1 %collective-permute-start.11 = (bf16[224,128]{1,0:T(8,128)(2,1)S(1)}, bf16[224,128]{1,0:T(8,128)(2,1)S(1)}, u32[]{:S(2)}, u32[]{:S(2)}) collective-permute-start(bf16[224,128]{1,0:T(8,128)(2,1)S(1)} %shard_map.117.rest_0_), channel_id=1, source_target_pairs={{0,8},{8,0},{16,24},{24,16},{1,9},{9,1},{17,25},{25,17},{2,10},{10... | collective-permute-start | bytes 172040 | tf_op jit(solution)/shard_map/ppermute | solution.py:415
  66.8 2.2 %collective-permute-done.13.rest_3_ = bf16[224,128]{1,0:T(8,128)(2,1)S(1)} collective-permute-done((bf16[224,128]{1,0:T(8,128)(2,1)S(1)}, bf16[224,128]{1,0:T(8,128)(2,1)S(1)}, u32[]{:S(2)}, u32[]{:S(2)}) %collective-permute-start.13) | collective-permute-done | bytes 57376 | tf_op jit(solution)/shard_map/ppermute | solution.py:415
  69.0 1.8 %collective-permute-done.12.rest_2_ = bf16[224,128]{1,0:T(8,128)(2,1)S(1)} collective-permute-done((bf16[224,128]{1,0:T(8,128)(2,1)S(1)}, bf16[224,128]{1,0:T(8,128)(2,1)S(1)}, u32[]{:S(2)}, u32[]{:S(2)}) %collective-permute-start.12) | collective-permute-done | bytes 57376 | tf_op jit(solution)/shard_map/ppermute | solution.py:415
  70.9 0.0 collective-permute-done.11.rest_1_
  70.9 0.8 %shard_map.118 = (f32[64,320]{1,0:T(8,128)}, f32[64,128]{1,0:T(8,128)}) custom-call(bf16[224,128]{1,0:T(8,128)(2,1)S(1)} %shard_map.117.rest_0_, bf16[224,128]{1,0:T(8,128)(2,1)S(1)} %collective-permute-done.11.rest_1_, bf16[224,128]{1,0:T(8,128)(2,1)S(1)} %collective-permute-done.12.rest_2_, bf16[224,128]{1,0:T(8,128)(2,1)S(1)} %collective-permute-done.13.rest_3_), custom_call_target="tpu_custom_call" | custom-call | bytes 400000 | tf_op jit(solution)/shard_map/pallas_call | solution.py:402
  (10 shorter events, 0.1 us)
Async XLA Ops:
  5.0 7.4 %copy-start.1 = (bf16[1,8,16,1024]{3,2,1,0:T(8,128)(2,1)S(1)}, bf16[1,8,16,1024]{3,2,1,0:T(8,128)(2,1)}, u32[]{:S(2)}) copy-start(bf16[1,8,16,1024]{3,2,1,0:T(8,128)(2,1)} %param.11) | copy-start | bytes 786436
  5.0 7.4 %copy-start.2 = (bf16[1,8,16,1024]{3,2,1,0:T(8,128)(2,1)S(1)}, bf16[1,8,16,1024]{3,2,1,0:T(8,128)(2,1)}, u32[]{:S(2)}) copy-start(bf16[1,8,16,1024]{3,2,1,0:T(8,128)(2,1)} %param.12) | copy-start | bytes 786436
  5.0 7.3 %copy-start.3 = (bf16[1,8,16,1024]{3,2,1,0:T(8,128)(2,1)S(1)}, bf16[1,8,16,1024]{3,2,1,0:T(8,128)(2,1)}, u32[]{:S(2)}) copy-start(bf16[1,8,16,1024]{3,2,1,0:T(8,128)(2,1)} %param.13) | copy-start | bytes 786436
  5.0 7.3 %copy-start.4 = (bf16[8,16,1024]{2,1,0:T(8,128)(2,1)S(1)}, bf16[8,16,1024]{2,1,0:T(8,128)(2,1)}, u32[]{:S(2)}) copy-start(bf16[8,16,1024]{2,1,0:T(8,128)(2,1)} %get-tuple-element.26.queries) | copy-start | bytes 786436
  5.1 7.3 %copy-start.6 = (bf16[8,16,128]{2,1,0:T(8,128)(2,1)S(1)}, bf16[8,16,128]{2,1,0:T(8,128)(2,1)}, u32[]{:S(2)}) copy-start(bf16[8,16,128]{2,1,0:T(8,128)(2,1)} %get-tuple-element.27.adapter) | copy-start | bytes 98308
  5.1 29.6 %all-to-all-start = ((bf16[32,7,16,128]{3,2,1,0:T(8,128)(2,1)}), bf16[32,7,16,128]{3,2,1,0:T(8,128)(2,1)S(1)}, u32[]{:S(2)}, u32[]{:S(2)}) async-start(bf16[32,7,16,128]{3,2,1,0:T(8,128)(2,1)} %get-tuple-element.25), calls=%async_computation | async-start | bytes 1835008 | tf_op jit(solution)/shard_map/all_to_all | solution.py:491
  12.4 0.7 copy-start.7
  13.0 21.7 %copy-start.5 = (bf16[64,1024]{1,0:T(8,128)(2,1)S(1)}, bf16[64,1024]{1,0:T(8,128)(2,1)}, u32[]{:S(2)}) copy-start(bf16[64,1024]{1,0:T(8,128)(2,1)} %up.1) | copy-start | bytes 393220
  14.2 3.8 %collective-permute-start = (bf16[16,16,128]{2,1,0:T(8,128)(2,1)S(1)}, bf16[16,16,128]{2,1,0:T(8,128)(2,1)S(1)}, u32[]{:S(2)}, u32[]{:S(2)}) collective-permute-start(bf16[16,16,128]{2,1,0:T(8,128)(2,1)S(1)} %get-tuple-element.29), channel_id=1, source_target_pairs={{0,1},{1,0},{2,3},{3,2},{4,5},{5,4},{6,7},{7,6},{8,9},{9,8},{10,11... | collective-permute-start | bytes 196616 | tf_op jit(solution)/shard_map/ppermute | solution.py:415
  14.5 7.9 %collective-permute-start.1 = (bf16[16,16,128]{2,1,0:T(8,128)(2,1)S(1)}, bf16[16,16,128]{2,1,0:T(8,128)(2,1)S(1)}, u32[]{:S(2)}, u32[]{:S(2)}) collective-permute-start(bf16[16,16,128]{2,1,0:T(8,128)(2,1)S(1)} %get-tuple-element.30), channel_id=1, source_target_pairs={{0,2},{1,3},{2,0},{3,1},{4,6},{5,7},{6,4},{7,5},{8,10},{9,11},{10,... | collective-permute-start | bytes 196616 | tf_op jit(solution)/shard_map/ppermute | solution.py:415
  16.2 7.9 %collective-permute-start.2 = (bf16[16,16,128]{2,1,0:T(8,128)(2,1)S(1)}, bf16[16,16,128]{2,1,0:T(8,128)(2,1)S(1)}, u32[]{:S(2)}, u32[]{:S(2)}) collective-permute-start(bf16[16,16,128]{2,1,0:T(8,128)(2,1)S(1)} %get-tuple-element.31), channel_id=1, source_target_pairs={{0,3},{1,2},{2,1},{3,0},{4,7},{5,6},{6,5},{7,4},{8,11},{9,10},{10,... | collective-permute-start | bytes 196616 | tf_op jit(solution)/shard_map/ppermute | solution.py:415
  16.2 18.5 %copy-start.8 = (s32[1,1024]{1,0:T(1,128)S(1)}, s32[1,1024]{1,0:T(1,128)}, u32[]{:S(2)}) copy-start(s32[1,1024]{1,0:T(1,128)} %seg.1) | copy-start | bytes 12292
  16.2 7.9 %collective-permute-start.3 = (bf16[16,16,128]{2,1,0:T(8,128)(2,1)S(1)}, bf16[16,16,128]{2,1,0:T(8,128)(2,1)S(1)}, u32[]{:S(2)}, u32[]{:S(2)}) collective-permute-start(bf16[16,16,128]{2,1,0:T(8,128)(2,1)S(1)} %get-tuple-element.32), channel_id=1, source_target_pairs={{0,4},{1,5},{2,6},{3,7},{4,0},{5,1},{6,2},{7,3},{8,12},{9,13},{10,... | collective-permute-start | bytes 196616 | tf_op jit(solution)/shard_map/ppermute | solution.py:415
  17.9 8.5 %collective-permute-start.4 = (bf16[16,16,128]{2,1,0:T(8,128)(2,1)S(1)}, bf16[16,16,128]{2,1,0:T(8,128)(2,1)S(1)}, u32[]{:S(2)}, u32[]{:S(2)}) collective-permute-start(bf16[16,16,128]{2,1,0:T(8,128)(2,1)S(1)} %get-tuple-element.33), channel_id=1, source_target_pairs={{0,5},{1,4},{2,7},{3,6},{4,1},{5,0},{6,3},{7,2},{8,13},{9,12},{10,... | collective-permute-start | bytes 196616 | tf_op jit(solution)/shard_map/ppermute | solution.py:415
  18.0 10.0 %collective-permute-start.5 = (bf16[16,16,128]{2,1,0:T(8,128)(2,1)S(1)}, bf16[16,16,128]{2,1,0:T(8,128)(2,1)S(1)}, u32[]{:S(2)}, u32[]{:S(2)}) collective-permute-start(bf16[16,16,128]{2,1,0:T(8,128)(2,1)S(1)} %get-tuple-element.34), channel_id=1, source_target_pairs={{0,6},{1,7},{2,4},{3,5},{4,2},{5,3},{6,0},{7,1},{8,14},{9,15},{10,... | collective-permute-start | bytes 196616 | tf_op jit(solution)/shard_map/ppermute | solution.py:415
  22.4 6.2 %collective-permute-start.6 = (bf16[16,16,128]{2,1,0:T(8,128)(2,1)S(1)}, bf16[16,16,128]{2,1,0:T(8,128)(2,1)S(1)}, u32[]{:S(2)}, u32[]{:S(2)}) collective-permute-start(bf16[16,16,128]{2,1,0:T(8,128)(2,1)S(1)} %get-tuple-element.35), channel_id=1, source_target_pairs={{0,7},{1,6},{2,5},{3,4},{4,3},{5,2},{6,1},{7,0},{8,15},{9,14},{10,... | collective-permute-start | bytes 196616 | tf_op jit(solution)/shard_map/ppermute | solution.py:415
  34.7 16.1 %copy-start = (bf16[1,8,16,2560]{3,2,1,0:T(8,128)(2,1)S(1)}, bf16[1,8,16,2560]{3,2,1,0:T(8,128)(2,1)}, u32[]{:S(2)}) copy-start(bf16[1,8,16,2560]{3,2,1,0:T(8,128)(2,1)} %param.9) | copy-start | bytes 1966084
  38.0 12.8 %all-to-all-start.1 = ((bf16[32,16,128]{2,1,0:T(8,128)(2,1)}), bf16[32,16,128]{2,1,0:T(8,128)(2,1)S(1)}, u32[]{:S(2)}, u32[]{:S(2)}) async-start(bf16[32,16,128]{2,1,0:T(8,128)(2,1)} %get-tuple-element.36), calls=%async_computation.1 | async-start | bytes 262144 | tf_op jit(solution)/shard_map/all_to_all | solution.py:522
  42.4 4.7 %collective-permute-start.7 = (bf16[2,2,16,128]{3,2,1,0:T(8,128)(2,1)S(1)}, bf16[2,2,16,128]{3,2,1,0:T(8,128)(2,1)S(1)}, u32[]{:S(2)}, u32[]{:S(2)}) collective-permute-start(bf16[2,2,16,128]{3,2,1,0:T(8,128)(2,1)S(1)} %get-tuple-element.37), channel_id=1, source_target_pairs={{0,6},{1,7},{2,4},{3,5},{4,2},{5,3},{6,0},{7,1},{8,14},{9,15},{10,... | collective-permute-start | bytes 49160 | tf_op jit(solution)/shard_map/ppermute | solution.py:415
  45.1 3.8 %collective-permute-start.8 = (bf16[2,2,16,128]{3,2,1,0:T(8,128)(2,1)S(1)}, bf16[2,2,16,128]{3,2,1,0:T(8,128)(2,1)S(1)}, u32[]{:S(2)}, u32[]{:S(2)}) collective-permute-start(bf16[2,2,16,128]{3,2,1,0:T(8,128)(2,1)S(1)} %get-tuple-element.38), channel_id=1, source_target_pairs={{0,4},{1,5},{2,6},{3,7},{4,0},{5,1},{6,2},{7,3},{8,12},{9,13},{10,... | collective-permute-start | bytes 49160 | tf_op jit(solution)/shard_map/ppermute | solution.py:415
  45.7 3.7 %collective-permute-start.9 = (bf16[2,2,16,128]{3,2,1,0:T(8,128)(2,1)S(1)}, bf16[2,2,16,128]{3,2,1,0:T(8,128)(2,1)S(1)}, u32[]{:S(2)}, u32[]{:S(2)}) collective-permute-start(bf16[2,2,16,128]{3,2,1,0:T(8,128)(2,1)S(1)} %get-tuple-element.39), channel_id=1, source_target_pairs={{0,2},{1,3},{2,0},{3,1},{4,6},{5,7},{6,4},{7,5},{8,10},{9,11},{10,... | collective-permute-start | bytes 49160 | tf_op jit(solution)/shard_map/ppermute | solution.py:415
  49.4 1.2 %collective-permute-start.10 = (bf16[2,16,128]{2,1,0:T(8,128)(2,1)S(1)}, bf16[2,16,128]{2,1,0:T(8,128)(2,1)S(1)}, u32[]{:S(2)}, u32[]{:S(2)}) collective-permute-start(bf16[2,16,128]{2,1,0:T(8,128)(2,1)S(1)} %get-tuple-element.42), channel_id=1, source_target_pairs={{0,1},{1,0},{2,3},{3,2},{4,5},{5,4},{6,7},{7,6},{8,9},{9,8},{10,11... | collective-permute-start | bytes 24584 | tf_op jit(solution)/shard_map/ppermute | solution.py:415
  62.3 6.7 %collective-permute-start.13 = (bf16[224,128]{1,0:T(8,128)(2,1)S(1)}, bf16[224,128]{1,0:T(8,128)(2,1)S(1)}, u32[]{:S(2)}, u32[]{:S(2)}) collective-permute-start(bf16[224,128]{1,0:T(8,128)(2,1)S(1)} %shard_map.117.rest_0_), channel_id=1, source_target_pairs={{0,24},{8,16},{16,8},{24,0},{1,25},{9,17},{17,9},{25,1},{2,26},{10... | collective-permute-start | bytes 172040 | tf_op jit(solution)/shard_map/ppermute | solution.py:415
  65.7 5.2 %collective-permute-start.12 = (bf16[224,128]{1,0:T(8,128)(2,1)S(1)}, bf16[224,128]{1,0:T(8,128)(2,1)S(1)}, u32[]{:S(2)}, u32[]{:S(2)}) collective-permute-start(bf16[224,128]{1,0:T(8,128)(2,1)S(1)} %shard_map.117.rest_0_), channel_id=1, source_target_pairs={{0,16},{8,24},{16,0},{24,8},{1,17},{9,25},{17,1},{25,9},{2,18},{10... | collective-permute-start | bytes 172040 | tf_op jit(solution)/shard_map/ppermute | solution.py:415
  65.7 5.2 %collective-permute-start.11 = (bf16[224,128]{1,0:T(8,128)(2,1)S(1)}, bf16[224,128]{1,0:T(8,128)(2,1)S(1)}, u32[]{:S(2)}, u32[]{:S(2)}) collective-permute-start(bf16[224,128]{1,0:T(8,128)(2,1)S(1)} %shard_map.117.rest_0_), channel_id=1, source_target_pairs={{0,8},{8,0},{16,24},{24,16},{1,9},{9,1},{17,25},{25,17},{2,10},{10... | collective-permute-start | bytes 172040 | tf_op jit(solution)/shard_map/ppermute | solution.py:415

commit v3 on v2

--- a/solution.py
+++ b/solution.py
@@ -93,8 +93,8 @@
 
 def pack_far_kernel(dims, plan_hbm, feat_hbm, base_hbm, keys_hbm, vals_hbm, down_hbm, up_hbm, *rest):
     groups, blocks, heads, rows, live = dims
-    far_hbm, qbuf, abuf = rest[:3]
-    plan, feat, base, keys, vals, down, up, far_out, sems, out_sems = rest[3:]
+    far_hbm, queries_hbm, adapter_hbm = rest[:3]
+    plan, feat, base, keys, vals, down, up, far_out, qbuf, abuf, sems, out_sems = rest[3:]
     me = lax.axis_index("dp")
     copies = [
         pltpu.make_async_copy(source, target, sems.at[index])
@@ -113,18 +113,13 @@
     for copy in copies:
         copy.start()
 
-    def put_blocks(sources, first):
-        def put(dest, slot, local):
-            @pl.when(slot < CAP)
-            def _():
-                for head in range(heads):
-                    columns = slice(head * LANES, (head + 1) * LANES)
-                    for index, source in enumerate(sources):
-                        far_out[head * groups + dest, (first + index) * CAP + slot] = source[
-                            local, :, columns
-                        ]
-
-        each_hit(plan, me, groups, blocks, live, put)
+    def put_early(dest, slot, local):
+        @pl.when(slot < CAP)
+        def _():
+            for head in range(heads):
+                columns = slice(head * LANES, (head + 1) * LANES)
+                far_out[head * groups + dest, slot] = keys[local, :, columns]
+                far_out[head * groups + dest, CAP + slot] = vals[local, :, columns]
 
     def send(first, count, index):
         tiles = pl.ds(first, count)
@@ -134,7 +129,7 @@
 
     for copy in copies[:3]:
         copy.wait()
-    put_blocks((keys, vals), 0)
+    each_hit(plan, me, groups, blocks, live, put_early)
     early = send(0, 2 * CAP, 0)
     for copy in copies[3:]:
         copy.wait()
@@ -144,20 +139,27 @@
     abuf[...] = jnp.concatenate([narrow, narrow], axis=1).astype(jnp.bfloat16).reshape(abuf.shape)
     qbuf[...] = (base[...].astype(jnp.float32) + lift.reshape(base.shape)).astype(jnp.bfloat16)
 
-    def put_adapter(dest, slot, local):
+    def put_late(dest, slot, local):
         def store(lanes):
             for head in range(heads):
+                columns = slice(head * LANES, (head + 1) * LANES)
+                far_out[head * groups + dest, 2 * CAP + slot] = qbuf[local, :, columns]
                 far_out[head * groups + dest, CAP * 3, :, lanes] = abuf[local, :, lanes]
 
         @pl.when(slot < CAP)
         def _():
             each_half(slot, store)
 
-    each_hit(plan, me, groups, blocks, live, put_adapter)
-    put_blocks((qbuf,), 2)
+    each_hit(plan, me, groups, blocks, live, put_late)
     late = send(2 * CAP, CAP + 1, 1)
-    early.wait()
-    late.wait()
+    rest_out = [
+        pltpu.make_async_copy(qbuf, queries_hbm, out_sems.at[2]),
+        pltpu.make_async_copy(abuf, adapter_hbm, out_sems.at[3]),
+    ]
+    for copy in rest_out:
+        copy.start()
+    for copy in [early, late] + rest_out:
+        copy.wait()
 
 
 def pack_own_kernel(dims, plan, keys, vals, grad, queries, adapter, *own_outs):
@@ -458,8 +460,10 @@
             pltpu.VMEM((rank, width), bf16),
             pltpu.VMEM((rank, heads * LANES), bf16),
             pltpu.VMEM(far_shape, bf16),
+            pltpu.VMEM(rows_shape, bf16),
+            pltpu.VMEM((blocks, rows, LANES), bf16),
             pltpu.SemaphoreType.DMA((7,)),
-            pltpu.SemaphoreType.DMA((2,)),
+            pltpu.SemaphoreType.DMA((4,)),
         ],
         60_000_000,
         4_000_000,
@@ -471,7 +475,7 @@
         adapter_down_weight.T,
         adapter_up_weight,
         vmem_mib=60,
-        out_specs=[ANY, VMEM, VMEM],
+        out_specs=[ANY] * 3,
     )
     own_send = call(
         functools.partial(pack_own_kernel, dims),

time: 72 us -> 71.2 us (0.989)
  Pallas kernels: 11.1 us -> 10.1 us
    pallas_call x7, Pallas kernels: 11.1 us -> 10.1 us  [call(): pl.pallas_call(kernel, out_shape=shapes, in_specs=specs, out_specs=out_sp...]
where the time goes in v3:
time: 71.2 us; the launch traced here: 70.8 us
  starting transfers between devices  26.6 us (37%)
  waiting for transfers between devices  22.6 us (32%)
  Pallas kernels  10.1 us (14%)
  blocking collectives  10.1 us (14%)
  between operations  0.78 us (1%)
    ppermute x14, waiting for transfers between devices, exchange(): lax.ppermute(value, axis, [(peer, peer ^ turn) for peer in range(peers)])  16.4 us
    ppermute x14, starting transfers between devices, exchange(): lax.ppermute(value, axis, [(peer, peer ^ turn) for peer in range(peers)])  14.8 us
    pallas_call x7, Pallas kernels, call(): pl.pallas_call(kernel, out_shape=shapes, in_specs=specs, out_specs=out_sp...  10.1 us
    all_to_all x1, blocking collectives, per_device_tiles(): shares = lax.all_to_all(shares, 'seq', 0, 0, tiled=True)  10.1 us
    all_to_all x1, starting transfers between devices, per_device_tiles(): far = lax.all_to_all(far_send, everyone, 0, 0, tiled=True)  7.32 us
    all_to_all x1, waiting for transfers between devices, per_device_tiles(): far = lax.all_to_all(far_send, everyone, 0, 0, tiled=True)  6.06 us
    all_to_all x1, starting transfers between devices, per_device_tiles(): part = lax.all_to_all(attended[0], everyone, 0, 0, tiled=True)  4.41 us
  transfers between devices with their start and end apart: 16, of which 13 were waited for; matrix products, arithmetic and copies ran while one was open for 0% of the time, Pallas kernels for 2%

profile of v3, /device:TPU:0, one launch (start us, length us, event | category | flops | bytes accessed | tf_op | source)
XLA Modules:
  0.0 70.8 jit_solution(4297722821621654406)
XLA Ops:
  0.6 3.4 %shard_map.112 = (bf16[32,7,16,128]{3,2,1,0:T(8,128)(2,1)}, bf16[8,16,1024]{2,1,0:T(8,128)(2,1)}, bf16[8,16,128]{2,1,0:T(8,128)(2,1)}) custom-call(s32[4,8]{1,0:T(4,128)} %plan.5, bf16[128,2560]{1,0:T(8,128)(2,1)} %bitcast.7, bf16[8,16,1024]{2,1,0:T(8,128)(2,1)} %bitcast.15, bf16[8,16,1024]{2,1,0:T(8,128)(2,1)} %bitcast.9, bf16[8,16,1024]{2,1,0:T(8,128)(2,1)} %bitcast.11, ...), custom_call_target="tpu_custom_call" | custom-call | flops 60000000 | bytes 4000000 | tf_op jit(solution)/shard_map/pallas_call | solution.py:404
  4.0 0.0 copy-start.1
  4.1 0.0 copy-start.2
  4.1 0.0 copy-start.3
  4.1 0.0 copy-start.6
  4.1 7.3 %all-to-all-start = ((bf16[32,7,16,128]{3,2,1,0:T(8,128)(2,1)}), bf16[32,7,16,128]{3,2,1,0:T(8,128)(2,1)S(1)}, u32[]{:S(2)}, u32[]{:S(2)}) async-start(bf16[32,7,16,128]{3,2,1,0:T(8,128)(2,1)} %get-tuple-element.25), calls=%async_computation | async-start | bytes 1835008 | tf_op jit(solution)/shard_map/all_to_all | solution.py:495
  11.4 0.0 copy-start.7
  11.4 0.0 copy-done.1
  11.4 0.0 copy-done.2
  11.5 0.0 copy-done.3
  11.5 0.0 copy-done.4
  11.5 0.6 copy-done.7
  12.1 1.1 %shard_map.113 = (bf16[16,16,128]{2,1,0:T(8,128)(2,1)S(1)}, bf16[16,16,128]{2,1,0:T(8,128)(2,1)S(1)}, bf16[16,16,128]{2,1,0:T(8,128)(2,1)S(1)}, bf16[16,16,128]{...) custom-call(s32[4,8]{1,0:T(4,128)S(1)} %copy-done.7, ...), custom_call_target="tpu_custom_call" | custom-call | bytes 1600000 | tf_op jit(solution)/shard_map/pallas_call | solution.py:404
  13.2 0.3 collective-permute-start
  13.6 1.7 %collective-permute-start.1 = (bf16[16,16,128]{2,1,0:T(8,128)(2,1)S(1)}, bf16[16,16,128]{2,1,0:T(8,128)(2,1)S(1)}, u32[]{:S(2)}, u32[]{:S(2)}) collective-permute-start(bf16[16,16,128]{2,1,0:T(8,128)(2,1)S(1)} %get-tuple-element.30), channel_id=1, source_target_pairs={{0,2},{1,3},{2,0},{3,1},{4,6},{5,7},{6,4},{7,5},{8,10},{9,11},{10,... | collective-permute-start | bytes 196616 | tf_op jit(solution)/shard_map/ppermute | solution.py:417
  15.2 0.0 collective-permute-start.2
  15.2 1.7 %collective-permute-start.3 = (bf16[16,16,128]{2,1,0:T(8,128)(2,1)S(1)}, bf16[16,16,128]{2,1,0:T(8,128)(2,1)S(1)}, u32[]{:S(2)}, u32[]{:S(2)}) collective-permute-start(bf16[16,16,128]{2,1,0:T(8,128)(2,1)S(1)} %get-tuple-element.32), channel_id=1, source_target_pairs={{0,4},{1,5},{2,6},{3,7},{4,0},{5,1},{6,2},{7,3},{8,12},{9,13},{10,... | collective-permute-start | bytes 196616 | tf_op jit(solution)/shard_map/ppermute | solution.py:417
  16.9 0.1 collective-permute-start.4
  17.0 0.0 collective-permute-done.rest_1_
  17.1 2.6 %collective-permute-start.5 = (bf16[16,16,128]{2,1,0:T(8,128)(2,1)S(1)}, bf16[16,16,128]{2,1,0:T(8,128)(2,1)S(1)}, u32[]{:S(2)}, u32[]{:S(2)}) collective-permute-start(bf16[16,16,128]{2,1,0:T(8,128)(2,1)S(1)} %get-tuple-element.34), channel_id=1, source_target_pairs={{0,6},{1,7},{2,4},{3,5},{4,2},{5,3},{6,0},{7,1},{8,14},{9,15},{10,... | collective-permute-start | bytes 196616 | tf_op jit(solution)/shard_map/ppermute | solution.py:417
  19.6 1.8 %collective-permute-done.1.rest_2_ = bf16[16,16,128]{2,1,0:T(8,128)(2,1)S(1)} collective-permute-done((bf16[16,16,128]{2,1,0:T(8,128)(2,1)S(1)}, bf16[16,16,128]{2,1,0:T(8,128)(2,1)S(1)}, u32[]{:S(2)}, u32[]{:S(2)}) %collective-permute-start.1) | collective-permute-done | bytes 65568 | tf_op jit(solution)/shard_map/ppermute | solution.py:417
  21.5 0.4 collective-permute-start.6
  21.8 1.3 %collective-permute-done.2.rest_3_ = bf16[16,16,128]{2,1,0:T(8,128)(2,1)S(1)} collective-permute-done((bf16[16,16,128]{2,1,0:T(8,128)(2,1)S(1)}, bf16[16,16,128]{2,1,0:T(8,128)(2,1)S(1)}, u32[]{:S(2)}, u32[]{:S(2)}) %collective-permute-start.2) | collective-permute-done | bytes 65568 | tf_op jit(solution)/shard_map/ppermute | solution.py:417
  23.2 0.0 collective-permute-done.3.rest_4_
  23.2 2.3 %collective-permute-done.4.rest_5_ = bf16[16,16,128]{2,1,0:T(8,128)(2,1)S(1)} collective-permute-done((bf16[16,16,128]{2,1,0:T(8,128)(2,1)S(1)}, bf16[16,16,128]{2,1,0:T(8,128)(2,1)S(1)}, u32[]{:S(2)}, u32[]{:S(2)}) %collective-permute-start.4) | collective-permute-done | bytes 65568 | tf_op jit(solution)/shard_map/ppermute | solution.py:417
  25.5 1.6 %collective-permute-done.5.rest_6_ = bf16[16,16,128]{2,1,0:T(8,128)(2,1)S(1)} collective-permute-done((bf16[16,16,128]{2,1,0:T(8,128)(2,1)S(1)}, bf16[16,16,128]{2,1,0:T(8,128)(2,1)S(1)}, u32[]{:S(2)}, u32[]{:S(2)}) %collective-permute-start.5) | collective-permute-done | bytes 65568 | tf_op jit(solution)/shard_map/ppermute | solution.py:417
  27.0 0.7 collective-permute-done.6.rest_7_
  27.7 6.1 %all-to-all-done.far_in = bf16[32,7,16,128]{3,2,1,0:T(8,128)(2,1)S(1)} async-done(((bf16[32,7,16,128]{3,2,1,0:T(8,128)(2,1)}), bf16[32,7,16,128]{3,2,1,0:T(8,128)(2,1)S(1)}, u32[]{:S(2)}, u32[]{:S(2)}) %all-to-all-start) | async-done | bytes 917536 | tf_op jit(solution)/shard_map/all_to_all | solution.py:495
  33.8 3.3 %shard_map.114 = (bf16[32,16,128]{2,1,0:T(8,128)(2,1)}, bf16[2,2,16,128]{3,2,1,0:T(8,128)(2,1)S(1)}, bf16[2,2,16,128]{3,2,1,0:T(8,128)(2,1)S(1)}, bf16[2,2,16,12...) custom-call(s32[4,8]{1,0:T(4,128)S(1)} %copy-done.7, ...), custom_call_target="tpu_custom_call" | custom-call | flops 600000000 | bytes 3000000 | tf_op jit(solution)/shard_map/pallas_call | solution.py:404
  37.1 4.4 %all-to-all-start.1 = ((bf16[32,16,128]{2,1,0:T(8,128)(2,1)}), bf16[32,16,128]{2,1,0:T(8,128)(2,1)S(1)}, u32[]{:S(2)}, u32[]{:S(2)}) async-start(bf16[32,16,128]{2,1,0:T(8,128)(2,1)} %get-tuple-element.36), calls=%async_computation.1 | async-start | bytes 262144 | tf_op jit(solution)/shard_map/all_to_all | solution.py:526
  41.5 2.7 %collective-permute-start.7 = (bf16[2,2,16,128]{3,2,1,0:T(8,128)(2,1)S(1)}, bf16[2,2,16,128]{3,2,1,0:T(8,128)(2,1)S(1)}, u32[]{:S(2)}, u32[]{:S(2)}) collective-permute-start(bf16[2,2,16,128]{3,2,1,0:T(8,128)(2,1)S(1)} %get-tuple-element.37), channel_id=1, source_target_pairs={{0,6},{1,7},{2,4},{3,5},{4,2},{5,3},{6,0},{7,1},{8,14},{9,15},{10,... | collective-permute-start | bytes 49160 | tf_op jit(solution)/shard_map/ppermute | solution.py:417
  44.2 0.6 collective-permute-start.8
  44.8 0.3 collective-permute-start.9
  45.0 1.1 %collective-permute-done.7.refs_0_ = bf16[2,2,16,128]{3,2,1,0:T(8,128)(2,1)S(1)} collective-permute-done((bf16[2,2,16,128]{3,2,1,0:T(8,128)(2,1)S(1)}, bf16[2,2,16,128]{3,2,1,0:T(8,128)(2,1)S(1)}, u32[]{:S(2)}, u32[]{:S(2)}) %collective-permute-start.7) | collective-permute-done | bytes 16416 | tf_op jit(solution)/shard_map/ppermute | solution.py:417
  46.2 1.8 %collective-permute-done.8.refs_1_ = bf16[2,2,16,128]{3,2,1,0:T(8,128)(2,1)S(1)} collective-permute-done((bf16[2,2,16,128]{3,2,1,0:T(8,128)(2,1)S(1)}, bf16[2,2,16,128]{3,2,1,0:T(8,128)(2,1)S(1)}, u32[]{:S(2)}, u32[]{:S(2)}) %collective-permute-start.8) | collective-permute-done | bytes 16416 | tf_op jit(solution)/shard_map/ppermute | solution.py:417
  48.0 0.5 collective-permute-done.9.refs_2_
  48.5 0.1 collective-permute-start.10
  48.6 1.2 %collective-permute-done.10.own_other = bf16[2,16,128]{2,1,0:T(8,128)(2,1)S(1)} collective-permute-done((bf16[2,16,128]{2,1,0:T(8,128)(2,1)S(1)}, bf16[2,16,128]{2,1,0:T(8,128)(2,1)S(1)}, u32[]{:S(2)}, u32[]{:S(2)}) %collective-permute-start.10) | collective-permute-done | bytes 8224 | tf_op jit(solution)/shard_map/ppermute | solution.py:417
  49.8 0.1 all-to-all-done.1.parts
  49.9 1.4 %shard_map.116 = bf16[8,160,128]{2,1,0:T(8,128)(2,1)S(1)} custom-call(s32[4,8]{1,0:T(4,128)S(1)} %copy-done.7, bf16[32,16,128]{2,1,0:T(8,128)(2,1)S(1)} %all-to-all-done.1.parts, bf16[128,2560]{1,0:T(8,128)(2,1)S(1)} %bitcast.8, bf16[2,16,128]{2,1,0:T(8,128)(2,1)S(1)} %get-tuple-element.41.own_mine, bf16[2,16,128]{2,1,0:T(8,128)(2,1)S(1)} %collective-permute-done.10.own_other), custom_call_target="tpu_custom_call" | custom-call | flops 40000000 | bytes 2000000 | tf_op jit(solution)/shard_map/pallas_call | solution.py:404
  51.3 10.1 %all_to_all.15.parts = bf16[8,160,128]{2,1,0:T(8,128)(2,1)S(1)} all-to-all(bf16[8,160,128]{2,1,0:T(8,128)(2,1)S(1)} %shard_map.116), channel_id=1, replica_groups=mesh['dp'=4,'seq'=8] {'seq'}, dimensions={0} | all-to-all | bytes 655360 | tf_op jit(solution)/shard_map/all_to_all | solution.py:544
  61.4 3.4 %collective-permute-start.13 = (bf16[224,128]{1,0:T(8,128)(2,1)S(1)}, bf16[224,128]{1,0:T(8,128)(2,1)S(1)}, u32[]{:S(2)}, u32[]{:S(2)}) collective-permute-start(bf16[224,128]{1,0:T(8,128)(2,1)S(1)} %shard_map.117.rest_0_), channel_id=1, source_target_pairs={{0,24},{8,16},{16,8},{24,0},{1,25},{9,17},{17,9},{25,1},{2,26},{10... | collective-permute-start | bytes 172040 | tf_op jit(solution)/shard_map/ppermute | solution.py:417
  64.8 0.0 collective-permute-start.12
  64.8 1.0 %collective-permute-start.11 = (bf16[224,128]{1,0:T(8,128)(2,1)S(1)}, bf16[224,128]{1,0:T(8,128)(2,1)S(1)}, u32[]{:S(2)}, u32[]{:S(2)}) collective-permute-start(bf16[224,128]{1,0:T(8,128)(2,1)S(1)} %shard_map.117.rest_0_), channel_id=1, source_target_pairs={{0,8},{8,0},{16,24},{24,16},{1,9},{9,1},{17,25},{25,17},{2,10},{10... | collective-permute-start | bytes 172040 | tf_op jit(solution)/shard_map/ppermute | solution.py:417
  65.9 2.2 %collective-permute-done.13.rest_3_ = bf16[224,128]{1,0:T(8,128)(2,1)S(1)} collective-permute-done((bf16[224,128]{1,0:T(8,128)(2,1)S(1)}, bf16[224,128]{1,0:T(8,128)(2,1)S(1)}, u32[]{:S(2)}, u32[]{:S(2)}) %collective-permute-start.13) | collective-permute-done | bytes 57376 | tf_op jit(solution)/shard_map/ppermute | solution.py:417
  68.1 1.9 %collective-permute-done.12.rest_2_ = bf16[224,128]{1,0:T(8,128)(2,1)S(1)} collective-permute-done((bf16[224,128]{1,0:T(8,128)(2,1)S(1)}, bf16[224,128]{1,0:T(8,128)(2,1)S(1)}, u32[]{:S(2)}, u32[]{:S(2)}) %collective-permute-start.12) | collective-permute-done | bytes 57376 | tf_op jit(solution)/shard_map/ppermute | solution.py:417
  70.0 0.0 collective-permute-done.11.rest_1_
  70.0 0.8 %shard_map.118 = (f32[64,320]{1,0:T(8,128)}, f32[64,128]{1,0:T(8,128)}) custom-call(bf16[224,128]{1,0:T(8,128)(2,1)S(1)} %shard_map.117.rest_0_, bf16[224,128]{1,0:T(8,128)(2,1)S(1)} %collective-permute-done.11.rest_1_, bf16[224,128]{1,0:T(8,128)(2,1)S(1)} %collective-permute-done.12.rest_2_, bf16[224,128]{1,0:T(8,128)(2,1)S(1)} %collective-permute-done.13.rest_3_), custom_call_target="tpu_custom_call" | custom-call | bytes 400000 | tf_op jit(solution)/shard_map/pallas_call | solution.py:404
  (10 shorter events, 0.1 us)
Async XLA Ops:
  4.0 7.4 %copy-start.1 = (bf16[1,8,16,1024]{3,2,1,0:T(8,128)(2,1)S(1)}, bf16[1,8,16,1024]{3,2,1,0:T(8,128)(2,1)}, u32[]{:S(2)}) copy-start(bf16[1,8,16,1024]{3,2,1,0:T(8,128)(2,1)} %param.11) | copy-start | bytes 786436
  4.1 7.4 %copy-start.2 = (bf16[1,8,16,1024]{3,2,1,0:T(8,128)(2,1)S(1)}, bf16[1,8,16,1024]{3,2,1,0:T(8,128)(2,1)}, u32[]{:S(2)}) copy-start(bf16[1,8,16,1024]{3,2,1,0:T(8,128)(2,1)} %param.12) | copy-start | bytes 786436
  4.1 7.4 %copy-start.3 = (bf16[1,8,16,1024]{3,2,1,0:T(8,128)(2,1)S(1)}, bf16[1,8,16,1024]{3,2,1,0:T(8,128)(2,1)}, u32[]{:S(2)}) copy-start(bf16[1,8,16,1024]{3,2,1,0:T(8,128)(2,1)} %param.13) | copy-start | bytes 786436
  4.1 7.4 %copy-start.4 = (bf16[8,16,1024]{2,1,0:T(8,128)(2,1)S(1)}, bf16[8,16,1024]{2,1,0:T(8,128)(2,1)}, u32[]{:S(2)}) copy-start(bf16[8,16,1024]{2,1,0:T(8,128)(2,1)} %get-tuple-element.26.queries) | copy-start | bytes 786436
  4.1 7.4 %copy-start.6 = (bf16[8,16,128]{2,1,0:T(8,128)(2,1)S(1)}, bf16[8,16,128]{2,1,0:T(8,128)(2,1)}, u32[]{:S(2)}) copy-start(bf16[8,16,128]{2,1,0:T(8,128)(2,1)} %get-tuple-element.27.adapter) | copy-start | bytes 98308
  4.1 29.7 %all-to-all-start = ((bf16[32,7,16,128]{3,2,1,0:T(8,128)(2,1)}), bf16[32,7,16,128]{3,2,1,0:T(8,128)(2,1)S(1)}, u32[]{:S(2)}, u32[]{:S(2)}) async-start(bf16[32,7,16,128]{3,2,1,0:T(8,128)(2,1)} %get-tuple-element.25), calls=%async_computation | async-start | bytes 1835008 | tf_op jit(solution)/shard_map/all_to_all | solution.py:495
  11.4 0.7 copy-start.7
  12.1 21.7 %copy-start.5 = (bf16[64,1024]{1,0:T(8,128)(2,1)S(1)}, bf16[64,1024]{1,0:T(8,128)(2,1)}, u32[]{:S(2)}) copy-start(bf16[64,1024]{1,0:T(8,128)(2,1)} %up.1) | copy-start | bytes 393220
  13.2 3.8 %collective-permute-start = (bf16[16,16,128]{2,1,0:T(8,128)(2,1)S(1)}, bf16[16,16,128]{2,1,0:T(8,128)(2,1)S(1)}, u32[]{:S(2)}, u32[]{:S(2)}) collective-permute-start(bf16[16,16,128]{2,1,0:T(8,128)(2,1)S(1)} %get-tuple-element.29), channel_id=1, source_target_pairs={{0,1},{1,0},{2,3},{3,2},{4,5},{5,4},{6,7},{7,6},{8,9},{9,8},{10,11... | collective-permute-start | bytes 196616 | tf_op jit(solution)/shard_map/ppermute | solution.py:417
  13.6 7.9 %collective-permute-start.1 = (bf16[16,16,128]{2,1,0:T(8,128)(2,1)S(1)}, bf16[16,16,128]{2,1,0:T(8,128)(2,1)S(1)}, u32[]{:S(2)}, u32[]{:S(2)}) collective-permute-start(bf16[16,16,128]{2,1,0:T(8,128)(2,1)S(1)} %get-tuple-element.30), channel_id=1, source_target_pairs={{0,2},{1,3},{2,0},{3,1},{4,6},{5,7},{6,4},{7,5},{8,10},{9,11},{10,... | collective-permute-start | bytes 196616 | tf_op jit(solution)/shard_map/ppermute | solution.py:417
  15.2 7.9 %collective-permute-start.2 = (bf16[16,16,128]{2,1,0:T(8,128)(2,1)S(1)}, bf16[16,16,128]{2,1,0:T(8,128)(2,1)S(1)}, u32[]{:S(2)}, u32[]{:S(2)}) collective-permute-start(bf16[16,16,128]{2,1,0:T(8,128)(2,1)S(1)} %get-tuple-element.31), channel_id=1, source_target_pairs={{0,3},{1,2},{2,1},{3,0},{4,7},{5,6},{6,5},{7,4},{8,11},{9,10},{10,... | collective-permute-start | bytes 196616 | tf_op jit(solution)/shard_map/ppermute | solution.py:417
  15.2 18.5 %copy-start.8 = (s32[1,1024]{1,0:T(1,128)S(1)}, s32[1,1024]{1,0:T(1,128)}, u32[]{:S(2)}) copy-start(s32[1,1024]{1,0:T(1,128)} %seg.1) | copy-start | bytes 12292
  15.2 7.9 %collective-permute-start.3 = (bf16[16,16,128]{2,1,0:T(8,128)(2,1)S(1)}, bf16[16,16,128]{2,1,0:T(8,128)(2,1)S(1)}, u32[]{:S(2)}, u32[]{:S(2)}) collective-permute-start(bf16[16,16,128]{2,1,0:T(8,128)(2,1)S(1)} %get-tuple-element.32), channel_id=1, source_target_pairs={{0,4},{1,5},{2,6},{3,7},{4,0},{5,1},{6,2},{7,3},{8,12},{9,13},{10,... | collective-permute-start | bytes 196616 | tf_op jit(solution)/shard_map/ppermute | solution.py:417
  16.9 8.5 %collective-permute-start.4 = (bf16[16,16,128]{2,1,0:T(8,128)(2,1)S(1)}, bf16[16,16,128]{2,1,0:T(8,128)(2,1)S(1)}, u32[]{:S(2)}, u32[]{:S(2)}) collective-permute-start(bf16[16,16,128]{2,1,0:T(8,128)(2,1)S(1)} %get-tuple-element.33), channel_id=1, source_target_pairs={{0,5},{1,4},{2,7},{3,6},{4,1},{5,0},{6,3},{7,2},{8,13},{9,12},{10,... | collective-permute-start | bytes 196616 | tf_op jit(solution)/shard_map/ppermute | solution.py:417
  17.1 10.0 %collective-permute-start.5 = (bf16[16,16,128]{2,1,0:T(8,128)(2,1)S(1)}, bf16[16,16,128]{2,1,0:T(8,128)(2,1)S(1)}, u32[]{:S(2)}, u32[]{:S(2)}) collective-permute-start(bf16[16,16,128]{2,1,0:T(8,128)(2,1)S(1)} %get-tuple-element.34), channel_id=1, source_target_pairs={{0,6},{1,7},{2,4},{3,5},{4,2},{5,3},{6,0},{7,1},{8,14},{9,15},{10,... | collective-permute-start | bytes 196616 | tf_op jit(solution)/shard_map/ppermute | solution.py:417
  21.5 6.2 %collective-permute-start.6 = (bf16[16,16,128]{2,1,0:T(8,128)(2,1)S(1)}, bf16[16,16,128]{2,1,0:T(8,128)(2,1)S(1)}, u32[]{:S(2)}, u32[]{:S(2)}) collective-permute-start(bf16[16,16,128]{2,1,0:T(8,128)(2,1)S(1)} %get-tuple-element.35), channel_id=1, source_target_pairs={{0,7},{1,6},{2,5},{3,4},{4,3},{5,2},{6,1},{7,0},{8,15},{9,14},{10,... | collective-permute-start | bytes 196616 | tf_op jit(solution)/shard_map/ppermute | solution.py:417
  33.8 16.1 %copy-start = (bf16[1,8,16,2560]{3,2,1,0:T(8,128)(2,1)S(1)}, bf16[1,8,16,2560]{3,2,1,0:T(8,128)(2,1)}, u32[]{:S(2)}) copy-start(bf16[1,8,16,2560]{3,2,1,0:T(8,128)(2,1)} %param.9) | copy-start | bytes 1966084
  37.1 12.8 %all-to-all-start.1 = ((bf16[32,16,128]{2,1,0:T(8,128)(2,1)}), bf16[32,16,128]{2,1,0:T(8,128)(2,1)S(1)}, u32[]{:S(2)}, u32[]{:S(2)}) async-start(bf16[32,16,128]{2,1,0:T(8,128)(2,1)} %get-tuple-element.36), calls=%async_computation.1 | async-start | bytes 262144 | tf_op jit(solution)/shard_map/all_to_all | solution.py:526
  41.5 4.7 %collective-permute-start.7 = (bf16[2,2,16,128]{3,2,1,0:T(8,128)(2,1)S(1)}, bf16[2,2,16,128]{3,2,1,0:T(8,128)(2,1)S(1)}, u32[]{:S(2)}, u32[]{:S(2)}) collective-permute-start(bf16[2,2,16,128]{3,2,1,0:T(8,128)(2,1)S(1)} %get-tuple-element.37), channel_id=1, source_target_pairs={{0,6},{1,7},{2,4},{3,5},{4,2},{5,3},{6,0},{7,1},{8,14},{9,15},{10,... | collective-permute-start | bytes 49160 | tf_op jit(solution)/shard_map/ppermute | solution.py:417
  44.2 3.8 %collective-permute-start.8 = (bf16[2,2,16,128]{3,2,1,0:T(8,128)(2,1)S(1)}, bf16[2,2,16,128]{3,2,1,0:T(8,128)(2,1)S(1)}, u32[]{:S(2)}, u32[]{:S(2)}) collective-permute-start(bf16[2,2,16,128]{3,2,1,0:T(8,128)(2,1)S(1)} %get-tuple-element.38), channel_id=1, source_target_pairs={{0,4},{1,5},{2,6},{3,7},{4,0},{5,1},{6,2},{7,3},{8,12},{9,13},{10,... | collective-permute-start | bytes 49160 | tf_op jit(solution)/shard_map/ppermute | solution.py:417
  44.8 3.7 %collective-permute-start.9 = (bf16[2,2,16,128]{3,2,1,0:T(8,128)(2,1)S(1)}, bf16[2,2,16,128]{3,2,1,0:T(8,128)(2,1)S(1)}, u32[]{:S(2)}, u32[]{:S(2)}) collective-permute-start(bf16[2,2,16,128]{3,2,1,0:T(8,128)(2,1)S(1)} %get-tuple-element.39), channel_id=1, source_target_pairs={{0,2},{1,3},{2,0},{3,1},{4,6},{5,7},{6,4},{7,5},{8,10},{9,11},{10,... | collective-permute-start | bytes 49160 | tf_op jit(solution)/shard_map/ppermute | solution.py:417
  48.5 1.2 %collective-permute-start.10 = (bf16[2,16,128]{2,1,0:T(8,128)(2,1)S(1)}, bf16[2,16,128]{2,1,0:T(8,128)(2,1)S(1)}, u32[]{:S(2)}, u32[]{:S(2)}) collective-permute-start(bf16[2,16,128]{2,1,0:T(8,128)(2,1)S(1)} %get-tuple-element.42), channel_id=1, source_target_pairs={{0,1},{1,0},{2,3},{3,2},{4,5},{5,4},{6,7},{7,6},{8,9},{9,8},{10,11... | collective-permute-start | bytes 24584 | tf_op jit(solution)/shard_map/ppermute | solution.py:417
  61.4 6.7 %collective-permute-start.13 = (bf16[224,128]{1,0:T(8,128)(2,1)S(1)}, bf16[224,128]{1,0:T(8,128)(2,1)S(1)}, u32[]{:S(2)}, u32[]{:S(2)}) collective-permute-start(bf16[224,128]{1,0:T(8,128)(2,1)S(1)} %shard_map.117.rest_0_), channel_id=1, source_target_pairs={{0,24},{8,16},{16,8},{24,0},{1,25},{9,17},{17,9},{25,1},{2,26},{10... | collective-permute-start | bytes 172040 | tf_op jit(solution)/shard_map/ppermute | solution.py:417
  64.8 5.1 %collective-permute-start.12 = (bf16[224,128]{1,0:T(8,128)(2,1)S(1)}, bf16[224,128]{1,0:T(8,128)(2,1)S(1)}, u32[]{:S(2)}, u32[]{:S(2)}) collective-permute-start(bf16[224,128]{1,0:T(8,128)(2,1)S(1)} %shard_map.117.rest_0_), channel_id=1, source_target_pairs={{0,16},{8,24},{16,0},{24,8},{1,17},{9,25},{17,1},{25,9},{2,18},{10... | collective-permute-start | bytes 172040 | tf_op jit(solution)/shard_map/ppermute | solution.py:417
  64.8 5.1 %collective-permute-start.11 = (bf16[224,128]{1,0:T(8,128)(2,1)S(1)}, bf16[224,128]{1,0:T(8,128)(2,1)S(1)}, u32[]{:S(2)}, u32[]{:S(2)}) collective-permute-start(bf16[224,128]{1,0:T(8,128)(2,1)S(1)} %shard_map.117.rest_0_), channel_id=1, source_target_pairs={{0,8},{8,0},{16,24},{24,16},{1,9},{9,1},{17,25},{25,17},{2,10},{10... | collective-permute-start | bytes 172040 | tf_op jit(solution)/shard_map/ppermute | solution.py:417

commit v4 on v3

--- a/solution.py
+++ b/solution.py
@@ -3,9 +3,11 @@
 
 import jax
 import jax.numpy as jnp
+import numpy as np
 from jax import lax
 from jax.experimental import pallas as pl
 from jax.experimental.pallas import tpu as pltpu
+from jax.sharding import Mesh
 from jax.sharding import PartitionSpec as P
 
 CAP = 2
@@ -13,6 +15,7 @@
 LANES = 128
 HALF = 64
 CORES = 2
+SEQ = ("chip", "core")
 QUERIES = 640
 LOG2E = math.log2(math.e)
 VMEM = pl.BlockSpec(memory_space=pltpu.VMEM)
@@ -43,6 +46,10 @@
 
 def remainder(value, size):
     return value & (size - 1)
+
+
+def seq_index():
+    return lax.axis_index("chip") * CORES + lax.axis_index("core")
 
 
 def each_hit(plan, me, groups, blocks, live, put):
@@ -94,7 +101,7 @@
 def pack_far_kernel(dims, plan_hbm, feat_hbm, base_hbm, keys_hbm, vals_hbm, down_hbm, up_hbm, *rest):
     groups, blocks, heads, rows, live = dims
     far_hbm, queries_hbm, adapter_hbm = rest[:3]
-    plan, feat, base, keys, vals, down, up, far_out, qbuf, abuf, sems, out_sems = rest[3:]
+    plan, routes, feat, base, keys, vals, down, up, far_out, qbuf, abuf, sems, out_sems = rest[3:]
     me = lax.axis_index("dp")
     copies = [
         pltpu.make_async_copy(source, target, sems.at[index])
@@ -116,6 +123,10 @@
     def put_early(dest, slot, local):
         @pl.when(slot < CAP)
         def _():
+            index = routes[0, 0]
+            routes[0, 0] = index + 1
+            for row, value in enumerate((dest, slot, local)):
+                routes[row + 1, index] = value
             for head in range(heads):
                 columns = slice(head * LANES, (head + 1) * LANES)
                 far_out[head * groups + dest, slot] = keys[local, :, columns]
@@ -129,6 +140,7 @@
 
     for copy in copies[:3]:
         copy.wait()
+    routes[0, 0] = 0
     each_hit(plan, me, groups, blocks, live, put_early)
     early = send(0, 2 * CAP, 0)
     for copy in copies[3:]:
@@ -139,18 +151,19 @@
     abuf[...] = jnp.concatenate([narrow, narrow], axis=1).astype(jnp.bfloat16).reshape(abuf.shape)
     qbuf[...] = (base[...].astype(jnp.float32) + lift.reshape(base.shape)).astype(jnp.bfloat16)
 
-    def put_late(dest, slot, local):
+    def put_late(index, _):
+        dest, slot, local = routes[1, index], routes[2, index], routes[3, index]
+
         def store(lanes):
             for head in range(heads):
                 columns = slice(head * LANES, (head + 1) * LANES)
                 far_out[head * groups + dest, 2 * CAP + slot] = qbuf[local, :, columns]
                 far_out[head * groups + dest, CAP * 3, :, lanes] = abuf[local, :, lanes]
 
-        @pl.when(slot < CAP)
-        def _():
-            each_half(slot, store)
-
-    each_hit(plan, me, groups, blocks, live, put_late)
+        each_half(slot, store)
+        return 0
+
+    lax.fori_loop(0, routes[0, 0], put_late, 0)
     late = send(2 * CAP, CAP + 1, 1)
     rest_out = [
         pltpu.make_async_copy(qbuf, queries_hbm, out_sems.at[2]),
@@ -166,7 +179,7 @@
     groups, blocks, heads, rows, live = dims
     extras = live - CAP
     me = lax.axis_index("dp")
-    seq = lax.axis_index("seq")
+    seq = seq_index()
     sources = (keys, vals, queries)
 
     def put(dest, slot, local):
@@ -195,12 +208,14 @@
 def attend_kernel(dims, plan, seg, up, far_in, *rest):
     groups, blocks, heads, rows, live = dims
     own_ins = rest[:heads]
-    part_out = rest[heads]
+    part_hbm = rest[heads]
     own_parts = rest[heads + 1 : heads + 1 + heads // CORES]
-    up_out, log_out, qs, ks, vs, gs, ads, dqs, parts = rest[heads + 1 + heads // CORES :]
+    up_out, log_hbm, part_out, log_out, routes, sems, qs, ks, vs, gs, ads, dqs, parts = rest[
+        heads + 1 + heads // CORES :
+    ]
     extras = live - CAP
     me = lax.axis_index("dp")
-    seq = lax.axis_index("seq")
+    seq = seq_index()
     rank = up.shape[0]
     length = seg.shape[1]
     reach = live * LANES
@@ -209,6 +224,8 @@
     ads[...] = jnp.zeros_like(ads)
 
     def take(position, group, slot):
+        routes[0, position] = group
+        routes[1, position] = slot
         far = (group != me) | (slot < CAP)
 
         @pl.when(far)
@@ -285,12 +302,15 @@
         dqs[:, span] = dquery
         log_out[0, :, span] = jnp.where(in_clip, maximum * scaling + jnp.log(total), 0.0)
     log_out[0, :, reach:] = jnp.zeros((1, length - reach), jnp.float32)
+    log_copy = pltpu.make_async_copy(log_out, log_hbm, sems.at[0])
+    log_copy.start()
     dquery_all = dqs[...]
     parts[...] = lax.dot_general(
         dquery_all, up_twice, (((0,), (1,)), ((), ())), preferred_element_type=jnp.float32
     ).astype(jnp.bfloat16)
 
-    def put(position, group, slot):
+    def put(position, _):
+        group, slot = routes[0, position], routes[1, position]
         far = (group != me) | (slot < CAP)
 
         @pl.when(far)
@@ -313,9 +333,15 @@
 
             each_half(slot, store)
 
-    each_block(plan, me, blocks, live, put)
+        return 0
+
+    lax.fori_loop(0, live, put, 0)
+    part_copy = pltpu.make_async_copy(part_out, part_hbm, sems.at[1])
+    part_copy.start()
     up_part = jnp.dot(dquery_all, ads[...], preferred_element_type=jnp.float32)
     up_out[...] = (up_part + swap_halves(up_part)).T[:rank].astype(jnp.bfloat16)
+    log_copy.wait()
+    part_copy.wait()
 
 
 def chip_sum_kernel(*refs):
@@ -327,7 +353,7 @@
         outs[core][...] = total.astype(jnp.bfloat16)
 
 
-def product_kernel(dims, plan, parts, feat, own_mine, own_other, out, sums, grads):
+def product_kernel(dims, plan, parts, feat, own_mine, own_other, keep, send, sums, grads):
     groups, blocks, heads, rows, live = dims
     me = lax.axis_index("dp")
     for group in range(groups):
@@ -349,23 +375,36 @@
     low = low_lanes(HALF // 2)
     columns = grads[...].reshape(blocks * rows, LANES).astype(jnp.float32).T[:HALF]
     columns = columns.astype(jnp.bfloat16)
-    for pair in range(heads // 2):
+    even = lax.axis_index("core") == 0
+    for chip in range(heads // CORES):
         tiles = jnp.dot(
             columns,
-            feat[:, pair * 5 * LANES : (pair + 1) * 5 * LANES],
+            feat[:, chip * 5 * LANES : (chip + 1) * 5 * LANES],
             preferred_element_type=jnp.float32,
         )
         shared = tiles[:, 2 * LANES : 3 * LANES]
         upper, lower = shared[: HALF // 2], shared[HALF // 2 :]
-        for part in range(2):
-            ahead = tiles[:, part * 3 * LANES : (part * 3 + 2) * LANES].astype(jnp.bfloat16)
-            out[pair * 2 + part, :HALF] = ahead[:, :LANES]
-            out[pair * 2 + part, HALF : 2 * HALF] = ahead[:, LANES:]
-            if part == 0:
-                rest = jnp.where(low, upper, swap_halves(lower))
-            else:
-                rest = jnp.where(low, swap_halves(upper), lower)
-            out[pair * 2 + part, 2 * HALF :] = rest.astype(jnp.bfloat16)
+        first = jnp.concatenate(
+            [tiles[:, :LANES], tiles[:, LANES : 2 * LANES], jnp.where(low, upper, swap_halves(lower))],
+            axis=0,
+        )
+        second = jnp.concatenate(
+            [
+                tiles[:, 3 * LANES : 4 * LANES],
+                tiles[:, 4 * LANES :],
+                jnp.where(low, swap_halves(upper), lower),
+            ],
+            axis=0,
+        )
+        keep[chip] = jnp.where(even, first, second).astype(jnp.bfloat16)
+        send[chip] = jnp.where(even, second, first).astype(jnp.bfloat16)
+
+
+def add_kernel(kept, received, out):
+    for index in range(out.shape[0]):
+        out[index] = (
+            kept[index].astype(jnp.float32) + received[index].astype(jnp.float32)
+        ).astype(jnp.bfloat16)
 
 
 def join_kernel(parts, up_part, out):
@@ -380,7 +419,7 @@
     groups = len(rest) - 3
     down_out, up_out, held = rest[groups:]
     me = lax.axis_index("dp")
-    seq = lax.axis_index("seq")
+    seq = seq_index()
     for turn in range(groups):
         held[me ^ turn] = rest[turn][...].astype(jnp.float32)
     total = held[0]
@@ -412,9 +451,8 @@
     )(*args)
 
 
-def exchange(value, axis, turn):
-    peers = lax.axis_size(axis)
-    return lax.ppermute(value, axis, [(peer, peer ^ turn) for peer in range(peers)])
+def exchange(value, axis, size, turn):
+    return lax.ppermute(value, axis, [(peer, peer ^ turn) for peer in range(size)])
 
 
 def per_device_tiles(
@@ -429,7 +467,8 @@
     segments,
 ):
     groups = lax.axis_size("dp")
-    heads = lax.axis_size("seq")
+    chips = lax.axis_size("chip")
+    heads = chips * CORES
     _, blocks, rows, width = features.shape
     length = segments.shape[1]
     live = (length // 2 + length // 8) // LANES
@@ -441,7 +480,7 @@
     bf16 = jnp.bfloat16
     f32 = jnp.float32
     peers = groups * heads
-    everyone = ("seq", "dp")
+    everyone = SEQ + ("dp",)
     flat = features[0].reshape(blocks * rows, width)
     far_shape = (peers, CAP * 3 + 1, rows, LANES)
     own_shape = (extras * 3 + live + pairs, rows, LANES)
@@ -453,6 +492,7 @@
         [ANY] * 7,
         [
             pltpu.SMEM((groups, blocks), jnp.int32),
+            pltpu.SMEM((4, blocks), jnp.int32),
             pltpu.VMEM((blocks * rows, width), bf16),
             pltpu.VMEM(rows_shape, bf16),
             pltpu.VMEM(rows_shape, bf16),
@@ -491,7 +531,7 @@
         queries,
         adapter,
     )
-    own = [own_send[0]] + [exchange(own_send[turn], "seq", turn) for turn in range(1, heads)]
+    own = [own_send[0]] + [exchange(own_send[turn], SEQ, heads, turn) for turn in range(1, heads)]
     far = lax.all_to_all(far_send, everyone, 0, 0, tiled=True)
     attended = call(
         functools.partial(attend_kernel, dims),
@@ -499,7 +539,13 @@
         + [((CORES, pairs, rows, LANES), bf16)] * (heads // CORES)
         + [((rank, LANES), bf16), ((1, 1, length), f32)],
         [SMEM] + [VMEM] * (3 + heads),
-        [pltpu.VMEM((reach, LANES), bf16)] * 5
+        [
+            pltpu.VMEM((peers, rows, LANES), bf16),
+            pltpu.VMEM((1, 1, length), f32),
+            pltpu.SMEM((2, live), jnp.int32),
+            pltpu.SemaphoreType.DMA((2,)),
+        ]
+        + [pltpu.VMEM((reach, LANES), bf16)] * 5
         + [pltpu.VMEM((LANES, reach), bf16), pltpu.VMEM((reach, LANES), bf16)],
         600_000_000,
         3_000_000,
@@ -508,9 +554,10 @@
         adapter_up_weight,
         far,
         *own,
+        out_specs=[ANY] + [VMEM] * (chips + 1) + [ANY],
     )
     own_parts = [
-        exchange(attended[1 + chip], "seq", chip * CORES) for chip in range(heads // CORES - 1, 0, -1)
+        exchange(attended[1 + turn], "chip", chips, turn) for turn in range(chips - 1, 0, -1)
     ]
     own_mine, own_other = call(
         chip_sum_kernel,
@@ -522,12 +569,12 @@
         *own_parts,
         attended[1],
     )
-    own_other = exchange(own_other, "seq", 1)
+    own_other = exchange(own_other, "core", CORES, 1)
     part = lax.all_to_all(attended[0], everyone, 0, 0, tiled=True)
     up_part, log_norm = attended[1 + heads // CORES :]
-    (shares,) = call(
+    keep, send = call(
         functools.partial(product_kernel, dims),
-        [((heads, HALF * 5 // 2, LANES), bf16)],
+        [((chips, HALF * 5 // 2, LANES), bf16)] * 2,
         [SMEM] + [VMEM] * 4,
         [
             pltpu.VMEM((groups + pairs, rows, LANES), f32),
@@ -541,7 +588,17 @@
         own_mine,
         own_other,
     )
-    shares = lax.all_to_all(shares, "seq", 0, 0, tiled=True)
+    (shares,) = call(
+        add_kernel,
+        [((chips, HALF * 5 // 2, LANES), bf16)],
+        [VMEM] * 2,
+        [],
+        0,
+        600_000,
+        keep,
+        exchange(send, "core", CORES, 1),
+    )
+    shares = lax.all_to_all(shares, "chip", 0, 0, tiled=True)
     (joined,) = call(
         join_kernel,
         [((HALF * 5 // 2 + rank, LANES), bf16)],
@@ -552,7 +609,7 @@
         shares,
         up_part,
     )
-    sums = [joined] + [exchange(joined, "dp", turn) for turn in range(1, groups)]
+    sums = [joined] + [exchange(joined, "dp", groups, turn) for turn in range(1, groups)]
     down, up = call(
         functools.partial(total_kernel, 4.0 / math.sqrt(groups * length)),
         [((rank, width // heads), f32), ((rank, LANES), f32)],
@@ -580,6 +637,23 @@
         and power_of_two(groups)
         and power_of_two(features.shape[1])
         and adapter_up_weight.shape == (HALF, heads * LANES)
+    )
+
+
+def split_mesh(mesh):
+    groups, heads = mesh.shape["dp"], mesh.shape["seq"]
+    devices = np.asarray(mesh.devices).reshape(groups, heads // CORES, CORES)
+    return Mesh(devices, ("dp",) + SEQ)
+
+
+def tiles_solution(mesh):
+    row_spec = P("dp", None, SEQ, None)
+    return jax.shard_map(
+        per_device_tiles,
+        mesh=split_mesh(mesh),
+        in_specs=(row_spec,) * 5 + (P(), P(), P(), P("dp", None)),
+        out_specs=(P(SEQ, None), P(None, SEQ), P("dp", SEQ, None)),
+        check_vma=False,
     )
 
 
@@ -821,14 +895,12 @@
     )
     out_specs = (P("seq", None), P(None, "seq"), P("dp", "seq", None))
 
+    plain = jax.shard_map(
+        per_device, mesh=mesh, in_specs=in_specs, out_specs=out_specs, check_vma=False
+    )
+
     def whole(features, *rest):
         fits = fits_tiles(mesh, features, rest[5])
-        return jax.shard_map(
-            per_device_tiles if fits else per_device,
-            mesh=mesh,
-            in_specs=in_specs,
-            out_specs=out_specs,
-            check_vma=False,
-        )(features, *rest)
+        return (tiles_solution(mesh) if fits else plain)(features, *rest)
 
     return whole

time: 71.2 us -> 70 us (0.983)
  blocking collectives: 10.1 us -> 7.89 us
  waiting for transfers between devices: 22.6 us -> 23.9 us
    all_to_all x1, blocking collectives: 10.1 us -> 7.89 us  [per_device_tiles(): shares = lax.all_to_all(shares, 'chip', 0, 0, tiled=True)]
    ppermute x14 -> x15, waiting for transfers between devices: 16.4 us -> 17.7 us  [exchange(): lax.ppermute(value, axis, [(peer, peer ^ turn) for peer in range(size)])]
    pallas_call x7 -> x8, Pallas kernels: 10.1 us -> 9.78 us  [call(): pl.pallas_call(kernel, out_shape=shapes, in_specs=specs, out_specs=out_sp...]
    ppermute x14 -> x15, starting transfers between devices: 14.8 us -> 15 us  [exchange(): lax.ppermute(value, axis, [(peer, peer ^ turn) for peer in range(size)])]
  transfers between devices with their start and end apart: 16 -> 17, of which waited for: 13 -> 14; matrix products, arithmetic and copies ran while one was open for 0% -> 0% of each run, Pallas kernels for 2% -> 2%
where the time goes in v4:
time: 70 us; the launch traced here: 69.6 us
  starting transfers between devices  26.6 us (38%)
  waiting for transfers between devices  23.9 us (34%)
  Pallas kernels  9.78 us (14%)
  blocking collectives  7.89 us (11%)
  between operations  0.79 us (1%)
    ppermute x15, waiting for transfers between devices, exchange(): lax.ppermute(value, axis, [(peer, peer ^ turn) for peer in range(size)])  17.7 us
    ppermute x15, starting transfers between devices, exchange(): lax.ppermute(value, axis, [(peer, peer ^ turn) for peer in range(size)])  15 us
    pallas_call x8, Pallas kernels, call(): pl.pallas_call(kernel, out_shape=shapes, in_specs=specs, out_specs=out_sp...  9.78 us
    all_to_all x1, blocking collectives, per_device_tiles(): shares = lax.all_to_all(shares, 'chip', 0, 0, tiled=True)  7.89 us
    all_to_all x1, starting transfers between devices, per_device_tiles(): far = lax.all_to_all(far_send, everyone, 0, 0, tiled=True)  7.24 us
    all_to_all x1, waiting for transfers between devices, per_device_tiles(): far = lax.all_to_all(far_send, everyone, 0, 0, tiled=True)  6.06 us
    all_to_all x1, starting transfers between devices, per_device_tiles(): part = lax.all_to_all(attended[0], everyone, 0, 0, tiled=True)  4.41 us
  transfers between devices with their start and end apart: 17, of which 14 were waited for; matrix products, arithmetic and copies ran while one was open for 0% of the time, Pallas kernels for 2%

profile of v4, /device:TPU:0, one launch (start us, length us, event | category | flops | bytes accessed | tf_op | source)
XLA Modules:
  0.0 69.6 jit_solution(14717898890020449821)
XLA Ops:
  0.6 3.1 %shard_map.112 = (bf16[32,7,16,128]{3,2,1,0:T(8,128)(2,1)}, bf16[8,16,1024]{2,1,0:T(8,128)(2,1)}, bf16[8,16,128]{2,1,0:T(8,128)(2,1)}) custom-call(s32[4,8]{1,0:T(4,128)} %plan.5, bf16[128,2560]{1,0:T(8,128)(2,1)} %bitcast.7, bf16[8,16,1024]{2,1,0:T(8,128)(2,1)} %bitcast.15, bf16[8,16,1024]{2,1,0:T(8,128)(2,1)} %bitcast.9, bf16[8,16,1024]{2,1,0:T(8,128)(2,1)} %bitcast.11, ...), custom_call_target="tpu_custom_call" | custom-call | flops 60000000 | bytes 4000000 | tf_op jit(solution)/shard_map/pallas_call | solution.py:443
  3.8 0.0 copy-start.1
  3.8 0.0 copy-start.2
  3.8 0.0 copy-start.3
  3.8 0.0 copy-start.4
  3.8 0.0 copy-start.6
  3.8 7.2 %all-to-all-start = ((bf16[32,7,16,128]{3,2,1,0:T(8,128)(2,1)}), bf16[32,7,16,128]{3,2,1,0:T(8,128)(2,1)S(1)}, u32[]{:S(2)}, u32[]{:S(2)}) async-start(bf16[32,7,16,128]{3,2,1,0:T(8,128)(2,1)} %get-tuple-element.27), calls=%async_computation | async-start | bytes 1835008 | tf_op jit(solution)/shard_map/all_to_all | solution.py:535
  11.1 0.0 copy-start.7
  11.1 0.6 copy-done.7
  11.8 1.1 %shard_map.113 = (bf16[16,16,128]{2,1,0:T(8,128)(2,1)S(1)}, bf16[16,16,128]{2,1,0:T(8,128)(2,1)S(1)}, bf16[16,16,128]{2,1,0:T(8,128)(2,1)S(1)}, bf16[16,16,128]{...) custom-call(s32[4,8]{1,0:T(4,128)S(1)} %copy-done.7, ...), custom_call_target="tpu_custom_call" | custom-call | bytes 1600000 | tf_op jit(solution)/shard_map/pallas_call | solution.py:443
  12.9 0.3 collective-permute-start
  13.2 1.7 %collective-permute-start.1 = (bf16[16,16,128]{2,1,0:T(8,128)(2,1)S(1)}, bf16[16,16,128]{2,1,0:T(8,128)(2,1)S(1)}, u32[]{:S(2)}, u32[]{:S(2)}) collective-permute-start(bf16[16,16,128]{2,1,0:T(8,128)(2,1)S(1)} %get-tuple-element.32), channel_id=1, source_target_pairs={{0,2},{1,3},{2,0},{3,1},{4,6},{5,7},{6,4},{7,5},{8,10},{9,11},{10,... | collective-permute-start | bytes 196616 | tf_op jit(solution)/shard_map/ppermute | solution.py:455
  14.9 0.0 collective-permute-start.2
  14.9 1.7 %collective-permute-start.3 = (bf16[16,16,128]{2,1,0:T(8,128)(2,1)S(1)}, bf16[16,16,128]{2,1,0:T(8,128)(2,1)S(1)}, u32[]{:S(2)}, u32[]{:S(2)}) collective-permute-start(bf16[16,16,128]{2,1,0:T(8,128)(2,1)S(1)} %get-tuple-element.34), channel_id=1, source_target_pairs={{0,4},{1,5},{2,6},{3,7},{4,0},{5,1},{6,2},{7,3},{8,12},{9,13},{10,... | collective-permute-start | bytes 196616 | tf_op jit(solution)/shard_map/ppermute | solution.py:455
  16.6 0.1 collective-permute-start.4
  16.7 0.0 collective-permute-done.rest_1_
  16.7 2.6 %collective-permute-start.5 = (bf16[16,16,128]{2,1,0:T(8,128)(2,1)S(1)}, bf16[16,16,128]{2,1,0:T(8,128)(2,1)S(1)}, u32[]{:S(2)}, u32[]{:S(2)}) collective-permute-start(bf16[16,16,128]{2,1,0:T(8,128)(2,1)S(1)} %get-tuple-element.36), channel_id=1, source_target_pairs={{0,6},{1,7},{2,4},{3,5},{4,2},{5,3},{6,0},{7,1},{8,14},{9,15},{10,... | collective-permute-start | bytes 196616 | tf_op jit(solution)/shard_map/ppermute | solution.py:455
  19.3 1.8 %collective-permute-done.1.rest_2_ = bf16[16,16,128]{2,1,0:T(8,128)(2,1)S(1)} collective-permute-done((bf16[16,16,128]{2,1,0:T(8,128)(2,1)S(1)}, bf16[16,16,128]{2,1,0:T(8,128)(2,1)S(1)}, u32[]{:S(2)}, u32[]{:S(2)}) %collective-permute-start.1) | collective-permute-done | bytes 65568 | tf_op jit(solution)/shard_map/ppermute | solution.py:455
  21.1 0.4 collective-permute-start.6
  21.5 1.3 %collective-permute-done.2.rest_3_ = bf16[16,16,128]{2,1,0:T(8,128)(2,1)S(1)} collective-permute-done((bf16[16,16,128]{2,1,0:T(8,128)(2,1)S(1)}, bf16[16,16,128]{2,1,0:T(8,128)(2,1)S(1)}, u32[]{:S(2)}, u32[]{:S(2)}) %collective-permute-start.2) | collective-permute-done | bytes 65568 | tf_op jit(solution)/shard_map/ppermute | solution.py:455
  22.8 0.0 collective-permute-done.3.rest_4_
  22.8 2.3 %collective-permute-done.4.rest_5_ = bf16[16,16,128]{2,1,0:T(8,128)(2,1)S(1)} collective-permute-done((bf16[16,16,128]{2,1,0:T(8,128)(2,1)S(1)}, bf16[16,16,128]{2,1,0:T(8,128)(2,1)S(1)}, u32[]{:S(2)}, u32[]{:S(2)}) %collective-permute-start.4) | collective-permute-done | bytes 65568 | tf_op jit(solution)/shard_map/ppermute | solution.py:455
  25.1 1.5 %collective-permute-done.5.rest_6_ = bf16[16,16,128]{2,1,0:T(8,128)(2,1)S(1)} collective-permute-done((bf16[16,16,128]{2,1,0:T(8,128)(2,1)S(1)}, bf16[16,16,128]{2,1,0:T(8,128)(2,1)S(1)}, u32[]{:S(2)}, u32[]{:S(2)}) %collective-permute-start.5) | collective-permute-done | bytes 65568 | tf_op jit(solution)/shard_map/ppermute | solution.py:455
  26.7 0.7 collective-permute-done.6.rest_7_
  27.4 6.1 %all-to-all-done.far_in = bf16[32,7,16,128]{3,2,1,0:T(8,128)(2,1)S(1)} async-done(((bf16[32,7,16,128]{3,2,1,0:T(8,128)(2,1)}), bf16[32,7,16,128]{3,2,1,0:T(8,128)(2,1)S(1)}, u32[]{:S(2)}, u32[]{:S(2)}) %all-to-all-start) | async-done | bytes 917536 | tf_op jit(solution)/shard_map/all_to_all | solution.py:535
  33.4 0.0 copy-done.8
  33.4 3.3 %shard_map.114 = (bf16[32,16,128]{2,1,0:T(8,128)(2,1)}, bf16[2,2,16,128]{3,2,1,0:T(8,128)(2,1)S(1)}, bf16[2,2,16,128]{3,2,1,0:T(8,128)(2,1)S(1)}, bf16[2,2,16,12...) custom-call(s32[4,8]{1,0:T(4,128)S(1)} %copy-done.7, ...), custom_call_target="tpu_custom_call" | custom-call | flops 600000000 | bytes 3000000 | tf_op jit(solution)/shard_map/pallas_call | solution.py:443
  36.7 4.4 %all-to-all-start.1 = ((bf16[32,16,128]{2,1,0:T(8,128)(2,1)}), bf16[32,16,128]{2,1,0:T(8,128)(2,1)S(1)}, u32[]{:S(2)}, u32[]{:S(2)}) async-start(bf16[32,16,128]{2,1,0:T(8,128)(2,1)} %get-tuple-element.38), calls=%async_computation.1 | async-start | bytes 262144 | tf_op jit(solution)/shard_map/all_to_all | solution.py:573
  41.1 2.7 %collective-permute-start.7 = (bf16[2,2,16,128]{3,2,1,0:T(8,128)(2,1)S(1)}, bf16[2,2,16,128]{3,2,1,0:T(8,128)(2,1)S(1)}, u32[]{:S(2)}, u32[]{:S(2)}) collective-permute-start(bf16[2,2,16,128]{3,2,1,0:T(8,128)(2,1)S(1)} %get-tuple-element.39), channel_id=1, source_target_pairs={{0,6},{2,4},{4,2},{6,0},{1,7},{3,5},{5,3},{7,1},{8,14},{10,12},{12... | collective-permute-start | bytes 49160 | tf_op jit(solution)/shard_map/ppermute | solution.py:455
  43.8 0.6 collective-permute-start.8
  44.4 0.3 collective-permute-start.9
  44.7 1.1 %collective-permute-done.7.refs_0_ = bf16[2,2,16,128]{3,2,1,0:T(8,128)(2,1)S(1)} collective-permute-done((bf16[2,2,16,128]{3,2,1,0:T(8,128)(2,1)S(1)}, bf16[2,2,16,128]{3,2,1,0:T(8,128)(2,1)S(1)}, u32[]{:S(2)}, u32[]{:S(2)}) %collective-permute-start.7) | collective-permute-done | bytes 16416 | tf_op jit(solution)/shard_map/ppermute | solution.py:455
  45.8 1.8 %collective-permute-done.8.refs_1_ = bf16[2,2,16,128]{3,2,1,0:T(8,128)(2,1)S(1)} collective-permute-done((bf16[2,2,16,128]{3,2,1,0:T(8,128)(2,1)S(1)}, bf16[2,2,16,128]{3,2,1,0:T(8,128)(2,1)S(1)}, u32[]{:S(2)}, u32[]{:S(2)}) %collective-permute-start.8) | collective-permute-done | bytes 16416 | tf_op jit(solution)/shard_map/ppermute | solution.py:455
  47.6 0.5 collective-permute-done.9.refs_2_
  48.2 0.1 collective-permute-start.10
  48.2 1.2 %collective-permute-done.10.own_other = bf16[2,16,128]{2,1,0:T(8,128)(2,1)S(1)} collective-permute-done((bf16[2,16,128]{2,1,0:T(8,128)(2,1)S(1)}, bf16[2,16,128]{2,1,0:T(8,128)(2,1)S(1)}, u32[]{:S(2)}, u32[]{:S(2)}) %collective-permute-start.10) | collective-permute-done | bytes 8224 | tf_op jit(solution)/shard_map/ppermute | solution.py:455
  49.4 0.1 all-to-all-done.1.parts
  49.5 1.4 %shard_map.116 = (bf16[4,160,128]{2,1,0:T(8,128)(2,1)S(1)}, bf16[4,160,128]{2,1,0:T(8,128)(2,1)S(1)}) custom-call(s32[4,8]{1,0:T(4,128)S(1)} %copy-done.7, bf16[32,16,128]{2,1,0:T(8,128)(2,1)S(1)} %all-to-all-done.1.parts, bf16[128,2560]{1,0:T(8,128)(2,1)S(1)} %bitcast.8, bf16[2,16,128]{2,1,0:T(8,128)(2,1)S(1)} %get-tuple-element.43.own_mine, ...), custom_call_target="tpu_custom_call" | custom-call | flops 40000000 | bytes 2000000 | tf_op jit(solution)/shard_map/pallas_call | solution.py:443
  50.9 0.1 collective-permute-start.11
  51.0 1.3 %collective-permute-done.11.received = bf16[4,160,128]{2,1,0:T(8,128)(2,1)S(1)} collective-permute-done((bf16[4,160,128]{2,1,0:T(8,128)(2,1)S(1)}, bf16[4,160,128]{2,1,0:T(8,128)(2,1)S(1)}, u32[]{:S(2)}, u32[]{:S(2)}) %collective-permute-start.11) | collective-permute-done | bytes 163872 | tf_op jit(solution)/shard_map/ppermute | solution.py:455
  52.4 7.9 %all_to_all.15.parts = bf16[4,160,128]{2,1,0:T(8,128)(2,1)S(1)} all-to-all(bf16[4,160,128]{2,1,0:T(8,128)(2,1)S(1)} %shard_map.117), channel_id=1, replica_groups=mesh['dp'=4,'chip'=4,'core'=2] {'chip'}, dimensions={0} | all-to-all | bytes 327680 | tf_op jit(solution)/shard_map/all_to_all | solution.py:601
  60.3 3.4 %collective-permute-start.14 = (bf16[224,128]{1,0:T(8,128)(2,1)S(1)}, bf16[224,128]{1,0:T(8,128)(2,1)S(1)}, u32[]{:S(2)}, u32[]{:S(2)}) collective-permute-start(bf16[224,128]{1,0:T(8,128)(2,1)S(1)} %shard_map.118.rest_0_), channel_id=1, source_target_pairs={{0,24},{8,16},{16,8},{24,0},{1,25},{9,17},{17,9},{25,1},{2,26},{10... | collective-permute-start | bytes 172040 | tf_op jit(solution)/shard_map/ppermute | solution.py:455
  63.7 0.0 collective-permute-start.13
  63.7 1.0 %collective-permute-start.12 = (bf16[224,128]{1,0:T(8,128)(2,1)S(1)}, bf16[224,128]{1,0:T(8,128)(2,1)S(1)}, u32[]{:S(2)}, u32[]{:S(2)}) collective-permute-start(bf16[224,128]{1,0:T(8,128)(2,1)S(1)} %shard_map.118.rest_0_), channel_id=1, source_target_pairs={{0,8},{8,0},{16,24},{24,16},{1,9},{9,1},{17,25},{25,17},{2,10},{10... | collective-permute-start | bytes 172040 | tf_op jit(solution)/shard_map/ppermute | solution.py:455
  64.8 1.6 %collective-permute-done.14.rest_3_ = bf16[224,128]{1,0:T(8,128)(2,1)S(1)} collective-permute-done((bf16[224,128]{1,0:T(8,128)(2,1)S(1)}, bf16[224,128]{1,0:T(8,128)(2,1)S(1)}, u32[]{:S(2)}, u32[]{:S(2)}) %collective-permute-start.14) | collective-permute-done | bytes 57376 | tf_op jit(solution)/shard_map/ppermute | solution.py:455
  66.3 2.5 %collective-permute-done.13.rest_2_ = bf16[224,128]{1,0:T(8,128)(2,1)S(1)} collective-permute-done((bf16[224,128]{1,0:T(8,128)(2,1)S(1)}, bf16[224,128]{1,0:T(8,128)(2,1)S(1)}, u32[]{:S(2)}, u32[]{:S(2)}) %collective-permute-start.13) | collective-permute-done | bytes 57376 | tf_op jit(solution)/shard_map/ppermute | solution.py:455
  68.8 0.0 collective-permute-done.12.rest_1_
  68.8 0.8 %shard_map.119 = (f32[64,320]{1,0:T(8,128)}, f32[64,128]{1,0:T(8,128)}) custom-call(bf16[224,128]{1,0:T(8,128)(2,1)S(1)} %shard_map.118.rest_0_, bf16[224,128]{1,0:T(8,128)(2,1)S(1)} %collective-permute-done.12.rest_1_, bf16[224,128]{1,0:T(8,128)(2,1)S(1)} %collective-permute-done.13.rest_2_, bf16[224,128]{1,0:T(8,128)(2,1)S(1)} %collective-permute-done.14.rest_3_), custom_call_target="tpu_custom_call" | custom-call | bytes 400000 | tf_op jit(solution)/shard_map/pallas_call | solution.py:443
  (13 shorter events, 0.1 us)
Async XLA Ops:
  3.8 7.3 %copy-start.1 = (bf16[1,8,16,1024]{3,2,1,0:T(8,128)(2,1)S(1)}, bf16[1,8,16,1024]{3,2,1,0:T(8,128)(2,1)}, u32[]{:S(2)}) copy-start(bf16[1,8,16,1024]{3,2,1,0:T(8,128)(2,1)} %param.11) | copy-start | bytes 786436
  3.8 7.3 %copy-start.2 = (bf16[1,8,16,1024]{3,2,1,0:T(8,128)(2,1)S(1)}, bf16[1,8,16,1024]{3,2,1,0:T(8,128)(2,1)}, u32[]{:S(2)}) copy-start(bf16[1,8,16,1024]{3,2,1,0:T(8,128)(2,1)} %param.12) | copy-start | bytes 786436
  3.8 7.3 %copy-start.3 = (bf16[1,8,16,1024]{3,2,1,0:T(8,128)(2,1)S(1)}, bf16[1,8,16,1024]{3,2,1,0:T(8,128)(2,1)}, u32[]{:S(2)}) copy-start(bf16[1,8,16,1024]{3,2,1,0:T(8,128)(2,1)} %param.13) | copy-start | bytes 786436
  3.8 7.3 %copy-start.4 = (bf16[8,16,1024]{2,1,0:T(8,128)(2,1)S(1)}, bf16[8,16,1024]{2,1,0:T(8,128)(2,1)}, u32[]{:S(2)}) copy-start(bf16[8,16,1024]{2,1,0:T(8,128)(2,1)} %get-tuple-element.28.queries) | copy-start | bytes 786436
  3.8 7.3 %copy-start.6 = (bf16[8,16,128]{2,1,0:T(8,128)(2,1)S(1)}, bf16[8,16,128]{2,1,0:T(8,128)(2,1)}, u32[]{:S(2)}) copy-start(bf16[8,16,128]{2,1,0:T(8,128)(2,1)} %get-tuple-element.29.adapter) | copy-start | bytes 98308
  3.8 29.6 %all-to-all-start = ((bf16[32,7,16,128]{3,2,1,0:T(8,128)(2,1)}), bf16[32,7,16,128]{3,2,1,0:T(8,128)(2,1)S(1)}, u32[]{:S(2)}, u32[]{:S(2)}) async-start(bf16[32,7,16,128]{3,2,1,0:T(8,128)(2,1)} %get-tuple-element.27), calls=%async_computation | async-start | bytes 1835008 | tf_op jit(solution)/shard_map/all_to_all | solution.py:535
  11.1 0.7 copy-start.7
  11.8 21.7 %copy-start.5 = (bf16[64,1024]{1,0:T(8,128)(2,1)S(1)}, bf16[64,1024]{1,0:T(8,128)(2,1)}, u32[]{:S(2)}) copy-start(bf16[64,1024]{1,0:T(8,128)(2,1)} %up.1) | copy-start | bytes 393220
  12.9 3.8 %collective-permute-start = (bf16[16,16,128]{2,1,0:T(8,128)(2,1)S(1)}, bf16[16,16,128]{2,1,0:T(8,128)(2,1)S(1)}, u32[]{:S(2)}, u32[]{:S(2)}) collective-permute-start(bf16[16,16,128]{2,1,0:T(8,128)(2,1)S(1)} %get-tuple-element.31), channel_id=1, source_target_pairs={{0,1},{1,0},{2,3},{3,2},{4,5},{5,4},{6,7},{7,6},{8,9},{9,8},{10,11... | collective-permute-start | bytes 196616 | tf_op jit(solution)/shard_map/ppermute | solution.py:455
  13.2 7.9 %collective-permute-start.1 = (bf16[16,16,128]{2,1,0:T(8,128)(2,1)S(1)}, bf16[16,16,128]{2,1,0:T(8,128)(2,1)S(1)}, u32[]{:S(2)}, u32[]{:S(2)}) collective-permute-start(bf16[16,16,128]{2,1,0:T(8,128)(2,1)S(1)} %get-tuple-element.32), channel_id=1, source_target_pairs={{0,2},{1,3},{2,0},{3,1},{4,6},{5,7},{6,4},{7,5},{8,10},{9,11},{10,... | collective-permute-start | bytes 196616 | tf_op jit(solution)/shard_map/ppermute | solution.py:455
  14.9 7.9 %collective-permute-start.2 = (bf16[16,16,128]{2,1,0:T(8,128)(2,1)S(1)}, bf16[16,16,128]{2,1,0:T(8,128)(2,1)S(1)}, u32[]{:S(2)}, u32[]{:S(2)}) collective-permute-start(bf16[16,16,128]{2,1,0:T(8,128)(2,1)S(1)} %get-tuple-element.33), channel_id=1, source_target_pairs={{0,3},{1,2},{2,1},{3,0},{4,7},{5,6},{6,5},{7,4},{8,11},{9,10},{10,... | collective-permute-start | bytes 196616 | tf_op jit(solution)/shard_map/ppermute | solution.py:455
  14.9 18.5 %copy-start.8 = (s32[1,1024]{1,0:T(1,128)S(1)}, s32[1,1024]{1,0:T(1,128)}, u32[]{:S(2)}) copy-start(s32[1,1024]{1,0:T(1,128)} %seg.1) | copy-start | bytes 12292
  14.9 7.9 %collective-permute-start.3 = (bf16[16,16,128]{2,1,0:T(8,128)(2,1)S(1)}, bf16[16,16,128]{2,1,0:T(8,128)(2,1)S(1)}, u32[]{:S(2)}, u32[]{:S(2)}) collective-permute-start(bf16[16,16,128]{2,1,0:T(8,128)(2,1)S(1)} %get-tuple-element.34), channel_id=1, source_target_pairs={{0,4},{1,5},{2,6},{3,7},{4,0},{5,1},{6,2},{7,3},{8,12},{9,13},{10,... | collective-permute-start | bytes 196616 | tf_op jit(solution)/shard_map/ppermute | solution.py:455
  16.6 8.5 %collective-permute-start.4 = (bf16[16,16,128]{2,1,0:T(8,128)(2,1)S(1)}, bf16[16,16,128]{2,1,0:T(8,128)(2,1)S(1)}, u32[]{:S(2)}, u32[]{:S(2)}) collective-permute-start(bf16[16,16,128]{2,1,0:T(8,128)(2,1)S(1)} %get-tuple-element.35), channel_id=1, source_target_pairs={{0,5},{1,4},{2,7},{3,6},{4,1},{5,0},{6,3},{7,2},{8,13},{9,12},{10,... | collective-permute-start | bytes 196616 | tf_op jit(solution)/shard_map/ppermute | solution.py:455
  16.7 10.0 %collective-permute-start.5 = (bf16[16,16,128]{2,1,0:T(8,128)(2,1)S(1)}, bf16[16,16,128]{2,1,0:T(8,128)(2,1)S(1)}, u32[]{:S(2)}, u32[]{:S(2)}) collective-permute-start(bf16[16,16,128]{2,1,0:T(8,128)(2,1)S(1)} %get-tuple-element.36), channel_id=1, source_target_pairs={{0,6},{1,7},{2,4},{3,5},{4,2},{5,3},{6,0},{7,1},{8,14},{9,15},{10,... | collective-permute-start | bytes 196616 | tf_op jit(solution)/shard_map/ppermute | solution.py:455
  21.1 6.2 %collective-permute-start.6 = (bf16[16,16,128]{2,1,0:T(8,128)(2,1)S(1)}, bf16[16,16,128]{2,1,0:T(8,128)(2,1)S(1)}, u32[]{:S(2)}, u32[]{:S(2)}) collective-permute-start(bf16[16,16,128]{2,1,0:T(8,128)(2,1)S(1)} %get-tuple-element.37), channel_id=1, source_target_pairs={{0,7},{1,6},{2,5},{3,4},{4,3},{5,2},{6,1},{7,0},{8,15},{9,14},{10,... | collective-permute-start | bytes 196616 | tf_op jit(solution)/shard_map/ppermute | solution.py:455
  33.4 16.1 %copy-start = (bf16[1,8,16,2560]{3,2,1,0:T(8,128)(2,1)S(1)}, bf16[1,8,16,2560]{3,2,1,0:T(8,128)(2,1)}, u32[]{:S(2)}) copy-start(bf16[1,8,16,2560]{3,2,1,0:T(8,128)(2,1)} %param.9) | copy-start | bytes 1966084
  36.7 12.8 %all-to-all-start.1 = ((bf16[32,16,128]{2,1,0:T(8,128)(2,1)}), bf16[32,16,128]{2,1,0:T(8,128)(2,1)S(1)}, u32[]{:S(2)}, u32[]{:S(2)}) async-start(bf16[32,16,128]{2,1,0:T(8,128)(2,1)} %get-tuple-element.38), calls=%async_computation.1 | async-start | bytes 262144 | tf_op jit(solution)/shard_map/all_to_all | solution.py:573
  41.1 4.7 %collective-permute-start.7 = (bf16[2,2,16,128]{3,2,1,0:T(8,128)(2,1)S(1)}, bf16[2,2,16,128]{3,2,1,0:T(8,128)(2,1)S(1)}, u32[]{:S(2)}, u32[]{:S(2)}) collective-permute-start(bf16[2,2,16,128]{3,2,1,0:T(8,128)(2,1)S(1)} %get-tuple-element.39), channel_id=1, source_target_pairs={{0,6},{2,4},{4,2},{6,0},{1,7},{3,5},{5,3},{7,1},{8,14},{10,12},{12... | collective-permute-start | bytes 49160 | tf_op jit(solution)/shard_map/ppermute | solution.py:455
  43.8 3.8 %collective-permute-start.8 = (bf16[2,2,16,128]{3,2,1,0:T(8,128)(2,1)S(1)}, bf16[2,2,16,128]{3,2,1,0:T(8,128)(2,1)S(1)}, u32[]{:S(2)}, u32[]{:S(2)}) collective-permute-start(bf16[2,2,16,128]{3,2,1,0:T(8,128)(2,1)S(1)} %get-tuple-element.40), channel_id=1, source_target_pairs={{0,4},{2,6},{4,0},{6,2},{1,5},{3,7},{5,1},{7,3},{8,12},{10,14},{12... | collective-permute-start | bytes 49160 | tf_op jit(solution)/shard_map/ppermute | solution.py:455
  44.4 3.7 %collective-permute-start.9 = (bf16[2,2,16,128]{3,2,1,0:T(8,128)(2,1)S(1)}, bf16[2,2,16,128]{3,2,1,0:T(8,128)(2,1)S(1)}, u32[]{:S(2)}, u32[]{:S(2)}) collective-permute-start(bf16[2,2,16,128]{3,2,1,0:T(8,128)(2,1)S(1)} %get-tuple-element.41), channel_id=1, source_target_pairs={{0,2},{2,0},{4,6},{6,4},{1,3},{3,1},{5,7},{7,5},{8,10},{10,8},{12,... | collective-permute-start | bytes 49160 | tf_op jit(solution)/shard_map/ppermute | solution.py:455
  48.2 1.2 %collective-permute-start.10 = (bf16[2,16,128]{2,1,0:T(8,128)(2,1)S(1)}, bf16[2,16,128]{2,1,0:T(8,128)(2,1)S(1)}, u32[]{:S(2)}, u32[]{:S(2)}) collective-permute-start(bf16[2,16,128]{2,1,0:T(8,128)(2,1)S(1)} %get-tuple-element.44), channel_id=1, source_target_pairs={{0,1},{1,0},{2,3},{3,2},{4,5},{5,4},{6,7},{7,6},{8,9},{9,8},{10,11... | collective-permute-start | bytes 24584 | tf_op jit(solution)/shard_map/ppermute | solution.py:455
  50.9 1.5 %collective-permute-start.11 = (bf16[4,160,128]{2,1,0:T(8,128)(2,1)S(1)}, bf16[4,160,128]{2,1,0:T(8,128)(2,1)S(1)}, u32[]{:S(2)}, u32[]{:S(2)}) collective-permute-start(bf16[4,160,128]{2,1,0:T(8,128)(2,1)S(1)} %get-tuple-element.46), channel_id=1, source_target_pairs={{0,1},{1,0},{2,3},{3,2},{4,5},{5,4},{6,7},{7,6},{8,9},{9,8},{10,11... | collective-permute-start | bytes 491528 | tf_op jit(solution)/shard_map/ppermute | solution.py:455
  60.3 6.0 %collective-permute-start.14 = (bf16[224,128]{1,0:T(8,128)(2,1)S(1)}, bf16[224,128]{1,0:T(8,128)(2,1)S(1)}, u32[]{:S(2)}, u32[]{:S(2)}) collective-permute-start(bf16[224,128]{1,0:T(8,128)(2,1)S(1)} %shard_map.118.rest_0_), channel_id=1, source_target_pairs={{0,24},{8,16},{16,8},{24,0},{1,25},{9,17},{17,9},{25,1},{2,26},{10... | collective-permute-start | bytes 172040 | tf_op jit(solution)/shard_map/ppermute | solution.py:455
  63.7 5.1 %collective-permute-start.13 = (bf16[224,128]{1,0:T(8,128)(2,1)S(1)}, bf16[224,128]{1,0:T(8,128)(2,1)S(1)}, u32[]{:S(2)}, u32[]{:S(2)}) collective-permute-start(bf16[224,128]{1,0:T(8,128)(2,1)S(1)} %shard_map.118.rest_0_), channel_id=1, source_target_pairs={{0,16},{8,24},{16,0},{24,8},{1,17},{9,25},{17,1},{25,9},{2,18},{10... | collective-permute-start | bytes 172040 | tf_op jit(solution)/shard_map/ppermute | solution.py:455
  63.7 5.1 %collective-permute-start.12 = (bf16[224,128]{1,0:T(8,128)(2,1)S(1)}, bf16[224,128]{1,0:T(8,128)(2,1)S(1)}, u32[]{:S(2)}, u32[]{:S(2)}) collective-permute-start(bf16[224,128]{1,0:T(8,128)(2,1)S(1)} %shard_map.118.rest_0_), channel_id=1, source_target_pairs={{0,8},{8,0},{16,24},{24,16},{1,9},{9,1},{17,25},{25,17},{2,10},{10... | collective-permute-start | bytes 172040 | tf_op jit(solution)/shard_map/ppermute | solution.py:455

commit v5 on v4

--- a/solution.py
+++ b/solution.py
@@ -175,8 +175,15 @@
         copy.wait()
 
 
-def pack_own_kernel(dims, plan, keys, vals, grad, queries, adapter, *own_outs):
+def core_columns(chip, core):
+    return pl.ds(pl.multiple_of((chip * 5 + core * 2) * LANES, LANES), 3 * LANES)
+
+
+def pack_own_kernel(dims, plan, keys, vals, grad, queries, adapter, feat, *outs):
     groups, blocks, heads, rows, live = dims
+    own_outs, feat_out = outs[:heads], outs[heads]
+    for chip in range(heads // CORES):
+        feat_out[chip] = feat[:, core_columns(chip, 1 - lax.axis_index("core"))]
     extras = live - CAP
     me = lax.axis_index("dp")
     seq = seq_index()
@@ -207,11 +214,12 @@
 
 def attend_kernel(dims, plan, seg, up, far_in, *rest):
     groups, blocks, heads, rows, live = dims
+    chips = heads // CORES
     own_ins = rest[:heads]
-    part_hbm = rest[heads]
-    own_parts = rest[heads + 1 : heads + 1 + heads // CORES]
+    part_hbm = rest[heads + 1]
+    own_parts = rest[heads + 2 : heads + 2 + chips]
     up_out, log_hbm, part_out, log_out, routes, sems, qs, ks, vs, gs, ads, dqs, parts = rest[
-        heads + 1 + heads // CORES :
+        heads + 2 + chips :
     ]
     extras = live - CAP
     me = lax.axis_index("dp")
@@ -344,66 +352,65 @@
     part_copy.wait()
 
 
-def chip_sum_kernel(*refs):
-    parts, outs = refs[:-CORES], refs[-CORES:]
+def head_sum_kernel(parts, *refs):
+    extras, out = refs[:-1], refs[-1]
+    pairs = extras[0].shape[1]
+    groups = out.shape[0] - CORES * pairs
+
+    def total(terms):
+        value = terms[0].astype(jnp.float32)
+        for term in terms[1:]:
+            value = value + term.astype(jnp.float32)
+        return value.astype(jnp.bfloat16)
+
+    for group in range(groups):
+        out[group] = total([parts[peer] for peer in range(group, parts.shape[0], groups)])
     for core in range(CORES):
-        total = parts[0][core].astype(jnp.float32)
-        for part in parts[1:]:
-            total = total + part[core].astype(jnp.float32)
-        outs[core][...] = total.astype(jnp.bfloat16)
-
-
-def product_kernel(dims, plan, parts, feat, own_mine, own_other, keep, send, sums, grads):
+        for pair in range(pairs):
+            out[groups + core * pairs + pair] = total([extra[core, pair] for extra in extras])
+
+
+def product_kernel(dims, plan, feat, feat_other, mine, other, out, sums, grads):
     groups, blocks, heads, rows, live = dims
     me = lax.axis_index("dp")
-    for group in range(groups):
-        total = parts[group].astype(jnp.float32)
-        for head in range(1, heads):
-            total = total + parts[head * groups + group].astype(jnp.float32)
-        sums[group] = total
-    for pair in range(own_mine.shape[0]):
-        sums[groups + pair] = own_mine[pair].astype(jnp.float32) + own_other[pair].astype(
-            jnp.float32
-        )
+    core = lax.axis_index("core")
+    pairs = sums.shape[1] - groups
+    for owner, (tiles, partner) in enumerate(((mine, other), (other, mine))):
+        for group in range(groups):
+            sums[owner, group] = tiles[group].astype(jnp.float32)
+        for index in range(groups, groups + pairs):
+            sums[owner, index] = tiles[index].astype(jnp.float32) + partner[index + pairs].astype(
+                jnp.float32
+            )
     grads[...] = jnp.zeros_like(grads)
 
     def put(dest, slot, local):
         index = jnp.where(slot < CAP, dest, groups - 1 + quotient(slot, 2))
-        grads[local] = split(slot, sums[index]).astype(jnp.bfloat16)
+        for owner in range(CORES):
+            grads[owner, local] = split(slot, sums[owner, index])
 
     each_hit(plan, me, groups, blocks, live, put)
     low = low_lanes(HALF // 2)
-    columns = grads[...].reshape(blocks * rows, LANES).astype(jnp.float32).T[:HALF]
-    columns = columns.astype(jnp.bfloat16)
-    even = lax.axis_index("core") == 0
+    columns = [
+        grads[owner].reshape(blocks * rows, LANES).T[:HALF].astype(jnp.bfloat16)
+        for owner in range(CORES)
+    ]
+    even = core == 0
     for chip in range(heads // CORES):
         tiles = jnp.dot(
-            columns,
-            feat[:, chip * 5 * LANES : (chip + 1) * 5 * LANES],
-            preferred_element_type=jnp.float32,
+            columns[0], feat[:, core_columns(chip, core)], preferred_element_type=jnp.float32
+        ) + jnp.dot(columns[1], feat_other[chip], preferred_element_type=jnp.float32)
+        first, second, third = (
+            tiles[:, index * LANES : (index + 1) * LANES] for index in range(3)
         )
-        shared = tiles[:, 2 * LANES : 3 * LANES]
+        shared = jnp.where(even, third, first)
         upper, lower = shared[: HALF // 2], shared[HALF // 2 :]
-        first = jnp.concatenate(
-            [tiles[:, :LANES], tiles[:, LANES : 2 * LANES], jnp.where(low, upper, swap_halves(lower))],
-            axis=0,
-        )
-        second = jnp.concatenate(
-            [
-                tiles[:, 3 * LANES : 4 * LANES],
-                tiles[:, 4 * LANES :],
-                jnp.where(low, swap_halves(upper), lower),
-            ],
-            axis=0,
-        )
-        keep[chip] = jnp.where(even, first, second).astype(jnp.bfloat16)
-        send[chip] = jnp.where(even, second, first).astype(jnp.bfloat16)
-
-
-def add_kernel(kept, received, out):
-    for index in range(out.shape[0]):
-        out[index] = (
-            kept[index].astype(jnp.float32) + received[index].astype(jnp.float32)
+        out[chip, :HALF] = jnp.where(even, first, second).astype(jnp.bfloat16)
+        out[chip, HALF : 2 * HALF] = jnp.where(even, second, third).astype(jnp.bfloat16)
+        out[chip, 2 * HALF :] = jnp.where(
+            even,
+            jnp.where(low, upper, swap_halves(lower)),
+            jnp.where(low, swap_halves(upper), lower),
         ).astype(jnp.bfloat16)
 
 
@@ -519,8 +526,8 @@
     )
     own_send = call(
         functools.partial(pack_own_kernel, dims),
-        [(own_shape, bf16)] * heads,
-        [SMEM] + [VMEM] * 5,
+        [(own_shape, bf16)] * heads + [((chips, blocks * rows, 3 * LANES), bf16)],
+        [SMEM] + [VMEM] * 6,
         [],
         0,
         1_600_000,
@@ -530,7 +537,9 @@
         output_gradient[0],
         queries,
         adapter,
-    )
+        flat,
+    )
+    feat_other = exchange(own_send[heads], "core", CORES, 1)
     own = [own_send[0]] + [exchange(own_send[turn], SEQ, heads, turn) for turn in range(1, heads)]
     far = lax.all_to_all(far_send, everyone, 0, 0, tiled=True)
     attended = call(
@@ -538,7 +547,7 @@
         [((peers, rows, LANES), bf16)]
         + [((CORES, pairs, rows, LANES), bf16)] * (heads // CORES)
         + [((rank, LANES), bf16), ((1, 1, length), f32)],
-        [SMEM] + [VMEM] * (3 + heads),
+        [SMEM] + [VMEM] * (3 + heads) + [ANY],
         [
             pltpu.VMEM((peers, rows, LANES), bf16),
             pltpu.VMEM((1, 1, length), f32),
@@ -554,49 +563,41 @@
         adapter_up_weight,
         far,
         *own,
+        feat_other,
         out_specs=[ANY] + [VMEM] * (chips + 1) + [ANY],
     )
     own_parts = [
         exchange(attended[1 + turn], "chip", chips, turn) for turn in range(chips - 1, 0, -1)
     ]
-    own_mine, own_other = call(
-        chip_sum_kernel,
-        [((pairs, rows, LANES), bf16)] * CORES,
-        [VMEM] * (heads // CORES),
+    part = lax.all_to_all(attended[0], everyone, 0, 0, tiled=True)
+    up_part, log_norm = attended[1 + chips :]
+    tiles = groups + CORES * pairs
+    (mine,) = call(
+        head_sum_kernel,
+        [((tiles, rows, LANES), bf16)],
+        [VMEM] * (1 + chips),
         [],
         0,
-        100_000,
+        300_000,
+        part,
         *own_parts,
         attended[1],
     )
-    own_other = exchange(own_other, "core", CORES, 1)
-    part = lax.all_to_all(attended[0], everyone, 0, 0, tiled=True)
-    up_part, log_norm = attended[1 + heads // CORES :]
-    keep, send = call(
+    (shares,) = call(
         functools.partial(product_kernel, dims),
-        [((chips, HALF * 5 // 2, LANES), bf16)] * 2,
+        [((chips, HALF * 5 // 2, LANES), bf16)],
         [SMEM] + [VMEM] * 4,
         [
-            pltpu.VMEM((groups + pairs, rows, LANES), f32),
-            pltpu.VMEM((blocks, rows, LANES), bf16),
+            pltpu.VMEM((CORES, groups + pairs, rows, LANES), f32),
+            pltpu.VMEM((CORES, blocks, rows, LANES), f32),
         ],
         40_000_000,
         2_000_000,
         source_block_plan,
-        part,
         flat,
-        own_mine,
-        own_other,
-    )
-    (shares,) = call(
-        add_kernel,
-        [((chips, HALF * 5 // 2, LANES), bf16)],
-        [VMEM] * 2,
-        [],
-        0,
-        600_000,
-        keep,
-        exchange(send, "core", CORES, 1),
+        feat_other,
+        mine,
+        exchange(mine, "core", CORES, 1),
     )
     shares = lax.all_to_all(shares, "chip", 0, 0, tiled=True)
     (joined,) = call(

time: 70 us -> 69.2 us (0.989)
  waiting for transfers between devices: 23.9 us -> 22.8 us
    ppermute x15, waiting for transfers between devices: 17.7 us -> 16 us  [exchange(): lax.ppermute(value, axis, [(peer, peer ^ turn) for peer in range(size)])]
    all_to_all x1, waiting for transfers between devices: 0.11 us -> 1.37 us  [per_device_tiles(): part = lax.all_to_all(attended[0], everyone, 0, 0, tiled=True)]
    pallas_call x8 -> x7, Pallas kernels: 9.78 us -> 9.93 us  [call(): pl.pallas_call(kernel, out_shape=shapes, in_specs=specs, out_specs=out_sp...]
  transfers between devices with their start and end apart: 17 -> 17, of which waited for: 14 -> 13; matrix products, arithmetic and copies ran while one was open for 0% -> 0% of each run, Pallas kernels for 2% -> 2%
where the time goes in v5:
time: 69.2 us; the launch traced here: 69 us
  starting transfers between devices  26.9 us (39%)
  waiting for transfers between devices  22.8 us (33%)
  Pallas kernels  9.93 us (14%)
  blocking collectives  7.88 us (11%)
  between operations  0.81 us (1%)
    ppermute x15, waiting for transfers between devices, exchange(): lax.ppermute(value, axis, [(peer, peer ^ turn) for peer in range(size)])  16 us
    ppermute x15, starting transfers between devices, exchange(): lax.ppermute(value, axis, [(peer, peer ^ turn) for peer in range(size)])  15.2 us
    pallas_call x7, Pallas kernels, call(): pl.pallas_call(kernel, out_shape=shapes, in_specs=specs, out_specs=out_sp...  9.93 us
    all_to_all x1, blocking collectives, per_device_tiles(): shares = lax.all_to_all(shares, 'chip', 0, 0, tiled=True)  7.88 us
    all_to_all x1, starting transfers between devices, per_device_tiles(): far = lax.all_to_all(far_send, everyone, 0, 0, tiled=True)  7.3 us
    all_to_all x1, waiting for transfers between devices, per_device_tiles(): far = lax.all_to_all(far_send, everyone, 0, 0, tiled=True)  5.42 us
    all_to_all x1, starting transfers between devices, per_device_tiles(): part = lax.all_to_all(attended[0], everyone, 0, 0, tiled=True)  4.41 us
  transfers between devices with their start and end apart: 17, of which 13 were waited for; matrix products, arithmetic and copies ran while one was open for 0% of the time, Pallas kernels for 2%

profile of v5, /device:TPU:0, one launch (start us, length us, event | category | flops | bytes accessed | tf_op | source)
XLA Modules:
  0.0 69.0 jit_solution(1947137456044025157)
XLA Ops:
  0.6 3.2 %shard_map.112 = (bf16[32,7,16,128]{3,2,1,0:T(8,128)(2,1)}, bf16[8,16,1024]{2,1,0:T(8,128)(2,1)}, bf16[8,16,128]{2,1,0:T(8,128)(2,1)}) custom-call(s32[4,8]{1,0:T(4,128)} %plan.5, bf16[128,2560]{1,0:T(8,128)(2,1)} %bitcast.7, bf16[8,16,1024]{2,1,0:T(8,128)(2,1)} %bitcast.16, bf16[8,16,1024]{2,1,0:T(8,128)(2,1)} %bitcast.10, bf16[8,16,1024]{2,1,0:T(8,128)(2,1)} %bitcast.12, ...), custom_call_target="tpu_custom_call" | custom-call | flops 60000000 | bytes 4000000 | tf_op jit(solution)/shard_map/pallas_call | solution.py:450
  3.8 0.0 copy-start
  3.8 0.0 copy-start.1
  3.8 0.0 copy-start.2
  3.8 0.0 copy-start.3
  3.9 0.0 copy-start.6
  3.9 7.3 %all-to-all-start = ((bf16[32,7,16,128]{3,2,1,0:T(8,128)(2,1)}), bf16[32,7,16,128]{3,2,1,0:T(8,128)(2,1)S(1)}, u32[]{:S(2)}, u32[]{:S(2)}) async-start(bf16[32,7,16,128]{3,2,1,0:T(8,128)(2,1)} %get-tuple-element.27), calls=%async_computation | async-start | bytes 1835008 | tf_op jit(solution)/shard_map/all_to_all | solution.py:544
  11.2 0.0 copy-start.7
  11.2 0.0 copy-done
  11.3 0.6 copy-done.7
  11.9 1.2 %shard_map.113 = (bf16[16,16,128]{2,1,0:T(8,128)(2,1)S(1)}, bf16[16,16,128]{2,1,0:T(8,128)(2,1)S(1)}, bf16[16,16,128]{2,1,0:T(8,128)(2,1)S(1)}, bf16[16,16,128]{...) custom-call(s32[4,8]{1,0:T(4,128)S(1)} %copy-done.7, ...), custom_call_target="tpu_custom_call" | custom-call | bytes 1600000 | tf_op jit(solution)/shard_map/pallas_call | solution.py:450
  13.0 0.3 collective-permute-start
  13.3 0.3 collective-permute-start.1
  13.6 1.8 %collective-permute-start.2 = (bf16[16,16,128]{2,1,0:T(8,128)(2,1)S(1)}, bf16[16,16,128]{2,1,0:T(8,128)(2,1)S(1)}, u32[]{:S(2)}, u32[]{:S(2)}) collective-permute-start(bf16[16,16,128]{2,1,0:T(8,128)(2,1)S(1)} %get-tuple-element.30), channel_id=1, source_target_pairs={{0,2},{1,3},{2,0},{3,1},{4,6},{5,7},{6,4},{7,5},{8,10},{9,11},{10,... | collective-permute-start | bytes 196616 | tf_op jit(solution)/shard_map/ppermute | solution.py:462
  15.4 0.0 collective-permute-start.3
  15.4 1.5 %collective-permute-start.4 = (bf16[16,16,128]{2,1,0:T(8,128)(2,1)S(1)}, bf16[16,16,128]{2,1,0:T(8,128)(2,1)S(1)}, u32[]{:S(2)}, u32[]{:S(2)}) collective-permute-start(bf16[16,16,128]{2,1,0:T(8,128)(2,1)S(1)} %get-tuple-element.32), channel_id=1, source_target_pairs={{0,4},{1,5},{2,6},{3,7},{4,0},{5,1},{6,2},{7,3},{8,12},{9,13},{10,... | collective-permute-start | bytes 196616 | tf_op jit(solution)/shard_map/ppermute | solution.py:462
  16.9 0.0 collective-permute-done.1.rest_1_
  16.9 0.3 collective-permute-start.5
  17.2 4.0 %collective-permute-done.2.rest_2_ = bf16[16,16,128]{2,1,0:T(8,128)(2,1)S(1)} collective-permute-done((bf16[16,16,128]{2,1,0:T(8,128)(2,1)S(1)}, bf16[16,16,128]{2,1,0:T(8,128)(2,1)S(1)}, u32[]{:S(2)}, u32[]{:S(2)}) %collective-permute-start.2) | collective-permute-done | bytes 65568 | tf_op jit(solution)/shard_map/ppermute | solution.py:462
  21.2 1.1 %collective-permute-start.6 = (bf16[16,16,128]{2,1,0:T(8,128)(2,1)S(1)}, bf16[16,16,128]{2,1,0:T(8,128)(2,1)S(1)}, u32[]{:S(2)}, u32[]{:S(2)}) collective-permute-start(bf16[16,16,128]{2,1,0:T(8,128)(2,1)S(1)} %get-tuple-element.34), channel_id=1, source_target_pairs={{0,6},{1,7},{2,4},{3,5},{4,2},{5,3},{6,0},{7,1},{8,14},{9,15},{10,... | collective-permute-start | bytes 196616 | tf_op jit(solution)/shard_map/ppermute | solution.py:462
  22.3 0.6 collective-permute-done.3.rest_3_
  22.9 1.8 %collective-permute-start.7 = (bf16[16,16,128]{2,1,0:T(8,128)(2,1)S(1)}, bf16[16,16,128]{2,1,0:T(8,128)(2,1)S(1)}, u32[]{:S(2)}, u32[]{:S(2)}) collective-permute-start(bf16[16,16,128]{2,1,0:T(8,128)(2,1)S(1)} %get-tuple-element.35), channel_id=1, source_target_pairs={{0,7},{1,6},{2,5},{3,4},{4,3},{5,2},{6,1},{7,0},{8,15},{9,14},{10,... | collective-permute-start | bytes 196616 | tf_op jit(solution)/shard_map/ppermute | solution.py:462
  24.8 0.0 collective-permute-done.4.rest_4_
  24.8 0.6 collective-permute-done.5.rest_5_
  25.4 1.1 %collective-permute-done.6.rest_6_ = bf16[16,16,128]{2,1,0:T(8,128)(2,1)S(1)} collective-permute-done((bf16[16,16,128]{2,1,0:T(8,128)(2,1)S(1)}, bf16[16,16,128]{2,1,0:T(8,128)(2,1)S(1)}, u32[]{:S(2)}, u32[]{:S(2)}) %collective-permute-start.6) | collective-permute-done | bytes 65568 | tf_op jit(solution)/shard_map/ppermute | solution.py:462
  26.5 1.6 %collective-permute-done.7.rest_7_ = bf16[16,16,128]{2,1,0:T(8,128)(2,1)S(1)} collective-permute-done((bf16[16,16,128]{2,1,0:T(8,128)(2,1)S(1)}, bf16[16,16,128]{2,1,0:T(8,128)(2,1)S(1)}, u32[]{:S(2)}, u32[]{:S(2)}) %collective-permute-start.7) | collective-permute-done | bytes 65568 | tf_op jit(solution)/shard_map/ppermute | solution.py:462
  28.1 0.0 collective-permute-done.rest_8_.feat_other
  28.1 5.4 %all-to-all-done.far_in = bf16[32,7,16,128]{3,2,1,0:T(8,128)(2,1)S(1)} async-done(((bf16[32,7,16,128]{3,2,1,0:T(8,128)(2,1)}), bf16[32,7,16,128]{3,2,1,0:T(8,128)(2,1)S(1)}, u32[]{:S(2)}, u32[]{:S(2)}) %all-to-all-start) | async-done | bytes 917536 | tf_op jit(solution)/shard_map/all_to_all | solution.py:544
  33.5 3.2 %shard_map.114 = (bf16[32,16,128]{2,1,0:T(8,128)(2,1)}, bf16[2,2,16,128]{3,2,1,0:T(8,128)(2,1)S(1)}, bf16[2,2,16,128]{3,2,1,0:T(8,128)(2,1)S(1)}, bf16[2,2,16,12...) custom-call(s32[4,8]{1,0:T(4,128)S(1)} %copy-done.7, ...), custom_call_target="tpu_custom_call" | custom-call | flops 600000000 | bytes 3000000 | tf_op jit(solution)/shard_map/pallas_call | solution.py:450
  36.8 4.4 %all-to-all-start.1 = ((bf16[32,16,128]{2,1,0:T(8,128)(2,1)}), bf16[32,16,128]{2,1,0:T(8,128)(2,1)S(1)}, u32[]{:S(2)}, u32[]{:S(2)}) async-start(bf16[32,16,128]{2,1,0:T(8,128)(2,1)} %get-tuple-element.36), calls=%async_computation.1 | async-start | bytes 262144 | tf_op jit(solution)/shard_map/all_to_all | solution.py:572
  41.2 2.7 %collective-permute-start.8 = (bf16[2,2,16,128]{3,2,1,0:T(8,128)(2,1)S(1)}, bf16[2,2,16,128]{3,2,1,0:T(8,128)(2,1)S(1)}, u32[]{:S(2)}, u32[]{:S(2)}) collective-permute-start(bf16[2,2,16,128]{3,2,1,0:T(8,128)(2,1)S(1)} %get-tuple-element.37), channel_id=1, source_target_pairs={{0,6},{2,4},{4,2},{6,0},{1,7},{3,5},{5,3},{7,1},{8,14},{10,12},{12... | collective-permute-start | bytes 49160 | tf_op jit(solution)/shard_map/ppermute | solution.py:462
  43.9 0.6 collective-permute-start.9
  44.5 0.3 collective-permute-start.10
  44.7 1.1 %collective-permute-done.8.refs_0_ = bf16[2,2,16,128]{3,2,1,0:T(8,128)(2,1)S(1)} collective-permute-done((bf16[2,2,16,128]{3,2,1,0:T(8,128)(2,1)S(1)}, bf16[2,2,16,128]{3,2,1,0:T(8,128)(2,1)S(1)}, u32[]{:S(2)}, u32[]{:S(2)}) %collective-permute-start.8) | collective-permute-done | bytes 16416 | tf_op jit(solution)/shard_map/ppermute | solution.py:462
  45.9 1.8 %collective-permute-done.9.refs_1_ = bf16[2,2,16,128]{3,2,1,0:T(8,128)(2,1)S(1)} collective-permute-done((bf16[2,2,16,128]{3,2,1,0:T(8,128)(2,1)S(1)}, bf16[2,2,16,128]{3,2,1,0:T(8,128)(2,1)S(1)}, u32[]{:S(2)}, u32[]{:S(2)}) %collective-permute-start.9) | collective-permute-done | bytes 16416 | tf_op jit(solution)/shard_map/ppermute | solution.py:462
  47.7 0.5 collective-permute-done.10.refs_2_
  48.2 1.4 %all-to-all-done.1.parts = bf16[32,16,128]{2,1,0:T(8,128)(2,1)S(1)} async-done(((bf16[32,16,128]{2,1,0:T(8,128)(2,1)}), bf16[32,16,128]{2,1,0:T(8,128)(2,1)S(1)}, u32[]{:S(2)}, u32[]{:S(2)}) %all-to-all-start.1) | async-done | bytes 131104 | tf_op jit(solution)/shard_map/all_to_all | solution.py:572
  49.6 0.1 collective-permute-start.11
  49.7 1.2 %collective-permute-done.11.other = bf16[8,16,128]{2,1,0:T(8,128)(2,1)S(1)} collective-permute-done((bf16[8,16,128]{2,1,0:T(8,128)(2,1)S(1)}, bf16[8,16,128]{2,1,0:T(8,128)(2,1)S(1)}, u32[]{:S(2)}, u32[]{:S(2)}) %collective-permute-start.11) | collective-permute-done | bytes 32800 | tf_op jit(solution)/shard_map/ppermute | solution.py:462
  50.9 1.5 %shard_map.116 = bf16[4,160,128]{2,1,0:T(8,128)(2,1)S(1)} custom-call(s32[4,8]{1,0:T(4,128)S(1)} %copy-done.7, bf16[128,2560]{1,0:T(8,128)(2,1)S(1)} %bitcast.9, bf16[4,128,384]{2,1,0:T(8,128)(2,1)S(1)} %collective-permute-done.rest_8_.feat_other, bf16[8,16,128]{2,1,0:T(8,128)(2,1)S(1)} %shard_map.115.mine, bf16[8,16,128]{2,1,0:T(8,128)(2,1)S(1)} %collective-permute-done.11.other), custom_call_target="tpu_custom_call" | custom-call | flops 40000000 | bytes 2000000 | tf_op jit(solution)/shard_map/pallas_call | solution.py:450
  52.4 7.9 %all_to_all.15.parts = bf16[4,160,128]{2,1,0:T(8,128)(2,1)S(1)} all-to-all(bf16[4,160,128]{2,1,0:T(8,128)(2,1)S(1)} %shard_map.116), channel_id=1, replica_groups=mesh['dp'=4,'chip'=4,'core'=2] {'chip'}, dimensions={0} | all-to-all | bytes 327680 | tf_op jit(solution)/shard_map/all_to_all | solution.py:602
  60.3 2.2 %collective-permute-start.14 = (bf16[224,128]{1,0:T(8,128)(2,1)S(1)}, bf16[224,128]{1,0:T(8,128)(2,1)S(1)}, u32[]{:S(2)}, u32[]{:S(2)}) collective-permute-start(bf16[224,128]{1,0:T(8,128)(2,1)S(1)} %shard_map.117.rest_0_), channel_id=1, source_target_pairs={{0,24},{8,16},{16,8},{24,0},{1,25},{9,17},{17,9},{25,1},{2,26},{10... | collective-permute-start | bytes 172040 | tf_op jit(solution)/shard_map/ppermute | solution.py:462
  62.5 0.0 collective-permute-start.13
  62.5 2.3 %collective-permute-start.12 = (bf16[224,128]{1,0:T(8,128)(2,1)S(1)}, bf16[224,128]{1,0:T(8,128)(2,1)S(1)}, u32[]{:S(2)}, u32[]{:S(2)}) collective-permute-start(bf16[224,128]{1,0:T(8,128)(2,1)S(1)} %shard_map.117.rest_0_), channel_id=1, source_target_pairs={{0,8},{8,0},{16,24},{24,16},{1,9},{9,1},{17,25},{25,17},{2,10},{10... | collective-permute-start | bytes 172040 | tf_op jit(solution)/shard_map/ppermute | solution.py:462
  64.8 2.3 %collective-permute-done.14.rest_3_ = bf16[224,128]{1,0:T(8,128)(2,1)S(1)} collective-permute-done((bf16[224,128]{1,0:T(8,128)(2,1)S(1)}, bf16[224,128]{1,0:T(8,128)(2,1)S(1)}, u32[]{:S(2)}, u32[]{:S(2)}) %collective-permute-start.14) | collective-permute-done | bytes 57376 | tf_op jit(solution)/shard_map/ppermute | solution.py:462
  67.0 1.1 %collective-permute-done.13.rest_2_ = bf16[224,128]{1,0:T(8,128)(2,1)S(1)} collective-permute-done((bf16[224,128]{1,0:T(8,128)(2,1)S(1)}, bf16[224,128]{1,0:T(8,128)(2,1)S(1)}, u32[]{:S(2)}, u32[]{:S(2)}) %collective-permute-start.13) | collective-permute-done | bytes 57376 | tf_op jit(solution)/shard_map/ppermute | solution.py:462
  68.2 0.0 collective-permute-done.12.rest_1_
  68.2 0.8 %shard_map.118 = (f32[64,320]{1,0:T(8,128)}, f32[64,128]{1,0:T(8,128)}) custom-call(bf16[224,128]{1,0:T(8,128)(2,1)S(1)} %shard_map.117.rest_0_, bf16[224,128]{1,0:T(8,128)(2,1)S(1)} %collective-permute-done.12.rest_1_, bf16[224,128]{1,0:T(8,128)(2,1)S(1)} %collective-permute-done.13.rest_2_, bf16[224,128]{1,0:T(8,128)(2,1)S(1)} %collective-permute-done.14.rest_3_), custom_call_target="tpu_custom_call" | custom-call | bytes 400000 | tf_op jit(solution)/shard_map/pallas_call | solution.py:450
  (12 shorter events, 0.1 us)
Async XLA Ops:
  3.8 7.4 %copy-start = (bf16[1,8,16,2560]{3,2,1,0:T(8,128)(2,1)S(1)}, bf16[1,8,16,2560]{3,2,1,0:T(8,128)(2,1)}, u32[]{:S(2)}) copy-start(bf16[1,8,16,2560]{3,2,1,0:T(8,128)(2,1)} %param.9) | copy-start | bytes 1966084
  3.8 7.4 %copy-start.1 = (bf16[1,8,16,1024]{3,2,1,0:T(8,128)(2,1)S(1)}, bf16[1,8,16,1024]{3,2,1,0:T(8,128)(2,1)}, u32[]{:S(2)}) copy-start(bf16[1,8,16,1024]{3,2,1,0:T(8,128)(2,1)} %param.11) | copy-start | bytes 786436
  3.8 7.4 %copy-start.2 = (bf16[1,8,16,1024]{3,2,1,0:T(8,128)(2,1)S(1)}, bf16[1,8,16,1024]{3,2,1,0:T(8,128)(2,1)}, u32[]{:S(2)}) copy-start(bf16[1,8,16,1024]{3,2,1,0:T(8,128)(2,1)} %param.12) | copy-start | bytes 786436
  3.8 7.4 %copy-start.3 = (bf16[1,8,16,1024]{3,2,1,0:T(8,128)(2,1)S(1)}, bf16[1,8,16,1024]{3,2,1,0:T(8,128)(2,1)}, u32[]{:S(2)}) copy-start(bf16[1,8,16,1024]{3,2,1,0:T(8,128)(2,1)} %param.13) | copy-start | bytes 786436
  3.9 7.4 %copy-start.4 = (bf16[8,16,1024]{2,1,0:T(8,128)(2,1)S(1)}, bf16[8,16,1024]{2,1,0:T(8,128)(2,1)}, u32[]{:S(2)}) copy-start(bf16[8,16,1024]{2,1,0:T(8,128)(2,1)} %get-tuple-element.24.queries) | copy-start | bytes 786436
  3.9 7.4 %copy-start.6 = (bf16[8,16,128]{2,1,0:T(8,128)(2,1)S(1)}, bf16[8,16,128]{2,1,0:T(8,128)(2,1)}, u32[]{:S(2)}) copy-start(bf16[8,16,128]{2,1,0:T(8,128)(2,1)} %get-tuple-element.25.adapter) | copy-start | bytes 98308
  3.9 29.6 %all-to-all-start = ((bf16[32,7,16,128]{3,2,1,0:T(8,128)(2,1)}), bf16[32,7,16,128]{3,2,1,0:T(8,128)(2,1)S(1)}, u32[]{:S(2)}, u32[]{:S(2)}) async-start(bf16[32,7,16,128]{3,2,1,0:T(8,128)(2,1)} %get-tuple-element.27), calls=%async_computation | async-start | bytes 1835008 | tf_op jit(solution)/shard_map/all_to_all | solution.py:544
  11.2 0.7 copy-start.7
  11.9 21.7 %copy-start.5 = (bf16[64,1024]{1,0:T(8,128)(2,1)S(1)}, bf16[64,1024]{1,0:T(8,128)(2,1)}, u32[]{:S(2)}) copy-start(bf16[64,1024]{1,0:T(8,128)(2,1)} %up.1) | copy-start | bytes 393220
  13.0 15.1 %collective-permute-start = (bf16[4,128,384]{2,1,0:T(8,128)(2,1)S(1)}, bf16[4,128,384]{2,1,0:T(8,128)(2,1)S(1)}, u32[]{:S(2)}, u32[]{:S(2)}) collective-permute-start(bf16[4,128,384]{2,1,0:T(8,128)(2,1)S(1)} %get-tuple-element.26), channel_id=1, source_target_pairs={{0,1},{1,0},{2,3},{3,2},{4,5},{5,4},{6,7},{7,6},{8,9},{9,8},{10,11... | collective-permute-start | bytes 1179656 | tf_op jit(solution)/shard_map/ppermute | solution.py:462
  13.3 3.5 %collective-permute-start.1 = (bf16[16,16,128]{2,1,0:T(8,128)(2,1)S(1)}, bf16[16,16,128]{2,1,0:T(8,128)(2,1)S(1)}, u32[]{:S(2)}, u32[]{:S(2)}) collective-permute-start(bf16[16,16,128]{2,1,0:T(8,128)(2,1)S(1)} %get-tuple-element.29), channel_id=1, source_target_pairs={{0,1},{1,0},{2,3},{3,2},{4,5},{5,4},{6,7},{7,6},{8,9},{9,8},{10,11... | collective-permute-start | bytes 196616 | tf_op jit(solution)/shard_map/ppermute | solution.py:462
  13.6 7.6 %collective-permute-start.2 = (bf16[16,16,128]{2,1,0:T(8,128)(2,1)S(1)}, bf16[16,16,128]{2,1,0:T(8,128)(2,1)S(1)}, u32[]{:S(2)}, u32[]{:S(2)}) collective-permute-start(bf16[16,16,128]{2,1,0:T(8,128)(2,1)S(1)} %get-tuple-element.30), channel_id=1, source_target_pairs={{0,2},{1,3},{2,0},{3,1},{4,6},{5,7},{6,4},{7,5},{8,10},{9,11},{10,... | collective-permute-start | bytes 196616 | tf_op jit(solution)/shard_map/ppermute | solution.py:462
  15.4 7.6 %collective-permute-start.3 = (bf16[16,16,128]{2,1,0:T(8,128)(2,1)S(1)}, bf16[16,16,128]{2,1,0:T(8,128)(2,1)S(1)}, u32[]{:S(2)}, u32[]{:S(2)}) collective-permute-start(bf16[16,16,128]{2,1,0:T(8,128)(2,1)S(1)} %get-tuple-element.31), channel_id=1, source_target_pairs={{0,3},{1,2},{2,1},{3,0},{4,7},{5,6},{6,5},{7,4},{8,11},{9,10},{10,... | collective-permute-start | bytes 196616 | tf_op jit(solution)/shard_map/ppermute | solution.py:462
  15.4 18.1 %copy-start.8 = (s32[1,1024]{1,0:T(1,128)S(1)}, s32[1,1024]{1,0:T(1,128)}, u32[]{:S(2)}) copy-start(s32[1,1024]{1,0:T(1,128)} %seg.1) | copy-start | bytes 12292
  15.4 9.4 %collective-permute-start.4 = (bf16[16,16,128]{2,1,0:T(8,128)(2,1)S(1)}, bf16[16,16,128]{2,1,0:T(8,128)(2,1)S(1)}, u32[]{:S(2)}, u32[]{:S(2)}) collective-permute-start(bf16[16,16,128]{2,1,0:T(8,128)(2,1)S(1)} %get-tuple-element.32), channel_id=1, source_target_pairs={{0,4},{1,5},{2,6},{3,7},{4,0},{5,1},{6,2},{7,3},{8,12},{9,13},{10,... | collective-permute-start | bytes 196616 | tf_op jit(solution)/shard_map/ppermute | solution.py:462
  16.9 8.5 %collective-permute-start.5 = (bf16[16,16,128]{2,1,0:T(8,128)(2,1)S(1)}, bf16[16,16,128]{2,1,0:T(8,128)(2,1)S(1)}, u32[]{:S(2)}, u32[]{:S(2)}) collective-permute-start(bf16[16,16,128]{2,1,0:T(8,128)(2,1)S(1)} %get-tuple-element.33), channel_id=1, source_target_pairs={{0,5},{1,4},{2,7},{3,6},{4,1},{5,0},{6,3},{7,2},{8,13},{9,12},{10,... | collective-permute-start | bytes 196616 | tf_op jit(solution)/shard_map/ppermute | solution.py:462
  21.2 5.3 %collective-permute-start.6 = (bf16[16,16,128]{2,1,0:T(8,128)(2,1)S(1)}, bf16[16,16,128]{2,1,0:T(8,128)(2,1)S(1)}, u32[]{:S(2)}, u32[]{:S(2)}) collective-permute-start(bf16[16,16,128]{2,1,0:T(8,128)(2,1)S(1)} %get-tuple-element.34), channel_id=1, source_target_pairs={{0,6},{1,7},{2,4},{3,5},{4,2},{5,3},{6,0},{7,1},{8,14},{9,15},{10,... | collective-permute-start | bytes 196616 | tf_op jit(solution)/shard_map/ppermute | solution.py:462
  22.9 5.2 %collective-permute-start.7 = (bf16[16,16,128]{2,1,0:T(8,128)(2,1)S(1)}, bf16[16,16,128]{2,1,0:T(8,128)(2,1)S(1)}, u32[]{:S(2)}, u32[]{:S(2)}) collective-permute-start(bf16[16,16,128]{2,1,0:T(8,128)(2,1)S(1)} %get-tuple-element.35), channel_id=1, source_target_pairs={{0,7},{1,6},{2,5},{3,4},{4,3},{5,2},{6,1},{7,0},{8,15},{9,14},{10,... | collective-permute-start | bytes 196616 | tf_op jit(solution)/shard_map/ppermute | solution.py:462
  36.8 12.8 %all-to-all-start.1 = ((bf16[32,16,128]{2,1,0:T(8,128)(2,1)}), bf16[32,16,128]{2,1,0:T(8,128)(2,1)S(1)}, u32[]{:S(2)}, u32[]{:S(2)}) async-start(bf16[32,16,128]{2,1,0:T(8,128)(2,1)} %get-tuple-element.36), calls=%async_computation.1 | async-start | bytes 262144 | tf_op jit(solution)/shard_map/all_to_all | solution.py:572
  41.2 4.7 %collective-permute-start.8 = (bf16[2,2,16,128]{3,2,1,0:T(8,128)(2,1)S(1)}, bf16[2,2,16,128]{3,2,1,0:T(8,128)(2,1)S(1)}, u32[]{:S(2)}, u32[]{:S(2)}) collective-permute-start(bf16[2,2,16,128]{3,2,1,0:T(8,128)(2,1)S(1)} %get-tuple-element.37), channel_id=1, source_target_pairs={{0,6},{2,4},{4,2},{6,0},{1,7},{3,5},{5,3},{7,1},{8,14},{10,12},{12... | collective-permute-start | bytes 49160 | tf_op jit(solution)/shard_map/ppermute | solution.py:462
  43.9 3.8 %collective-permute-start.9 = (bf16[2,2,16,128]{3,2,1,0:T(8,128)(2,1)S(1)}, bf16[2,2,16,128]{3,2,1,0:T(8,128)(2,1)S(1)}, u32[]{:S(2)}, u32[]{:S(2)}) collective-permute-start(bf16[2,2,16,128]{3,2,1,0:T(8,128)(2,1)S(1)} %get-tuple-element.38), channel_id=1, source_target_pairs={{0,4},{2,6},{4,0},{6,2},{1,5},{3,7},{5,1},{7,3},{8,12},{10,14},{12... | collective-permute-start | bytes 49160 | tf_op jit(solution)/shard_map/ppermute | solution.py:462
  44.5 3.7 %collective-permute-start.10 = (bf16[2,2,16,128]{3,2,1,0:T(8,128)(2,1)S(1)}, bf16[2,2,16,128]{3,2,1,0:T(8,128)(2,1)S(1)}, u32[]{:S(2)}, u32[]{:S(2)}) collective-permute-start(bf16[2,2,16,128]{3,2,1,0:T(8,128)(2,1)S(1)} %get-tuple-element.39), channel_id=1, source_target_pairs={{0,2},{2,0},{4,6},{6,4},{1,3},{3,1},{5,7},{7,5},{8,10},{10,8},{12,... | collective-permute-start | bytes 49160 | tf_op jit(solution)/shard_map/ppermute | solution.py:462
  49.6 1.3 %collective-permute-start.11 = (bf16[8,16,128]{2,1,0:T(8,128)(2,1)S(1)}, bf16[8,16,128]{2,1,0:T(8,128)(2,1)S(1)}, u32[]{:S(2)}, u32[]{:S(2)}) collective-permute-start(bf16[8,16,128]{2,1,0:T(8,128)(2,1)S(1)} %shard_map.115.mine), channel_id=1, source_target_pairs={{0,1},{1,0},{2,3},{3,2},{4,5},{5,4},{6,7},{7,6},{8,9},{9,8},{10,11... | collective-permute-start | bytes 98312 | tf_op jit(solution)/shard_map/ppermute | solution.py:462
  60.3 6.7 %collective-permute-start.14 = (bf16[224,128]{1,0:T(8,128)(2,1)S(1)}, bf16[224,128]{1,0:T(8,128)(2,1)S(1)}, u32[]{:S(2)}, u32[]{:S(2)}) collective-permute-start(bf16[224,128]{1,0:T(8,128)(2,1)S(1)} %shard_map.117.rest_0_), channel_id=1, source_target_pairs={{0,24},{8,16},{16,8},{24,0},{1,25},{9,17},{17,9},{25,1},{2,26},{10... | collective-permute-start | bytes 172040 | tf_op jit(solution)/shard_map/ppermute | solution.py:462
  62.5 5.7 %collective-permute-start.13 = (bf16[224,128]{1,0:T(8,128)(2,1)S(1)}, bf16[224,128]{1,0:T(8,128)(2,1)S(1)}, u32[]{:S(2)}, u32[]{:S(2)}) collective-permute-start(bf16[224,128]{1,0:T(8,128)(2,1)S(1)} %shard_map.117.rest_0_), channel_id=1, source_target_pairs={{0,16},{8,24},{16,0},{24,8},{1,17},{9,25},{17,1},{25,9},{2,18},{10... | collective-permute-start | bytes 172040 | tf_op jit(solution)/shard_map/ppermute | solution.py:462
  62.5 5.7 %collective-permute-start.12 = (bf16[224,128]{1,0:T(8,128)(2,1)S(1)}, bf16[224,128]{1,0:T(8,128)(2,1)S(1)}, u32[]{:S(2)}, u32[]{:S(2)}) collective-permute-start(bf16[224,128]{1,0:T(8,128)(2,1)S(1)} %shard_map.117.rest_0_), channel_id=1, source_target_pairs={{0,8},{8,0},{16,24},{24,16},{1,9},{9,1},{17,25},{25,17},{2,10},{10... | collective-permute-start | bytes 172040 | tf_op jit(solution)/shard_map/ppermute | solution.py:462

commit v6 on v5

--- a/solution.py
+++ b/solution.py
@@ -154,17 +154,13 @@
     def put_late(index, _):
         dest, slot, local = routes[1, index], routes[2, index], routes[3, index]
 
-        def store(lanes):
-            for head in range(heads):
-                columns = slice(head * LANES, (head + 1) * LANES)
-                far_out[head * groups + dest, 2 * CAP + slot] = qbuf[local, :, columns]
-                far_out[head * groups + dest, CAP * 3, :, lanes] = abuf[local, :, lanes]
-
-        each_half(slot, store)
+        for head in range(heads):
+            columns = slice(head * LANES, (head + 1) * LANES)
+            far_out[head * groups + dest, 2 * CAP + slot] = qbuf[local, :, columns]
         return 0
 
     lax.fori_loop(0, routes[0, 0], put_late, 0)
-    late = send(2 * CAP, CAP + 1, 1)
+    late = send(2 * CAP, CAP, 1)
     rest_out = [
         pltpu.make_async_copy(qbuf, queries_hbm, out_sems.at[2]),
         pltpu.make_async_copy(abuf, adapter_hbm, out_sems.at[3]),
@@ -181,7 +177,7 @@
 
 def pack_own_kernel(dims, plan, keys, vals, grad, queries, adapter, feat, *outs):
     groups, blocks, heads, rows, live = dims
-    own_outs, feat_out = outs[:heads], outs[heads]
+    own_outs, feat_out, adapter_out = outs[:heads], outs[heads], outs[heads + 1]
     for chip in range(heads // CORES):
         feat_out[chip] = feat[:, core_columns(chip, 1 - lax.axis_index("core"))]
     extras = live - CAP
@@ -190,6 +186,13 @@
     sources = (keys, vals, queries)
 
     def put(dest, slot, local):
+        @pl.when(slot < CAP)
+        def _():
+            def store(lanes):
+                adapter_out[dest, :, lanes] = adapter[local, :, lanes]
+
+            each_half(slot, store)
+
         @pl.when(slot >= CAP)
         def _():
             extra = slot - CAP
@@ -212,24 +215,22 @@
             own_outs[turn][extras * 3 + position] = grad[position, :, columns]
 
 
-def attend_kernel(dims, plan, seg, up, far_in, *rest):
+def attend_kernel(dims, plan, seg, up, adapter, far_in, *rest):
     groups, blocks, heads, rows, live = dims
     chips = heads // CORES
+    core = lax.axis_index("core")
     own_ins = rest[:heads]
     part_hbm = rest[heads + 1]
     own_parts = rest[heads + 2 : heads + 2 + chips]
-    up_out, log_hbm, part_out, log_out, routes, sems, qs, ks, vs, gs, ads, dqs, parts = rest[
+    dqs, log_hbm, part_out, log_out, routes, sems, qs, ks, vs, gs, parts = rest[
         heads + 2 + chips :
     ]
     extras = live - CAP
     me = lax.axis_index("dp")
     seq = seq_index()
-    rank = up.shape[0]
     length = seg.shape[1]
     reach = live * LANES
     scaling = 1.0 / math.sqrt(LANES)
-
-    ads[...] = jnp.zeros_like(ads)
 
     def take(position, group, slot):
         routes[0, position] = group
@@ -245,29 +246,14 @@
                 vs[where, :] = far_in[index, CAP + slot]
                 qs[where, :] = far_in[index, 2 * CAP + slot]
 
-            def store(lanes):
-                for part in range(heads):
-                    where = row_tile(position * heads + part, rows)
-                    ads[where, lanes] = far_in[part * groups + group, CAP * 3, :, lanes]
-
-            each_half(slot, store)
-
         @pl.when(jnp.logical_not(far))
         def _():
             extra = slot - CAP
-            pair = extras * 3 + live + quotient(extra, 2)
             for turn in range(heads):
                 where = row_tile(position * heads + (seq ^ turn), rows)
                 ks[where, :] = own_ins[turn][extra]
                 vs[where, :] = own_ins[turn][extras + extra]
                 qs[where, :] = own_ins[turn][2 * extras + extra]
-
-            def store(lanes):
-                for turn in range(heads):
-                    where = row_tile(position * heads + (seq ^ turn), rows)
-                    ads[where, lanes] = own_ins[turn][pair, :, lanes]
-
-            each_half(slot, store)
 
     each_block(plan, me, blocks, live, take)
     for turn in range(heads):
@@ -324,9 +310,10 @@
         @pl.when(far)
         def _():
             def store(lanes):
-                for part in range(heads):
-                    where = row_tile(position * heads + part, rows)
-                    part_out[part * groups + group, :, lanes] = parts[where, lanes]
+                for turn in range(heads):
+                    chip, side = turn // CORES, turn % CORES
+                    where = row_tile(position * heads + chip * CORES + (core ^ side), rows)
+                    part_out[chip * groups + group, side, :, lanes] = parts[where, lanes]
 
             each_half(slot, store)
 
@@ -344,10 +331,11 @@
         return 0
 
     lax.fori_loop(0, live, put, 0)
+    for chip in range(chips):
+        for group in range(groups):
+            part_out[chip * groups + group, CORES] = adapter[group]
     part_copy = pltpu.make_async_copy(part_out, part_hbm, sems.at[1])
     part_copy.start()
-    up_part = jnp.dot(dquery_all, ads[...], preferred_element_type=jnp.float32)
-    up_out[...] = (up_part + swap_halves(up_part)).T[:rank].astype(jnp.bfloat16)
     log_copy.wait()
     part_copy.wait()
 
@@ -355,7 +343,9 @@
 def head_sum_kernel(parts, *refs):
     extras, out = refs[:-1], refs[-1]
     pairs = extras[0].shape[1]
-    groups = out.shape[0] - CORES * pairs
+    peers = parts.shape[0]
+    tiles = (out.shape[0] - peers) // CORES
+    groups = tiles - pairs
 
     def total(terms):
         value = terms[0].astype(jnp.float32)
@@ -363,25 +353,59 @@
             value = value + term.astype(jnp.float32)
         return value.astype(jnp.bfloat16)
 
-    for group in range(groups):
-        out[group] = total([parts[peer] for peer in range(group, parts.shape[0], groups)])
-    for core in range(CORES):
+    for side in range(CORES):
+        for group in range(groups):
+            out[side * tiles + group] = total(
+                [parts[peer, side] for peer in range(group, peers, groups)]
+            )
         for pair in range(pairs):
-            out[groups + core * pairs + pair] = total([extra[core, pair] for extra in extras])
-
-
-def product_kernel(dims, plan, feat, feat_other, mine, other, out, sums, grads):
+            out[side * tiles + groups + pair] = total([extra[side, pair] for extra in extras])
+    for peer in range(peers):
+        out[CORES * tiles + peer] = parts[peer, CORES]
+
+
+def product_kernel(dims, plan, feat, feat_other, mine, other, dquery, *rest):
     groups, blocks, heads, rows, live = dims
+    own_ins = rest[:heads]
+    out, up_out, sums, grads, ads = rest[heads:]
+    extras = live - CAP
     me = lax.axis_index("dp")
     core = lax.axis_index("core")
-    pairs = sums.shape[1] - groups
-    for owner, (tiles, partner) in enumerate(((mine, other), (other, mine))):
-        for group in range(groups):
-            sums[owner, group] = tiles[group].astype(jnp.float32)
-        for index in range(groups, groups + pairs):
-            sums[owner, index] = tiles[index].astype(jnp.float32) + partner[index + pairs].astype(
-                jnp.float32
-            )
+    seq = seq_index()
+    tiles = sums.shape[1]
+    ads[...] = jnp.zeros_like(ads)
+
+    def take(position, group, slot):
+        far = (group != me) | (slot < CAP)
+
+        @pl.when(far)
+        def _():
+            def store(lanes):
+                for chip in range(heads // CORES):
+                    tile = CORES * tiles + chip * groups + group
+                    for source, which in ((mine, core), (other, 1 - core)):
+                        where = row_tile(position * heads + chip * CORES + which, rows)
+                        ads[where, lanes] = source[tile, :, lanes]
+
+            each_half(slot, store)
+
+        @pl.when(jnp.logical_not(far))
+        def _():
+            pair = extras * 3 + live + quotient(slot - CAP, 2)
+
+            def store(lanes):
+                for turn in range(heads):
+                    where = row_tile(position * heads + (seq ^ turn), rows)
+                    ads[where, lanes] = own_ins[turn][pair, :, lanes]
+
+            each_half(slot, store)
+
+    each_block(plan, me, blocks, live, take)
+    up_part = jnp.dot(dquery[...], ads[...], preferred_element_type=jnp.float32)
+    up_out[...] = (up_part + swap_halves(up_part)).T[: up_out.shape[0]].astype(jnp.bfloat16)
+    for index in range(tiles):
+        sums[0, index] = mine[index].astype(jnp.float32) + other[tiles + index].astype(jnp.float32)
+        sums[1, index] = other[index].astype(jnp.float32) + mine[tiles + index].astype(jnp.float32)
     grads[...] = jnp.zeros_like(grads)
 
     def put(dest, slot, local):
@@ -391,17 +415,13 @@
 
     each_hit(plan, me, groups, blocks, live, put)
     low = low_lanes(HALF // 2)
-    columns = [
-        grads[owner].reshape(blocks * rows, LANES).T[:HALF].astype(jnp.bfloat16)
-        for owner in range(CORES)
-    ]
+    columns = grads[...].reshape(CORES * blocks * rows, LANES).T[:HALF].astype(jnp.bfloat16)
     even = core == 0
     for chip in range(heads // CORES):
-        tiles = jnp.dot(
-            columns[0], feat[:, core_columns(chip, core)], preferred_element_type=jnp.float32
-        ) + jnp.dot(columns[1], feat_other[chip], preferred_element_type=jnp.float32)
+        features = jnp.concatenate([feat[:, core_columns(chip, core)], feat_other[chip]], axis=0)
+        product = jnp.dot(columns, features, preferred_element_type=jnp.float32)
         first, second, third = (
-            tiles[:, index * LANES : (index + 1) * LANES] for index in range(3)
+            product[:, index * LANES : (index + 1) * LANES] for index in range(3)
         )
         shared = jnp.where(even, third, first)
         upper, lower = shared[: HALF // 2], shared[HALF // 2 :]
@@ -489,7 +509,7 @@
     peers = groups * heads
     everyone = SEQ + ("dp",)
     flat = features[0].reshape(blocks * rows, width)
-    far_shape = (peers, CAP * 3 + 1, rows, LANES)
+    far_shape = (peers, CAP * 3, rows, LANES)
     own_shape = (extras * 3 + live + pairs, rows, LANES)
     rows_shape = (blocks, rows, heads * LANES)
 
@@ -526,7 +546,8 @@
     )
     own_send = call(
         functools.partial(pack_own_kernel, dims),
-        [(own_shape, bf16)] * heads + [((chips, blocks * rows, 3 * LANES), bf16)],
+        [(own_shape, bf16)] * heads
+        + [((chips, blocks * rows, 3 * LANES), bf16), ((groups, rows, LANES), bf16)],
         [SMEM] + [VMEM] * 6,
         [],
         0,
@@ -540,27 +561,28 @@
         flat,
     )
     feat_other = exchange(own_send[heads], "core", CORES, 1)
-    own = [own_send[0]] + [exchange(own_send[turn], SEQ, heads, turn) for turn in range(1, heads)]
+    own = [exchange(own_send[turn], SEQ, heads, turn) for turn in range(heads - 1, 0, -1)]
+    own = [own_send[0]] + own[::-1]
     far = lax.all_to_all(far_send, everyone, 0, 0, tiled=True)
     attended = call(
         functools.partial(attend_kernel, dims),
-        [((peers, rows, LANES), bf16)]
-        + [((CORES, pairs, rows, LANES), bf16)] * (heads // CORES)
-        + [((rank, LANES), bf16), ((1, 1, length), f32)],
-        [SMEM] + [VMEM] * (3 + heads) + [ANY],
+        [((chips * groups, CORES + 1, rows, LANES), bf16)]
+        + [((CORES, pairs, rows, LANES), bf16)] * chips
+        + [((LANES, reach), bf16), ((1, 1, length), f32)],
+        [SMEM] + [VMEM] * (4 + heads) + [ANY],
         [
-            pltpu.VMEM((peers, rows, LANES), bf16),
+            pltpu.VMEM((chips * groups, CORES + 1, rows, LANES), bf16),
             pltpu.VMEM((1, 1, length), f32),
             pltpu.SMEM((2, live), jnp.int32),
             pltpu.SemaphoreType.DMA((2,)),
         ]
-        + [pltpu.VMEM((reach, LANES), bf16)] * 5
-        + [pltpu.VMEM((LANES, reach), bf16), pltpu.VMEM((reach, LANES), bf16)],
+        + [pltpu.VMEM((reach, LANES), bf16)] * 5,
         600_000_000,
         3_000_000,
         source_block_plan,
         segments,
         adapter_up_weight,
+        own_send[heads + 1],
         far,
         *own,
         feat_other,
@@ -569,12 +591,12 @@
     own_parts = [
         exchange(attended[1 + turn], "chip", chips, turn) for turn in range(chips - 1, 0, -1)
     ]
-    part = lax.all_to_all(attended[0], everyone, 0, 0, tiled=True)
-    up_part, log_norm = attended[1 + chips :]
-    tiles = groups + CORES * pairs
+    part = lax.all_to_all(attended[0], ("chip", "dp"), 0, 0, tiled=True)
+    dquery, log_norm = attended[1 + chips :]
+    tiles = groups + pairs
     (mine,) = call(
         head_sum_kernel,
-        [((tiles, rows, LANES), bf16)],
+        [((CORES * tiles + chips * groups, rows, LANES), bf16)],
         [VMEM] * (1 + chips),
         [],
         0,
@@ -583,21 +605,24 @@
         *own_parts,
         attended[1],
     )
-    (shares,) = call(
+    shares, up_part = call(
         functools.partial(product_kernel, dims),
-        [((chips, HALF * 5 // 2, LANES), bf16)],
-        [SMEM] + [VMEM] * 4,
+        [((chips, HALF * 5 // 2, LANES), bf16), ((rank, LANES), bf16)],
+        [SMEM] + [VMEM] * (5 + heads),
         [
-            pltpu.VMEM((CORES, groups + pairs, rows, LANES), f32),
+            pltpu.VMEM((CORES, tiles, rows, LANES), f32),
             pltpu.VMEM((CORES, blocks, rows, LANES), f32),
+            pltpu.VMEM((reach, LANES), bf16),
         ],
-        40_000_000,
+        60_000_000,
         2_000_000,
         source_block_plan,
         flat,
         feat_other,
         mine,
         exchange(mine, "core", CORES, 1),
+        dquery,
+        *own,
     )
     shares = lax.all_to_all(shares, "chip", 0, 0, tiled=True)
     (joined,) = call(

time: 69.2 us -> 68.7 us (level)
  waiting for transfers between devices: 22.8 us -> 18.5 us
  starting transfers between devices: 26.9 us -> 29.1 us
  local copies, waits for them, and re-layouts: 0.66 us -> 1.62 us
    all_to_all x1, waiting for transfers between devices: 5.42 us -> 1.62 us  [per_device_tiles(): far = lax.all_to_all(far_send, everyone, 0, 0, tiled=True)]
    ppermute x15, starting transfers between devices: 15.2 us -> 16.4 us  [exchange(): lax.ppermute(value, axis, [(peer, peer ^ turn) for peer in range(size)])]
    ppermute x15, waiting for transfers between devices: 16 us -> 14.9 us  [exchange(): lax.ppermute(value, axis, [(peer, peer ^ turn) for peer in range(size)])]
    all_to_all x1, starting transfers between devices: 4.41 us -> 5.42 us  [per_device_tiles(): part = lax.all_to_all(attended[0], ('chip', 'dp'), 0, 0, tiled=True)]
    unnamed x18, local copies, waits for them, and re-layouts: 0.66 us -> 1.62 us
  transfers between devices with their start and end apart: 17 -> 17, of which waited for: 13 -> 11; matrix products, arithmetic and copies ran while one was open for 0% -> 0% of each run, Pallas kernels for 2% -> 2%
where the time goes in v6:
time: 68.7 us; the launch traced here: 68.3 us
  starting transfers between devices  29.1 us (42%)
  waiting for transfers between devices  18.5 us (27%)
  Pallas kernels  10.4 us (15%)
  blocking collectives  7.88 us (11%)
  local copies, waits for them, and re-layouts  1.62 us (2%)
  between operations  0.79 us (1%)
    ppermute x15, starting transfers between devices, exchange(): lax.ppermute(value, axis, [(peer, peer ^ turn) for peer in range(size)])  16.4 us
    ppermute x15, waiting for transfers between devices, exchange(): lax.ppermute(value, axis, [(peer, peer ^ turn) for peer in range(size)])  14.9 us
    pallas_call x7, Pallas kernels, call(): pl.pallas_call(kernel, out_shape=shapes, in_specs=specs, out_specs=out_sp...  10.4 us
    all_to_all x1, blocking collectives, per_device_tiles(): shares = lax.all_to_all(shares, 'chip', 0, 0, tiled=True)  7.88 us
    all_to_all x1, starting transfers between devices, per_device_tiles(): far = lax.all_to_all(far_send, everyone, 0, 0, tiled=True)  7.26 us
    all_to_all x1, starting transfers between devices, per_device_tiles(): part = lax.all_to_all(attended[0], ('chip', 'dp'), 0, 0, tiled=True)  5.42 us
    all_to_all x1, waiting for transfers between devices, per_device_tiles(): part = lax.all_to_all(attended[0], ('chip', 'dp'), 0, 0, tiled=True)  1.97 us
    unnamed x18, local copies, waits for them, and re-layouts  1.62 us
  transfers between devices with their start and end apart: 17, of which 11 were waited for; matrix products, arithmetic and copies ran while one was open for 0% of the time, Pallas kernels for 2%

profile of v6, /device:TPU:0, one launch (start us, length us, event | category | flops | bytes accessed | tf_op | source)
XLA Modules:
  0.0 68.3 jit_solution(16103839123255058469)
XLA Ops:
  0.6 3.1 %shard_map.112 = (bf16[32,6,16,128]{3,2,1,0:T(8,128)(2,1)}, bf16[8,16,1024]{2,1,0:T(8,128)(2,1)}, bf16[8,16,128]{2,1,0:T(8,128)(2,1)}) custom-call(s32[4,8]{1,0:T(4,128)} %plan.5, bf16[128,2560]{1,0:T(8,128)(2,1)} %bitcast.7, bf16[8,16,1024]{2,1,0:T(8,128)(2,1)} %bitcast.16, bf16[8,16,1024]{2,1,0:T(8,128)(2,1)} %bitcast.10, bf16[8,16,1024]{2,1,0:T(8,128)(2,1)} %bitcast.12, ...), custom_call_target="tpu_custom_call" | custom-call | flops 60000000 | bytes 4000000 | tf_op jit(solution)/shard_map/pallas_call | solution.py:470
  3.7 0.0 copy-start
  3.7 0.0 copy-start.1
  3.7 0.0 copy-start.2
  3.8 0.0 copy-start.3
  3.8 0.0 copy-start.6
  3.8 7.3 %all-to-all-start = ((bf16[32,6,16,128]{3,2,1,0:T(8,128)(2,1)}), bf16[32,6,16,128]{3,2,1,0:T(8,128)(2,1)S(1)}, u32[]{:S(2)}, u32[]{:S(2)}) async-start(bf16[32,6,16,128]{3,2,1,0:T(8,128)(2,1)} %get-tuple-element.31), calls=%async_computation | async-start | bytes 1572864 | tf_op jit(solution)/shard_map/all_to_all | solution.py:566
  11.0 0.0 copy-start.7
  11.1 0.6 copy-done.7
  11.7 0.9 %copy-done.4 = bf16[8,16,1024]{2,1,0:T(8,128)(2,1)S(1)} copy-done((bf16[8,16,1024]{2,1,0:T(8,128)(2,1)S(1)}, bf16[8,16,1024]{2,1,0:T(8,128)(2,1)}, u32[]{:S(2)}) %copy-start.4) | copy-done | bytes 262168
  12.7 1.2 %shard_map.113 = (bf16[16,16,128]{2,1,0:T(8,128)(2,1)S(1)}, bf16[16,16,128]{2,1,0:T(8,128)(2,1)S(1)}, bf16[16,16,128]{2,1,0:T(8,128)(2,1)S(1)}, bf16[16,16,128]{...) custom-call(s32[4,8]{1,0:T(4,128)S(1)} %copy-done.7, ...), custom_call_target="tpu_custom_call" | custom-call | bytes 1600000 | tf_op jit(solution)/shard_map/pallas_call | solution.py:470
  13.9 0.3 collective-permute-start
  14.2 0.3 collective-permute-start.1
  14.5 1.8 %collective-permute-start.2 = (bf16[16,16,128]{2,1,0:T(8,128)(2,1)S(1)}, bf16[16,16,128]{2,1,0:T(8,128)(2,1)S(1)}, u32[]{:S(2)}, u32[]{:S(2)}) collective-permute-start(bf16[16,16,128]{2,1,0:T(8,128)(2,1)S(1)} %get-tuple-element.34), channel_id=1, source_target_pairs={{0,2},{1,3},{2,0},{3,1},{4,6},{5,7},{6,4},{7,5},{8,10},{9,11},{10,... | collective-permute-start | bytes 196616 | tf_op jit(solution)/shard_map/ppermute | solution.py:482
  16.3 0.0 collective-permute-start.3
  16.3 1.5 %collective-permute-start.4 = (bf16[16,16,128]{2,1,0:T(8,128)(2,1)S(1)}, bf16[16,16,128]{2,1,0:T(8,128)(2,1)S(1)}, u32[]{:S(2)}, u32[]{:S(2)}) collective-permute-start(bf16[16,16,128]{2,1,0:T(8,128)(2,1)S(1)} %get-tuple-element.36), channel_id=1, source_target_pairs={{0,4},{1,5},{2,6},{3,7},{4,0},{5,1},{6,2},{7,3},{8,12},{9,13},{10,... | collective-permute-start | bytes 196616 | tf_op jit(solution)/shard_map/ppermute | solution.py:482
  17.8 0.0 collective-permute-done.1.rest_1_
  17.8 0.3 collective-permute-start.5
  18.1 2.4 %collective-permute-done.2.rest_2_ = bf16[16,16,128]{2,1,0:T(8,128)(2,1)S(1)} collective-permute-done((bf16[16,16,128]{2,1,0:T(8,128)(2,1)S(1)}, bf16[16,16,128]{2,1,0:T(8,128)(2,1)S(1)}, u32[]{:S(2)}, u32[]{:S(2)}) %collective-permute-start.2) | collective-permute-done | bytes 65568 | tf_op jit(solution)/shard_map/ppermute | solution.py:482
  20.5 2.9 %collective-permute-start.6 = (bf16[16,16,128]{2,1,0:T(8,128)(2,1)S(1)}, bf16[16,16,128]{2,1,0:T(8,128)(2,1)S(1)}, u32[]{:S(2)}, u32[]{:S(2)}) collective-permute-start(bf16[16,16,128]{2,1,0:T(8,128)(2,1)S(1)} %get-tuple-element.38), channel_id=1, source_target_pairs={{0,6},{1,7},{2,4},{3,5},{4,2},{5,3},{6,0},{7,1},{8,14},{9,15},{10,... | collective-permute-start | bytes 196616 | tf_op jit(solution)/shard_map/ppermute | solution.py:482
  23.4 0.0 collective-permute-done.3.rest_3_
  23.4 1.2 %collective-permute-start.7 = (bf16[16,16,128]{2,1,0:T(8,128)(2,1)S(1)}, bf16[16,16,128]{2,1,0:T(8,128)(2,1)S(1)}, u32[]{:S(2)}, u32[]{:S(2)}) collective-permute-start(bf16[16,16,128]{2,1,0:T(8,128)(2,1)S(1)} %get-tuple-element.39), channel_id=1, source_target_pairs={{0,7},{1,6},{2,5},{3,4},{4,3},{5,2},{6,1},{7,0},{8,15},{9,14},{10,... | collective-permute-start | bytes 196616 | tf_op jit(solution)/shard_map/ppermute | solution.py:482
  24.6 0.0 collective-permute-done.4.rest_4_
  24.6 0.0 collective-permute-done.5.rest_5_
  24.6 1.2 %collective-permute-done.6.rest_6_ = bf16[16,16,128]{2,1,0:T(8,128)(2,1)S(1)} collective-permute-done((bf16[16,16,128]{2,1,0:T(8,128)(2,1)S(1)}, bf16[16,16,128]{2,1,0:T(8,128)(2,1)S(1)}, u32[]{:S(2)}, u32[]{:S(2)}) %collective-permute-start.6) | collective-permute-done | bytes 65568 | tf_op jit(solution)/shard_map/ppermute | solution.py:482
  25.8 3.3 %collective-permute-done.7.rest_7_ = bf16[16,16,128]{2,1,0:T(8,128)(2,1)S(1)} collective-permute-done((bf16[16,16,128]{2,1,0:T(8,128)(2,1)S(1)}, bf16[16,16,128]{2,1,0:T(8,128)(2,1)S(1)}, u32[]{:S(2)}, u32[]{:S(2)}) %collective-permute-start.7) | collective-permute-done | bytes 65568 | tf_op jit(solution)/shard_map/ppermute | solution.py:482
  29.0 0.0 collective-permute-done.rest_8_.feat_other
  29.0 1.6 %all-to-all-done.far_in = bf16[32,6,16,128]{3,2,1,0:T(8,128)(2,1)S(1)} async-done(((bf16[32,6,16,128]{3,2,1,0:T(8,128)(2,1)}), bf16[32,6,16,128]{3,2,1,0:T(8,128)(2,1)S(1)}, u32[]{:S(2)}, u32[]{:S(2)}) %all-to-all-start) | async-done | bytes 786464 | tf_op jit(solution)/shard_map/all_to_all | solution.py:566
  30.7 3.2 %shard_map.114 = (bf16[16,3,16,128]{3,2,1,0:T(8,128)(2,1)}, bf16[2,2,16,128]{3,2,1,0:T(8,128)(2,1)S(1)}, bf16[2,2,16,128]{3,2,1,0:T(8,128)(2,1)S(1)}, bf16[2,2,1...) custom-call(s32[4,8]{1,0:T(4,128)S(1)} %copy-done.7, ...), custom_call_target="tpu_custom_call" | custom-call | flops 600000000 | bytes 3000000 | tf_op jit(solution)/shard_map/pallas_call | solution.py:470
  33.9 5.4 %all-to-all-start.1 = ((bf16[16,3,16,128]{3,2,1,0:T(8,128)(2,1)}), bf16[16,3,16,128]{3,2,1,0:T(8,128)(2,1)S(1)}, u32[]{:S(2)}, u32[]{:S(2)}) async-start(bf16[16,3,16,128]{3,2,1,0:T(8,128)(2,1)} %get-tuple-element.40), calls=%async_computation.1 | async-start | bytes 393216 | tf_op jit(solution)/shard_map/all_to_all | solution.py:594
  39.3 2.8 %collective-permute-start.8 = (bf16[2,2,16,128]{3,2,1,0:T(8,128)(2,1)S(1)}, bf16[2,2,16,128]{3,2,1,0:T(8,128)(2,1)S(1)}, u32[]{:S(2)}, u32[]{:S(2)}) collective-permute-start(bf16[2,2,16,128]{3,2,1,0:T(8,128)(2,1)S(1)} %get-tuple-element.41), channel_id=1, source_target_pairs={{0,6},{2,4},{4,2},{6,0},{1,7},{3,5},{5,3},{7,1},{8,14},{10,12},{12... | collective-permute-start | bytes 49160 | tf_op jit(solution)/shard_map/ppermute | solution.py:482
  42.1 0.6 collective-permute-start.9
  42.7 0.2 collective-permute-start.10
  42.9 1.5 %collective-permute-done.8.refs_0_ = bf16[2,2,16,128]{3,2,1,0:T(8,128)(2,1)S(1)} collective-permute-done((bf16[2,2,16,128]{3,2,1,0:T(8,128)(2,1)S(1)}, bf16[2,2,16,128]{3,2,1,0:T(8,128)(2,1)S(1)}, u32[]{:S(2)}, u32[]{:S(2)}) %collective-permute-start.8) | collective-permute-done | bytes 16416 | tf_op jit(solution)/shard_map/ppermute | solution.py:482
  44.3 1.7 %collective-permute-done.9.refs_1_ = bf16[2,2,16,128]{3,2,1,0:T(8,128)(2,1)S(1)} collective-permute-done((bf16[2,2,16,128]{3,2,1,0:T(8,128)(2,1)S(1)}, bf16[2,2,16,128]{3,2,1,0:T(8,128)(2,1)S(1)}, u32[]{:S(2)}, u32[]{:S(2)}) %collective-permute-start.9) | collective-permute-done | bytes 16416 | tf_op jit(solution)/shard_map/ppermute | solution.py:482
  46.0 0.5 collective-permute-done.10.refs_2_
  46.5 2.0 %all-to-all-done.1.parts = bf16[16,3,16,128]{3,2,1,0:T(8,128)(2,1)S(1)} async-done(((bf16[16,3,16,128]{3,2,1,0:T(8,128)(2,1)}), bf16[16,3,16,128]{3,2,1,0:T(8,128)(2,1)S(1)}, u32[]{:S(2)}, u32[]{:S(2)}) %all-to-all-start.1) | async-done | bytes 196640 | tf_op jit(solution)/shard_map/all_to_all | solution.py:594
  48.5 0.1 collective-permute-start.11
  48.6 1.3 %collective-permute-done.11.other = bf16[28,16,128]{2,1,0:T(8,128)(2,1)S(1)} collective-permute-done((bf16[28,16,128]{2,1,0:T(8,128)(2,1)S(1)}, bf16[28,16,128]{2,1,0:T(8,128)(2,1)S(1)}, u32[]{:S(2)}, u32[]{:S(2)}) %collective-permute-start.11) | collective-permute-done | bytes 114720 | tf_op jit(solution)/shard_map/ppermute | solution.py:482
  49.9 2.0 %shard_map.116 = (bf16[4,160,128]{2,1,0:T(8,128)(2,1)S(1)}, bf16[64,128]{1,0:T(8,128)(2,1)S(1)}) custom-call(s32[4,8]{1,0:T(4,128)S(1)} %copy-done.7, bf16[128,2560]{1,0:T(8,128)(2,1)S(1)} %bitcast.9, bf16[4,128,384]{2,1,0:T(8,128)(2,1)S(1)} %collective-permute-done.rest_8_.feat_other, bf16[28,16,128]{2,1,0:T(8,128)(2,1)S(1)} %shard_map.115.mine, ...), custom_call_target="tpu_custom_call" | custom-call | flops 60000000 | bytes 2000000 | tf_op jit(solution)/shard_map/pallas_call | solution.py:470
  51.9 7.9 %all_to_all.15.parts = bf16[4,160,128]{2,1,0:T(8,128)(2,1)S(1)} all-to-all(bf16[4,160,128]{2,1,0:T(8,128)(2,1)S(1)} %get-tuple-element.46), channel_id=1, replica_groups=mesh['dp'=4,'chip'=4,'core'=2] {'chip'}, dimensions={0} | all-to-all | bytes 327680 | tf_op jit(solution)/shard_map/all_to_all | solution.py:627
  59.8 1.3 %collective-permute-start.14 = (bf16[224,128]{1,0:T(8,128)(2,1)S(1)}, bf16[224,128]{1,0:T(8,128)(2,1)S(1)}, u32[]{:S(2)}, u32[]{:S(2)}) collective-permute-start(bf16[224,128]{1,0:T(8,128)(2,1)S(1)} %shard_map.117.rest_0_), channel_id=1, source_target_pairs={{0,24},{8,16},{16,8},{24,0},{1,25},{9,17},{17,9},{25,1},{2,26},{10... | collective-permute-start | bytes 172040 | tf_op jit(solution)/shard_map/ppermute | solution.py:482
  61.1 0.6 collective-permute-start.13
  61.7 2.6 %collective-permute-start.12 = (bf16[224,128]{1,0:T(8,128)(2,1)S(1)}, bf16[224,128]{1,0:T(8,128)(2,1)S(1)}, u32[]{:S(2)}, u32[]{:S(2)}) collective-permute-start(bf16[224,128]{1,0:T(8,128)(2,1)S(1)} %shard_map.117.rest_0_), channel_id=1, source_target_pairs={{0,8},{8,0},{16,24},{24,16},{1,9},{9,1},{17,25},{25,17},{2,10},{10... | collective-permute-start | bytes 172040 | tf_op jit(solution)/shard_map/ppermute | solution.py:482
  64.3 1.7 %collective-permute-done.14.rest_3_ = bf16[224,128]{1,0:T(8,128)(2,1)S(1)} collective-permute-done((bf16[224,128]{1,0:T(8,128)(2,1)S(1)}, bf16[224,128]{1,0:T(8,128)(2,1)S(1)}, u32[]{:S(2)}, u32[]{:S(2)}) %collective-permute-start.14) | collective-permute-done | bytes 57376 | tf_op jit(solution)/shard_map/ppermute | solution.py:482
  66.0 1.5 %collective-permute-done.13.rest_2_ = bf16[224,128]{1,0:T(8,128)(2,1)S(1)} collective-permute-done((bf16[224,128]{1,0:T(8,128)(2,1)S(1)}, bf16[224,128]{1,0:T(8,128)(2,1)S(1)}, u32[]{:S(2)}, u32[]{:S(2)}) %collective-permute-start.13) | collective-permute-done | bytes 57376 | tf_op jit(solution)/shard_map/ppermute | solution.py:482
  67.5 0.0 collective-permute-done.12.rest_1_
  67.5 0.8 %shard_map.118 = (f32[64,320]{1,0:T(8,128)}, f32[64,128]{1,0:T(8,128)}) custom-call(bf16[224,128]{1,0:T(8,128)(2,1)S(1)} %shard_map.117.rest_0_, bf16[224,128]{1,0:T(8,128)(2,1)S(1)} %collective-permute-done.12.rest_1_, bf16[224,128]{1,0:T(8,128)(2,1)S(1)} %collective-permute-done.13.rest_2_, bf16[224,128]{1,0:T(8,128)(2,1)S(1)} %collective-permute-done.14.rest_3_), custom_call_target="tpu_custom_call" | custom-call | bytes 400000 | tf_op jit(solution)/shard_map/pallas_call | solution.py:470
  (12 shorter events, 0.1 us)
Async XLA Ops:
  3.7 7.3 %copy-start = (bf16[1,8,16,2560]{3,2,1,0:T(8,128)(2,1)S(1)}, bf16[1,8,16,2560]{3,2,1,0:T(8,128)(2,1)}, u32[]{:S(2)}) copy-start(bf16[1,8,16,2560]{3,2,1,0:T(8,128)(2,1)} %param.9) | copy-start | bytes 1966084
  3.7 7.3 %copy-start.1 = (bf16[1,8,16,1024]{3,2,1,0:T(8,128)(2,1)S(1)}, bf16[1,8,16,1024]{3,2,1,0:T(8,128)(2,1)}, u32[]{:S(2)}) copy-start(bf16[1,8,16,1024]{3,2,1,0:T(8,128)(2,1)} %param.11) | copy-start | bytes 786436
  3.7 7.3 %copy-start.2 = (bf16[1,8,16,1024]{3,2,1,0:T(8,128)(2,1)S(1)}, bf16[1,8,16,1024]{3,2,1,0:T(8,128)(2,1)}, u32[]{:S(2)}) copy-start(bf16[1,8,16,1024]{3,2,1,0:T(8,128)(2,1)} %param.12) | copy-start | bytes 786436
  3.8 7.3 %copy-start.3 = (bf16[1,8,16,1024]{3,2,1,0:T(8,128)(2,1)S(1)}, bf16[1,8,16,1024]{3,2,1,0:T(8,128)(2,1)}, u32[]{:S(2)}) copy-start(bf16[1,8,16,1024]{3,2,1,0:T(8,128)(2,1)} %param.13) | copy-start | bytes 786436
  3.8 7.3 %copy-start.6 = (bf16[8,16,128]{2,1,0:T(8,128)(2,1)S(1)}, bf16[8,16,128]{2,1,0:T(8,128)(2,1)}, u32[]{:S(2)}) copy-start(bf16[8,16,128]{2,1,0:T(8,128)(2,1)} %get-tuple-element.28.adapter) | copy-start | bytes 98308
  3.8 26.9 %all-to-all-start = ((bf16[32,6,16,128]{3,2,1,0:T(8,128)(2,1)}), bf16[32,6,16,128]{3,2,1,0:T(8,128)(2,1)S(1)}, u32[]{:S(2)}, u32[]{:S(2)}) async-start(bf16[32,6,16,128]{3,2,1,0:T(8,128)(2,1)} %get-tuple-element.31), calls=%async_computation | async-start | bytes 1572864 | tf_op jit(solution)/shard_map/all_to_all | solution.py:566
  11.0 0.7 %copy-start.7 = (s32[4,8]{1,0:T(4,128)S(1)}, s32[4,8]{1,0:T(4,128)}, u32[]{:S(2)}) copy-start(s32[4,8]{1,0:T(4,128)} %plan.5) | copy-start | bytes 388
  11.7 0.9 %copy-start.4 = (bf16[8,16,1024]{2,1,0:T(8,128)(2,1)S(1)}, bf16[8,16,1024]{2,1,0:T(8,128)(2,1)}, u32[]{:S(2)}) copy-start(bf16[8,16,1024]{2,1,0:T(8,128)(2,1)} %get-tuple-element.27.queries) | copy-start | bytes 786436
  12.7 18.0 %copy-start.5 = (bf16[64,1024]{1,0:T(8,128)(2,1)S(1)}, bf16[64,1024]{1,0:T(8,128)(2,1)}, u32[]{:S(2)}) copy-start(bf16[64,1024]{1,0:T(8,128)(2,1)} %up.1) | copy-start | bytes 393220
  13.9 15.1 %collective-permute-start = (bf16[4,128,384]{2,1,0:T(8,128)(2,1)S(1)}, bf16[4,128,384]{2,1,0:T(8,128)(2,1)S(1)}, u32[]{:S(2)}, u32[]{:S(2)}) collective-permute-start(bf16[4,128,384]{2,1,0:T(8,128)(2,1)S(1)} %get-tuple-element.29), channel_id=1, source_target_pairs={{0,1},{1,0},{2,3},{3,2},{4,5},{5,4},{6,7},{7,6},{8,9},{9,8},{10,11... | collective-permute-start | bytes 1179656 | tf_op jit(solution)/shard_map/ppermute | solution.py:482
  14.2 3.5 %collective-permute-start.1 = (bf16[16,16,128]{2,1,0:T(8,128)(2,1)S(1)}, bf16[16,16,128]{2,1,0:T(8,128)(2,1)S(1)}, u32[]{:S(2)}, u32[]{:S(2)}) collective-permute-start(bf16[16,16,128]{2,1,0:T(8,128)(2,1)S(1)} %get-tuple-element.33), channel_id=1, source_target_pairs={{0,1},{1,0},{2,3},{3,2},{4,5},{5,4},{6,7},{7,6},{8,9},{9,8},{10,11... | collective-permute-start | bytes 196616 | tf_op jit(solution)/shard_map/ppermute | solution.py:482
  14.5 6.0 %collective-permute-start.2 = (bf16[16,16,128]{2,1,0:T(8,128)(2,1)S(1)}, bf16[16,16,128]{2,1,0:T(8,128)(2,1)S(1)}, u32[]{:S(2)}, u32[]{:S(2)}) collective-permute-start(bf16[16,16,128]{2,1,0:T(8,128)(2,1)S(1)} %get-tuple-element.34), channel_id=1, source_target_pairs={{0,2},{1,3},{2,0},{3,1},{4,6},{5,7},{6,4},{7,5},{8,10},{9,11},{10,... | collective-permute-start | bytes 196616 | tf_op jit(solution)/shard_map/ppermute | solution.py:482
  16.3 7.1 %collective-permute-start.3 = (bf16[16,16,128]{2,1,0:T(8,128)(2,1)S(1)}, bf16[16,16,128]{2,1,0:T(8,128)(2,1)S(1)}, u32[]{:S(2)}, u32[]{:S(2)}) collective-permute-start(bf16[16,16,128]{2,1,0:T(8,128)(2,1)S(1)} %get-tuple-element.35), channel_id=1, source_target_pairs={{0,3},{1,2},{2,1},{3,0},{4,7},{5,6},{6,5},{7,4},{8,11},{9,10},{10,... | collective-permute-start | bytes 196616 | tf_op jit(solution)/shard_map/ppermute | solution.py:482
  16.3 8.4 %collective-permute-start.4 = (bf16[16,16,128]{2,1,0:T(8,128)(2,1)S(1)}, bf16[16,16,128]{2,1,0:T(8,128)(2,1)S(1)}, u32[]{:S(2)}, u32[]{:S(2)}) collective-permute-start(bf16[16,16,128]{2,1,0:T(8,128)(2,1)S(1)} %get-tuple-element.36), channel_id=1, source_target_pairs={{0,4},{1,5},{2,6},{3,7},{4,0},{5,1},{6,2},{7,3},{8,12},{9,13},{10,... | collective-permute-start | bytes 196616 | tf_op jit(solution)/shard_map/ppermute | solution.py:482
  17.8 12.9 %copy-start.8 = (s32[1,1024]{1,0:T(1,128)S(1)}, s32[1,1024]{1,0:T(1,128)}, u32[]{:S(2)}) copy-start(s32[1,1024]{1,0:T(1,128)} %seg.1) | copy-start | bytes 12292
  17.8 6.9 %collective-permute-start.5 = (bf16[16,16,128]{2,1,0:T(8,128)(2,1)S(1)}, bf16[16,16,128]{2,1,0:T(8,128)(2,1)S(1)}, u32[]{:S(2)}, u32[]{:S(2)}) collective-permute-start(bf16[16,16,128]{2,1,0:T(8,128)(2,1)S(1)} %get-tuple-element.37), channel_id=1, source_target_pairs={{0,5},{1,4},{2,7},{3,6},{4,1},{5,0},{6,3},{7,2},{8,13},{9,12},{10,... | collective-permute-start | bytes 196616 | tf_op jit(solution)/shard_map/ppermute | solution.py:482
  20.5 5.3 %collective-permute-start.6 = (bf16[16,16,128]{2,1,0:T(8,128)(2,1)S(1)}, bf16[16,16,128]{2,1,0:T(8,128)(2,1)S(1)}, u32[]{:S(2)}, u32[]{:S(2)}) collective-permute-start(bf16[16,16,128]{2,1,0:T(8,128)(2,1)S(1)} %get-tuple-element.38), channel_id=1, source_target_pairs={{0,6},{1,7},{2,4},{3,5},{4,2},{5,3},{6,0},{7,1},{8,14},{9,15},{10,... | collective-permute-start | bytes 196616 | tf_op jit(solution)/shard_map/ppermute | solution.py:482
  23.4 5.7 %collective-permute-start.7 = (bf16[16,16,128]{2,1,0:T(8,128)(2,1)S(1)}, bf16[16,16,128]{2,1,0:T(8,128)(2,1)S(1)}, u32[]{:S(2)}, u32[]{:S(2)}) collective-permute-start(bf16[16,16,128]{2,1,0:T(8,128)(2,1)S(1)} %get-tuple-element.39), channel_id=1, source_target_pairs={{0,7},{1,6},{2,5},{3,4},{4,3},{5,2},{6,1},{7,0},{8,15},{9,14},{10,... | collective-permute-start | bytes 196616 | tf_op jit(solution)/shard_map/ppermute | solution.py:482
  33.9 14.6 %all-to-all-start.1 = ((bf16[16,3,16,128]{3,2,1,0:T(8,128)(2,1)}), bf16[16,3,16,128]{3,2,1,0:T(8,128)(2,1)S(1)}, u32[]{:S(2)}, u32[]{:S(2)}) async-start(bf16[16,3,16,128]{3,2,1,0:T(8,128)(2,1)} %get-tuple-element.40), calls=%async_computation.1 | async-start | bytes 393216 | tf_op jit(solution)/shard_map/all_to_all | solution.py:594
  39.3 5.0 %collective-permute-start.8 = (bf16[2,2,16,128]{3,2,1,0:T(8,128)(2,1)S(1)}, bf16[2,2,16,128]{3,2,1,0:T(8,128)(2,1)S(1)}, u32[]{:S(2)}, u32[]{:S(2)}) collective-permute-start(bf16[2,2,16,128]{3,2,1,0:T(8,128)(2,1)S(1)} %get-tuple-element.41), channel_id=1, source_target_pairs={{0,6},{2,4},{4,2},{6,0},{1,7},{3,5},{5,3},{7,1},{8,14},{10,12},{12... | collective-permute-start | bytes 49160 | tf_op jit(solution)/shard_map/ppermute | solution.py:482
  42.1 3.9 %collective-permute-start.9 = (bf16[2,2,16,128]{3,2,1,0:T(8,128)(2,1)S(1)}, bf16[2,2,16,128]{3,2,1,0:T(8,128)(2,1)S(1)}, u32[]{:S(2)}, u32[]{:S(2)}) collective-permute-start(bf16[2,2,16,128]{3,2,1,0:T(8,128)(2,1)S(1)} %get-tuple-element.42), channel_id=1, source_target_pairs={{0,4},{2,6},{4,0},{6,2},{1,5},{3,7},{5,1},{7,3},{8,12},{10,14},{12... | collective-permute-start | bytes 49160 | tf_op jit(solution)/shard_map/ppermute | solution.py:482
  42.7 3.8 %collective-permute-start.10 = (bf16[2,2,16,128]{3,2,1,0:T(8,128)(2,1)S(1)}, bf16[2,2,16,128]{3,2,1,0:T(8,128)(2,1)S(1)}, u32[]{:S(2)}, u32[]{:S(2)}) collective-permute-start(bf16[2,2,16,128]{3,2,1,0:T(8,128)(2,1)S(1)} %get-tuple-element.43), channel_id=1, source_target_pairs={{0,2},{2,0},{4,6},{6,4},{1,3},{3,1},{5,7},{7,5},{8,10},{10,8},{12,... | collective-permute-start | bytes 49160 | tf_op jit(solution)/shard_map/ppermute | solution.py:482
  48.5 1.4 %collective-permute-start.11 = (bf16[28,16,128]{2,1,0:T(8,128)(2,1)S(1)}, bf16[28,16,128]{2,1,0:T(8,128)(2,1)S(1)}, u32[]{:S(2)}, u32[]{:S(2)}) collective-permute-start(bf16[28,16,128]{2,1,0:T(8,128)(2,1)S(1)} %shard_map.115.mine), channel_id=1, source_target_pairs={{0,1},{1,0},{2,3},{3,2},{4,5},{5,4},{6,7},{7,6},{8,9},{9,8},{10,11... | collective-permute-start | bytes 344072 | tf_op jit(solution)/shard_map/ppermute | solution.py:482
  59.8 6.2 %collective-permute-start.14 = (bf16[224,128]{1,0:T(8,128)(2,1)S(1)}, bf16[224,128]{1,0:T(8,128)(2,1)S(1)}, u32[]{:S(2)}, u32[]{:S(2)}) collective-permute-start(bf16[224,128]{1,0:T(8,128)(2,1)S(1)} %shard_map.117.rest_0_), channel_id=1, source_target_pairs={{0,24},{8,16},{16,8},{24,0},{1,25},{9,17},{17,9},{25,1},{2,26},{10... | collective-permute-start | bytes 172040 | tf_op jit(solution)/shard_map/ppermute | solution.py:482
  61.1 6.3 %collective-permute-start.13 = (bf16[224,128]{1,0:T(8,128)(2,1)S(1)}, bf16[224,128]{1,0:T(8,128)(2,1)S(1)}, u32[]{:S(2)}, u32[]{:S(2)}) collective-permute-start(bf16[224,128]{1,0:T(8,128)(2,1)S(1)} %shard_map.117.rest_0_), channel_id=1, source_target_pairs={{0,16},{8,24},{16,0},{24,8},{1,17},{9,25},{17,1},{25,9},{2,18},{10... | collective-permute-start | bytes 172040 | tf_op jit(solution)/shard_map/ppermute | solution.py:482
  61.7 5.8 %collective-permute-start.12 = (bf16[224,128]{1,0:T(8,128)(2,1)S(1)}, bf16[224,128]{1,0:T(8,128)(2,1)S(1)}, u32[]{:S(2)}, u32[]{:S(2)}) collective-permute-start(bf16[224,128]{1,0:T(8,128)(2,1)S(1)} %shard_map.117.rest_0_), channel_id=1, source_target_pairs={{0,8},{8,0},{16,24},{24,16},{1,9},{9,1},{17,25},{25,17},{2,10},{10... | collective-permute-start | bytes 172040 | tf_op jit(solution)/shard_map/ppermute | solution.py:482

commit v7 on v6

--- a/solution.py
+++ b/solution.py
@@ -219,7 +219,7 @@
     groups, blocks, heads, rows, live = dims
     chips = heads // CORES
     core = lax.axis_index("core")
-    own_ins = rest[:heads]
+    own_ins = rest[:heads][::-1]
     part_hbm = rest[heads + 1]
     own_parts = rest[heads + 2 : heads + 2 + chips]
     dqs, log_hbm, part_out, log_out, routes, sems, qs, ks, vs, gs, parts = rest[
@@ -584,7 +584,7 @@
         adapter_up_weight,
         own_send[heads + 1],
         far,
-        *own,
+        *own[::-1],
         feat_other,
         out_specs=[ANY] + [VMEM] * (chips + 1) + [ANY],
     )

time: 68.7 us -> 68.7 us (level)
    ppermute x15, waiting for transfers between devices: 14.9 us -> 13.5 us  [exchange(): lax.ppermute(value, axis, [(peer, peer ^ turn) for peer in range(size)])]
    all_to_all x1, waiting for transfers between devices: 1.62 us -> 2.57 us  [per_device_tiles(): far = lax.all_to_all(far_send, everyone, 0, 0, tiled=True)]
  transfers between devices with their start and end apart: 17 -> 17, of which waited for: 11 -> 12; matrix products, arithmetic and copies ran while one was open for 0% -> 0% of each run, Pallas kernels for 2% -> 2%
where the time goes in v7:
time: 68.7 us; the launch traced here: 68.4 us
  starting transfers between devices  29.6 us (43%)
  waiting for transfers between devices  18.1 us (26%)
  Pallas kernels  10.4 us (15%)
  blocking collectives  7.89 us (11%)
  local copies, waits for them, and re-layouts  1.62 us (2%)
  between operations  0.79 us (1%)
    ppermute x15, starting transfers between devices, exchange(): lax.ppermute(value, axis, [(peer, peer ^ turn) for peer in range(size)])  16.9 us
    ppermute x15, waiting for transfers between devices, exchange(): lax.ppermute(value, axis, [(peer, peer ^ turn) for peer in range(size)])  13.5 us
    pallas_call x7, Pallas kernels, call(): pl.pallas_call(kernel, out_shape=shapes, in_specs=specs, out_specs=out_sp...  10.4 us
    all_to_all x1, blocking collectives, per_device_tiles(): shares = lax.all_to_all(shares, 'chip', 0, 0, tiled=True)  7.89 us
    all_to_all x1, starting transfers between devices, per_device_tiles(): far = lax.all_to_all(far_send, everyone, 0, 0, tiled=True)  7.29 us
    all_to_all x1, starting transfers between devices, per_device_tiles(): part = lax.all_to_all(attended[0], ('chip', 'dp'), 0, 0, tiled=True)  5.4 us
    all_to_all x1, waiting for transfers between devices, per_device_tiles(): far = lax.all_to_all(far_send, everyone, 0, 0, tiled=True)  2.57 us
    all_to_all x1, waiting for transfers between devices, per_device_tiles(): part = lax.all_to_all(attended[0], ('chip', 'dp'), 0, 0, tiled=True)  1.97 us
  transfers between devices with their start and end apart: 17, of which 12 were waited for; matrix products, arithmetic and copies ran while one was open for 0% of the time, Pallas kernels for 2%

profile of v7, /device:TPU:0, one launch (start us, length us, event | category | flops | bytes accessed | tf_op | source)
XLA Modules:
  0.0 68.4 jit_solution(8756850091028362919)
XLA Ops:
  0.6 3.1 %shard_map.112 = (bf16[32,6,16,128]{3,2,1,0:T(8,128)(2,1)}, bf16[8,16,1024]{2,1,0:T(8,128)(2,1)}, bf16[8,16,128]{2,1,0:T(8,128)(2,1)}) custom-call(s32[4,8]{1,0:T(4,128)} %plan.5, bf16[128,2560]{1,0:T(8,128)(2,1)} %bitcast.7, bf16[8,16,1024]{2,1,0:T(8,128)(2,1)} %bitcast.16, bf16[8,16,1024]{2,1,0:T(8,128)(2,1)} %bitcast.10, bf16[8,16,1024]{2,1,0:T(8,128)(2,1)} %bitcast.12, ...), custom_call_target="tpu_custom_call" | custom-call | flops 60000000 | bytes 4000000 | tf_op jit(solution)/shard_map/pallas_call | solution.py:470
  3.7 0.0 copy-start
  3.7 0.0 copy-start.1
  3.7 0.0 copy-start.2
  3.7 0.0 copy-start.3
  3.8 0.0 copy-start.6
  3.8 7.3 %all-to-all-start = ((bf16[32,6,16,128]{3,2,1,0:T(8,128)(2,1)}), bf16[32,6,16,128]{3,2,1,0:T(8,128)(2,1)S(1)}, u32[]{:S(2)}, u32[]{:S(2)}) async-start(bf16[32,6,16,128]{3,2,1,0:T(8,128)(2,1)} %get-tuple-element.31), calls=%async_computation | async-start | bytes 1572864 | tf_op jit(solution)/shard_map/all_to_all | solution.py:566
  11.1 0.0 copy-start.7
  11.1 0.6 copy-done.7
  11.7 0.9 %copy-done.4 = bf16[8,16,1024]{2,1,0:T(8,128)(2,1)S(1)} copy-done((bf16[8,16,1024]{2,1,0:T(8,128)(2,1)S(1)}, bf16[8,16,1024]{2,1,0:T(8,128)(2,1)}, u32[]{:S(2)}) %copy-start.4) | copy-done | bytes 262168
  12.7 1.2 %shard_map.113 = (bf16[16,16,128]{2,1,0:T(8,128)(2,1)S(1)}, bf16[16,16,128]{2,1,0:T(8,128)(2,1)S(1)}, bf16[16,16,128]{2,1,0:T(8,128)(2,1)S(1)}, bf16[16,16,128]{...) custom-call(s32[4,8]{1,0:T(4,128)S(1)} %copy-done.7, ...), custom_call_target="tpu_custom_call" | custom-call | bytes 1600000 | tf_op jit(solution)/shard_map/pallas_call | solution.py:470
  13.9 0.3 collective-permute-start
  14.2 2.5 %collective-permute-start.1 = (bf16[16,16,128]{2,1,0:T(8,128)(2,1)S(1)}, bf16[16,16,128]{2,1,0:T(8,128)(2,1)S(1)}, u32[]{:S(2)}, u32[]{:S(2)}) collective-permute-start(bf16[16,16,128]{2,1,0:T(8,128)(2,1)S(1)} %get-tuple-element.32), channel_id=1, source_target_pairs={{0,7},{1,6},{2,5},{3,4},{4,3},{5,2},{6,1},{7,0},{8,15},{9,14},{10,... | collective-permute-start | bytes 196616 | tf_op jit(solution)/shard_map/ppermute | solution.py:482
  16.8 0.3 collective-permute-start.2
  17.0 1.3 %collective-permute-start.3 = (bf16[16,16,128]{2,1,0:T(8,128)(2,1)S(1)}, bf16[16,16,128]{2,1,0:T(8,128)(2,1)S(1)}, u32[]{:S(2)}, u32[]{:S(2)}) collective-permute-start(bf16[16,16,128]{2,1,0:T(8,128)(2,1)S(1)} %get-tuple-element.34), channel_id=1, source_target_pairs={{0,5},{1,4},{2,7},{3,6},{4,1},{5,0},{6,3},{7,2},{8,13},{9,12},{10,... | collective-permute-start | bytes 196616 | tf_op jit(solution)/shard_map/ppermute | solution.py:482
  18.3 0.5 collective-permute-start.4
  18.8 2.1 %collective-permute-done.1.rest_0_.rest_7_ = bf16[16,16,128]{2,1,0:T(8,128)(2,1)S(1)} collective-permute-done((bf16[16,16,128]{2,1,0:T(8,128)(2,1)S(1)}, bf16[16,16,128]{2,1,0:T(8,128)(2,1)S(1)}, u32[]{:S(2)}, u32[]{:S(2)}) %collective-permute-start.1) | collective-permute-done | bytes 65568 | tf_op jit(solution)/shard_map/ppermute | solution.py:482
  20.9 2.0 %collective-permute-start.5 = (bf16[16,16,128]{2,1,0:T(8,128)(2,1)S(1)}, bf16[16,16,128]{2,1,0:T(8,128)(2,1)S(1)}, u32[]{:S(2)}, u32[]{:S(2)}) collective-permute-start(bf16[16,16,128]{2,1,0:T(8,128)(2,1)S(1)} %get-tuple-element.36), channel_id=1, source_target_pairs={{0,3},{1,2},{2,1},{3,0},{4,7},{5,6},{6,5},{7,4},{8,11},{9,10},{10,... | collective-permute-start | bytes 196616 | tf_op jit(solution)/shard_map/ppermute | solution.py:482
  23.0 0.6 collective-permute-done.2.rest_1_.rest_6_
  23.6 1.9 %collective-permute-start.6 = (bf16[16,16,128]{2,1,0:T(8,128)(2,1)S(1)}, bf16[16,16,128]{2,1,0:T(8,128)(2,1)S(1)}, u32[]{:S(2)}, u32[]{:S(2)}) collective-permute-start(bf16[16,16,128]{2,1,0:T(8,128)(2,1)S(1)} %get-tuple-element.37), channel_id=1, source_target_pairs={{0,2},{1,3},{2,0},{3,1},{4,6},{5,7},{6,4},{7,5},{8,10},{9,11},{10,... | collective-permute-start | bytes 196616 | tf_op jit(solution)/shard_map/ppermute | solution.py:482
  25.5 0.0 collective-permute-done.3.rest_2_.rest_5_
  25.5 0.0 collective-permute-start.7
  25.5 1.2 %collective-permute-done.4.rest_3_.rest_4_ = bf16[16,16,128]{2,1,0:T(8,128)(2,1)S(1)} collective-permute-done((bf16[16,16,128]{2,1,0:T(8,128)(2,1)S(1)}, bf16[16,16,128]{2,1,0:T(8,128)(2,1)S(1)}, u32[]{:S(2)}, u32[]{:S(2)}) %collective-permute-start.4) | collective-permute-done | bytes 65568 | tf_op jit(solution)/shard_map/ppermute | solution.py:482
  26.6 0.0 collective-permute-done.5.rest_4_.rest_3_
  26.6 1.4 %collective-permute-done.6.rest_5_.rest_2_ = bf16[16,16,128]{2,1,0:T(8,128)(2,1)S(1)} collective-permute-done((bf16[16,16,128]{2,1,0:T(8,128)(2,1)S(1)}, bf16[16,16,128]{2,1,0:T(8,128)(2,1)S(1)}, u32[]{:S(2)}, u32[]{:S(2)}) %collective-permute-start.6) | collective-permute-done | bytes 65568 | tf_op jit(solution)/shard_map/ppermute | solution.py:482
  28.1 0.0 collective-permute-done.7.rest_6_.rest_1_
  28.1 0.0 collective-permute-done.rest_8_.feat_other
  28.1 2.6 %all-to-all-done.far_in = bf16[32,6,16,128]{3,2,1,0:T(8,128)(2,1)S(1)} async-done(((bf16[32,6,16,128]{3,2,1,0:T(8,128)(2,1)}), bf16[32,6,16,128]{3,2,1,0:T(8,128)(2,1)S(1)}, u32[]{:S(2)}, u32[]{:S(2)}) %all-to-all-start) | async-done | bytes 786464 | tf_op jit(solution)/shard_map/all_to_all | solution.py:566
  30.7 3.2 %shard_map.114 = (bf16[16,3,16,128]{3,2,1,0:T(8,128)(2,1)}, bf16[2,2,16,128]{3,2,1,0:T(8,128)(2,1)S(1)}, bf16[2,2,16,128]{3,2,1,0:T(8,128)(2,1)S(1)}, bf16[2,2,1...) custom-call(s32[4,8]{1,0:T(4,128)S(1)} %copy-done.7, ...), custom_call_target="tpu_custom_call" | custom-call | flops 600000000 | bytes 3000000 | tf_op jit(solution)/shard_map/pallas_call | solution.py:470
  33.9 5.4 %all-to-all-start.1 = ((bf16[16,3,16,128]{3,2,1,0:T(8,128)(2,1)}), bf16[16,3,16,128]{3,2,1,0:T(8,128)(2,1)S(1)}, u32[]{:S(2)}, u32[]{:S(2)}) async-start(bf16[16,3,16,128]{3,2,1,0:T(8,128)(2,1)} %get-tuple-element.40), calls=%async_computation.1 | async-start | bytes 393216 | tf_op jit(solution)/shard_map/all_to_all | solution.py:594
  39.3 2.8 %collective-permute-start.8 = (bf16[2,2,16,128]{3,2,1,0:T(8,128)(2,1)S(1)}, bf16[2,2,16,128]{3,2,1,0:T(8,128)(2,1)S(1)}, u32[]{:S(2)}, u32[]{:S(2)}) collective-permute-start(bf16[2,2,16,128]{3,2,1,0:T(8,128)(2,1)S(1)} %get-tuple-element.41), channel_id=1, source_target_pairs={{0,6},{2,4},{4,2},{6,0},{1,7},{3,5},{5,3},{7,1},{8,14},{10,12},{12... | collective-permute-start | bytes 49160 | tf_op jit(solution)/shard_map/ppermute | solution.py:482
  42.1 0.6 collective-permute-start.9
  42.7 0.2 collective-permute-start.10
  42.9 1.5 %collective-permute-done.8.refs_0_ = bf16[2,2,16,128]{3,2,1,0:T(8,128)(2,1)S(1)} collective-permute-done((bf16[2,2,16,128]{3,2,1,0:T(8,128)(2,1)S(1)}, bf16[2,2,16,128]{3,2,1,0:T(8,128)(2,1)S(1)}, u32[]{:S(2)}, u32[]{:S(2)}) %collective-permute-start.8) | collective-permute-done | bytes 16416 | tf_op jit(solution)/shard_map/ppermute | solution.py:482
  44.3 1.7 %collective-permute-done.9.refs_1_ = bf16[2,2,16,128]{3,2,1,0:T(8,128)(2,1)S(1)} collective-permute-done((bf16[2,2,16,128]{3,2,1,0:T(8,128)(2,1)S(1)}, bf16[2,2,16,128]{3,2,1,0:T(8,128)(2,1)S(1)}, u32[]{:S(2)}, u32[]{:S(2)}) %collective-permute-start.9) | collective-permute-done | bytes 16416 | tf_op jit(solution)/shard_map/ppermute | solution.py:482
  46.0 0.5 collective-permute-done.10.refs_2_
  46.5 2.0 %all-to-all-done.1.parts = bf16[16,3,16,128]{3,2,1,0:T(8,128)(2,1)S(1)} async-done(((bf16[16,3,16,128]{3,2,1,0:T(8,128)(2,1)}), bf16[16,3,16,128]{3,2,1,0:T(8,128)(2,1)S(1)}, u32[]{:S(2)}, u32[]{:S(2)}) %all-to-all-start.1) | async-done | bytes 196640 | tf_op jit(solution)/shard_map/all_to_all | solution.py:594
  48.5 0.1 collective-permute-start.11
  48.6 1.3 %collective-permute-done.11.other = bf16[28,16,128]{2,1,0:T(8,128)(2,1)S(1)} collective-permute-done((bf16[28,16,128]{2,1,0:T(8,128)(2,1)S(1)}, bf16[28,16,128]{2,1,0:T(8,128)(2,1)S(1)}, u32[]{:S(2)}, u32[]{:S(2)}) %collective-permute-start.11) | collective-permute-done | bytes 114720 | tf_op jit(solution)/shard_map/ppermute | solution.py:482
  49.9 2.0 %shard_map.116 = (bf16[4,160,128]{2,1,0:T(8,128)(2,1)S(1)}, bf16[64,128]{1,0:T(8,128)(2,1)S(1)}) custom-call(s32[4,8]{1,0:T(4,128)S(1)} %copy-done.7, bf16[128,2560]{1,0:T(8,128)(2,1)S(1)} %bitcast.9, bf16[4,128,384]{2,1,0:T(8,128)(2,1)S(1)} %collective-permute-done.rest_8_.feat_other, bf16[28,16,128]{2,1,0:T(8,128)(2,1)S(1)} %shard_map.115.mine, ...), custom_call_target="tpu_custom_call" | custom-call | flops 60000000 | bytes 2000000 | tf_op jit(solution)/shard_map/pallas_call | solution.py:470
  51.9 7.9 %all_to_all.15.parts = bf16[4,160,128]{2,1,0:T(8,128)(2,1)S(1)} all-to-all(bf16[4,160,128]{2,1,0:T(8,128)(2,1)S(1)} %get-tuple-element.46), channel_id=1, replica_groups=mesh['dp'=4,'chip'=4,'core'=2] {'chip'}, dimensions={0} | all-to-all | bytes 327680 | tf_op jit(solution)/shard_map/all_to_all | solution.py:627
  59.8 1.3 %collective-permute-start.14 = (bf16[224,128]{1,0:T(8,128)(2,1)S(1)}, bf16[224,128]{1,0:T(8,128)(2,1)S(1)}, u32[]{:S(2)}, u32[]{:S(2)}) collective-permute-start(bf16[224,128]{1,0:T(8,128)(2,1)S(1)} %shard_map.117.rest_0_), channel_id=1, source_target_pairs={{0,24},{8,16},{16,8},{24,0},{1,25},{9,17},{17,9},{25,1},{2,26},{10... | collective-permute-start | bytes 172040 | tf_op jit(solution)/shard_map/ppermute | solution.py:482
  61.2 0.5 collective-permute-start.13
  61.7 2.6 %collective-permute-start.12 = (bf16[224,128]{1,0:T(8,128)(2,1)S(1)}, bf16[224,128]{1,0:T(8,128)(2,1)S(1)}, u32[]{:S(2)}, u32[]{:S(2)}) collective-permute-start(bf16[224,128]{1,0:T(8,128)(2,1)S(1)} %shard_map.117.rest_0_), channel_id=1, source_target_pairs={{0,8},{8,0},{16,24},{24,16},{1,9},{9,1},{17,25},{25,17},{2,10},{10... | collective-permute-start | bytes 172040 | tf_op jit(solution)/shard_map/ppermute | solution.py:482
  64.3 1.7 %collective-permute-done.14.rest_3_ = bf16[224,128]{1,0:T(8,128)(2,1)S(1)} collective-permute-done((bf16[224,128]{1,0:T(8,128)(2,1)S(1)}, bf16[224,128]{1,0:T(8,128)(2,1)S(1)}, u32[]{:S(2)}, u32[]{:S(2)}) %collective-permute-start.14) | collective-permute-done | bytes 57376 | tf_op jit(solution)/shard_map/ppermute | solution.py:482
  66.0 1.5 %collective-permute-done.13.rest_2_ = bf16[224,128]{1,0:T(8,128)(2,1)S(1)} collective-permute-done((bf16[224,128]{1,0:T(8,128)(2,1)S(1)}, bf16[224,128]{1,0:T(8,128)(2,1)S(1)}, u32[]{:S(2)}, u32[]{:S(2)}) %collective-permute-start.13) | collective-permute-done | bytes 57376 | tf_op jit(solution)/shard_map/ppermute | solution.py:482
  67.5 0.0 collective-permute-done.12.rest_1_
  67.5 0.8 %shard_map.118 = (f32[64,320]{1,0:T(8,128)}, f32[64,128]{1,0:T(8,128)}) custom-call(bf16[224,128]{1,0:T(8,128)(2,1)S(1)} %shard_map.117.rest_0_, bf16[224,128]{1,0:T(8,128)(2,1)S(1)} %collective-permute-done.12.rest_1_, bf16[224,128]{1,0:T(8,128)(2,1)S(1)} %collective-permute-done.13.rest_2_, bf16[224,128]{1,0:T(8,128)(2,1)S(1)} %collective-permute-done.14.rest_3_), custom_call_target="tpu_custom_call" | custom-call | bytes 400000 | tf_op jit(solution)/shard_map/pallas_call | solution.py:470
  (12 shorter events, 0.1 us)
Async XLA Ops:
  3.7 7.4 %copy-start = (bf16[1,8,16,2560]{3,2,1,0:T(8,128)(2,1)S(1)}, bf16[1,8,16,2560]{3,2,1,0:T(8,128)(2,1)}, u32[]{:S(2)}) copy-start(bf16[1,8,16,2560]{3,2,1,0:T(8,128)(2,1)} %param.9) | copy-start | bytes 1966084
  3.7 7.4 %copy-start.1 = (bf16[1,8,16,1024]{3,2,1,0:T(8,128)(2,1)S(1)}, bf16[1,8,16,1024]{3,2,1,0:T(8,128)(2,1)}, u32[]{:S(2)}) copy-start(bf16[1,8,16,1024]{3,2,1,0:T(8,128)(2,1)} %param.11) | copy-start | bytes 786436
  3.7 7.4 %copy-start.2 = (bf16[1,8,16,1024]{3,2,1,0:T(8,128)(2,1)S(1)}, bf16[1,8,16,1024]{3,2,1,0:T(8,128)(2,1)}, u32[]{:S(2)}) copy-start(bf16[1,8,16,1024]{3,2,1,0:T(8,128)(2,1)} %param.12) | copy-start | bytes 786436
  3.7 7.4 %copy-start.3 = (bf16[1,8,16,1024]{3,2,1,0:T(8,128)(2,1)S(1)}, bf16[1,8,16,1024]{3,2,1,0:T(8,128)(2,1)}, u32[]{:S(2)}) copy-start(bf16[1,8,16,1024]{3,2,1,0:T(8,128)(2,1)} %param.13) | copy-start | bytes 786436
  3.8 7.4 %copy-start.6 = (bf16[8,16,128]{2,1,0:T(8,128)(2,1)S(1)}, bf16[8,16,128]{2,1,0:T(8,128)(2,1)}, u32[]{:S(2)}) copy-start(bf16[8,16,128]{2,1,0:T(8,128)(2,1)} %get-tuple-element.28.adapter) | copy-start | bytes 98308
  3.8 26.9 %all-to-all-start = ((bf16[32,6,16,128]{3,2,1,0:T(8,128)(2,1)}), bf16[32,6,16,128]{3,2,1,0:T(8,128)(2,1)S(1)}, u32[]{:S(2)}, u32[]{:S(2)}) async-start(bf16[32,6,16,128]{3,2,1,0:T(8,128)(2,1)} %get-tuple-element.31), calls=%async_computation | async-start | bytes 1572864 | tf_op jit(solution)/shard_map/all_to_all | solution.py:566
  11.1 0.7 %copy-start.7 = (s32[4,8]{1,0:T(4,128)S(1)}, s32[4,8]{1,0:T(4,128)}, u32[]{:S(2)}) copy-start(s32[4,8]{1,0:T(4,128)} %plan.5) | copy-start | bytes 388
  11.7 0.9 %copy-start.4 = (bf16[8,16,1024]{2,1,0:T(8,128)(2,1)S(1)}, bf16[8,16,1024]{2,1,0:T(8,128)(2,1)}, u32[]{:S(2)}) copy-start(bf16[8,16,1024]{2,1,0:T(8,128)(2,1)} %get-tuple-element.27.queries) | copy-start | bytes 786436
  12.7 18.0 %copy-start.5 = (bf16[64,1024]{1,0:T(8,128)(2,1)S(1)}, bf16[64,1024]{1,0:T(8,128)(2,1)}, u32[]{:S(2)}) copy-start(bf16[64,1024]{1,0:T(8,128)(2,1)} %up.1) | copy-start | bytes 393220
  13.9 14.2 %collective-permute-start = (bf16[4,128,384]{2,1,0:T(8,128)(2,1)S(1)}, bf16[4,128,384]{2,1,0:T(8,128)(2,1)S(1)}, u32[]{:S(2)}, u32[]{:S(2)}) collective-permute-start(bf16[4,128,384]{2,1,0:T(8,128)(2,1)S(1)} %get-tuple-element.29), channel_id=1, source_target_pairs={{0,1},{1,0},{2,3},{3,2},{4,5},{5,4},{6,7},{7,6},{8,9},{9,8},{10,11... | collective-permute-start | bytes 1179656 | tf_op jit(solution)/shard_map/ppermute | solution.py:482
  14.2 6.7 %collective-permute-start.1 = (bf16[16,16,128]{2,1,0:T(8,128)(2,1)S(1)}, bf16[16,16,128]{2,1,0:T(8,128)(2,1)S(1)}, u32[]{:S(2)}, u32[]{:S(2)}) collective-permute-start(bf16[16,16,128]{2,1,0:T(8,128)(2,1)S(1)} %get-tuple-element.32), channel_id=1, source_target_pairs={{0,7},{1,6},{2,5},{3,4},{4,3},{5,2},{6,1},{7,0},{8,15},{9,14},{10,... | collective-permute-start | bytes 196616 | tf_op jit(solution)/shard_map/ppermute | solution.py:482
  16.8 6.8 %collective-permute-start.2 = (bf16[16,16,128]{2,1,0:T(8,128)(2,1)S(1)}, bf16[16,16,128]{2,1,0:T(8,128)(2,1)S(1)}, u32[]{:S(2)}, u32[]{:S(2)}) collective-permute-start(bf16[16,16,128]{2,1,0:T(8,128)(2,1)S(1)} %get-tuple-element.33), channel_id=1, source_target_pairs={{0,6},{1,7},{2,4},{3,5},{4,2},{5,3},{6,0},{7,1},{8,14},{9,15},{10,... | collective-permute-start | bytes 196616 | tf_op jit(solution)/shard_map/ppermute | solution.py:482
  17.0 8.4 %collective-permute-start.3 = (bf16[16,16,128]{2,1,0:T(8,128)(2,1)S(1)}, bf16[16,16,128]{2,1,0:T(8,128)(2,1)S(1)}, u32[]{:S(2)}, u32[]{:S(2)}) collective-permute-start(bf16[16,16,128]{2,1,0:T(8,128)(2,1)S(1)} %get-tuple-element.34), channel_id=1, source_target_pairs={{0,5},{1,4},{2,7},{3,6},{4,1},{5,0},{6,3},{7,2},{8,13},{9,12},{10,... | collective-permute-start | bytes 196616 | tf_op jit(solution)/shard_map/ppermute | solution.py:482
  18.3 8.4 %collective-permute-start.4 = (bf16[16,16,128]{2,1,0:T(8,128)(2,1)S(1)}, bf16[16,16,128]{2,1,0:T(8,128)(2,1)S(1)}, u32[]{:S(2)}, u32[]{:S(2)}) collective-permute-start(bf16[16,16,128]{2,1,0:T(8,128)(2,1)S(1)} %get-tuple-element.35), channel_id=1, source_target_pairs={{0,4},{1,5},{2,6},{3,7},{4,0},{5,1},{6,2},{7,3},{8,12},{9,13},{10,... | collective-permute-start | bytes 196616 | tf_op jit(solution)/shard_map/ppermute | solution.py:482
  20.9 9.8 %copy-start.8 = (s32[1,1024]{1,0:T(1,128)S(1)}, s32[1,1024]{1,0:T(1,128)}, u32[]{:S(2)}) copy-start(s32[1,1024]{1,0:T(1,128)} %seg.1) | copy-start | bytes 12292
  20.9 5.7 %collective-permute-start.5 = (bf16[16,16,128]{2,1,0:T(8,128)(2,1)S(1)}, bf16[16,16,128]{2,1,0:T(8,128)(2,1)S(1)}, u32[]{:S(2)}, u32[]{:S(2)}) collective-permute-start(bf16[16,16,128]{2,1,0:T(8,128)(2,1)S(1)} %get-tuple-element.36), channel_id=1, source_target_pairs={{0,3},{1,2},{2,1},{3,0},{4,7},{5,6},{6,5},{7,4},{8,11},{9,10},{10,... | collective-permute-start | bytes 196616 | tf_op jit(solution)/shard_map/ppermute | solution.py:482
  23.6 4.5 %collective-permute-start.6 = (bf16[16,16,128]{2,1,0:T(8,128)(2,1)S(1)}, bf16[16,16,128]{2,1,0:T(8,128)(2,1)S(1)}, u32[]{:S(2)}, u32[]{:S(2)}) collective-permute-start(bf16[16,16,128]{2,1,0:T(8,128)(2,1)S(1)} %get-tuple-element.37), channel_id=1, source_target_pairs={{0,2},{1,3},{2,0},{3,1},{4,6},{5,7},{6,4},{7,5},{8,10},{9,11},{10,... | collective-permute-start | bytes 196616 | tf_op jit(solution)/shard_map/ppermute | solution.py:482
  25.5 2.6 %collective-permute-start.7 = (bf16[16,16,128]{2,1,0:T(8,128)(2,1)S(1)}, bf16[16,16,128]{2,1,0:T(8,128)(2,1)S(1)}, u32[]{:S(2)}, u32[]{:S(2)}) collective-permute-start(bf16[16,16,128]{2,1,0:T(8,128)(2,1)S(1)} %get-tuple-element.38), channel_id=1, source_target_pairs={{0,1},{1,0},{2,3},{3,2},{4,5},{5,4},{6,7},{7,6},{8,9},{9,8},{10,11... | collective-permute-start | bytes 196616 | tf_op jit(solution)/shard_map/ppermute | solution.py:482
  33.9 14.6 %all-to-all-start.1 = ((bf16[16,3,16,128]{3,2,1,0:T(8,128)(2,1)}), bf16[16,3,16,128]{3,2,1,0:T(8,128)(2,1)S(1)}, u32[]{:S(2)}, u32[]{:S(2)}) async-start(bf16[16,3,16,128]{3,2,1,0:T(8,128)(2,1)} %get-tuple-element.40), calls=%async_computation.1 | async-start | bytes 393216 | tf_op jit(solution)/shard_map/all_to_all | solution.py:594
  39.3 5.0 %collective-permute-start.8 = (bf16[2,2,16,128]{3,2,1,0:T(8,128)(2,1)S(1)}, bf16[2,2,16,128]{3,2,1,0:T(8,128)(2,1)S(1)}, u32[]{:S(2)}, u32[]{:S(2)}) collective-permute-start(bf16[2,2,16,128]{3,2,1,0:T(8,128)(2,1)S(1)} %get-tuple-element.41), channel_id=1, source_target_pairs={{0,6},{2,4},{4,2},{6,0},{1,7},{3,5},{5,3},{7,1},{8,14},{10,12},{12... | collective-permute-start | bytes 49160 | tf_op jit(solution)/shard_map/ppermute | solution.py:482
  42.1 3.9 %collective-permute-start.9 = (bf16[2,2,16,128]{3,2,1,0:T(8,128)(2,1)S(1)}, bf16[2,2,16,128]{3,2,1,0:T(8,128)(2,1)S(1)}, u32[]{:S(2)}, u32[]{:S(2)}) collective-permute-start(bf16[2,2,16,128]{3,2,1,0:T(8,128)(2,1)S(1)} %get-tuple-element.42), channel_id=1, source_target_pairs={{0,4},{2,6},{4,0},{6,2},{1,5},{3,7},{5,1},{7,3},{8,12},{10,14},{12... | collective-permute-start | bytes 49160 | tf_op jit(solution)/shard_map/ppermute | solution.py:482
  42.7 3.8 %collective-permute-start.10 = (bf16[2,2,16,128]{3,2,1,0:T(8,128)(2,1)S(1)}, bf16[2,2,16,128]{3,2,1,0:T(8,128)(2,1)S(1)}, u32[]{:S(2)}, u32[]{:S(2)}) collective-permute-start(bf16[2,2,16,128]{3,2,1,0:T(8,128)(2,1)S(1)} %get-tuple-element.43), channel_id=1, source_target_pairs={{0,2},{2,0},{4,6},{6,4},{1,3},{3,1},{5,7},{7,5},{8,10},{10,8},{12,... | collective-permute-start | bytes 49160 | tf_op jit(solution)/shard_map/ppermute | solution.py:482
  48.5 1.4 %collective-permute-start.11 = (bf16[28,16,128]{2,1,0:T(8,128)(2,1)S(1)}, bf16[28,16,128]{2,1,0:T(8,128)(2,1)S(1)}, u32[]{:S(2)}, u32[]{:S(2)}) collective-permute-start(bf16[28,16,128]{2,1,0:T(8,128)(2,1)S(1)} %shard_map.115.mine), channel_id=1, source_target_pairs={{0,1},{1,0},{2,3},{3,2},{4,5},{5,4},{6,7},{7,6},{8,9},{9,8},{10,11... | collective-permute-start | bytes 344072 | tf_op jit(solution)/shard_map/ppermute | solution.py:482
  59.8 6.2 %collective-permute-start.14 = (bf16[224,128]{1,0:T(8,128)(2,1)S(1)}, bf16[224,128]{1,0:T(8,128)(2,1)S(1)}, u32[]{:S(2)}, u32[]{:S(2)}) collective-permute-start(bf16[224,128]{1,0:T(8,128)(2,1)S(1)} %shard_map.117.rest_0_), channel_id=1, source_target_pairs={{0,24},{8,16},{16,8},{24,0},{1,25},{9,17},{17,9},{25,1},{2,26},{10... | collective-permute-start | bytes 172040 | tf_op jit(solution)/shard_map/ppermute | solution.py:482
  61.2 6.3 %collective-permute-start.13 = (bf16[224,128]{1,0:T(8,128)(2,1)S(1)}, bf16[224,128]{1,0:T(8,128)(2,1)S(1)}, u32[]{:S(2)}, u32[]{:S(2)}) collective-permute-start(bf16[224,128]{1,0:T(8,128)(2,1)S(1)} %shard_map.117.rest_0_), channel_id=1, source_target_pairs={{0,16},{8,24},{16,0},{24,8},{1,17},{9,25},{17,1},{25,9},{2,18},{10... | collective-permute-start | bytes 172040 | tf_op jit(solution)/shard_map/ppermute | solution.py:482
  61.7 5.8 %collective-permute-start.12 = (bf16[224,128]{1,0:T(8,128)(2,1)S(1)}, bf16[224,128]{1,0:T(8,128)(2,1)S(1)}, u32[]{:S(2)}, u32[]{:S(2)}) collective-permute-start(bf16[224,128]{1,0:T(8,128)(2,1)S(1)} %shard_map.117.rest_0_), channel_id=1, source_target_pairs={{0,8},{8,0},{16,24},{24,16},{1,9},{9,1},{17,25},{25,17},{2,10},{10... | collective-permute-start | bytes 172040 | tf_op jit(solution)/shard_map/ppermute | solution.py:482

commit v8 on v6

--- a/solution.py
+++ b/solution.py
@@ -71,16 +71,12 @@
 
 
 def each_block(plan, me, blocks, live, take):
-    def over_position(position, _):
-        group = quotient(plan[me, position], blocks)
+    groups_of = [quotient(plan[me, position], blocks) for position in range(live)]
+    for position, group in enumerate(groups_of):
         slot = jnp.int32(0)
-        for other in range(live):
-            same = (quotient(plan[me, other], blocks) == group) & (other < position)
-            slot = slot + same.astype(jnp.int32)
+        for earlier in groups_of[:position]:
+            slot = slot + (earlier == group).astype(jnp.int32)
         take(position, group, slot)
-        return 0
-
-    lax.fori_loop(0, live, over_position, 0)
 
 
 def each_half(slot, store):
@@ -303,7 +299,7 @@
         dquery_all, up_twice, (((0,), (1,)), ((), ())), preferred_element_type=jnp.float32
     ).astype(jnp.bfloat16)
 
-    def put(position, _):
+    def put(position):
         group, slot = routes[0, position], routes[1, position]
         far = (group != me) | (slot < CAP)
 
@@ -328,9 +324,8 @@
 
             each_half(slot, store)
 
-        return 0
-
-    lax.fori_loop(0, live, put, 0)
+    for position in range(live):
+        put(position)
     for chip in range(chips):
         for group in range(groups):
             part_out[chip * groups + group, CORES] = adapter[group]

time: 68.7 us -> 68.4 us (level)
  no operation moved by 1% of the time
where the time goes in v8:
time: 68.4 us; the launch traced here: 68.1 us
  starting transfers between devices  29.1 us (43%)
  waiting for transfers between devices  18.5 us (27%)
  Pallas kernels  10.2 us (15%)
  blocking collectives  7.88 us (12%)
  local copies, waits for them, and re-layouts  1.62 us (2%)
  between operations  0.79 us (1%)
    ppermute x15, starting transfers between devices, exchange(): lax.ppermute(value, axis, [(peer, peer ^ turn) for peer in range(size)])  16.4 us
    ppermute x15, waiting for transfers between devices, exchange(): lax.ppermute(value, axis, [(peer, peer ^ turn) for peer in range(size)])  14.9 us
    pallas_call x7, Pallas kernels, call(): pl.pallas_call(kernel, out_shape=shapes, in_specs=specs, out_specs=out_sp...  10.2 us
    all_to_all x1, blocking collectives, per_device_tiles(): shares = lax.all_to_all(shares, 'chip', 0, 0, tiled=True)  7.88 us
    all_to_all x1, starting transfers between devices, per_device_tiles(): far = lax.all_to_all(far_send, everyone, 0, 0, tiled=True)  7.26 us
    all_to_all x1, starting transfers between devices, per_device_tiles(): part = lax.all_to_all(attended[0], ('chip', 'dp'), 0, 0, tiled=True)  5.43 us
    all_to_all x1, waiting for transfers between devices, per_device_tiles(): part = lax.all_to_all(attended[0], ('chip', 'dp'), 0, 0, tiled=True)  1.97 us
    unnamed x18, local copies, waits for them, and re-layouts  1.62 us
  transfers between devices with their start and end apart: 17, of which 11 were waited for; matrix products, arithmetic and copies ran while one was open for 0% of the time, Pallas kernels for 2%

profile of v8, /device:TPU:0, one launch (start us, length us, event | category | flops | bytes accessed | tf_op | source)
XLA Modules:
  0.0 68.1 jit_solution(17492463545415236135)
XLA Ops:
  0.6 3.1 %shard_map.112 = (bf16[32,6,16,128]{3,2,1,0:T(8,128)(2,1)}, bf16[8,16,1024]{2,1,0:T(8,128)(2,1)}, bf16[8,16,128]{2,1,0:T(8,128)(2,1)}) custom-call(s32[4,8]{1,0:T(4,128)} %plan.5, bf16[128,2560]{1,0:T(8,128)(2,1)} %bitcast.7, bf16[8,16,1024]{2,1,0:T(8,128)(2,1)} %bitcast.16, bf16[8,16,1024]{2,1,0:T(8,128)(2,1)} %bitcast.10, bf16[8,16,1024]{2,1,0:T(8,128)(2,1)} %bitcast.12, ...), custom_call_target="tpu_custom_call" | custom-call | flops 60000000 | bytes 4000000 | tf_op jit(solution)/shard_map/pallas_call | solution.py:465
  3.7 0.0 copy-start
  3.7 0.0 copy-start.1
  3.8 0.0 copy-start.2
  3.8 0.0 copy-start.3
  3.8 0.0 copy-start.6
  3.8 7.3 %all-to-all-start = ((bf16[32,6,16,128]{3,2,1,0:T(8,128)(2,1)}), bf16[32,6,16,128]{3,2,1,0:T(8,128)(2,1)S(1)}, u32[]{:S(2)}, u32[]{:S(2)}) async-start(bf16[32,6,16,128]{3,2,1,0:T(8,128)(2,1)} %get-tuple-element.31), calls=%async_computation | async-start | bytes 1572864 | tf_op jit(solution)/shard_map/all_to_all | solution.py:561
  11.1 0.0 copy-start.7
  11.1 0.6 copy-done.7
  11.7 0.9 %copy-done.4 = bf16[8,16,1024]{2,1,0:T(8,128)(2,1)S(1)} copy-done((bf16[8,16,1024]{2,1,0:T(8,128)(2,1)S(1)}, bf16[8,16,1024]{2,1,0:T(8,128)(2,1)}, u32[]{:S(2)}) %copy-start.4) | copy-done | bytes 262168
  12.7 1.2 %shard_map.113 = (bf16[16,16,128]{2,1,0:T(8,128)(2,1)S(1)}, bf16[16,16,128]{2,1,0:T(8,128)(2,1)S(1)}, bf16[16,16,128]{2,1,0:T(8,128)(2,1)S(1)}, bf16[16,16,128]{...) custom-call(s32[4,8]{1,0:T(4,128)S(1)} %copy-done.7, ...), custom_call_target="tpu_custom_call" | custom-call | bytes 1600000 | tf_op jit(solution)/shard_map/pallas_call | solution.py:465
  13.9 0.3 collective-permute-start
  14.3 0.3 collective-permute-start.1
  14.5 1.8 %collective-permute-start.2 = (bf16[16,16,128]{2,1,0:T(8,128)(2,1)S(1)}, bf16[16,16,128]{2,1,0:T(8,128)(2,1)S(1)}, u32[]{:S(2)}, u32[]{:S(2)}) collective-permute-start(bf16[16,16,128]{2,1,0:T(8,128)(2,1)S(1)} %get-tuple-element.34), channel_id=1, source_target_pairs={{0,2},{1,3},{2,0},{3,1},{4,6},{5,7},{6,4},{7,5},{8,10},{9,11},{10,... | collective-permute-start | bytes 196616 | tf_op jit(solution)/shard_map/ppermute | solution.py:477
  16.3 0.0 collective-permute-start.3
  16.3 1.5 %collective-permute-start.4 = (bf16[16,16,128]{2,1,0:T(8,128)(2,1)S(1)}, bf16[16,16,128]{2,1,0:T(8,128)(2,1)S(1)}, u32[]{:S(2)}, u32[]{:S(2)}) collective-permute-start(bf16[16,16,128]{2,1,0:T(8,128)(2,1)S(1)} %get-tuple-element.36), channel_id=1, source_target_pairs={{0,4},{1,5},{2,6},{3,7},{4,0},{5,1},{6,2},{7,3},{8,12},{9,13},{10,... | collective-permute-start | bytes 196616 | tf_op jit(solution)/shard_map/ppermute | solution.py:477
  17.8 0.0 collective-permute-done.1.rest_1_
  17.8 0.3 collective-permute-start.5
  18.1 2.4 %collective-permute-done.2.rest_2_ = bf16[16,16,128]{2,1,0:T(8,128)(2,1)S(1)} collective-permute-done((bf16[16,16,128]{2,1,0:T(8,128)(2,1)S(1)}, bf16[16,16,128]{2,1,0:T(8,128)(2,1)S(1)}, u32[]{:S(2)}, u32[]{:S(2)}) %collective-permute-start.2) | collective-permute-done | bytes 65568 | tf_op jit(solution)/shard_map/ppermute | solution.py:477
  20.5 2.9 %collective-permute-start.6 = (bf16[16,16,128]{2,1,0:T(8,128)(2,1)S(1)}, bf16[16,16,128]{2,1,0:T(8,128)(2,1)S(1)}, u32[]{:S(2)}, u32[]{:S(2)}) collective-permute-start(bf16[16,16,128]{2,1,0:T(8,128)(2,1)S(1)} %get-tuple-element.38), channel_id=1, source_target_pairs={{0,6},{1,7},{2,4},{3,5},{4,2},{5,3},{6,0},{7,1},{8,14},{9,15},{10,... | collective-permute-start | bytes 196616 | tf_op jit(solution)/shard_map/ppermute | solution.py:477
  23.4 0.0 collective-permute-done.3.rest_3_
  23.4 1.3 %collective-permute-start.7 = (bf16[16,16,128]{2,1,0:T(8,128)(2,1)S(1)}, bf16[16,16,128]{2,1,0:T(8,128)(2,1)S(1)}, u32[]{:S(2)}, u32[]{:S(2)}) collective-permute-start(bf16[16,16,128]{2,1,0:T(8,128)(2,1)S(1)} %get-tuple-element.39), channel_id=1, source_target_pairs={{0,7},{1,6},{2,5},{3,4},{4,3},{5,2},{6,1},{7,0},{8,15},{9,14},{10,... | collective-permute-start | bytes 196616 | tf_op jit(solution)/shard_map/ppermute | solution.py:477
  24.7 0.0 collective-permute-done.4.rest_4_
  24.7 0.0 collective-permute-done.5.rest_5_
  24.7 1.2 %collective-permute-done.6.rest_6_ = bf16[16,16,128]{2,1,0:T(8,128)(2,1)S(1)} collective-permute-done((bf16[16,16,128]{2,1,0:T(8,128)(2,1)S(1)}, bf16[16,16,128]{2,1,0:T(8,128)(2,1)S(1)}, u32[]{:S(2)}, u32[]{:S(2)}) %collective-permute-start.6) | collective-permute-done | bytes 65568 | tf_op jit(solution)/shard_map/ppermute | solution.py:477
  25.8 3.3 %collective-permute-done.7.rest_7_ = bf16[16,16,128]{2,1,0:T(8,128)(2,1)S(1)} collective-permute-done((bf16[16,16,128]{2,1,0:T(8,128)(2,1)S(1)}, bf16[16,16,128]{2,1,0:T(8,128)(2,1)S(1)}, u32[]{:S(2)}, u32[]{:S(2)}) %collective-permute-start.7) | collective-permute-done | bytes 65568 | tf_op jit(solution)/shard_map/ppermute | solution.py:477
  29.1 0.0 collective-permute-done.rest_8_.feat_other
  29.1 1.6 %all-to-all-done.far_in = bf16[32,6,16,128]{3,2,1,0:T(8,128)(2,1)S(1)} async-done(((bf16[32,6,16,128]{3,2,1,0:T(8,128)(2,1)}), bf16[32,6,16,128]{3,2,1,0:T(8,128)(2,1)S(1)}, u32[]{:S(2)}, u32[]{:S(2)}) %all-to-all-start) | async-done | bytes 786464 | tf_op jit(solution)/shard_map/all_to_all | solution.py:561
  30.7 3.0 %shard_map.114 = (bf16[16,3,16,128]{3,2,1,0:T(8,128)(2,1)}, bf16[2,2,16,128]{3,2,1,0:T(8,128)(2,1)S(1)}, bf16[2,2,16,128]{3,2,1,0:T(8,128)(2,1)S(1)}, bf16[2,2,1...) custom-call(s32[4,8]{1,0:T(4,128)S(1)} %copy-done.7, ...), custom_call_target="tpu_custom_call" | custom-call | flops 600000000 | bytes 3000000 | tf_op jit(solution)/shard_map/pallas_call | solution.py:465
  33.7 5.4 %all-to-all-start.1 = ((bf16[16,3,16,128]{3,2,1,0:T(8,128)(2,1)}), bf16[16,3,16,128]{3,2,1,0:T(8,128)(2,1)S(1)}, u32[]{:S(2)}, u32[]{:S(2)}) async-start(bf16[16,3,16,128]{3,2,1,0:T(8,128)(2,1)} %get-tuple-element.40), calls=%async_computation.1 | async-start | bytes 393216 | tf_op jit(solution)/shard_map/all_to_all | solution.py:589
  39.1 2.8 %collective-permute-start.8 = (bf16[2,2,16,128]{3,2,1,0:T(8,128)(2,1)S(1)}, bf16[2,2,16,128]{3,2,1,0:T(8,128)(2,1)S(1)}, u32[]{:S(2)}, u32[]{:S(2)}) collective-permute-start(bf16[2,2,16,128]{3,2,1,0:T(8,128)(2,1)S(1)} %get-tuple-element.41), channel_id=1, source_target_pairs={{0,6},{2,4},{4,2},{6,0},{1,7},{3,5},{5,3},{7,1},{8,14},{10,12},{12... | collective-permute-start | bytes 49160 | tf_op jit(solution)/shard_map/ppermute | solution.py:477
  42.0 0.6 collective-permute-start.9
  42.5 0.2 collective-permute-start.10
  42.7 1.5 %collective-permute-done.8.refs_0_ = bf16[2,2,16,128]{3,2,1,0:T(8,128)(2,1)S(1)} collective-permute-done((bf16[2,2,16,128]{3,2,1,0:T(8,128)(2,1)S(1)}, bf16[2,2,16,128]{3,2,1,0:T(8,128)(2,1)S(1)}, u32[]{:S(2)}, u32[]{:S(2)}) %collective-permute-start.8) | collective-permute-done | bytes 16416 | tf_op jit(solution)/shard_map/ppermute | solution.py:477
  44.2 1.7 %collective-permute-done.9.refs_1_ = bf16[2,2,16,128]{3,2,1,0:T(8,128)(2,1)S(1)} collective-permute-done((bf16[2,2,16,128]{3,2,1,0:T(8,128)(2,1)S(1)}, bf16[2,2,16,128]{3,2,1,0:T(8,128)(2,1)S(1)}, u32[]{:S(2)}, u32[]{:S(2)}) %collective-permute-start.9) | collective-permute-done | bytes 16416 | tf_op jit(solution)/shard_map/ppermute | solution.py:477
  45.8 0.5 collective-permute-done.10.refs_2_
  46.3 2.0 %all-to-all-done.1.parts = bf16[16,3,16,128]{3,2,1,0:T(8,128)(2,1)S(1)} async-done(((bf16[16,3,16,128]{3,2,1,0:T(8,128)(2,1)}), bf16[16,3,16,128]{3,2,1,0:T(8,128)(2,1)S(1)}, u32[]{:S(2)}, u32[]{:S(2)}) %all-to-all-start.1) | async-done | bytes 196640 | tf_op jit(solution)/shard_map/all_to_all | solution.py:589
  48.3 0.1 collective-permute-start.11
  48.4 1.3 %collective-permute-done.11.other = bf16[28,16,128]{2,1,0:T(8,128)(2,1)S(1)} collective-permute-done((bf16[28,16,128]{2,1,0:T(8,128)(2,1)S(1)}, bf16[28,16,128]{2,1,0:T(8,128)(2,1)S(1)}, u32[]{:S(2)}, u32[]{:S(2)}) %collective-permute-start.11) | collective-permute-done | bytes 114720 | tf_op jit(solution)/shard_map/ppermute | solution.py:477
  49.7 1.9 %shard_map.116 = (bf16[4,160,128]{2,1,0:T(8,128)(2,1)S(1)}, bf16[64,128]{1,0:T(8,128)(2,1)S(1)}) custom-call(s32[4,8]{1,0:T(4,128)S(1)} %copy-done.7, bf16[128,2560]{1,0:T(8,128)(2,1)S(1)} %bitcast.9, bf16[4,128,384]{2,1,0:T(8,128)(2,1)S(1)} %collective-permute-done.rest_8_.feat_other, bf16[28,16,128]{2,1,0:T(8,128)(2,1)S(1)} %shard_map.115.mine, ...), custom_call_target="tpu_custom_call" | custom-call | flops 60000000 | bytes 2000000 | tf_op jit(solution)/shard_map/pallas_call | solution.py:465
  51.7 7.9 %all_to_all.15.parts = bf16[4,160,128]{2,1,0:T(8,128)(2,1)S(1)} all-to-all(bf16[4,160,128]{2,1,0:T(8,128)(2,1)S(1)} %get-tuple-element.46), channel_id=1, replica_groups=mesh['dp'=4,'chip'=4,'core'=2] {'chip'}, dimensions={0} | all-to-all | bytes 327680 | tf_op jit(solution)/shard_map/all_to_all | solution.py:622
  59.6 1.3 %collective-permute-start.14 = (bf16[224,128]{1,0:T(8,128)(2,1)S(1)}, bf16[224,128]{1,0:T(8,128)(2,1)S(1)}, u32[]{:S(2)}, u32[]{:S(2)}) collective-permute-start(bf16[224,128]{1,0:T(8,128)(2,1)S(1)} %shard_map.117.rest_0_), channel_id=1, source_target_pairs={{0,24},{8,16},{16,8},{24,0},{1,25},{9,17},{17,9},{25,1},{2,26},{10... | collective-permute-start | bytes 172040 | tf_op jit(solution)/shard_map/ppermute | solution.py:477
  60.9 0.5 collective-permute-start.13
  61.4 2.6 %collective-permute-start.12 = (bf16[224,128]{1,0:T(8,128)(2,1)S(1)}, bf16[224,128]{1,0:T(8,128)(2,1)S(1)}, u32[]{:S(2)}, u32[]{:S(2)}) collective-permute-start(bf16[224,128]{1,0:T(8,128)(2,1)S(1)} %shard_map.117.rest_0_), channel_id=1, source_target_pairs={{0,8},{8,0},{16,24},{24,16},{1,9},{9,1},{17,25},{25,17},{2,10},{10... | collective-permute-start | bytes 172040 | tf_op jit(solution)/shard_map/ppermute | solution.py:477
  64.0 1.7 %collective-permute-done.14.rest_3_ = bf16[224,128]{1,0:T(8,128)(2,1)S(1)} collective-permute-done((bf16[224,128]{1,0:T(8,128)(2,1)S(1)}, bf16[224,128]{1,0:T(8,128)(2,1)S(1)}, u32[]{:S(2)}, u32[]{:S(2)}) %collective-permute-start.14) | collective-permute-done | bytes 57376 | tf_op jit(solution)/shard_map/ppermute | solution.py:477
  65.7 1.5 %collective-permute-done.13.rest_2_ = bf16[224,128]{1,0:T(8,128)(2,1)S(1)} collective-permute-done((bf16[224,128]{1,0:T(8,128)(2,1)S(1)}, bf16[224,128]{1,0:T(8,128)(2,1)S(1)}, u32[]{:S(2)}, u32[]{:S(2)}) %collective-permute-start.13) | collective-permute-done | bytes 57376 | tf_op jit(solution)/shard_map/ppermute | solution.py:477
  67.2 0.0 collective-permute-done.12.rest_1_
  67.2 0.8 %shard_map.118 = (f32[64,320]{1,0:T(8,128)}, f32[64,128]{1,0:T(8,128)}) custom-call(bf16[224,128]{1,0:T(8,128)(2,1)S(1)} %shard_map.117.rest_0_, bf16[224,128]{1,0:T(8,128)(2,1)S(1)} %collective-permute-done.12.rest_1_, bf16[224,128]{1,0:T(8,128)(2,1)S(1)} %collective-permute-done.13.rest_2_, bf16[224,128]{1,0:T(8,128)(2,1)S(1)} %collective-permute-done.14.rest_3_), custom_call_target="tpu_custom_call" | custom-call | bytes 400000 | tf_op jit(solution)/shard_map/pallas_call | solution.py:465
  (12 shorter events, 0.1 us)
Async XLA Ops:
  3.7 7.3 %copy-start = (bf16[1,8,16,2560]{3,2,1,0:T(8,128)(2,1)S(1)}, bf16[1,8,16,2560]{3,2,1,0:T(8,128)(2,1)}, u32[]{:S(2)}) copy-start(bf16[1,8,16,2560]{3,2,1,0:T(8,128)(2,1)} %param.9) | copy-start | bytes 1966084
  3.7 7.3 %copy-start.1 = (bf16[1,8,16,1024]{3,2,1,0:T(8,128)(2,1)S(1)}, bf16[1,8,16,1024]{3,2,1,0:T(8,128)(2,1)}, u32[]{:S(2)}) copy-start(bf16[1,8,16,1024]{3,2,1,0:T(8,128)(2,1)} %param.11) | copy-start | bytes 786436
  3.8 7.3 %copy-start.2 = (bf16[1,8,16,1024]{3,2,1,0:T(8,128)(2,1)S(1)}, bf16[1,8,16,1024]{3,2,1,0:T(8,128)(2,1)}, u32[]{:S(2)}) copy-start(bf16[1,8,16,1024]{3,2,1,0:T(8,128)(2,1)} %param.12) | copy-start | bytes 786436
  3.8 7.3 %copy-start.3 = (bf16[1,8,16,1024]{3,2,1,0:T(8,128)(2,1)S(1)}, bf16[1,8,16,1024]{3,2,1,0:T(8,128)(2,1)}, u32[]{:S(2)}) copy-start(bf16[1,8,16,1024]{3,2,1,0:T(8,128)(2,1)} %param.13) | copy-start | bytes 786436
  3.8 7.3 %copy-start.6 = (bf16[8,16,128]{2,1,0:T(8,128)(2,1)S(1)}, bf16[8,16,128]{2,1,0:T(8,128)(2,1)}, u32[]{:S(2)}) copy-start(bf16[8,16,128]{2,1,0:T(8,128)(2,1)} %get-tuple-element.28.adapter) | copy-start | bytes 98308
  3.8 26.9 %all-to-all-start = ((bf16[32,6,16,128]{3,2,1,0:T(8,128)(2,1)}), bf16[32,6,16,128]{3,2,1,0:T(8,128)(2,1)S(1)}, u32[]{:S(2)}, u32[]{:S(2)}) async-start(bf16[32,6,16,128]{3,2,1,0:T(8,128)(2,1)} %get-tuple-element.31), calls=%async_computation | async-start | bytes 1572864 | tf_op jit(solution)/shard_map/all_to_all | solution.py:561
  11.1 0.7 %copy-start.7 = (s32[4,8]{1,0:T(4,128)S(1)}, s32[4,8]{1,0:T(4,128)}, u32[]{:S(2)}) copy-start(s32[4,8]{1,0:T(4,128)} %plan.5) | copy-start | bytes 388
  11.7 0.9 %copy-start.4 = (bf16[8,16,1024]{2,1,0:T(8,128)(2,1)S(1)}, bf16[8,16,1024]{2,1,0:T(8,128)(2,1)}, u32[]{:S(2)}) copy-start(bf16[8,16,1024]{2,1,0:T(8,128)(2,1)} %get-tuple-element.27.queries) | copy-start | bytes 786436
  12.7 18.0 %copy-start.5 = (bf16[64,1024]{1,0:T(8,128)(2,1)S(1)}, bf16[64,1024]{1,0:T(8,128)(2,1)}, u32[]{:S(2)}) copy-start(bf16[64,1024]{1,0:T(8,128)(2,1)} %up.1) | copy-start | bytes 393220
  13.9 15.1 %collective-permute-start = (bf16[4,128,384]{2,1,0:T(8,128)(2,1)S(1)}, bf16[4,128,384]{2,1,0:T(8,128)(2,1)S(1)}, u32[]{:S(2)}, u32[]{:S(2)}) collective-permute-start(bf16[4,128,384]{2,1,0:T(8,128)(2,1)S(1)} %get-tuple-element.29), channel_id=1, source_target_pairs={{0,1},{1,0},{2,3},{3,2},{4,5},{5,4},{6,7},{7,6},{8,9},{9,8},{10,11... | collective-permute-start | bytes 1179656 | tf_op jit(solution)/shard_map/ppermute | solution.py:477
  14.3 3.5 %collective-permute-start.1 = (bf16[16,16,128]{2,1,0:T(8,128)(2,1)S(1)}, bf16[16,16,128]{2,1,0:T(8,128)(2,1)S(1)}, u32[]{:S(2)}, u32[]{:S(2)}) collective-permute-start(bf16[16,16,128]{2,1,0:T(8,128)(2,1)S(1)} %get-tuple-element.33), channel_id=1, source_target_pairs={{0,1},{1,0},{2,3},{3,2},{4,5},{5,4},{6,7},{7,6},{8,9},{9,8},{10,11... | collective-permute-start | bytes 196616 | tf_op jit(solution)/shard_map/ppermute | solution.py:477
  14.5 6.0 %collective-permute-start.2 = (bf16[16,16,128]{2,1,0:T(8,128)(2,1)S(1)}, bf16[16,16,128]{2,1,0:T(8,128)(2,1)S(1)}, u32[]{:S(2)}, u32[]{:S(2)}) collective-permute-start(bf16[16,16,128]{2,1,0:T(8,128)(2,1)S(1)} %get-tuple-element.34), channel_id=1, source_target_pairs={{0,2},{1,3},{2,0},{3,1},{4,6},{5,7},{6,4},{7,5},{8,10},{9,11},{10,... | collective-permute-start | bytes 196616 | tf_op jit(solution)/shard_map/ppermute | solution.py:477
  16.3 7.1 %collective-permute-start.3 = (bf16[16,16,128]{2,1,0:T(8,128)(2,1)S(1)}, bf16[16,16,128]{2,1,0:T(8,128)(2,1)S(1)}, u32[]{:S(2)}, u32[]{:S(2)}) collective-permute-start(bf16[16,16,128]{2,1,0:T(8,128)(2,1)S(1)} %get-tuple-element.35), channel_id=1, source_target_pairs={{0,3},{1,2},{2,1},{3,0},{4,7},{5,6},{6,5},{7,4},{8,11},{9,10},{10,... | collective-permute-start | bytes 196616 | tf_op jit(solution)/shard_map/ppermute | solution.py:477
  16.3 8.4 %collective-permute-start.4 = (bf16[16,16,128]{2,1,0:T(8,128)(2,1)S(1)}, bf16[16,16,128]{2,1,0:T(8,128)(2,1)S(1)}, u32[]{:S(2)}, u32[]{:S(2)}) collective-permute-start(bf16[16,16,128]{2,1,0:T(8,128)(2,1)S(1)} %get-tuple-element.36), channel_id=1, source_target_pairs={{0,4},{1,5},{2,6},{3,7},{4,0},{5,1},{6,2},{7,3},{8,12},{9,13},{10,... | collective-permute-start | bytes 196616 | tf_op jit(solution)/shard_map/ppermute | solution.py:477
  17.8 12.9 %copy-start.8 = (s32[1,1024]{1,0:T(1,128)S(1)}, s32[1,1024]{1,0:T(1,128)}, u32[]{:S(2)}) copy-start(s32[1,1024]{1,0:T(1,128)} %seg.1) | copy-start | bytes 12292
  17.8 6.9 %collective-permute-start.5 = (bf16[16,16,128]{2,1,0:T(8,128)(2,1)S(1)}, bf16[16,16,128]{2,1,0:T(8,128)(2,1)S(1)}, u32[]{:S(2)}, u32[]{:S(2)}) collective-permute-start(bf16[16,16,128]{2,1,0:T(8,128)(2,1)S(1)} %get-tuple-element.37), channel_id=1, source_target_pairs={{0,5},{1,4},{2,7},{3,6},{4,1},{5,0},{6,3},{7,2},{8,13},{9,12},{10,... | collective-permute-start | bytes 196616 | tf_op jit(solution)/shard_map/ppermute | solution.py:477
  20.5 5.3 %collective-permute-start.6 = (bf16[16,16,128]{2,1,0:T(8,128)(2,1)S(1)}, bf16[16,16,128]{2,1,0:T(8,128)(2,1)S(1)}, u32[]{:S(2)}, u32[]{:S(2)}) collective-permute-start(bf16[16,16,128]{2,1,0:T(8,128)(2,1)S(1)} %get-tuple-element.38), channel_id=1, source_target_pairs={{0,6},{1,7},{2,4},{3,5},{4,2},{5,3},{6,0},{7,1},{8,14},{9,15},{10,... | collective-permute-start | bytes 196616 | tf_op jit(solution)/shard_map/ppermute | solution.py:477
  23.4 5.7 %collective-permute-start.7 = (bf16[16,16,128]{2,1,0:T(8,128)(2,1)S(1)}, bf16[16,16,128]{2,1,0:T(8,128)(2,1)S(1)}, u32[]{:S(2)}, u32[]{:S(2)}) collective-permute-start(bf16[16,16,128]{2,1,0:T(8,128)(2,1)S(1)} %get-tuple-element.39), channel_id=1, source_target_pairs={{0,7},{1,6},{2,5},{3,4},{4,3},{5,2},{6,1},{7,0},{8,15},{9,14},{10,... | collective-permute-start | bytes 196616 | tf_op jit(solution)/shard_map/ppermute | solution.py:477
  33.7 14.6 %all-to-all-start.1 = ((bf16[16,3,16,128]{3,2,1,0:T(8,128)(2,1)}), bf16[16,3,16,128]{3,2,1,0:T(8,128)(2,1)S(1)}, u32[]{:S(2)}, u32[]{:S(2)}) async-start(bf16[16,3,16,128]{3,2,1,0:T(8,128)(2,1)} %get-tuple-element.40), calls=%async_computation.1 | async-start | bytes 393216 | tf_op jit(solution)/shard_map/all_to_all | solution.py:589
  39.1 5.0 %collective-permute-start.8 = (bf16[2,2,16,128]{3,2,1,0:T(8,128)(2,1)S(1)}, bf16[2,2,16,128]{3,2,1,0:T(8,128)(2,1)S(1)}, u32[]{:S(2)}, u32[]{:S(2)}) collective-permute-start(bf16[2,2,16,128]{3,2,1,0:T(8,128)(2,1)S(1)} %get-tuple-element.41), channel_id=1, source_target_pairs={{0,6},{2,4},{4,2},{6,0},{1,7},{3,5},{5,3},{7,1},{8,14},{10,12},{12... | collective-permute-start | bytes 49160 | tf_op jit(solution)/shard_map/ppermute | solution.py:477
  42.0 3.9 %collective-permute-start.9 = (bf16[2,2,16,128]{3,2,1,0:T(8,128)(2,1)S(1)}, bf16[2,2,16,128]{3,2,1,0:T(8,128)(2,1)S(1)}, u32[]{:S(2)}, u32[]{:S(2)}) collective-permute-start(bf16[2,2,16,128]{3,2,1,0:T(8,128)(2,1)S(1)} %get-tuple-element.42), channel_id=1, source_target_pairs={{0,4},{2,6},{4,0},{6,2},{1,5},{3,7},{5,1},{7,3},{8,12},{10,14},{12... | collective-permute-start | bytes 49160 | tf_op jit(solution)/shard_map/ppermute | solution.py:477
  42.5 3.8 %collective-permute-start.10 = (bf16[2,2,16,128]{3,2,1,0:T(8,128)(2,1)S(1)}, bf16[2,2,16,128]{3,2,1,0:T(8,128)(2,1)S(1)}, u32[]{:S(2)}, u32[]{:S(2)}) collective-permute-start(bf16[2,2,16,128]{3,2,1,0:T(8,128)(2,1)S(1)} %get-tuple-element.43), channel_id=1, source_target_pairs={{0,2},{2,0},{4,6},{6,4},{1,3},{3,1},{5,7},{7,5},{8,10},{10,8},{12,... | collective-permute-start | bytes 49160 | tf_op jit(solution)/shard_map/ppermute | solution.py:477
  48.3 1.4 %collective-permute-start.11 = (bf16[28,16,128]{2,1,0:T(8,128)(2,1)S(1)}, bf16[28,16,128]{2,1,0:T(8,128)(2,1)S(1)}, u32[]{:S(2)}, u32[]{:S(2)}) collective-permute-start(bf16[28,16,128]{2,1,0:T(8,128)(2,1)S(1)} %shard_map.115.mine), channel_id=1, source_target_pairs={{0,1},{1,0},{2,3},{3,2},{4,5},{5,4},{6,7},{7,6},{8,9},{9,8},{10,11... | collective-permute-start | bytes 344072 | tf_op jit(solution)/shard_map/ppermute | solution.py:477
  59.6 6.2 %collective-permute-start.14 = (bf16[224,128]{1,0:T(8,128)(2,1)S(1)}, bf16[224,128]{1,0:T(8,128)(2,1)S(1)}, u32[]{:S(2)}, u32[]{:S(2)}) collective-permute-start(bf16[224,128]{1,0:T(8,128)(2,1)S(1)} %shard_map.117.rest_0_), channel_id=1, source_target_pairs={{0,24},{8,16},{16,8},{24,0},{1,25},{9,17},{17,9},{25,1},{2,26},{10... | collective-permute-start | bytes 172040 | tf_op jit(solution)/shard_map/ppermute | solution.py:477
  60.9 6.3 %collective-permute-start.13 = (bf16[224,128]{1,0:T(8,128)(2,1)S(1)}, bf16[224,128]{1,0:T(8,128)(2,1)S(1)}, u32[]{:S(2)}, u32[]{:S(2)}) collective-permute-start(bf16[224,128]{1,0:T(8,128)(2,1)S(1)} %shard_map.117.rest_0_), channel_id=1, source_target_pairs={{0,16},{8,24},{16,0},{24,8},{1,17},{9,25},{17,1},{25,9},{2,18},{10... | collective-permute-start | bytes 172040 | tf_op jit(solution)/shard_map/ppermute | solution.py:477
  61.4 5.8 %collective-permute-start.12 = (bf16[224,128]{1,0:T(8,128)(2,1)S(1)}, bf16[224,128]{1,0:T(8,128)(2,1)S(1)}, u32[]{:S(2)}, u32[]{:S(2)}) collective-permute-start(bf16[224,128]{1,0:T(8,128)(2,1)S(1)} %shard_map.117.rest_0_), channel_id=1, source_target_pairs={{0,8},{8,0},{16,24},{24,16},{1,9},{9,1},{17,25},{25,17},{2,10},{10... | collective-permute-start | bytes 172040 | tf_op jit(solution)/shard_map/ppermute | solution.py:477

commit v9 on v8

--- a/solution.py
+++ b/solution.py
@@ -139,30 +139,33 @@
     routes[0, 0] = 0
     each_hit(plan, me, groups, blocks, live, put_early)
     early = send(0, 2 * CAP, 0)
-    for copy in copies[3:]:
+    for copy in copies[3:5]:
         copy.wait()
     narrow = lax.dot_general(feat[...], down[...], NT, preferred_element_type=jnp.float32)
     adapter = narrow.astype(jnp.bfloat16)
+    for copy in copies[5:]:
+        copy.wait()
     lift = jnp.dot(adapter, up[...], preferred_element_type=jnp.float32)
     abuf[...] = jnp.concatenate([narrow, narrow], axis=1).astype(jnp.bfloat16).reshape(abuf.shape)
     qbuf[...] = (base[...].astype(jnp.float32) + lift.reshape(base.shape)).astype(jnp.bfloat16)
 
-    def put_late(index, _):
-        dest, slot, local = routes[1, index], routes[2, index], routes[3, index]
-
-        for head in range(heads):
-            columns = slice(head * LANES, (head + 1) * LANES)
-            far_out[head * groups + dest, 2 * CAP + slot] = qbuf[local, :, columns]
-        return 0
-
-    lax.fori_loop(0, routes[0, 0], put_late, 0)
-    late = send(2 * CAP, CAP, 1)
     rest_out = [
         pltpu.make_async_copy(qbuf, queries_hbm, out_sems.at[2]),
         pltpu.make_async_copy(abuf, adapter_hbm, out_sems.at[3]),
     ]
     for copy in rest_out:
         copy.start()
+
+    def put_late(index, _):
+        dest, slot, local = routes[1, index], routes[2, index], routes[3, index]
+
+        for head in range(heads):
+            columns = slice(head * LANES, (head + 1) * LANES)
+            far_out[head * groups + dest, 2 * CAP + slot] = qbuf[local, :, columns]
+        return 0
+
+    lax.fori_loop(0, routes[0, 0], put_late, 0)
+    late = send(2 * CAP, CAP, 1)
     for copy in [early, late] + rest_out:
         copy.wait()
 

time: 68.4 us -> 68.3 us (level)
  no operation moved by 1% of the time
where the time goes in v9:
time: 68.3 us; the launch traced here: 68 us
  starting transfers between devices  29.2 us (43%)
  waiting for transfers between devices  18.5 us (27%)
  Pallas kernels  10 us (15%)
  blocking collectives  7.88 us (12%)
  local copies, waits for them, and re-layouts  1.62 us (2%)
  between operations  0.79 us (1%)
    ppermute x15, starting transfers between devices, exchange(): lax.ppermute(value, axis, [(peer, peer ^ turn) for peer in range(size)])  16.4 us
    ppermute x15, waiting for transfers between devices, exchange(): lax.ppermute(value, axis, [(peer, peer ^ turn) for peer in range(size)])  15 us
    pallas_call x7, Pallas kernels, call(): pl.pallas_call(kernel, out_shape=shapes, in_specs=specs, out_specs=out_sp...  10 us
    all_to_all x1, blocking collectives, per_device_tiles(): shares = lax.all_to_all(shares, 'chip', 0, 0, tiled=True)  7.88 us
    all_to_all x1, starting transfers between devices, per_device_tiles(): far = lax.all_to_all(far_send, everyone, 0, 0, tiled=True)  7.34 us
    all_to_all x1, starting transfers between devices, per_device_tiles(): part = lax.all_to_all(attended[0], ('chip', 'dp'), 0, 0, tiled=True)  5.44 us
    all_to_all x1, waiting for transfers between devices, per_device_tiles(): part = lax.all_to_all(attended[0], ('chip', 'dp'), 0, 0, tiled=True)  1.97 us
    unnamed x18, local copies, waits for them, and re-layouts  1.62 us
  transfers between devices with their start and end apart: 17, of which 11 were waited for; matrix products, arithmetic and copies ran while one was open for 0% of the time, Pallas kernels for 2%

profile of v9, /device:TPU:0, one launch (start us, length us, event | category | flops | bytes accessed | tf_op | source)
XLA Modules:
  0.0 68.0 jit_solution(4036569841375350652)
XLA Ops:
  0.6 3.0 %shard_map.112 = (bf16[32,6,16,128]{3,2,1,0:T(8,128)(2,1)}, bf16[8,16,1024]{2,1,0:T(8,128)(2,1)}, bf16[8,16,128]{2,1,0:T(8,128)(2,1)}) custom-call(s32[4,8]{1,0:T(4,128)} %plan.5, bf16[128,2560]{1,0:T(8,128)(2,1)} %bitcast.7, bf16[8,16,1024]{2,1,0:T(8,128)(2,1)} %bitcast.16, bf16[8,16,1024]{2,1,0:T(8,128)(2,1)} %bitcast.10, bf16[8,16,1024]{2,1,0:T(8,128)(2,1)} %bitcast.12, ...), custom_call_target="tpu_custom_call" | custom-call | flops 60000000 | bytes 4000000 | tf_op jit(solution)/shard_map/pallas_call | solution.py:468
  3.7 0.0 copy-start
  3.7 0.0 copy-start.1
  3.7 0.0 copy-start.2
  3.7 0.0 copy-start.3
  3.7 0.0 copy-start.6
  3.7 7.3 %all-to-all-start = ((bf16[32,6,16,128]{3,2,1,0:T(8,128)(2,1)}), bf16[32,6,16,128]{3,2,1,0:T(8,128)(2,1)S(1)}, u32[]{:S(2)}, u32[]{:S(2)}) async-start(bf16[32,6,16,128]{3,2,1,0:T(8,128)(2,1)} %get-tuple-element.31), calls=%async_computation | async-start | bytes 1572864 | tf_op jit(solution)/shard_map/all_to_all | solution.py:564
  11.1 0.0 copy-start.7
  11.1 0.6 copy-done.7
  11.8 0.9 %copy-done.4 = bf16[8,16,1024]{2,1,0:T(8,128)(2,1)S(1)} copy-done((bf16[8,16,1024]{2,1,0:T(8,128)(2,1)S(1)}, bf16[8,16,1024]{2,1,0:T(8,128)(2,1)}, u32[]{:S(2)}) %copy-start.4) | copy-done | bytes 262168
  12.7 1.2 %shard_map.113 = (bf16[16,16,128]{2,1,0:T(8,128)(2,1)S(1)}, bf16[16,16,128]{2,1,0:T(8,128)(2,1)S(1)}, bf16[16,16,128]{2,1,0:T(8,128)(2,1)S(1)}, bf16[16,16,128]{...) custom-call(s32[4,8]{1,0:T(4,128)S(1)} %copy-done.7, ...), custom_call_target="tpu_custom_call" | custom-call | bytes 1600000 | tf_op jit(solution)/shard_map/pallas_call | solution.py:468
  13.9 0.3 collective-permute-start
  14.2 0.3 collective-permute-start.1
  14.5 1.8 %collective-permute-start.2 = (bf16[16,16,128]{2,1,0:T(8,128)(2,1)S(1)}, bf16[16,16,128]{2,1,0:T(8,128)(2,1)S(1)}, u32[]{:S(2)}, u32[]{:S(2)}) collective-permute-start(bf16[16,16,128]{2,1,0:T(8,128)(2,1)S(1)} %get-tuple-element.34), channel_id=1, source_target_pairs={{0,2},{1,3},{2,0},{3,1},{4,6},{5,7},{6,4},{7,5},{8,10},{9,11},{10,... | collective-permute-start | bytes 196616 | tf_op jit(solution)/shard_map/ppermute | solution.py:480
  16.3 0.0 collective-permute-start.3
  16.3 1.5 %collective-permute-start.4 = (bf16[16,16,128]{2,1,0:T(8,128)(2,1)S(1)}, bf16[16,16,128]{2,1,0:T(8,128)(2,1)S(1)}, u32[]{:S(2)}, u32[]{:S(2)}) collective-permute-start(bf16[16,16,128]{2,1,0:T(8,128)(2,1)S(1)} %get-tuple-element.36), channel_id=1, source_target_pairs={{0,4},{1,5},{2,6},{3,7},{4,0},{5,1},{6,2},{7,3},{8,12},{9,13},{10,... | collective-permute-start | bytes 196616 | tf_op jit(solution)/shard_map/ppermute | solution.py:480
  17.8 0.0 collective-permute-done.1.rest_1_
  17.8 0.3 collective-permute-start.5
  18.1 2.4 %collective-permute-done.2.rest_2_ = bf16[16,16,128]{2,1,0:T(8,128)(2,1)S(1)} collective-permute-done((bf16[16,16,128]{2,1,0:T(8,128)(2,1)S(1)}, bf16[16,16,128]{2,1,0:T(8,128)(2,1)S(1)}, u32[]{:S(2)}, u32[]{:S(2)}) %collective-permute-start.2) | collective-permute-done | bytes 65568 | tf_op jit(solution)/shard_map/ppermute | solution.py:480
  20.5 2.9 %collective-permute-start.6 = (bf16[16,16,128]{2,1,0:T(8,128)(2,1)S(1)}, bf16[16,16,128]{2,1,0:T(8,128)(2,1)S(1)}, u32[]{:S(2)}, u32[]{:S(2)}) collective-permute-start(bf16[16,16,128]{2,1,0:T(8,128)(2,1)S(1)} %get-tuple-element.38), channel_id=1, source_target_pairs={{0,6},{1,7},{2,4},{3,5},{4,2},{5,3},{6,0},{7,1},{8,14},{9,15},{10,... | collective-permute-start | bytes 196616 | tf_op jit(solution)/shard_map/ppermute | solution.py:480
  23.4 0.0 collective-permute-done.3.rest_3_
  23.4 1.2 %collective-permute-start.7 = (bf16[16,16,128]{2,1,0:T(8,128)(2,1)S(1)}, bf16[16,16,128]{2,1,0:T(8,128)(2,1)S(1)}, u32[]{:S(2)}, u32[]{:S(2)}) collective-permute-start(bf16[16,16,128]{2,1,0:T(8,128)(2,1)S(1)} %get-tuple-element.39), channel_id=1, source_target_pairs={{0,7},{1,6},{2,5},{3,4},{4,3},{5,2},{6,1},{7,0},{8,15},{9,14},{10,... | collective-permute-start | bytes 196616 | tf_op jit(solution)/shard_map/ppermute | solution.py:480
  24.6 0.0 collective-permute-done.4.rest_4_
  24.6 0.0 collective-permute-done.5.rest_5_
  24.6 1.2 %collective-permute-done.6.rest_6_ = bf16[16,16,128]{2,1,0:T(8,128)(2,1)S(1)} collective-permute-done((bf16[16,16,128]{2,1,0:T(8,128)(2,1)S(1)}, bf16[16,16,128]{2,1,0:T(8,128)(2,1)S(1)}, u32[]{:S(2)}, u32[]{:S(2)}) %collective-permute-start.6) | collective-permute-done | bytes 65568 | tf_op jit(solution)/shard_map/ppermute | solution.py:480
  25.8 3.3 %collective-permute-done.7.rest_7_ = bf16[16,16,128]{2,1,0:T(8,128)(2,1)S(1)} collective-permute-done((bf16[16,16,128]{2,1,0:T(8,128)(2,1)S(1)}, bf16[16,16,128]{2,1,0:T(8,128)(2,1)S(1)}, u32[]{:S(2)}, u32[]{:S(2)}) %collective-permute-start.7) | collective-permute-done | bytes 65568 | tf_op jit(solution)/shard_map/ppermute | solution.py:480
  29.1 0.0 collective-permute-done.rest_8_.feat_other
  29.1 1.6 %all-to-all-done.far_in = bf16[32,6,16,128]{3,2,1,0:T(8,128)(2,1)S(1)} async-done(((bf16[32,6,16,128]{3,2,1,0:T(8,128)(2,1)}), bf16[32,6,16,128]{3,2,1,0:T(8,128)(2,1)S(1)}, u32[]{:S(2)}, u32[]{:S(2)}) %all-to-all-start) | async-done | bytes 786464 | tf_op jit(solution)/shard_map/all_to_all | solution.py:564
  30.7 3.0 %shard_map.114 = (bf16[16,3,16,128]{3,2,1,0:T(8,128)(2,1)}, bf16[2,2,16,128]{3,2,1,0:T(8,128)(2,1)S(1)}, bf16[2,2,16,128]{3,2,1,0:T(8,128)(2,1)S(1)}, bf16[2,2,1...) custom-call(s32[4,8]{1,0:T(4,128)S(1)} %copy-done.7, ...), custom_call_target="tpu_custom_call" | custom-call | flops 600000000 | bytes 3000000 | tf_op jit(solution)/shard_map/pallas_call | solution.py:468
  33.7 5.4 %all-to-all-start.1 = ((bf16[16,3,16,128]{3,2,1,0:T(8,128)(2,1)}), bf16[16,3,16,128]{3,2,1,0:T(8,128)(2,1)S(1)}, u32[]{:S(2)}, u32[]{:S(2)}) async-start(bf16[16,3,16,128]{3,2,1,0:T(8,128)(2,1)} %get-tuple-element.40), calls=%async_computation.1 | async-start | bytes 393216 | tf_op jit(solution)/shard_map/all_to_all | solution.py:592
  39.2 2.8 %collective-permute-start.8 = (bf16[2,2,16,128]{3,2,1,0:T(8,128)(2,1)S(1)}, bf16[2,2,16,128]{3,2,1,0:T(8,128)(2,1)S(1)}, u32[]{:S(2)}, u32[]{:S(2)}) collective-permute-start(bf16[2,2,16,128]{3,2,1,0:T(8,128)(2,1)S(1)} %get-tuple-element.41), channel_id=1, source_target_pairs={{0,6},{2,4},{4,2},{6,0},{1,7},{3,5},{5,3},{7,1},{8,14},{10,12},{12... | collective-permute-start | bytes 49160 | tf_op jit(solution)/shard_map/ppermute | solution.py:480
  42.0 0.6 collective-permute-start.9
  42.6 0.2 collective-permute-start.10
  42.7 1.5 %collective-permute-done.8.refs_0_ = bf16[2,2,16,128]{3,2,1,0:T(8,128)(2,1)S(1)} collective-permute-done((bf16[2,2,16,128]{3,2,1,0:T(8,128)(2,1)S(1)}, bf16[2,2,16,128]{3,2,1,0:T(8,128)(2,1)S(1)}, u32[]{:S(2)}, u32[]{:S(2)}) %collective-permute-start.8) | collective-permute-done | bytes 16416 | tf_op jit(solution)/shard_map/ppermute | solution.py:480
  44.2 1.7 %collective-permute-done.9.refs_1_ = bf16[2,2,16,128]{3,2,1,0:T(8,128)(2,1)S(1)} collective-permute-done((bf16[2,2,16,128]{3,2,1,0:T(8,128)(2,1)S(1)}, bf16[2,2,16,128]{3,2,1,0:T(8,128)(2,1)S(1)}, u32[]{:S(2)}, u32[]{:S(2)}) %collective-permute-start.9) | collective-permute-done | bytes 16416 | tf_op jit(solution)/shard_map/ppermute | solution.py:480
  45.8 0.5 collective-permute-done.10.refs_2_
  46.3 2.0 %all-to-all-done.1.parts = bf16[16,3,16,128]{3,2,1,0:T(8,128)(2,1)S(1)} async-done(((bf16[16,3,16,128]{3,2,1,0:T(8,128)(2,1)}), bf16[16,3,16,128]{3,2,1,0:T(8,128)(2,1)S(1)}, u32[]{:S(2)}, u32[]{:S(2)}) %all-to-all-start.1) | async-done | bytes 196640 | tf_op jit(solution)/shard_map/all_to_all | solution.py:592
  48.3 0.1 collective-permute-start.11
  48.4 1.3 %collective-permute-done.11.other = bf16[28,16,128]{2,1,0:T(8,128)(2,1)S(1)} collective-permute-done((bf16[28,16,128]{2,1,0:T(8,128)(2,1)S(1)}, bf16[28,16,128]{2,1,0:T(8,128)(2,1)S(1)}, u32[]{:S(2)}, u32[]{:S(2)}) %collective-permute-start.11) | collective-permute-done | bytes 114720 | tf_op jit(solution)/shard_map/ppermute | solution.py:480
  49.7 1.9 %shard_map.116 = (bf16[4,160,128]{2,1,0:T(8,128)(2,1)S(1)}, bf16[64,128]{1,0:T(8,128)(2,1)S(1)}) custom-call(s32[4,8]{1,0:T(4,128)S(1)} %copy-done.7, bf16[128,2560]{1,0:T(8,128)(2,1)S(1)} %bitcast.9, bf16[4,128,384]{2,1,0:T(8,128)(2,1)S(1)} %collective-permute-done.rest_8_.feat_other, bf16[28,16,128]{2,1,0:T(8,128)(2,1)S(1)} %shard_map.115.mine, ...), custom_call_target="tpu_custom_call" | custom-call | flops 60000000 | bytes 2000000 | tf_op jit(solution)/shard_map/pallas_call | solution.py:468
  51.6 7.9 %all_to_all.15.parts = bf16[4,160,128]{2,1,0:T(8,128)(2,1)S(1)} all-to-all(bf16[4,160,128]{2,1,0:T(8,128)(2,1)S(1)} %get-tuple-element.46), channel_id=1, replica_groups=mesh['dp'=4,'chip'=4,'core'=2] {'chip'}, dimensions={0} | all-to-all | bytes 327680 | tf_op jit(solution)/shard_map/all_to_all | solution.py:625
  59.5 1.5 %collective-permute-start.14 = (bf16[224,128]{1,0:T(8,128)(2,1)S(1)}, bf16[224,128]{1,0:T(8,128)(2,1)S(1)}, u32[]{:S(2)}, u32[]{:S(2)}) collective-permute-start(bf16[224,128]{1,0:T(8,128)(2,1)S(1)} %shard_map.117.rest_0_), channel_id=1, source_target_pairs={{0,24},{8,16},{16,8},{24,0},{1,25},{9,17},{17,9},{25,1},{2,26},{10... | collective-permute-start | bytes 172040 | tf_op jit(solution)/shard_map/ppermute | solution.py:480
  61.0 0.4 collective-permute-start.13
  61.4 2.5 %collective-permute-start.12 = (bf16[224,128]{1,0:T(8,128)(2,1)S(1)}, bf16[224,128]{1,0:T(8,128)(2,1)S(1)}, u32[]{:S(2)}, u32[]{:S(2)}) collective-permute-start(bf16[224,128]{1,0:T(8,128)(2,1)S(1)} %shard_map.117.rest_0_), channel_id=1, source_target_pairs={{0,8},{8,0},{16,24},{24,16},{1,9},{9,1},{17,25},{25,17},{2,10},{10... | collective-permute-start | bytes 172040 | tf_op jit(solution)/shard_map/ppermute | solution.py:480
  63.9 1.7 %collective-permute-done.14.rest_3_ = bf16[224,128]{1,0:T(8,128)(2,1)S(1)} collective-permute-done((bf16[224,128]{1,0:T(8,128)(2,1)S(1)}, bf16[224,128]{1,0:T(8,128)(2,1)S(1)}, u32[]{:S(2)}, u32[]{:S(2)}) %collective-permute-start.14) | collective-permute-done | bytes 57376 | tf_op jit(solution)/shard_map/ppermute | solution.py:480
  65.6 1.5 %collective-permute-done.13.rest_2_ = bf16[224,128]{1,0:T(8,128)(2,1)S(1)} collective-permute-done((bf16[224,128]{1,0:T(8,128)(2,1)S(1)}, bf16[224,128]{1,0:T(8,128)(2,1)S(1)}, u32[]{:S(2)}, u32[]{:S(2)}) %collective-permute-start.13) | collective-permute-done | bytes 57376 | tf_op jit(solution)/shard_map/ppermute | solution.py:480
  67.2 0.0 collective-permute-done.12.rest_1_
  67.2 0.8 %shard_map.118 = (f32[64,320]{1,0:T(8,128)}, f32[64,128]{1,0:T(8,128)}) custom-call(bf16[224,128]{1,0:T(8,128)(2,1)S(1)} %shard_map.117.rest_0_, bf16[224,128]{1,0:T(8,128)(2,1)S(1)} %collective-permute-done.12.rest_1_, bf16[224,128]{1,0:T(8,128)(2,1)S(1)} %collective-permute-done.13.rest_2_, bf16[224,128]{1,0:T(8,128)(2,1)S(1)} %collective-permute-done.14.rest_3_), custom_call_target="tpu_custom_call" | custom-call | bytes 400000 | tf_op jit(solution)/shard_map/pallas_call | solution.py:468
  (12 shorter events, 0.1 us)
Async XLA Ops:
  3.7 7.4 %copy-start = (bf16[1,8,16,2560]{3,2,1,0:T(8,128)(2,1)S(1)}, bf16[1,8,16,2560]{3,2,1,0:T(8,128)(2,1)}, u32[]{:S(2)}) copy-start(bf16[1,8,16,2560]{3,2,1,0:T(8,128)(2,1)} %param.9) | copy-start | bytes 1966084
  3.7 7.4 %copy-start.1 = (bf16[1,8,16,1024]{3,2,1,0:T(8,128)(2,1)S(1)}, bf16[1,8,16,1024]{3,2,1,0:T(8,128)(2,1)}, u32[]{:S(2)}) copy-start(bf16[1,8,16,1024]{3,2,1,0:T(8,128)(2,1)} %param.11) | copy-start | bytes 786436
  3.7 7.4 %copy-start.2 = (bf16[1,8,16,1024]{3,2,1,0:T(8,128)(2,1)S(1)}, bf16[1,8,16,1024]{3,2,1,0:T(8,128)(2,1)}, u32[]{:S(2)}) copy-start(bf16[1,8,16,1024]{3,2,1,0:T(8,128)(2,1)} %param.12) | copy-start | bytes 786436
  3.7 7.4 %copy-start.3 = (bf16[1,8,16,1024]{3,2,1,0:T(8,128)(2,1)S(1)}, bf16[1,8,16,1024]{3,2,1,0:T(8,128)(2,1)}, u32[]{:S(2)}) copy-start(bf16[1,8,16,1024]{3,2,1,0:T(8,128)(2,1)} %param.13) | copy-start | bytes 786436
  3.7 7.4 %copy-start.6 = (bf16[8,16,128]{2,1,0:T(8,128)(2,1)S(1)}, bf16[8,16,128]{2,1,0:T(8,128)(2,1)}, u32[]{:S(2)}) copy-start(bf16[8,16,128]{2,1,0:T(8,128)(2,1)} %get-tuple-element.28.adapter) | copy-start | bytes 98308
  3.7 27.0 %all-to-all-start = ((bf16[32,6,16,128]{3,2,1,0:T(8,128)(2,1)}), bf16[32,6,16,128]{3,2,1,0:T(8,128)(2,1)S(1)}, u32[]{:S(2)}, u32[]{:S(2)}) async-start(bf16[32,6,16,128]{3,2,1,0:T(8,128)(2,1)} %get-tuple-element.31), calls=%async_computation | async-start | bytes 1572864 | tf_op jit(solution)/shard_map/all_to_all | solution.py:564
  11.1 0.7 %copy-start.7 = (s32[4,8]{1,0:T(4,128)S(1)}, s32[4,8]{1,0:T(4,128)}, u32[]{:S(2)}) copy-start(s32[4,8]{1,0:T(4,128)} %plan.5) | copy-start | bytes 388
  11.7 0.9 %copy-start.4 = (bf16[8,16,1024]{2,1,0:T(8,128)(2,1)S(1)}, bf16[8,16,1024]{2,1,0:T(8,128)(2,1)}, u32[]{:S(2)}) copy-start(bf16[8,16,1024]{2,1,0:T(8,128)(2,1)} %get-tuple-element.27.queries) | copy-start | bytes 786436
  12.7 18.0 %copy-start.5 = (bf16[64,1024]{1,0:T(8,128)(2,1)S(1)}, bf16[64,1024]{1,0:T(8,128)(2,1)}, u32[]{:S(2)}) copy-start(bf16[64,1024]{1,0:T(8,128)(2,1)} %up.1) | copy-start | bytes 393220
  13.9 15.1 %collective-permute-start = (bf16[4,128,384]{2,1,0:T(8,128)(2,1)S(1)}, bf16[4,128,384]{2,1,0:T(8,128)(2,1)S(1)}, u32[]{:S(2)}, u32[]{:S(2)}) collective-permute-start(bf16[4,128,384]{2,1,0:T(8,128)(2,1)S(1)} %get-tuple-element.29), channel_id=1, source_target_pairs={{0,1},{1,0},{2,3},{3,2},{4,5},{5,4},{6,7},{7,6},{8,9},{9,8},{10,11... | collective-permute-start | bytes 1179656 | tf_op jit(solution)/shard_map/ppermute | solution.py:480
  14.2 3.5 %collective-permute-start.1 = (bf16[16,16,128]{2,1,0:T(8,128)(2,1)S(1)}, bf16[16,16,128]{2,1,0:T(8,128)(2,1)S(1)}, u32[]{:S(2)}, u32[]{:S(2)}) collective-permute-start(bf16[16,16,128]{2,1,0:T(8,128)(2,1)S(1)} %get-tuple-element.33), channel_id=1, source_target_pairs={{0,1},{1,0},{2,3},{3,2},{4,5},{5,4},{6,7},{7,6},{8,9},{9,8},{10,11... | collective-permute-start | bytes 196616 | tf_op jit(solution)/shard_map/ppermute | solution.py:480
  14.5 6.0 %collective-permute-start.2 = (bf16[16,16,128]{2,1,0:T(8,128)(2,1)S(1)}, bf16[16,16,128]{2,1,0:T(8,128)(2,1)S(1)}, u32[]{:S(2)}, u32[]{:S(2)}) collective-permute-start(bf16[16,16,128]{2,1,0:T(8,128)(2,1)S(1)} %get-tuple-element.34), channel_id=1, source_target_pairs={{0,2},{1,3},{2,0},{3,1},{4,6},{5,7},{6,4},{7,5},{8,10},{9,11},{10,... | collective-permute-start | bytes 196616 | tf_op jit(solution)/shard_map/ppermute | solution.py:480
  16.3 7.1 %collective-permute-start.3 = (bf16[16,16,128]{2,1,0:T(8,128)(2,1)S(1)}, bf16[16,16,128]{2,1,0:T(8,128)(2,1)S(1)}, u32[]{:S(2)}, u32[]{:S(2)}) collective-permute-start(bf16[16,16,128]{2,1,0:T(8,128)(2,1)S(1)} %get-tuple-element.35), channel_id=1, source_target_pairs={{0,3},{1,2},{2,1},{3,0},{4,7},{5,6},{6,5},{7,4},{8,11},{9,10},{10,... | collective-permute-start | bytes 196616 | tf_op jit(solution)/shard_map/ppermute | solution.py:480
  16.3 8.4 %collective-permute-start.4 = (bf16[16,16,128]{2,1,0:T(8,128)(2,1)S(1)}, bf16[16,16,128]{2,1,0:T(8,128)(2,1)S(1)}, u32[]{:S(2)}, u32[]{:S(2)}) collective-permute-start(bf16[16,16,128]{2,1,0:T(8,128)(2,1)S(1)} %get-tuple-element.36), channel_id=1, source_target_pairs={{0,4},{1,5},{2,6},{3,7},{4,0},{5,1},{6,2},{7,3},{8,12},{9,13},{10,... | collective-permute-start | bytes 196616 | tf_op jit(solution)/shard_map/ppermute | solution.py:480
  17.8 12.9 %copy-start.8 = (s32[1,1024]{1,0:T(1,128)S(1)}, s32[1,1024]{1,0:T(1,128)}, u32[]{:S(2)}) copy-start(s32[1,1024]{1,0:T(1,128)} %seg.1) | copy-start | bytes 12292
  17.8 6.9 %collective-permute-start.5 = (bf16[16,16,128]{2,1,0:T(8,128)(2,1)S(1)}, bf16[16,16,128]{2,1,0:T(8,128)(2,1)S(1)}, u32[]{:S(2)}, u32[]{:S(2)}) collective-permute-start(bf16[16,16,128]{2,1,0:T(8,128)(2,1)S(1)} %get-tuple-element.37), channel_id=1, source_target_pairs={{0,5},{1,4},{2,7},{3,6},{4,1},{5,0},{6,3},{7,2},{8,13},{9,12},{10,... | collective-permute-start | bytes 196616 | tf_op jit(solution)/shard_map/ppermute | solution.py:480
  20.5 5.3 %collective-permute-start.6 = (bf16[16,16,128]{2,1,0:T(8,128)(2,1)S(1)}, bf16[16,16,128]{2,1,0:T(8,128)(2,1)S(1)}, u32[]{:S(2)}, u32[]{:S(2)}) collective-permute-start(bf16[16,16,128]{2,1,0:T(8,128)(2,1)S(1)} %get-tuple-element.38), channel_id=1, source_target_pairs={{0,6},{1,7},{2,4},{3,5},{4,2},{5,3},{6,0},{7,1},{8,14},{9,15},{10,... | collective-permute-start | bytes 196616 | tf_op jit(solution)/shard_map/ppermute | solution.py:480
  23.4 5.7 %collective-permute-start.7 = (bf16[16,16,128]{2,1,0:T(8,128)(2,1)S(1)}, bf16[16,16,128]{2,1,0:T(8,128)(2,1)S(1)}, u32[]{:S(2)}, u32[]{:S(2)}) collective-permute-start(bf16[16,16,128]{2,1,0:T(8,128)(2,1)S(1)} %get-tuple-element.39), channel_id=1, source_target_pairs={{0,7},{1,6},{2,5},{3,4},{4,3},{5,2},{6,1},{7,0},{8,15},{9,14},{10,... | collective-permute-start | bytes 196616 | tf_op jit(solution)/shard_map/ppermute | solution.py:480
  33.7 14.6 %all-to-all-start.1 = ((bf16[16,3,16,128]{3,2,1,0:T(8,128)(2,1)}), bf16[16,3,16,128]{3,2,1,0:T(8,128)(2,1)S(1)}, u32[]{:S(2)}, u32[]{:S(2)}) async-start(bf16[16,3,16,128]{3,2,1,0:T(8,128)(2,1)} %get-tuple-element.40), calls=%async_computation.1 | async-start | bytes 393216 | tf_op jit(solution)/shard_map/all_to_all | solution.py:592
  39.2 5.0 %collective-permute-start.8 = (bf16[2,2,16,128]{3,2,1,0:T(8,128)(2,1)S(1)}, bf16[2,2,16,128]{3,2,1,0:T(8,128)(2,1)S(1)}, u32[]{:S(2)}, u32[]{:S(2)}) collective-permute-start(bf16[2,2,16,128]{3,2,1,0:T(8,128)(2,1)S(1)} %get-tuple-element.41), channel_id=1, source_target_pairs={{0,6},{2,4},{4,2},{6,0},{1,7},{3,5},{5,3},{7,1},{8,14},{10,12},{12... | collective-permute-start | bytes 49160 | tf_op jit(solution)/shard_map/ppermute | solution.py:480
  42.0 3.8 %collective-permute-start.9 = (bf16[2,2,16,128]{3,2,1,0:T(8,128)(2,1)S(1)}, bf16[2,2,16,128]{3,2,1,0:T(8,128)(2,1)S(1)}, u32[]{:S(2)}, u32[]{:S(2)}) collective-permute-start(bf16[2,2,16,128]{3,2,1,0:T(8,128)(2,1)S(1)} %get-tuple-element.42), channel_id=1, source_target_pairs={{0,4},{2,6},{4,0},{6,2},{1,5},{3,7},{5,1},{7,3},{8,12},{10,14},{12... | collective-permute-start | bytes 49160 | tf_op jit(solution)/shard_map/ppermute | solution.py:480
  42.6 3.8 %collective-permute-start.10 = (bf16[2,2,16,128]{3,2,1,0:T(8,128)(2,1)S(1)}, bf16[2,2,16,128]{3,2,1,0:T(8,128)(2,1)S(1)}, u32[]{:S(2)}, u32[]{:S(2)}) collective-permute-start(bf16[2,2,16,128]{3,2,1,0:T(8,128)(2,1)S(1)} %get-tuple-element.43), channel_id=1, source_target_pairs={{0,2},{2,0},{4,6},{6,4},{1,3},{3,1},{5,7},{7,5},{8,10},{10,8},{12,... | collective-permute-start | bytes 49160 | tf_op jit(solution)/shard_map/ppermute | solution.py:480
  48.3 1.4 %collective-permute-start.11 = (bf16[28,16,128]{2,1,0:T(8,128)(2,1)S(1)}, bf16[28,16,128]{2,1,0:T(8,128)(2,1)S(1)}, u32[]{:S(2)}, u32[]{:S(2)}) collective-permute-start(bf16[28,16,128]{2,1,0:T(8,128)(2,1)S(1)} %shard_map.115.mine), channel_id=1, source_target_pairs={{0,1},{1,0},{2,3},{3,2},{4,5},{5,4},{6,7},{7,6},{8,9},{9,8},{10,11... | collective-permute-start | bytes 344072 | tf_op jit(solution)/shard_map/ppermute | solution.py:480
  59.5 6.2 %collective-permute-start.14 = (bf16[224,128]{1,0:T(8,128)(2,1)S(1)}, bf16[224,128]{1,0:T(8,128)(2,1)S(1)}, u32[]{:S(2)}, u32[]{:S(2)}) collective-permute-start(bf16[224,128]{1,0:T(8,128)(2,1)S(1)} %shard_map.117.rest_0_), channel_id=1, source_target_pairs={{0,24},{8,16},{16,8},{24,0},{1,25},{9,17},{17,9},{25,1},{2,26},{10... | collective-permute-start | bytes 172040 | tf_op jit(solution)/shard_map/ppermute | solution.py:480
  61.0 6.2 %collective-permute-start.13 = (bf16[224,128]{1,0:T(8,128)(2,1)S(1)}, bf16[224,128]{1,0:T(8,128)(2,1)S(1)}, u32[]{:S(2)}, u32[]{:S(2)}) collective-permute-start(bf16[224,128]{1,0:T(8,128)(2,1)S(1)} %shard_map.117.rest_0_), channel_id=1, source_target_pairs={{0,16},{8,24},{16,0},{24,8},{1,17},{9,25},{17,1},{25,9},{2,18},{10... | collective-permute-start | bytes 172040 | tf_op jit(solution)/shard_map/ppermute | solution.py:480
  61.4 5.8 %collective-permute-start.12 = (bf16[224,128]{1,0:T(8,128)(2,1)S(1)}, bf16[224,128]{1,0:T(8,128)(2,1)S(1)}, u32[]{:S(2)}, u32[]{:S(2)}) collective-permute-start(bf16[224,128]{1,0:T(8,128)(2,1)S(1)} %shard_map.117.rest_0_), channel_id=1, source_target_pairs={{0,8},{8,0},{16,24},{24,16},{1,9},{9,1},{17,25},{25,17},{2,10},{10... | collective-permute-start | bytes 172040 | tf_op jit(solution)/shard_map/ppermute | solution.py:480

commit v10 on v9

--- a/solution.py
+++ b/solution.py
@@ -64,7 +64,7 @@
 
             return slot + hit.astype(jnp.int32)
 
-        lax.fori_loop(0, live, over_position, jnp.int32(0))
+        lax.fori_loop(0, live, over_position, jnp.int32(0), unroll=True)
         return 0
 
     lax.fori_loop(0, groups, over_dest, 0)

time: 68.3 us -> 68.1 us (level)
  transfers between devices with their start and end apart: 17 -> 17, of which waited for: 11 -> 12; matrix products, arithmetic and copies ran while one was open for 0% -> 0% of each run, Pallas kernels for 2% -> 1%
where the time goes in v10:
time: 68.1 us; the launch traced here: 67.8 us
  starting transfers between devices  29.1 us (43%)
  waiting for transfers between devices  18.9 us (28%)
  Pallas kernels  9.5 us (14%)
  blocking collectives  7.88 us (12%)
  local copies, waits for them, and re-layouts  1.62 us (2%)
  between operations  0.79 us (1%)
    ppermute x15, starting transfers between devices, exchange(): lax.ppermute(value, axis, [(peer, peer ^ turn) for peer in range(size)])  16.4 us
    ppermute x15, waiting for transfers between devices, exchange(): lax.ppermute(value, axis, [(peer, peer ^ turn) for peer in range(size)])  15.3 us
    pallas_call x7, Pallas kernels, call(): pl.pallas_call(kernel, out_shape=shapes, in_specs=specs, out_specs=out_sp...  9.5 us
    all_to_all x1, blocking collectives, per_device_tiles(): shares = lax.all_to_all(shares, 'chip', 0, 0, tiled=True)  7.88 us
    all_to_all x1, starting transfers between devices, per_device_tiles(): far = lax.all_to_all(far_send, everyone, 0, 0, tiled=True)  7.3 us
    all_to_all x1, starting transfers between devices, per_device_tiles(): part = lax.all_to_all(attended[0], ('chip', 'dp'), 0, 0, tiled=True)  5.4 us
    all_to_all x1, waiting for transfers between devices, per_device_tiles(): part = lax.all_to_all(attended[0], ('chip', 'dp'), 0, 0, tiled=True)  1.97 us
    all_to_all x1, waiting for transfers between devices, per_device_tiles(): far = lax.all_to_all(far_send, everyone, 0, 0, tiled=True)  1.66 us
  transfers between devices with their start and end apart: 17, of which 12 were waited for; matrix products, arithmetic and copies ran while one was open for 0% of the time, Pallas kernels for 1%

profile of v10, /device:TPU:0, one launch (start us, length us, event | category | flops | bytes accessed | tf_op | source)
XLA Modules:
  0.0 67.8 jit_solution(4243003564603312584)
XLA Ops:
  0.6 2.9 %shard_map.112 = (bf16[32,6,16,128]{3,2,1,0:T(8,128)(2,1)}, bf16[8,16,1024]{2,1,0:T(8,128)(2,1)}, bf16[8,16,128]{2,1,0:T(8,128)(2,1)}) custom-call(s32[4,8]{1,0:T(4,128)} %plan.5, bf16[128,2560]{1,0:T(8,128)(2,1)} %bitcast.7, bf16[8,16,1024]{2,1,0:T(8,128)(2,1)} %bitcast.16, bf16[8,16,1024]{2,1,0:T(8,128)(2,1)} %bitcast.10, bf16[8,16,1024]{2,1,0:T(8,128)(2,1)} %bitcast.12, ...), custom_call_target="tpu_custom_call" | custom-call | flops 60000000 | bytes 4000000 | tf_op jit(solution)/shard_map/pallas_call | solution.py:468
  3.6 0.0 copy-start
  3.6 0.0 copy-start.1
  3.6 0.0 copy-start.2
  3.6 0.0 copy-start.3
  3.6 0.0 copy-start.6
  3.6 7.3 %all-to-all-start = ((bf16[32,6,16,128]{3,2,1,0:T(8,128)(2,1)}), bf16[32,6,16,128]{3,2,1,0:T(8,128)(2,1)S(1)}, u32[]{:S(2)}, u32[]{:S(2)}) async-start(bf16[32,6,16,128]{3,2,1,0:T(8,128)(2,1)} %get-tuple-element.31), calls=%async_computation | async-start | bytes 1572864 | tf_op jit(solution)/shard_map/all_to_all | solution.py:564
  10.9 0.0 copy-start.7
  11.0 0.6 copy-done.7
  11.6 0.9 %copy-done.4 = bf16[8,16,1024]{2,1,0:T(8,128)(2,1)S(1)} copy-done((bf16[8,16,1024]{2,1,0:T(8,128)(2,1)S(1)}, bf16[8,16,1024]{2,1,0:T(8,128)(2,1)}, u32[]{:S(2)}) %copy-start.4) | copy-done | bytes 262168
  12.6 0.9 %shard_map.113 = (bf16[16,16,128]{2,1,0:T(8,128)(2,1)S(1)}, bf16[16,16,128]{2,1,0:T(8,128)(2,1)S(1)}, bf16[16,16,128]{2,1,0:T(8,128)(2,1)S(1)}, bf16[16,16,128]{...) custom-call(s32[4,8]{1,0:T(4,128)S(1)} %copy-done.7, ...), custom_call_target="tpu_custom_call" | custom-call | bytes 1600000 | tf_op jit(solution)/shard_map/pallas_call | solution.py:468
  13.5 0.3 collective-permute-start
  13.9 0.3 collective-permute-start.1
  14.1 1.8 %collective-permute-start.2 = (bf16[16,16,128]{2,1,0:T(8,128)(2,1)S(1)}, bf16[16,16,128]{2,1,0:T(8,128)(2,1)S(1)}, u32[]{:S(2)}, u32[]{:S(2)}) collective-permute-start(bf16[16,16,128]{2,1,0:T(8,128)(2,1)S(1)} %get-tuple-element.34), channel_id=1, source_target_pairs={{0,2},{1,3},{2,0},{3,1},{4,6},{5,7},{6,4},{7,5},{8,10},{9,11},{10,... | collective-permute-start | bytes 196616 | tf_op jit(solution)/shard_map/ppermute | solution.py:480
  15.9 0.0 collective-permute-start.3
  15.9 1.5 %collective-permute-start.4 = (bf16[16,16,128]{2,1,0:T(8,128)(2,1)S(1)}, bf16[16,16,128]{2,1,0:T(8,128)(2,1)S(1)}, u32[]{:S(2)}, u32[]{:S(2)}) collective-permute-start(bf16[16,16,128]{2,1,0:T(8,128)(2,1)S(1)} %get-tuple-element.36), channel_id=1, source_target_pairs={{0,4},{1,5},{2,6},{3,7},{4,0},{5,1},{6,2},{7,3},{8,12},{9,13},{10,... | collective-permute-start | bytes 196616 | tf_op jit(solution)/shard_map/ppermute | solution.py:480
  17.4 0.0 collective-permute-done.1.rest_1_
  17.4 0.3 collective-permute-start.5
  17.7 2.4 %collective-permute-done.2.rest_2_ = bf16[16,16,128]{2,1,0:T(8,128)(2,1)S(1)} collective-permute-done((bf16[16,16,128]{2,1,0:T(8,128)(2,1)S(1)}, bf16[16,16,128]{2,1,0:T(8,128)(2,1)S(1)}, u32[]{:S(2)}, u32[]{:S(2)}) %collective-permute-start.2) | collective-permute-done | bytes 65568 | tf_op jit(solution)/shard_map/ppermute | solution.py:480
  20.1 3.0 %collective-permute-start.6 = (bf16[16,16,128]{2,1,0:T(8,128)(2,1)S(1)}, bf16[16,16,128]{2,1,0:T(8,128)(2,1)S(1)}, u32[]{:S(2)}, u32[]{:S(2)}) collective-permute-start(bf16[16,16,128]{2,1,0:T(8,128)(2,1)S(1)} %get-tuple-element.38), channel_id=1, source_target_pairs={{0,6},{1,7},{2,4},{3,5},{4,2},{5,3},{6,0},{7,1},{8,14},{9,15},{10,... | collective-permute-start | bytes 196616 | tf_op jit(solution)/shard_map/ppermute | solution.py:480
  23.1 0.0 collective-permute-done.3.rest_3_
  23.1 1.2 %collective-permute-start.7 = (bf16[16,16,128]{2,1,0:T(8,128)(2,1)S(1)}, bf16[16,16,128]{2,1,0:T(8,128)(2,1)S(1)}, u32[]{:S(2)}, u32[]{:S(2)}) collective-permute-start(bf16[16,16,128]{2,1,0:T(8,128)(2,1)S(1)} %get-tuple-element.39), channel_id=1, source_target_pairs={{0,7},{1,6},{2,5},{3,4},{4,3},{5,2},{6,1},{7,0},{8,15},{9,14},{10,... | collective-permute-start | bytes 196616 | tf_op jit(solution)/shard_map/ppermute | solution.py:480
  24.3 0.0 collective-permute-done.4.rest_4_
  24.3 0.1 collective-permute-done.5.rest_5_
  24.4 1.1 %collective-permute-done.6.rest_6_ = bf16[16,16,128]{2,1,0:T(8,128)(2,1)S(1)} collective-permute-done((bf16[16,16,128]{2,1,0:T(8,128)(2,1)S(1)}, bf16[16,16,128]{2,1,0:T(8,128)(2,1)S(1)}, u32[]{:S(2)}, u32[]{:S(2)}) %collective-permute-start.6) | collective-permute-done | bytes 65568 | tf_op jit(solution)/shard_map/ppermute | solution.py:480
  25.5 3.4 %collective-permute-done.7.rest_7_ = bf16[16,16,128]{2,1,0:T(8,128)(2,1)S(1)} collective-permute-done((bf16[16,16,128]{2,1,0:T(8,128)(2,1)S(1)}, bf16[16,16,128]{2,1,0:T(8,128)(2,1)S(1)}, u32[]{:S(2)}, u32[]{:S(2)}) %collective-permute-start.7) | collective-permute-done | bytes 65568 | tf_op jit(solution)/shard_map/ppermute | solution.py:480
  28.9 0.0 collective-permute-done.rest_8_.feat_other
  28.9 1.7 %all-to-all-done.far_in = bf16[32,6,16,128]{3,2,1,0:T(8,128)(2,1)S(1)} async-done(((bf16[32,6,16,128]{3,2,1,0:T(8,128)(2,1)}), bf16[32,6,16,128]{3,2,1,0:T(8,128)(2,1)S(1)}, u32[]{:S(2)}, u32[]{:S(2)}) %all-to-all-start) | async-done | bytes 786464 | tf_op jit(solution)/shard_map/all_to_all | solution.py:564
  30.6 3.0 %shard_map.114 = (bf16[16,3,16,128]{3,2,1,0:T(8,128)(2,1)}, bf16[2,2,16,128]{3,2,1,0:T(8,128)(2,1)S(1)}, bf16[2,2,16,128]{3,2,1,0:T(8,128)(2,1)S(1)}, bf16[2,2,1...) custom-call(s32[4,8]{1,0:T(4,128)S(1)} %copy-done.7, ...), custom_call_target="tpu_custom_call" | custom-call | flops 600000000 | bytes 3000000 | tf_op jit(solution)/shard_map/pallas_call | solution.py:468
  33.6 5.4 %all-to-all-start.1 = ((bf16[16,3,16,128]{3,2,1,0:T(8,128)(2,1)}), bf16[16,3,16,128]{3,2,1,0:T(8,128)(2,1)S(1)}, u32[]{:S(2)}, u32[]{:S(2)}) async-start(bf16[16,3,16,128]{3,2,1,0:T(8,128)(2,1)} %get-tuple-element.40), calls=%async_computation.1 | async-start | bytes 393216 | tf_op jit(solution)/shard_map/all_to_all | solution.py:592
  39.0 2.8 %collective-permute-start.8 = (bf16[2,2,16,128]{3,2,1,0:T(8,128)(2,1)S(1)}, bf16[2,2,16,128]{3,2,1,0:T(8,128)(2,1)S(1)}, u32[]{:S(2)}, u32[]{:S(2)}) collective-permute-start(bf16[2,2,16,128]{3,2,1,0:T(8,128)(2,1)S(1)} %get-tuple-element.41), channel_id=1, source_target_pairs={{0,6},{2,4},{4,2},{6,0},{1,7},{3,5},{5,3},{7,1},{8,14},{10,12},{12... | collective-permute-start | bytes 49160 | tf_op jit(solution)/shard_map/ppermute | solution.py:480
  41.8 0.6 collective-permute-start.9
  42.4 0.2 collective-permute-start.10
  42.6 1.5 %collective-permute-done.8.refs_0_ = bf16[2,2,16,128]{3,2,1,0:T(8,128)(2,1)S(1)} collective-permute-done((bf16[2,2,16,128]{3,2,1,0:T(8,128)(2,1)S(1)}, bf16[2,2,16,128]{3,2,1,0:T(8,128)(2,1)S(1)}, u32[]{:S(2)}, u32[]{:S(2)}) %collective-permute-start.8) | collective-permute-done | bytes 16416 | tf_op jit(solution)/shard_map/ppermute | solution.py:480
  44.0 1.7 %collective-permute-done.9.refs_1_ = bf16[2,2,16,128]{3,2,1,0:T(8,128)(2,1)S(1)} collective-permute-done((bf16[2,2,16,128]{3,2,1,0:T(8,128)(2,1)S(1)}, bf16[2,2,16,128]{3,2,1,0:T(8,128)(2,1)S(1)}, u32[]{:S(2)}, u32[]{:S(2)}) %collective-permute-start.9) | collective-permute-done | bytes 16416 | tf_op jit(solution)/shard_map/ppermute | solution.py:480
  45.7 0.5 collective-permute-done.10.refs_2_
  46.2 2.0 %all-to-all-done.1.parts = bf16[16,3,16,128]{3,2,1,0:T(8,128)(2,1)S(1)} async-done(((bf16[16,3,16,128]{3,2,1,0:T(8,128)(2,1)}), bf16[16,3,16,128]{3,2,1,0:T(8,128)(2,1)S(1)}, u32[]{:S(2)}, u32[]{:S(2)}) %all-to-all-start.1) | async-done | bytes 196640 | tf_op jit(solution)/shard_map/all_to_all | solution.py:592
  48.2 0.1 collective-permute-start.11
  48.3 1.3 %collective-permute-done.11.other = bf16[28,16,128]{2,1,0:T(8,128)(2,1)S(1)} collective-permute-done((bf16[28,16,128]{2,1,0:T(8,128)(2,1)S(1)}, bf16[28,16,128]{2,1,0:T(8,128)(2,1)S(1)}, u32[]{:S(2)}, u32[]{:S(2)}) %collective-permute-start.11) | collective-permute-done | bytes 114720 | tf_op jit(solution)/shard_map/ppermute | solution.py:480
  49.6 1.7 %shard_map.116 = (bf16[4,160,128]{2,1,0:T(8,128)(2,1)S(1)}, bf16[64,128]{1,0:T(8,128)(2,1)S(1)}) custom-call(s32[4,8]{1,0:T(4,128)S(1)} %copy-done.7, bf16[128,2560]{1,0:T(8,128)(2,1)S(1)} %bitcast.9, bf16[4,128,384]{2,1,0:T(8,128)(2,1)S(1)} %collective-permute-done.rest_8_.feat_other, bf16[28,16,128]{2,1,0:T(8,128)(2,1)S(1)} %shard_map.115.mine, ...), custom_call_target="tpu_custom_call" | custom-call | flops 60000000 | bytes 2000000 | tf_op jit(solution)/shard_map/pallas_call | solution.py:468
  51.3 7.9 %all_to_all.15.parts = bf16[4,160,128]{2,1,0:T(8,128)(2,1)S(1)} all-to-all(bf16[4,160,128]{2,1,0:T(8,128)(2,1)S(1)} %get-tuple-element.46), channel_id=1, replica_groups=mesh['dp'=4,'chip'=4,'core'=2] {'chip'}, dimensions={0} | all-to-all | bytes 327680 | tf_op jit(solution)/shard_map/all_to_all | solution.py:625
  59.2 1.5 %collective-permute-start.14 = (bf16[224,128]{1,0:T(8,128)(2,1)S(1)}, bf16[224,128]{1,0:T(8,128)(2,1)S(1)}, u32[]{:S(2)}, u32[]{:S(2)}) collective-permute-start(bf16[224,128]{1,0:T(8,128)(2,1)S(1)} %shard_map.117.rest_0_), channel_id=1, source_target_pairs={{0,24},{8,16},{16,8},{24,0},{1,25},{9,17},{17,9},{25,1},{2,26},{10... | collective-permute-start | bytes 172040 | tf_op jit(solution)/shard_map/ppermute | solution.py:480
  60.7 0.5 collective-permute-start.13
  61.2 2.5 %collective-permute-start.12 = (bf16[224,128]{1,0:T(8,128)(2,1)S(1)}, bf16[224,128]{1,0:T(8,128)(2,1)S(1)}, u32[]{:S(2)}, u32[]{:S(2)}) collective-permute-start(bf16[224,128]{1,0:T(8,128)(2,1)S(1)} %shard_map.117.rest_0_), channel_id=1, source_target_pairs={{0,8},{8,0},{16,24},{24,16},{1,9},{9,1},{17,25},{25,17},{2,10},{10... | collective-permute-start | bytes 172040 | tf_op jit(solution)/shard_map/ppermute | solution.py:480
  63.7 1.7 %collective-permute-done.14.rest_3_ = bf16[224,128]{1,0:T(8,128)(2,1)S(1)} collective-permute-done((bf16[224,128]{1,0:T(8,128)(2,1)S(1)}, bf16[224,128]{1,0:T(8,128)(2,1)S(1)}, u32[]{:S(2)}, u32[]{:S(2)}) %collective-permute-start.14) | collective-permute-done | bytes 57376 | tf_op jit(solution)/shard_map/ppermute | solution.py:480
  65.4 1.5 %collective-permute-done.13.rest_2_ = bf16[224,128]{1,0:T(8,128)(2,1)S(1)} collective-permute-done((bf16[224,128]{1,0:T(8,128)(2,1)S(1)}, bf16[224,128]{1,0:T(8,128)(2,1)S(1)}, u32[]{:S(2)}, u32[]{:S(2)}) %collective-permute-start.13) | collective-permute-done | bytes 57376 | tf_op jit(solution)/shard_map/ppermute | solution.py:480
  66.9 0.0 collective-permute-done.12.rest_1_
  66.9 0.8 %shard_map.118 = (f32[64,320]{1,0:T(8,128)}, f32[64,128]{1,0:T(8,128)}) custom-call(bf16[224,128]{1,0:T(8,128)(2,1)S(1)} %shard_map.117.rest_0_, bf16[224,128]{1,0:T(8,128)(2,1)S(1)} %collective-permute-done.12.rest_1_, bf16[224,128]{1,0:T(8,128)(2,1)S(1)} %collective-permute-done.13.rest_2_, bf16[224,128]{1,0:T(8,128)(2,1)S(1)} %collective-permute-done.14.rest_3_), custom_call_target="tpu_custom_call" | custom-call | bytes 400000 | tf_op jit(solution)/shard_map/pallas_call | solution.py:468
  (12 shorter events, 0.1 us)
Async XLA Ops:
  3.6 7.4 %copy-start = (bf16[1,8,16,2560]{3,2,1,0:T(8,128)(2,1)S(1)}, bf16[1,8,16,2560]{3,2,1,0:T(8,128)(2,1)}, u32[]{:S(2)}) copy-start(bf16[1,8,16,2560]{3,2,1,0:T(8,128)(2,1)} %param.9) | copy-start | bytes 1966084
  3.6 7.4 %copy-start.1 = (bf16[1,8,16,1024]{3,2,1,0:T(8,128)(2,1)S(1)}, bf16[1,8,16,1024]{3,2,1,0:T(8,128)(2,1)}, u32[]{:S(2)}) copy-start(bf16[1,8,16,1024]{3,2,1,0:T(8,128)(2,1)} %param.11) | copy-start | bytes 786436
  3.6 7.4 %copy-start.2 = (bf16[1,8,16,1024]{3,2,1,0:T(8,128)(2,1)S(1)}, bf16[1,8,16,1024]{3,2,1,0:T(8,128)(2,1)}, u32[]{:S(2)}) copy-start(bf16[1,8,16,1024]{3,2,1,0:T(8,128)(2,1)} %param.12) | copy-start | bytes 786436
  3.6 7.4 %copy-start.3 = (bf16[1,8,16,1024]{3,2,1,0:T(8,128)(2,1)S(1)}, bf16[1,8,16,1024]{3,2,1,0:T(8,128)(2,1)}, u32[]{:S(2)}) copy-start(bf16[1,8,16,1024]{3,2,1,0:T(8,128)(2,1)} %param.13) | copy-start | bytes 786436
  3.6 7.4 %copy-start.6 = (bf16[8,16,128]{2,1,0:T(8,128)(2,1)S(1)}, bf16[8,16,128]{2,1,0:T(8,128)(2,1)}, u32[]{:S(2)}) copy-start(bf16[8,16,128]{2,1,0:T(8,128)(2,1)} %get-tuple-element.28.adapter) | copy-start | bytes 98308
  3.6 26.9 %all-to-all-start = ((bf16[32,6,16,128]{3,2,1,0:T(8,128)(2,1)}), bf16[32,6,16,128]{3,2,1,0:T(8,128)(2,1)S(1)}, u32[]{:S(2)}, u32[]{:S(2)}) async-start(bf16[32,6,16,128]{3,2,1,0:T(8,128)(2,1)} %get-tuple-element.31), calls=%async_computation | async-start | bytes 1572864 | tf_op jit(solution)/shard_map/all_to_all | solution.py:564
  10.9 0.7 %copy-start.7 = (s32[4,8]{1,0:T(4,128)S(1)}, s32[4,8]{1,0:T(4,128)}, u32[]{:S(2)}) copy-start(s32[4,8]{1,0:T(4,128)} %plan.5) | copy-start | bytes 388
  11.6 0.9 %copy-start.4 = (bf16[8,16,1024]{2,1,0:T(8,128)(2,1)S(1)}, bf16[8,16,1024]{2,1,0:T(8,128)(2,1)}, u32[]{:S(2)}) copy-start(bf16[8,16,1024]{2,1,0:T(8,128)(2,1)} %get-tuple-element.27.queries) | copy-start | bytes 786436
  12.6 18.0 %copy-start.5 = (bf16[64,1024]{1,0:T(8,128)(2,1)S(1)}, bf16[64,1024]{1,0:T(8,128)(2,1)}, u32[]{:S(2)}) copy-start(bf16[64,1024]{1,0:T(8,128)(2,1)} %up.1) | copy-start | bytes 393220
  13.5 15.4 %collective-permute-start = (bf16[4,128,384]{2,1,0:T(8,128)(2,1)S(1)}, bf16[4,128,384]{2,1,0:T(8,128)(2,1)S(1)}, u32[]{:S(2)}, u32[]{:S(2)}) collective-permute-start(bf16[4,128,384]{2,1,0:T(8,128)(2,1)S(1)} %get-tuple-element.29), channel_id=1, source_target_pairs={{0,1},{1,0},{2,3},{3,2},{4,5},{5,4},{6,7},{7,6},{8,9},{9,8},{10,11... | collective-permute-start | bytes 1179656 | tf_op jit(solution)/shard_map/ppermute | solution.py:480
  13.9 3.5 %collective-permute-start.1 = (bf16[16,16,128]{2,1,0:T(8,128)(2,1)S(1)}, bf16[16,16,128]{2,1,0:T(8,128)(2,1)S(1)}, u32[]{:S(2)}, u32[]{:S(2)}) collective-permute-start(bf16[16,16,128]{2,1,0:T(8,128)(2,1)S(1)} %get-tuple-element.33), channel_id=1, source_target_pairs={{0,1},{1,0},{2,3},{3,2},{4,5},{5,4},{6,7},{7,6},{8,9},{9,8},{10,11... | collective-permute-start | bytes 196616 | tf_op jit(solution)/shard_map/ppermute | solution.py:480
  14.1 6.0 %collective-permute-start.2 = (bf16[16,16,128]{2,1,0:T(8,128)(2,1)S(1)}, bf16[16,16,128]{2,1,0:T(8,128)(2,1)S(1)}, u32[]{:S(2)}, u32[]{:S(2)}) collective-permute-start(bf16[16,16,128]{2,1,0:T(8,128)(2,1)S(1)} %get-tuple-element.34), channel_id=1, source_target_pairs={{0,2},{1,3},{2,0},{3,1},{4,6},{5,7},{6,4},{7,5},{8,10},{9,11},{10,... | collective-permute-start | bytes 196616 | tf_op jit(solution)/shard_map/ppermute | solution.py:480
  15.9 7.2 %collective-permute-start.3 = (bf16[16,16,128]{2,1,0:T(8,128)(2,1)S(1)}, bf16[16,16,128]{2,1,0:T(8,128)(2,1)S(1)}, u32[]{:S(2)}, u32[]{:S(2)}) collective-permute-start(bf16[16,16,128]{2,1,0:T(8,128)(2,1)S(1)} %get-tuple-element.35), channel_id=1, source_target_pairs={{0,3},{1,2},{2,1},{3,0},{4,7},{5,6},{6,5},{7,4},{8,11},{9,10},{10,... | collective-permute-start | bytes 196616 | tf_op jit(solution)/shard_map/ppermute | solution.py:480
  15.9 8.4 %collective-permute-start.4 = (bf16[16,16,128]{2,1,0:T(8,128)(2,1)S(1)}, bf16[16,16,128]{2,1,0:T(8,128)(2,1)S(1)}, u32[]{:S(2)}, u32[]{:S(2)}) collective-permute-start(bf16[16,16,128]{2,1,0:T(8,128)(2,1)S(1)} %get-tuple-element.36), channel_id=1, source_target_pairs={{0,4},{1,5},{2,6},{3,7},{4,0},{5,1},{6,2},{7,3},{8,12},{9,13},{10,... | collective-permute-start | bytes 196616 | tf_op jit(solution)/shard_map/ppermute | solution.py:480
  17.4 13.2 %copy-start.8 = (s32[1,1024]{1,0:T(1,128)S(1)}, s32[1,1024]{1,0:T(1,128)}, u32[]{:S(2)}) copy-start(s32[1,1024]{1,0:T(1,128)} %seg.1) | copy-start | bytes 12292
  17.4 7.0 %collective-permute-start.5 = (bf16[16,16,128]{2,1,0:T(8,128)(2,1)S(1)}, bf16[16,16,128]{2,1,0:T(8,128)(2,1)S(1)}, u32[]{:S(2)}, u32[]{:S(2)}) collective-permute-start(bf16[16,16,128]{2,1,0:T(8,128)(2,1)S(1)} %get-tuple-element.37), channel_id=1, source_target_pairs={{0,5},{1,4},{2,7},{3,6},{4,1},{5,0},{6,3},{7,2},{8,13},{9,12},{10,... | collective-permute-start | bytes 196616 | tf_op jit(solution)/shard_map/ppermute | solution.py:480
  20.1 5.4 %collective-permute-start.6 = (bf16[16,16,128]{2,1,0:T(8,128)(2,1)S(1)}, bf16[16,16,128]{2,1,0:T(8,128)(2,1)S(1)}, u32[]{:S(2)}, u32[]{:S(2)}) collective-permute-start(bf16[16,16,128]{2,1,0:T(8,128)(2,1)S(1)} %get-tuple-element.38), channel_id=1, source_target_pairs={{0,6},{1,7},{2,4},{3,5},{4,2},{5,3},{6,0},{7,1},{8,14},{9,15},{10,... | collective-permute-start | bytes 196616 | tf_op jit(solution)/shard_map/ppermute | solution.py:480
  23.1 5.8 %collective-permute-start.7 = (bf16[16,16,128]{2,1,0:T(8,128)(2,1)S(1)}, bf16[16,16,128]{2,1,0:T(8,128)(2,1)S(1)}, u32[]{:S(2)}, u32[]{:S(2)}) collective-permute-start(bf16[16,16,128]{2,1,0:T(8,128)(2,1)S(1)} %get-tuple-element.39), channel_id=1, source_target_pairs={{0,7},{1,6},{2,5},{3,4},{4,3},{5,2},{6,1},{7,0},{8,15},{9,14},{10,... | collective-permute-start | bytes 196616 | tf_op jit(solution)/shard_map/ppermute | solution.py:480
  33.6 14.6 %all-to-all-start.1 = ((bf16[16,3,16,128]{3,2,1,0:T(8,128)(2,1)}), bf16[16,3,16,128]{3,2,1,0:T(8,128)(2,1)S(1)}, u32[]{:S(2)}, u32[]{:S(2)}) async-start(bf16[16,3,16,128]{3,2,1,0:T(8,128)(2,1)} %get-tuple-element.40), calls=%async_computation.1 | async-start | bytes 393216 | tf_op jit(solution)/shard_map/all_to_all | solution.py:592
  39.0 5.0 %collective-permute-start.8 = (bf16[2,2,16,128]{3,2,1,0:T(8,128)(2,1)S(1)}, bf16[2,2,16,128]{3,2,1,0:T(8,128)(2,1)S(1)}, u32[]{:S(2)}, u32[]{:S(2)}) collective-permute-start(bf16[2,2,16,128]{3,2,1,0:T(8,128)(2,1)S(1)} %get-tuple-element.41), channel_id=1, source_target_pairs={{0,6},{2,4},{4,2},{6,0},{1,7},{3,5},{5,3},{7,1},{8,14},{10,12},{12... | collective-permute-start | bytes 49160 | tf_op jit(solution)/shard_map/ppermute | solution.py:480
  41.8 3.9 %collective-permute-start.9 = (bf16[2,2,16,128]{3,2,1,0:T(8,128)(2,1)S(1)}, bf16[2,2,16,128]{3,2,1,0:T(8,128)(2,1)S(1)}, u32[]{:S(2)}, u32[]{:S(2)}) collective-permute-start(bf16[2,2,16,128]{3,2,1,0:T(8,128)(2,1)S(1)} %get-tuple-element.42), channel_id=1, source_target_pairs={{0,4},{2,6},{4,0},{6,2},{1,5},{3,7},{5,1},{7,3},{8,12},{10,14},{12... | collective-permute-start | bytes 49160 | tf_op jit(solution)/shard_map/ppermute | solution.py:480
  42.4 3.8 %collective-permute-start.10 = (bf16[2,2,16,128]{3,2,1,0:T(8,128)(2,1)S(1)}, bf16[2,2,16,128]{3,2,1,0:T(8,128)(2,1)S(1)}, u32[]{:S(2)}, u32[]{:S(2)}) collective-permute-start(bf16[2,2,16,128]{3,2,1,0:T(8,128)(2,1)S(1)} %get-tuple-element.43), channel_id=1, source_target_pairs={{0,2},{2,0},{4,6},{6,4},{1,3},{3,1},{5,7},{7,5},{8,10},{10,8},{12,... | collective-permute-start | bytes 49160 | tf_op jit(solution)/shard_map/ppermute | solution.py:480
  48.2 1.4 %collective-permute-start.11 = (bf16[28,16,128]{2,1,0:T(8,128)(2,1)S(1)}, bf16[28,16,128]{2,1,0:T(8,128)(2,1)S(1)}, u32[]{:S(2)}, u32[]{:S(2)}) collective-permute-start(bf16[28,16,128]{2,1,0:T(8,128)(2,1)S(1)} %shard_map.115.mine), channel_id=1, source_target_pairs={{0,1},{1,0},{2,3},{3,2},{4,5},{5,4},{6,7},{7,6},{8,9},{9,8},{10,11... | collective-permute-start | bytes 344072 | tf_op jit(solution)/shard_map/ppermute | solution.py:480
  59.2 6.2 %collective-permute-start.14 = (bf16[224,128]{1,0:T(8,128)(2,1)S(1)}, bf16[224,128]{1,0:T(8,128)(2,1)S(1)}, u32[]{:S(2)}, u32[]{:S(2)}) collective-permute-start(bf16[224,128]{1,0:T(8,128)(2,1)S(1)} %shard_map.117.rest_0_), channel_id=1, source_target_pairs={{0,24},{8,16},{16,8},{24,0},{1,25},{9,17},{17,9},{25,1},{2,26},{10... | collective-permute-start | bytes 172040 | tf_op jit(solution)/shard_map/ppermute | solution.py:480
  60.7 6.2 %collective-permute-start.13 = (bf16[224,128]{1,0:T(8,128)(2,1)S(1)}, bf16[224,128]{1,0:T(8,128)(2,1)S(1)}, u32[]{:S(2)}, u32[]{:S(2)}) collective-permute-start(bf16[224,128]{1,0:T(8,128)(2,1)S(1)} %shard_map.117.rest_0_), channel_id=1, source_target_pairs={{0,16},{8,24},{16,0},{24,8},{1,17},{9,25},{17,1},{25,9},{2,18},{10... | collective-permute-start | bytes 172040 | tf_op jit(solution)/shard_map/ppermute | solution.py:480
  61.2 5.7 %collective-permute-start.12 = (bf16[224,128]{1,0:T(8,128)(2,1)S(1)}, bf16[224,128]{1,0:T(8,128)(2,1)S(1)}, u32[]{:S(2)}, u32[]{:S(2)}) collective-permute-start(bf16[224,128]{1,0:T(8,128)(2,1)S(1)} %shard_map.117.rest_0_), channel_id=1, source_target_pairs={{0,8},{8,0},{16,24},{24,16},{1,9},{9,1},{17,25},{25,17},{2,10},{10... | collective-permute-start | bytes 172040 | tf_op jit(solution)/shard_map/ppermute | solution.py:480
